TPU v7x, 512 devices: a whole 4x4x16 slice. The times are simulated.
512 devices in a mesh: ep: 128 (over x, z, core), dp: 4 (over y).
Axes of the slice: x: 4, y: 4, z: 16, core: 2. Of those that a mesh axis runs over, the one named last changes fastest.
Arguments:
- tokens: bfloat16 [2, 4096, 3584], P(None, ('dp', 'ep')), parts along dimension 1, may hold values from -6 to 6
- expert_ids: int32 [2, 4096, 2], P(None, ('dp', 'ep')), parts along dimension 1, may hold values from 0 to 15, all different within a row; in each aligned block of 8 rows (0 to 7, 8 to 15, ..., all dimensions but the last counted through in order) at most 2 rows name the same one
- gate_scores: float32 [2, 4096, 2], P(None, ('dp', 'ep')), parts along dimension 1, may hold values from 0.2 to 1
- expert_weights: bfloat16 [128, 3584, 576], P('ep')
Outputs:
- mixed: bfloat16 [2, 4096, 3584], P(None, ('dp', 'ep')), parts along dimension 1
There are 4 independent parts, one for each index of `dp`. A program takes and returns all parts, laid end to end along the dimension named above; an argument that names none is the same for every part. Nothing has to cross between parts.
Inputs may be any that keep to these rules, and one draw needn't show every extreme that they name: `expert_ids`: each row names 2 different experts; in each micro-batch no expert is named by more than 2 of one device's 8 rows, a bound that some block reaches of them.
All inputs are finite; a program needn't handle non-finite values.
Results may differ from a plain program's by a relative error of at most 0.0057.
Values may be sent and summed in bfloat16 or wider, within the bound.
No kernel may reach another device: no remote copies, remote signals or barrier semaphores. Data moves between devices by JAX's collectives and lax.ppermute only.
A program may use at most 64 MiB of HBM per device.

v0:
```python
import jax
import jax.numpy as jnp
from jax import lax
from jax.sharding import PartitionSpec as P

FF = 1536


def expert_block(row_block, shard_weights, unit_count):
    projected = jnp.dot(
        row_block, shard_weights[:, : 2 * unit_count], preferred_element_type=jnp.float32
    )
    hidden = (jax.nn.silu(projected[:, :unit_count]) * projected[:, unit_count:]).astype(
        jnp.bfloat16
    )
    down_part = shard_weights[:, 2 * unit_count :]
    return lax.dot_general(
        hidden, down_part, (((1,), (1,)), ((), ())), preferred_element_type=jnp.float32
    ).astype(jnp.bfloat16)


def run_section(section, shard_weights, unit_count):
    model_width = section.shape[3]
    result = expert_block(section.reshape(-1, model_width), shard_weights, unit_count)
    return result.reshape(section.shape)


def apply_slots(received, home_weights, spare_weights, home_count, unit_count):
    first = run_section(received[:, :, :home_count], home_weights, unit_count)
    second = run_section(received[:, :, home_count:], spare_weights, unit_count)
    return jnp.concatenate([first, second], axis=2)


def on_device(tokens, expert_ids, gate_scores, expert_weights):
    devices = lax.axis_size("ep")
    unit_count = expert_weights.shape[2] // 3
    group_size = FF // unit_count
    experts = devices // group_size
    batches, row_count, model_width = tokens.shape
    pick_count = expert_ids.shape[2]
    capacity = max(2, row_count * pick_count // experts + 1)
    home_count = capacity - capacity // 2
    home_weights = expert_weights[0]
    matches = (expert_ids[..., None] == jnp.arange(experts, dtype=jnp.int32)).astype(jnp.int32)
    present = jnp.sum(matches, axis=2)
    before = jnp.cumsum(present, axis=1) - present
    occurrence = jnp.sum(matches * before[:, :, None, :], axis=3)
    groups = jnp.arange(experts, dtype=jnp.int32)
    slot_index = jnp.arange(capacity, dtype=jnp.int32)
    landing = (
        (expert_ids[..., None, None] == groups[:, None])
        & (occurrence[..., None, None] == slot_index)
    ).astype(jnp.float32)
    selector = jnp.sum(landing, axis=2)
    weighting = jnp.sum(landing * gate_scores[..., None, None], axis=2)
    packed = jnp.einsum(
        "mres,mrd->emsd", selector.astype(jnp.bfloat16), tokens, preferred_element_type=jnp.float32
    ).astype(jnp.bfloat16)
    outgoing = jnp.repeat(packed, group_size, axis=0)
    done = apply_slots(
        lax.all_to_all(outgoing, "ep", split_axis=0, concat_axis=0, tiled=True),
        home_weights,
        home_weights,
        home_count,
        unit_count,
    )
    returned = lax.all_to_all(done, "ep", split_axis=0, concat_axis=0, tiled=True)
    summed = jnp.sum(
        returned.reshape(experts, group_size, batches, capacity, model_width),
        axis=1,
        dtype=jnp.float32,
    )
    mixed = jnp.einsum("mres,emsd->mrd", weighting, summed, precision=lax.Precision.HIGHEST)
    return mixed.astype(jnp.bfloat16)


def solution(mesh):
    return jax.shard_map(
        on_device,
        mesh=mesh,
        in_specs=(
            P(None, ("dp", "ep"), None),
            P(None, ("dp", "ep"), None),
            P(None, ("dp", "ep"), None),
            P("ep", None, None),
        ),
        out_specs=P(None, ("dp", "ep"), None),
        check_vma=False,
    )
```

profile of v0, /device:TPU:24, one launch (start us, length us, event | category | flops | bytes accessed | tf_op | source)
XLA Modules:
  0.0 410.5 jit_solution(15076218725674472873)
XLA Ops:
  0.0 0.0 copy-start
  0.0 0.8 iota_compare_fusion
  0.8 0.8 convert_reduce_fusion.1
  1.6 0.9 select_reduce_fusion
  2.5 0.8 fusion.17
  3.3 0.0 copy-done
  3.3 0.3 fusion
  3.6 0.5 copy.18
  4.1 1.9 broadcast_in_dim.2
  6.0 185.0 %all_to_all.10 = bf16[128,2,2,3584]{3,1,2,0:T(2,128)(2,1)S(1)} all-to-all(bf16[128,2,2,3584]{3,1,2,0:T(2,128)(2,1)S(1)} %bitcast.27), channel_id=1, replica_groups=mesh['ep'=128,'dp'=4] {'ep'}, dimensions={0} | all-to-all | bytes 7340032 | tf_op jit(solution)/shard_map/all_to_all | solution.py:61
  191.0 3.8 fusion.21
  194.8 4.9 %reshape.46 = bf16[256,3584]{1,0:T(8,128)(2,1)} reshape(bf16[128,2,1,3584]{3,1,2,0:T(2,128)(2,1)} %get-tuple-element.7) | data formatting | bytes 3670016 | tf_op jit(solution)/shard_map/reshape | solution.py:24
  199.7 3.5 fusion.4
  203.2 3.3 convolution_convert_fusion.1
  206.4 4.8 %reshape.47 = bf16[128,2,1,3584]{3,1,0,2:T(2,128)(2,1)} reshape(bf16[256,3584]{1,0:T(8,128)(2,1)} %convolution_convert_fusion.1) | data formatting | bytes 3670016 | tf_op jit(solution)/shard_map/reshape | solution.py:25
  211.2 1.6 reshape.48
  212.9 3.4 fusion.2
  216.3 3.3 convolution_convert_fusion
  219.6 0.0 copy-start.1
  219.6 4.9 %reshape.49 = bf16[128,2,1,3584]{3,1,0,2:T(2,128)(2,1)} reshape(bf16[256,3584]{1,0:T(8,128)(2,1)} %convolution_convert_fusion) | data formatting | bytes 3670016 | tf_op jit(solution)/shard_map/reshape | solution.py:25
  224.5 0.0 copy-done.1
  224.5 6.4 %pad_maximum_fusion = bf16[128,2,2,3584]{3,1,2,0:T(2,128)(2,1)S(1)} fusion(bf16[128,2,1,3584]{3,1,2,0:T(2,128)(2,1)} %bitcast.29, bf16[128,2,1,3584]{3,1,2,0:T(2,128)(2,1)S(1)} %bitcast.28), kind=kLoop, calls=%fused_computation.7 | loop fusion | flops 1835008 | bytes 7340032 | tf_op jit(solution)/shard_map/concatenate | solution.py:31
  230.9 175.1 %all_to_all.11 = bf16[128,2,2,3584]{3,1,2,0:T(2,128)(2,1)S(1)} all-to-all(bf16[128,2,2,3584]{3,1,2,0:T(2,128)(2,1)S(1)} %pad_maximum_fusion), channel_id=1, replica_groups=mesh['ep'=128,'dp'=4] {'ep'}, dimensions={0} | all-to-all | bytes 7340032 | tf_op jit(solution)/shard_map/all_to_all | solution.py:67
  405.9 3.2 convert_reduce_fusion
  409.1 1.4 fusion.1
  (3 shorter events, 0.0 us)
Async XLA Ops:
  0.0 3.3 copy-start
  219.6 4.9 %copy-start.1 = (bf16[128,2,1,3584]{3,1,0,2:T(2,128)(2,1)S(1)}, bf16[128,2,1,3584]{3,1,0,2:T(2,128)(2,1)}, u32[]{:S(2)}) copy-start(bf16[128,2,1,3584]{3,1,0,2:T(2,128)(2,1)} %reshape.47) | copy-start | bytes 5505028
where the time goes:
time: 412 us; the launch traced here: 411 us
  blocking collectives  360 us (87%)
  local copies, waits for them, and re-layouts  22.4 us (5%)
  matrix products  15.2 us (4%)
  other arithmetic  12.8 us (3%)
    all_to_all x1, blocking collectives, on_device(): lax.all_to_all(outgoing, 'ep', split_axis=0, concat_axis=0, tiled=True)  185 us
    all_to_all x1, blocking collectives, on_device(): lax.all_to_all(done, 'ep', split_axis=0, concat_axis=0, tiled=True)  175 us
    reshape x2, local copies, waits for them, and re-layouts, run_section(): return result.reshape(section.shape)  9.67 us

commit v1 on v0

v1 whole, which is shorter than its diff:
```python
import jax
import jax.numpy as jnp
from jax import lax
from jax.sharding import Mesh, PartitionSpec as P

FF = 1536
BF = jnp.bfloat16
F32 = jnp.float32
ROWS_OF = ("x", "zb")


def expert_block(rows, weights):
    units = weights.shape[1] // 3
    projected = jnp.dot(rows, weights[:, : 2 * units], preferred_element_type=F32)
    hidden = (jax.nn.silu(projected[:, :units]) * projected[:, units:]).astype(BF)
    return lax.dot_general(
        hidden, weights[:, 2 * units :], (((1,), (1,)), ((), ())), preferred_element_type=F32
    )


def on_device(tokens, expert_ids, gate_scores, expert_weights):
    batches, row_count, width = tokens.shape
    experts = lax.axis_size("x") * lax.axis_size("zb")
    line = lax.axis_size("zi")
    capacity = 2
    slots = batches * capacity
    own = expert_weights[0]
    other = lax.ppermute(own, "c", [(0, 1), (1, 0)])

    matches = (expert_ids[..., None] == jnp.arange(experts, dtype=jnp.int32)).astype(jnp.int32)
    present = jnp.sum(matches, axis=2)
    before = jnp.cumsum(present, axis=1) - present
    occurrence = jnp.sum(matches * before[:, :, None, :], axis=3)
    slot = jnp.arange(capacity, dtype=jnp.int32)
    landing = (
        (expert_ids[..., None, None] == jnp.arange(experts, dtype=jnp.int32)[:, None])
        & (occurrence[..., None, None] == slot)
    ).astype(F32)
    selector = jnp.sum(landing, axis=2)
    weighting = jnp.sum(landing * gate_scores[..., None, None], axis=2)
    packed = jnp.einsum("mres,mrd->emsd", selector.astype(BF), tokens, preferred_element_type=F32)
    packed = packed.astype(BF).reshape(experts, slots, width)

    arrived = lax.all_to_all(packed, ROWS_OF, split_axis=0, concat_axis=0, tiled=True)
    half = experts // 2
    first = lax.all_gather(arrived[:half], "zi", axis=0)
    second = lax.all_gather(arrived[half:], "zi", axis=0)
    rows = jnp.concatenate([first, second], axis=1).reshape(-1, width)
    part = (expert_block(rows, own) + expert_block(rows, other)).astype(BF)
    part = part.reshape(line, experts * slots, width)
    parts = lax.all_to_all(part, "zi", split_axis=0, concat_axis=0, tiled=True)
    summed = jnp.sum(parts, axis=0, dtype=F32).astype(BF).reshape(experts, slots, width)
    returned = lax.all_to_all(summed, ROWS_OF, split_axis=0, concat_axis=0, tiled=True)
    returned = returned.reshape(experts, batches, capacity, width).astype(F32)
    mixed = jnp.einsum("mres,emsd->mrd", weighting, returned, precision=lax.Precision.HIGHEST)
    return mixed.astype(BF)


def solution(mesh):
    fine = Mesh(mesh.devices.reshape(4, 4, 4, 2, 4), ("x", "zb", "zi", "c", "dp"))
    ep = ("x", "zb", "zi", "c")
    by_row = P(None, ("dp",) + ep, None)
    return jax.shard_map(
        on_device,
        mesh=fine,
        in_specs=(by_row, by_row, by_row, P(ep, None, None)),
        out_specs=by_row,
        check_vma=False,
    )
```

time: 412 us -> 180 us (0.44)
  blocking collectives: 360 us -> 114 us
  waiting for transfers between devices: 0 us -> 23.4 us
  starting transfers between devices: 0 us -> 19.6 us
  local copies, waits for them, and re-layouts: 22.4 us -> 2.96 us
  other arithmetic: 12.8 us -> 4.81 us
    all_to_all x2, blocking collectives: 360 us -> 70.4 us  [the longest x1 41.7 us: on_device(): parts = lax.all_to_all(part, 'zi', split_axis=0, concat_axis=0, tiled=True)]
    all_gather x0 -> x2, blocking collectives: none -> 43.3 us  [the longest x1 24.8 us: on_device(): first = lax.all_gather(arrived[:half], 'zi', axis=0)]
    all_to_all x0 -> x1, waiting for transfers between devices: none -> 23.4 us  [on_device(): lax.all_to_all(packed, ROWS_OF, split_axis=0, concat_axis=0, tiled=True)]
    all_to_all x0 -> x1, starting transfers between devices: none -> 17.7 us  [on_device(): lax.all_to_all(packed, ROWS_OF, split_axis=0, concat_axis=0, tiled=True)]
    reshape x4 -> x3, local copies, waits for them, and re-layouts: 16.2 us -> 2.72 us  [the longest x1 1.48 us: on_device(): rows = jnp.concatenate([first, second], axis=1).reshape(-1, width)]
    concatenate x1, other arithmetic: 6.35 us -> 1.18 us  [on_device(): rows = jnp.concatenate([first, second], axis=1).reshape(-1, width)]
  transfers between devices with their start and end apart: 0 -> 2, of which waited for: 0 -> 1; matrix products, arithmetic and copies ran while one was open for 0% -> 5% of each run, Pallas kernels for 0% -> 0%
where the time goes in v1:
time: 180 us; the launch traced here: 176 us
  blocking collectives  114 us (63%)
  waiting for transfers between devices  23.4 us (13%)
  starting transfers between devices  19.6 us (11%)
  matrix products  11.9 us (7%)
  other arithmetic  4.81 us (3%)
  local copies, waits for them, and re-layouts  2.96 us (2%)
    all_to_all x1, blocking collectives, on_device(): parts = lax.all_to_all(part, 'zi', split_axis=0, concat_axis=0, tiled=True)  41.7 us
    all_to_all x1, blocking collectives, on_device(): lax.all_to_all(summed, ROWS_OF, split_axis=0, concat_axis=0, tiled=True)  28.7 us
    all_gather x1, blocking collectives, on_device(): first = lax.all_gather(arrived[:half], 'zi', axis=0)  24.8 us
    all_to_all x1, waiting for transfers between devices, on_device(): lax.all_to_all(packed, ROWS_OF, split_axis=0, concat_axis=0, tiled=True)  23.4 us
    all_gather x1, blocking collectives, on_device(): second = lax.all_gather(arrived[half:], 'zi', axis=0)  18.5 us
    all_to_all x1, starting transfers between devices, on_device(): lax.all_to_all(packed, ROWS_OF, split_axis=0, concat_axis=0, tiled=True)  17.7 us
    dot_general x2, matrix products, expert_block(): jnp.dot(rows, weights[:, :2 * units], preferred_element_type=F32)  6.35 us
    dot_general x2, matrix products, expert_block(): lax.dot_general(hidden, weights[:, 2 * units:], (((1,), (1,)), ((), ())),...  4.2 us
  transfers between devices with their start and end apart: 2, of which 1 were waited for; matrix products, arithmetic and copies ran while one was open for 5% of the time, Pallas kernels for 0%

profile of v1, /device:TPU:24, one launch (start us, length us, event | category | flops | bytes accessed | tf_op | source)
XLA Modules:
  0.0 176.5 jit_solution(3767449012768454245)
XLA Ops:
  0.0 0.0 copy-start
  0.0 0.8 iota_compare_fusion
  0.8 0.8 convert_reduce_fusion
  1.6 0.9 select_reduce_fusion
  2.5 0.8 fusion.17
  3.3 0.0 copy-done
  3.3 0.3 convolution_convert_fusion
  3.6 1.1 copy.20
  4.7 17.7 %all-to-all-start = ((bf16[16,4,3584]{2,1,0:T(4,128)(2,1)}), bf16[16,4,3584]{2,1,0:T(4,128)(2,1)S(1)}, u32[]{:S(2)}, u32[]{:S(2)}) async-start(bf16[16,4,3584]{2,1,0:T(4,128)(2,1)} %copy.20), calls=%async_computation | async-start | bytes 917504 | tf_op jit(solution)/shard_map/all_to_all | solution.py:44
  22.4 1.9 %collective-permute-start = (bf16[3584,576]{0,1:T(8,128)(2,1)}, bf16[3584,576]{0,1:T(8,128)(2,1)}, u32[]{:S(2)}, u32[]{:S(2)}) collective-permute-start(bf16[3584,576]{0,1:T(8,128)(2,1)} %bitcast.28), channel_id=1, source_target_pairs={{0,4},{4,0},{1,5},{5,1},{2,6},{6,2},{3,7},{7,3},{8,12},{12,8},{9,1... | collective-permute-start | bytes 12386312 | tf_op jit(solution)/shard_map/ppermute | solution.py:28
  24.3 23.4 %all-to-all-done = bf16[16,4,3584]{2,1,0:T(4,128)(2,1)S(1)} async-done(((bf16[16,4,3584]{2,1,0:T(4,128)(2,1)}), bf16[16,4,3584]{2,1,0:T(4,128)(2,1)S(1)}, u32[]{:S(2)}, u32[]{:S(2)}) %all-to-all-start) | async-done | bytes 458784 | tf_op jit(solution)/shard_map/all_to_all | solution.py:44
  47.7 0.2 fusion.21
  47.9 24.8 %all-gather = bf16[32,4,3584]{2,1,0:T(4,128)(2,1)S(1)} all-gather(bf16[8,4,3584]{2,1,0:T(4,128)(2,1)S(1)} %get-tuple-element.7), channel_id=2, replica_groups=mesh['x'=4,'zb'=4,'zi'=4,'c'=2,'dp'=4] {'zi'}, dimensions={0}, use_global_device_ids=true | all-gather | bytes 1146880 | tf_op jit(solution)/shard_map/all_gather | solution.py:46
  72.7 18.5 %all-gather.1 = bf16[32,4,3584]{2,1,0:T(4,128)(2,1)S(1)} all-gather(bf16[8,4,3584]{2,1,0:T(4,128)(2,1)S(1)} %get-tuple-element.8), channel_id=3, replica_groups=mesh['x'=4,'zb'=4,'zi'=4,'c'=2,'dp'=4] {'zi'}, dimensions={0}, use_global_device_ids=true | all-gather | bytes 1146880 | tf_op jit(solution)/shard_map/all_gather | solution.py:47
  91.2 1.2 pad_maximum_fusion
  92.4 1.5 reshape.43
  93.9 3.5 %fusion.4 = f32[256,384]{1,0:T(8,128)S(1)} fusion(bf16[256,3584]{1,0:T(8,128)(2,1)} %reshape.43, bf16[3584,576]{0,1:T(8,128)(2,1)} %bitcast.29), kind=kOutput, calls=%fused_computation.7 | convolution fusion | flops 704643072 | bytes 4980736 | tf_op jit(solution)/shard_map/dot_general | solution.py:14
  97.4 0.0 copy-start.1
  97.4 2.2 %fusion.7 = f32[256,3584]{1,0:T(8,128)S(1)} fusion(bf16[3584,576]{0,1:T(8,128)(2,1)} %bitcast.30, f32[256,384]{1,0:T(8,128)S(1)} %fusion.4), kind=kOutput, calls=%fused_computation.11 | convolution fusion | flops 352616448 | bytes 5570560 | tf_op jit(solution)/shard_map/dot_general | solution.py:16
  99.5 0.0 collective-permute-done
  99.5 0.0 copy-done.1
  99.6 2.9 %fusion.2 = f32[256,384]{1,0:T(8,128)S(1)} fusion(bf16[256,3584]{1,0:T(8,128)(2,1)S(1)} %copy-done.1, bf16[3584,576]{0,1:T(8,128)(2,1)} %collective-permute-done), kind=kOutput, calls=%fused_computation.5 | convolution fusion | flops 704643072 | bytes 4980736 | tf_op jit(solution)/shard_map/dot_general | solution.py:14
  102.5 2.0 %fusion = bf16[256,3584]{1,0:T(8,128)(2,1)S(1)} fusion(f32[256,3584]{1,0:T(8,128)S(1)} %fusion.7, bf16[3584,576]{0,1:T(8,128)(2,1)} %collective-permute-done, f32[256,384]{1,0:T(8,128)S(1)} %fusion.2), kind=kOutput, calls=%fused_computation.1 | convolution fusion | flops 354451456 | bytes 7405568 | tf_op jit(solution)/shard_map/dot_general | solution.py:16
  104.5 41.7 %all_to_all.15 = bf16[4,64,3584]{2,1,0:T(8,128)(2,1)S(1)} all-to-all(bf16[4,64,3584]{2,1,0:T(8,128)(2,1)S(1)} %bitcast.23), channel_id=1, replica_groups=mesh['x'=4,'zb'=4,'zi'=4,'c'=2,'dp'=4] {'zi'}, dimensions={0} | all-to-all | bytes 3670016 | tf_op jit(solution)/shard_map/all_to_all | solution.py:51
  146.2 0.4 reduce_sum.52
  146.5 0.1 reshape.45
  146.7 28.7 %all_to_all.16 = bf16[16,4,3584]{2,1,0:T(4,128)(2,1)S(1)} all-to-all(bf16[16,4,3584]{2,1,0:T(4,128)(2,1)S(1)} %reshape.45), channel_id=1, replica_groups=mesh['x'=4,'zb'=4,'zi'=4,'c'=2,'dp'=4] {'x','zb'}, dimensions={0} | all-to-all | bytes 917504 | tf_op jit(solution)/shard_map/all_to_all | solution.py:53
  175.4 0.1 copy.21
  175.4 1.0 fusion.1
  (3 shorter events, 0.0 us)
Async XLA Ops:
  0.0 3.3 %copy-start = (bf16[2,8,3584]{2,1,0:T(8,128)(2,1)S(1)}, bf16[2,8,3584]{2,1,0:T(8,128)(2,1)}, u32[]{:S(2)}) copy-start(bf16[2,8,3584]{2,1,0:T(8,128)(2,1)} %param.4) | copy-start | bytes 344068
  4.7 43.0 %all-to-all-start = ((bf16[16,4,3584]{2,1,0:T(4,128)(2,1)}), bf16[16,4,3584]{2,1,0:T(4,128)(2,1)S(1)}, u32[]{:S(2)}, u32[]{:S(2)}) async-start(bf16[16,4,3584]{2,1,0:T(4,128)(2,1)} %copy.20), calls=%async_computation | async-start | bytes 917504 | tf_op jit(solution)/shard_map/all_to_all | solution.py:44
  22.4 77.2 %collective-permute-start = (bf16[3584,576]{0,1:T(8,128)(2,1)}, bf16[3584,576]{0,1:T(8,128)(2,1)}, u32[]{:S(2)}, u32[]{:S(2)}) collective-permute-start(bf16[3584,576]{0,1:T(8,128)(2,1)} %bitcast.28), channel_id=1, source_target_pairs={{0,4},{4,0},{1,5},{5,1},{2,6},{6,2},{3,7},{7,3},{8,12},{12,8},{9,1... | collective-permute-start | bytes 12386312 | tf_op jit(solution)/shard_map/ppermute | solution.py:28
  97.4 2.2 %copy-start.1 = (bf16[256,3584]{1,0:T(8,128)(2,1)S(1)}, bf16[256,3584]{1,0:T(8,128)(2,1)}, u32[]{:S(2)}) copy-start(bf16[256,3584]{1,0:T(8,128)(2,1)} %reshape.43) | copy-start | bytes 5505028

commit v2 on v1

--- a/solution.py
+++ b/solution.py
@@ -23,7 +23,6 @@
     experts = lax.axis_size("x") * lax.axis_size("zb")
     line = lax.axis_size("zi")
     capacity = 2
-    slots = batches * capacity
     own = expert_weights[0]
     other = lax.ppermute(own, "c", [(0, 1), (1, 0)])
 
@@ -38,22 +37,25 @@
     ).astype(F32)
     selector = jnp.sum(landing, axis=2)
     weighting = jnp.sum(landing * gate_scores[..., None, None], axis=2)
-    packed = jnp.einsum("mres,mrd->emsd", selector.astype(BF), tokens, preferred_element_type=F32)
-    packed = packed.astype(BF).reshape(experts, slots, width)
+    selector = selector.astype(BF)
 
-    arrived = lax.all_to_all(packed, ROWS_OF, split_axis=0, concat_axis=0, tiled=True)
-    half = experts // 2
-    first = lax.all_gather(arrived[:half], "zi", axis=0)
-    second = lax.all_gather(arrived[half:], "zi", axis=0)
-    rows = jnp.concatenate([first, second], axis=1).reshape(-1, width)
-    part = (expert_block(rows, own) + expert_block(rows, other)).astype(BF)
-    part = part.reshape(line, experts * slots, width)
-    parts = lax.all_to_all(part, "zi", split_axis=0, concat_axis=0, tiled=True)
-    summed = jnp.sum(parts, axis=0, dtype=F32).astype(BF).reshape(experts, slots, width)
-    returned = lax.all_to_all(summed, ROWS_OF, split_axis=0, concat_axis=0, tiled=True)
-    returned = returned.reshape(experts, batches, capacity, width).astype(F32)
-    mixed = jnp.einsum("mres,emsd->mrd", weighting, returned, precision=lax.Precision.HIGHEST)
-    return mixed.astype(BF)
+    outs = []
+    for m in range(batches):
+        packed = jnp.einsum("res,rd->esd", selector[m], tokens[m], preferred_element_type=F32)
+        arrived = lax.all_to_all(
+            packed.astype(BF), ROWS_OF, split_axis=0, concat_axis=0, tiled=True
+        )
+        rows = lax.all_gather(arrived, "zi", axis=0).reshape(-1, width)
+        part = (expert_block(rows, own) + expert_block(rows, other)).astype(BF)
+        part = part.reshape(line, experts * capacity, width)
+        parts = lax.all_to_all(part, "zi", split_axis=0, concat_axis=0, tiled=True)
+        summed = jnp.sum(parts, axis=0, dtype=F32).astype(BF).reshape(experts, capacity, width)
+        returned = lax.all_to_all(summed, ROWS_OF, split_axis=0, concat_axis=0, tiled=True)
+        mixed = jnp.einsum(
+            "res,esd->rd", weighting[m], returned.astype(F32), precision=lax.Precision.HIGHEST
+        )
+        outs.append(mixed.astype(BF))
+    return jnp.stack(outs)
 
 
 def solution(mesh):

time: 180 us -> 219 us (1.22); the launches traced: 176 us -> 218 us
  blocking collectives: 114 us -> 64.6 us
  waiting for transfers between devices: 23.4 us -> 70.8 us
  starting transfers between devices: 19.6 us -> 51.7 us
  matrix products: 11.9 us -> 22.6 us
    all_to_all x2 -> x0, blocking collectives: 70.4 us -> none  [the longest x1 41.7 us: on_device(): parts = lax.all_to_all(part, 'zi', split_axis=0, concat_axis=0, tiled=True)]
    all_to_all x1 -> x6, waiting for transfers between devices: 23.4 us -> 70.8 us  [the longest x2 33.7 us: on_device(): lax.all_to_all(summed, ROWS_OF, split_axis=0, concat_axis=0, tiled=True)]
    all_to_all x1 -> x6, starting transfers between devices: 17.7 us -> 49.7 us  [the longest x2 23 us: on_device(): lax.all_to_all(packed.astype(BF), ROWS_OF, split_axis=0, concat_axis=0, t...]
    all_gather x2, blocking collectives: 43.3 us -> 64.6 us  [on_device(): rows = lax.all_gather(arrived, 'zi', axis=0).reshape(-1, width)]
    dot_general x2 -> x4, matrix products: 4.2 us -> 9.02 us  [expert_block(): lax.dot_general(hidden, weights[:, 2 * units:], (((1,), (1,)), ((), ())),...]
    dot_general x2 -> x4, matrix products: 6.35 us -> 10.9 us  [expert_block(): jnp.dot(rows, weights[:, :2 * units], preferred_element_type=F32)]
  transfers between devices with their start and end apart: 2 -> 7, of which waited for: 1 -> 4; matrix products, arithmetic and copies ran while one was open for 5% -> 14% of each run, Pallas kernels for 0% -> 0%
where the time goes in v2:
time: 219 us; the launch traced here: 218 us
  waiting for transfers between devices  70.8 us (32%)
  blocking collectives  64.6 us (29%)
  starting transfers between devices  51.7 us (24%)
  matrix products  22.6 us (10%)
  other arithmetic  4.24 us (2%)
  local copies, waits for them, and re-layouts  4.08 us (2%)
    all_gather x2, blocking collectives, on_device(): rows = lax.all_gather(arrived, 'zi', axis=0).reshape(-1, width)  64.6 us
    all_to_all x2, waiting for transfers between devices, on_device(): lax.all_to_all(summed, ROWS_OF, split_axis=0, concat_axis=0, tiled=True)  33.7 us
    all_to_all x2, starting transfers between devices, on_device(): lax.all_to_all(packed.astype(BF), ROWS_OF, split_axis=0, concat_axis=0, t...  23 us
    all_to_all x2, starting transfers between devices, on_device(): lax.all_to_all(summed, ROWS_OF, split_axis=0, concat_axis=0, tiled=True)  19.3 us
    all_to_all x2, waiting for transfers between devices, on_device(): parts = lax.all_to_all(part, 'zi', split_axis=0, concat_axis=0, tiled=True)  18.6 us
    all_to_all x2, waiting for transfers between devices, on_device(): lax.all_to_all(packed.astype(BF), ROWS_OF, split_axis=0, concat_axis=0, t...  18.5 us
    dot_general x4, matrix products, expert_block(): jnp.dot(rows, weights[:, :2 * units], preferred_element_type=F32)  10.9 us
    dot_general x4, matrix products, expert_block(): lax.dot_general(hidden, weights[:, 2 * units:], (((1,), (1,)), ((), ())),...  9.02 us
  transfers between devices with their start and end apart: 7, of which 4 were waited for; matrix products, arithmetic and copies ran while one was open for 14% of the time, Pallas kernels for 0%

profile of v2, /device:TPU:24, one launch (start us, length us, event | category | flops | bytes accessed | tf_op | source)
XLA Modules:
  0.0 218.2 jit_solution(11433332625329494520)
XLA Ops:
  0.0 1.9 collective-permute-start
  1.9 0.8 convert_reduce_fusion
  2.7 0.9 select_reduce_fusion
  3.6 0.8 iota_compare_fusion
  4.4 0.8 fusion.38
  5.2 1.1 convolution_convert_fusion.1
  6.2 0.9 copy.25
  7.2 17.7 %all-to-all-start = ((bf16[16,2,3584]{2,1,0:T(2,128)(2,1)}), bf16[16,2,3584]{2,1,0:T(2,128)(2,1)S(1)}, u32[]{:S(2)}, u32[]{:S(2)}) async-start(bf16[16,2,3584]{2,1,0:T(2,128)(2,1)} %copy.25), calls=%async_computation | async-start | bytes 458752 | tf_op jit(solution)/shard_map/all_to_all | solution.py:45
  24.8 1.1 convolution_convert_fusion
  25.9 0.9 copy.27
  26.8 18.5 %all-to-all-done = bf16[16,2,3584]{2,1,0:T(2,128)(2,1)S(1)} async-done(((bf16[16,2,3584]{2,1,0:T(2,128)(2,1)}), bf16[16,2,3584]{2,1,0:T(2,128)(2,1)S(1)}, u32[]{:S(2)}, u32[]{:S(2)}) %all-to-all-start) | async-done | bytes 229408 | tf_op jit(solution)/shard_map/all_to_all | solution.py:45
  45.3 5.4 %all-to-all-start.3 = ((bf16[16,2,3584]{2,1,0:T(2,128)(2,1)}), bf16[16,2,3584]{2,1,0:T(2,128)(2,1)S(1)}, u32[]{:S(2)}, u32[]{:S(2)}) async-start(bf16[16,2,3584]{2,1,0:T(2,128)(2,1)} %copy.27), calls=%async_computation.3 | async-start | bytes 458752 | tf_op jit(solution)/shard_map/all_to_all | solution.py:45
  50.7 26.6 %all-gather = bf16[64,2,3584]{2,1,0:T(2,128)(2,1)S(1)} all-gather(bf16[16,2,3584]{2,1,0:T(2,128)(2,1)S(1)} %all-to-all-done), channel_id=2, replica_groups=mesh['x'=4,'zb'=4,'zi'=4,'c'=2,'dp'=4] {'zi'}, dimensions={0}, use_global_device_ids=true | all-gather | bytes 1146880 | tf_op jit(solution)/shard_map/all_gather | solution.py:48
  77.3 0.3 reshape.45
  77.6 2.7 %fusion.12 = f32[128,384]{1,0:T(8,128)S(1)} fusion(bf16[128,3584]{1,0:T(8,128)(2,1)S(1)} %reshape.45, bf16[3584,576]{0,1:T(8,128)(2,1)} %bitcast.44), kind=kOutput, calls=%fused_computation.18 | convolution fusion | flops 352321536 | bytes 3866624 | tf_op jit(solution)/shard_map/dot_general | solution.py:14
  80.3 1.8 fusion.18
  82.1 0.0 collective-permute-done
  82.2 2.7 %fusion.8 = f32[128,384]{1,0:T(8,128)S(1)} fusion(bf16[128,3584]{1,0:T(8,128)(2,1)S(1)} %reshape.45, bf16[3584,576]{0,1:T(8,128)(2,1)} %collective-permute-done), kind=kOutput, calls=%fused_computation.14 | convolution fusion | flops 352321536 | bytes 3866624 | tf_op jit(solution)/shard_map/dot_general | solution.py:14
  84.9 2.7 %fusion = bf16[128,3584]{1,0:T(8,128)(2,1)} fusion(f32[128,3584]{1,0:T(8,128)S(1)} %fusion.18, bf16[3584,576]{0,1:T(8,128)(2,1)} %collective-permute-done, f32[128,384]{1,0:T(8,128)S(1)} %fusion.8), kind=kOutput, calls=%fused_computation.2 | convolution fusion | flops 177225728 | bytes 4390912 | tf_op jit(solution)/shard_map/dot_general | solution.py:16
  87.6 0.0 all-to-all-done.3
  87.6 3.6 %all-to-all-start.1 = ((bf16[4,32,3584]{2,1,0:T(8,128)(2,1)}), bf16[4,32,3584]{2,1,0:T(8,128)(2,1)S(1)}, u32[]{:S(2)}, u32[]{:S(2)}) async-start(bf16[4,32,3584]{2,1,0:T(8,128)(2,1)} %bitcast.5), calls=%async_computation.1 | async-start | bytes 1835008 | tf_op jit(solution)/shard_map/all_to_all | solution.py:51
  91.2 38.1 %all-gather.1 = bf16[64,2,3584]{2,1,0:T(2,128)(2,1)S(1)} all-gather(bf16[16,2,3584]{2,1,0:T(2,128)(2,1)S(1)} %all-to-all-done.3), channel_id=3, replica_groups=mesh['x'=4,'zb'=4,'zi'=4,'c'=2,'dp'=4] {'zi'}, dimensions={0}, use_global_device_ids=true | all-gather | bytes 1146880 | tf_op jit(solution)/shard_map/all_gather | solution.py:48
  129.3 0.3 reshape.48
  129.6 2.7 %fusion.10 = f32[128,384]{1,0:T(8,128)S(1)} fusion(bf16[128,3584]{1,0:T(8,128)(2,1)S(1)} %reshape.48, bf16[3584,576]{0,1:T(8,128)(2,1)} %bitcast.46), kind=kOutput, calls=%fused_computation.16 | convolution fusion | flops 352321536 | bytes 3866624 | tf_op jit(solution)/shard_map/dot_general | solution.py:14
  132.4 1.8 fusion.16
  134.1 2.7 %fusion.6 = f32[128,384]{1,0:T(8,128)S(1)} fusion(bf16[128,3584]{1,0:T(8,128)(2,1)S(1)} %reshape.48, bf16[3584,576]{0,1:T(8,128)(2,1)} %collective-permute-done), kind=kOutput, calls=%fused_computation.12 | convolution fusion | flops 352321536 | bytes 3866624 | tf_op jit(solution)/shard_map/dot_general | solution.py:14
  136.9 2.7 %fusion.1 = bf16[128,3584]{1,0:T(8,128)(2,1)} fusion(f32[128,3584]{1,0:T(8,128)S(1)} %fusion.16, bf16[3584,576]{0,1:T(8,128)(2,1)} %collective-permute-done, f32[128,384]{1,0:T(8,128)S(1)} %fusion.6), kind=kOutput, calls=%fused_computation.3 | convolution fusion | flops 177225728 | bytes 4390912 | tf_op jit(solution)/shard_map/dot_general | solution.py:16
  139.6 0.0 all-to-all-done.1
  139.6 3.8 %all-to-all-start.4 = ((bf16[4,32,3584]{2,1,0:T(8,128)(2,1)}), bf16[4,32,3584]{2,1,0:T(8,128)(2,1)S(1)}, u32[]{:S(2)}, u32[]{:S(2)}) async-start(bf16[4,32,3584]{2,1,0:T(8,128)(2,1)} %bitcast.12), calls=%async_computation.4 | async-start | bytes 1835008 | tf_op jit(solution)/shard_map/all_to_all | solution.py:51
  143.4 0.2 reduce_sum.64
  143.6 0.8 reshape.47
  144.3 18.6 %all-to-all-done.4 = bf16[4,32,3584]{2,1,0:T(8,128)(2,1)S(1)} async-done(((bf16[4,32,3584]{2,1,0:T(8,128)(2,1)}), bf16[4,32,3584]{2,1,0:T(8,128)(2,1)S(1)}, u32[]{:S(2)}, u32[]{:S(2)}) %all-to-all-start.4) | async-done | bytes 917536 | tf_op jit(solution)/shard_map/all_to_all | solution.py:51
  162.9 13.8 %all-to-all-start.2 = ((bf16[16,2,3584]{2,1,0:T(2,128)(2,1)}), bf16[16,2,3584]{2,1,0:T(2,128)(2,1)S(1)}, u32[]{:S(2)}, u32[]{:S(2)}) async-start(bf16[16,2,3584]{2,1,0:T(2,128)(2,1)} %reshape.47), calls=%async_computation.2 | async-start | bytes 458752 | tf_op jit(solution)/shard_map/all_to_all | solution.py:53
  176.7 0.2 reduce_sum.65
  176.9 0.8 reshape.50
  177.7 16.8 %all-to-all-done.2 = bf16[16,2,3584]{2,1,0:T(2,128)(2,1)S(1)} async-done(((bf16[16,2,3584]{2,1,0:T(2,128)(2,1)}), bf16[16,2,3584]{2,1,0:T(2,128)(2,1)S(1)}, u32[]{:S(2)}, u32[]{:S(2)}) %all-to-all-start.2) | async-done | bytes 229408 | tf_op jit(solution)/shard_map/all_to_all | solution.py:53
  194.5 5.5 %all-to-all-start.5 = ((bf16[16,2,3584]{2,1,0:T(2,128)(2,1)}), bf16[16,2,3584]{2,1,0:T(2,128)(2,1)S(1)}, u32[]{:S(2)}, u32[]{:S(2)}) async-start(bf16[16,2,3584]{2,1,0:T(2,128)(2,1)} %reshape.50), calls=%async_computation.5 | async-start | bytes 458752 | tf_op jit(solution)/shard_map/all_to_all | solution.py:53
  200.1 0.3 fusion.5
  200.3 16.9 %all-to-all-done.5 = bf16[16,2,3584]{2,1,0:T(2,128)(2,1)S(1)} async-done(((bf16[16,2,3584]{2,1,0:T(2,128)(2,1)}), bf16[16,2,3584]{2,1,0:T(2,128)(2,1)S(1)}, u32[]{:S(2)}, u32[]{:S(2)}) %all-to-all-start.5) | async-done | bytes 229408 | tf_op jit(solution)/shard_map/all_to_all | solution.py:53
  217.2 0.3 fusion.4
  217.5 0.7 pad_maximum_fusion
  (3 shorter events, 0.0 us)
Async XLA Ops:
  0.0 82.1 %collective-permute-start = (bf16[3584,576]{0,1:T(8,128)(2,1)}, bf16[3584,576]{0,1:T(8,128)(2,1)}, u32[]{:S(2)}, u32[]{:S(2)}) collective-permute-start(bf16[3584,576]{0,1:T(8,128)(2,1)} %bitcast.43), channel_id=1, source_target_pairs={{0,4},{4,0},{1,5},{5,1},{2,6},{6,2},{3,7},{7,3},{8,12},{12,8},{9,1... | collective-permute-start | bytes 12386312 | tf_op jit(solution)/shard_map/ppermute | solution.py:27
  7.2 38.1 %all-to-all-start = ((bf16[16,2,3584]{2,1,0:T(2,128)(2,1)}), bf16[16,2,3584]{2,1,0:T(2,128)(2,1)S(1)}, u32[]{:S(2)}, u32[]{:S(2)}) async-start(bf16[16,2,3584]{2,1,0:T(2,128)(2,1)} %copy.25), calls=%async_computation | async-start | bytes 458752 | tf_op jit(solution)/shard_map/all_to_all | solution.py:45
  45.3 42.3 %all-to-all-start.3 = ((bf16[16,2,3584]{2,1,0:T(2,128)(2,1)}), bf16[16,2,3584]{2,1,0:T(2,128)(2,1)S(1)}, u32[]{:S(2)}, u32[]{:S(2)}) async-start(bf16[16,2,3584]{2,1,0:T(2,128)(2,1)} %copy.27), calls=%async_computation.3 | async-start | bytes 458752 | tf_op jit(solution)/shard_map/all_to_all | solution.py:45
  87.6 52.0 %all-to-all-start.1 = ((bf16[4,32,3584]{2,1,0:T(8,128)(2,1)}), bf16[4,32,3584]{2,1,0:T(8,128)(2,1)S(1)}, u32[]{:S(2)}, u32[]{:S(2)}) async-start(bf16[4,32,3584]{2,1,0:T(8,128)(2,1)} %bitcast.5), calls=%async_computation.1 | async-start | bytes 1835008 | tf_op jit(solution)/shard_map/all_to_all | solution.py:51
  139.6 23.4 %all-to-all-start.4 = ((bf16[4,32,3584]{2,1,0:T(8,128)(2,1)}), bf16[4,32,3584]{2,1,0:T(8,128)(2,1)S(1)}, u32[]{:S(2)}, u32[]{:S(2)}) async-start(bf16[4,32,3584]{2,1,0:T(8,128)(2,1)} %bitcast.12), calls=%async_computation.4 | async-start | bytes 1835008 | tf_op jit(solution)/shard_map/all_to_all | solution.py:51
  162.9 31.6 %all-to-all-start.2 = ((bf16[16,2,3584]{2,1,0:T(2,128)(2,1)}), bf16[16,2,3584]{2,1,0:T(2,128)(2,1)S(1)}, u32[]{:S(2)}, u32[]{:S(2)}) async-start(bf16[16,2,3584]{2,1,0:T(2,128)(2,1)} %reshape.47), calls=%async_computation.2 | async-start | bytes 458752 | tf_op jit(solution)/shard_map/all_to_all | solution.py:53
  194.5 22.7 %all-to-all-start.5 = ((bf16[16,2,3584]{2,1,0:T(2,128)(2,1)}), bf16[16,2,3584]{2,1,0:T(2,128)(2,1)S(1)}, u32[]{:S(2)}, u32[]{:S(2)}) async-start(bf16[16,2,3584]{2,1,0:T(2,128)(2,1)} %reshape.50), calls=%async_computation.5 | async-start | bytes 458752 | tf_op jit(solution)/shard_map/all_to_all | solution.py:53

commit v3 on v1

--- a/solution.py
+++ b/solution.py
@@ -7,15 +7,22 @@
 BF = jnp.bfloat16
 F32 = jnp.float32
 ROWS_OF = ("x", "zb")
+HOME = ("zi", "x", "zb")
+NT = (((1,), (1,)), ((), ()))
 
 
-def expert_block(rows, weights):
-    units = weights.shape[1] // 3
-    projected = jnp.dot(rows, weights[:, : 2 * units], preferred_element_type=F32)
-    hidden = (jax.nn.silu(projected[:, :units]) * projected[:, units:]).astype(BF)
-    return lax.dot_general(
-        hidden, weights[:, 2 * units :], (((1,), (1,)), ((), ())), preferred_element_type=F32
-    )
+def exchange(array, step):
+    size = lax.axis_size("zi")
+    return lax.ppermute(array, "zi", [(i, i ^ step) for i in range(size)])
+
+
+def swap(array):
+    return lax.ppermute(array, "c", [(0, 1), (1, 0)])
+
+
+def hidden_of(rows, weights, units):
+    projected = lax.dot_general(rows, weights, NT, preferred_element_type=F32)
+    return (jax.nn.silu(projected[:, :units]) * projected[:, units:]).astype(BF)
 
 
 def on_device(tokens, expert_ids, gate_scores, expert_weights):
@@ -24,8 +31,23 @@
     line = lax.axis_size("zi")
     capacity = 2
     slots = batches * capacity
-    own = expert_weights[0]
-    other = lax.ppermute(own, "c", [(0, 1), (1, 0)])
+    columns = width // line
+    turned = expert_weights[0].T
+    units = turned.shape[0] // 3
+    up = turned[: 2 * units]
+    down = turned[2 * units :].reshape(units, line, columns)
+    place = lax.axis_index("zi")
+
+    def for_place(at):
+        return lax.dynamic_index_in_dim(down, at, 1, keepdims=False)
+
+    pieces = [for_place(place)] + [exchange(for_place(place ^ k), k) for k in range(1, line)]
+    pieces = jnp.stack(pieces)
+    pieces = jnp.stack(
+        [lax.dynamic_index_in_dim(pieces, place ^ k, 0, keepdims=False) for k in range(line)]
+    )
+    other_up = swap(up)
+    down_all = jnp.concatenate([pieces, swap(pieces)], axis=1)
 
     matches = (expert_ids[..., None] == jnp.arange(experts, dtype=jnp.int32)).astype(jnp.int32)
     present = jnp.sum(matches, axis=2)
@@ -46,14 +68,16 @@
     first = lax.all_gather(arrived[:half], "zi", axis=0)
     second = lax.all_gather(arrived[half:], "zi", axis=0)
     rows = jnp.concatenate([first, second], axis=1).reshape(-1, width)
-    part = (expert_block(rows, own) + expert_block(rows, other)).astype(BF)
-    part = part.reshape(line, experts * slots, width)
-    parts = lax.all_to_all(part, "zi", split_axis=0, concat_axis=0, tiled=True)
-    summed = jnp.sum(parts, axis=0, dtype=F32).astype(BF).reshape(experts, slots, width)
-    returned = lax.all_to_all(summed, ROWS_OF, split_axis=0, concat_axis=0, tiled=True)
-    returned = returned.reshape(experts, batches, capacity, width).astype(F32)
-    mixed = jnp.einsum("mres,emsd->mrd", weighting, returned, precision=lax.Precision.HIGHEST)
-    return mixed.astype(BF)
+    hidden = jnp.concatenate(
+        [hidden_of(rows, up, units), hidden_of(rows, other_up, units)], axis=1
+    )
+    gathered = lax.all_gather(hidden, "zi", axis=0)
+    done = jnp.einsum("zrh,zhd->rd", gathered, down_all, preferred_element_type=F32).astype(BF)
+    done = done.reshape(line * experts, slots, columns)
+    returned = lax.all_to_all(done, HOME, split_axis=0, concat_axis=0, tiled=True)
+    returned = returned.reshape(line, experts, batches, capacity, columns).astype(F32)
+    mixed = jnp.einsum("mres,zemsd->mrzd", weighting, returned, precision=lax.Precision.HIGHEST)
+    return mixed.astype(BF).reshape(batches, row_count, width)
 
 
 def solution(mesh):

time: 180 us -> 190 us (1.056)
  blocking collectives: 114 us -> 97.4 us
  starting transfers between devices: 19.6 us -> 31.6 us
  waiting for transfers between devices: 23.4 us -> 32.6 us
  local copies, waits for them, and re-layouts: 2.96 us -> 9.67 us
    ppermute x1 -> x5, waiting for transfers between devices: 0.01 us -> 32.6 us  [the longest x3 32.6 us: exchange(): return lax.ppermute(array, 'zi', [(i, i ^ step) for i in range(size)])]
    all_to_all x2 -> x1, blocking collectives: 70.4 us -> 40.1 us  [on_device(): lax.all_to_all(done, HOME, split_axis=0, concat_axis=0, tiled=True)]
    all_to_all x1, waiting for transfers between devices: 23.4 us -> 0.01 us  [on_device(): lax.all_to_all(packed, ROWS_OF, split_axis=0, concat_axis=0, tiled=True)]
    all_gather x0 -> x1, blocking collectives: none -> 17.4 us  [on_device(): gathered = lax.all_gather(hidden, 'zi', axis=0)]
    ppermute x1 -> x5, starting transfers between devices: 1.92 us -> 13.9 us  [the longest x3 10.1 us: exchange(): return lax.ppermute(array, 'zi', [(i, i ^ step) for i in range(size)])]
    all_gather x1, blocking collectives: 24.8 us -> 19.9 us  [on_device(): first = lax.all_gather(arrived[:half], 'zi', axis=0)]
    slice x0 -> x2, local copies, waits for them, and re-layouts: none -> 3.17 us  [the longest x1 1.74 us: on_device(): up = turned[:2 * units]]
    dynamic_slice x0 -> x2, local copies, waits for them, and re-layouts: none -> 2.97 us  [the longest x1 2.84 us: for_place(): return lax.dynamic_index_in_dim(down, at, 1, keepdims=False)]
  transfers between devices with their start and end apart: 2 -> 6, of which waited for: 1 -> 2; matrix products, arithmetic and copies ran while one was open for 5% -> 10% of each run, Pallas kernels for 0% -> 0%
where the time goes in v3:
time: 190 us; the launch traced here: 188 us
  blocking collectives  97.4 us (51%)
  waiting for transfers between devices  32.6 us (17%)
  starting transfers between devices  31.6 us (17%)
  matrix products  10.1 us (5%)
  local copies, waits for them, and re-layouts  9.67 us (5%)
  other arithmetic  6.36 us (3%)
    all_to_all x1, blocking collectives, on_device(): lax.all_to_all(done, HOME, split_axis=0, concat_axis=0, tiled=True)  40.1 us
    ppermute x3, waiting for transfers between devices, exchange(): return lax.ppermute(array, 'zi', [(i, i ^ step) for i in range(size)])  32.6 us
    all_gather x1, blocking collectives, on_device(): second = lax.all_gather(arrived[half:], 'zi', axis=0)  20 us
    all_gather x1, blocking collectives, on_device(): first = lax.all_gather(arrived[:half], 'zi', axis=0)  19.9 us
    all_to_all x1, starting transfers between devices, on_device(): lax.all_to_all(packed, ROWS_OF, split_axis=0, concat_axis=0, tiled=True)  17.7 us
    all_gather x1, blocking collectives, on_device(): gathered = lax.all_gather(hidden, 'zi', axis=0)  17.4 us
    ppermute x3, starting transfers between devices, exchange(): return lax.ppermute(array, 'zi', [(i, i ^ step) for i in range(size)])  10.1 us
    dot_general x2, matrix products, hidden_of(): projected = lax.dot_general(rows, weights, NT, preferred_element_type=F32)  6.48 us
  transfers between devices with their start and end apart: 6, of which 2 were waited for; matrix products, arithmetic and copies ran while one was open for 10% of the time, Pallas kernels for 0%

profile of v3, /device:TPU:24, one launch (start us, length us, event | category | flops | bytes accessed | tf_op | source)
XLA Modules:
  0.0 188.1 jit_solution(4692867727511087974)
XLA Ops:
  0.0 0.0 copy-start
  0.0 0.8 convert_reduce_fusion
  0.8 0.8 iota_compare_fusion
  1.6 0.9 select_reduce_fusion
  2.5 0.8 fusion.20
  3.3 0.0 copy-done
  3.3 0.3 convolution_convert_fusion
  3.6 1.2 copy.39
  4.8 17.7 %all-to-all-start = ((bf16[16,4,3584]{2,1,0:T(4,128)(2,1)}), bf16[16,4,3584]{2,1,0:T(4,128)(2,1)S(1)}, u32[]{:S(2)}, u32[]{:S(2)}) async-start(bf16[16,4,3584]{2,1,0:T(4,128)(2,1)} %copy.39), calls=%async_computation | async-start | bytes 917504 | tf_op jit(solution)/shard_map/all_to_all | solution.py:66
  22.4 1.4 slice.39
  23.9 0.4 reshape.48
  24.2 0.0 copy-start.1
  24.3 2.8 %constant_dynamic-slice_fusion.6 = (bf16[192,1,896]{2,1,0:T(2,128)(2,1)S(1)}, bf16[192,1,896]{2,1,0:T(2,128)(2,1)S(1)}, bf16[192,1,896]{2,1,0:T(2,128)(2,1)S(1)}, bf16[192,1,896]{2,1,0:T(2,128)(2,1)S(1)}) fusion(bf16[192,4,896]{2,1,0:T(4,128)(2,1)S(1)} %reshape.48, s32[]{:T(128)S(6)} %select_n.18, s32[]{:T(128)S(6)} %select_n.20, s32[]{:T(128)S(6)} %select_n.19, ...), kind=kLoop, calls=%fused_computation.44 | loop fusion | bytes 2752528 | tf_op jit(solution)/shard_map/jit(dynamic_index_in_dim)/dynamic_slice | solution.py:42
  27.2 3.8 %collective-permute-start.3 = (bf16[192,896]{1,0:T(8,128)(2,1)S(1)}, bf16[192,896]{1,0:T(8,128)(2,1)S(1)}, u32[]{:S(2)}, u32[]{:S(2)}) collective-permute-start(bf16[192,896]{1,0:T(8,128)(2,1)S(1)} %bitcast.64), channel_id=1, source_target_pairs={{0,24},{8,16},{16,8},{24,0},{1,25},{9,17},{17,9},{25,1},{2,26},{10... | collective-permute-start | bytes 1032200 | tf_op jit(solution)/shard_map/ppermute | solution.py:16
  31.1 2.5 %collective-permute-start.2 = (bf16[192,896]{1,0:T(8,128)(2,1)S(1)}, bf16[192,896]{1,0:T(8,128)(2,1)S(1)}, u32[]{:S(2)}, u32[]{:S(2)}) collective-permute-start(bf16[192,896]{1,0:T(8,128)(2,1)S(1)} %bitcast.65), channel_id=1, source_target_pairs={{0,16},{8,24},{16,0},{24,8},{1,17},{9,25},{17,1},{25,9},{2,18},{10... | collective-permute-start | bytes 1032200 | tf_op jit(solution)/shard_map/ppermute | solution.py:16
  33.6 3.8 %collective-permute-start.1 = (bf16[192,896]{1,0:T(8,128)(2,1)S(1)}, bf16[192,896]{1,0:T(8,128)(2,1)S(1)}, u32[]{:S(2)}, u32[]{:S(2)}) collective-permute-start(bf16[192,896]{1,0:T(8,128)(2,1)S(1)} %bitcast.66), channel_id=1, source_target_pairs={{0,8},{8,0},{16,24},{24,16},{1,9},{9,1},{17,25},{25,17},{2,10},{10... | collective-permute-start | bytes 1032200 | tf_op jit(solution)/shard_map/ppermute | solution.py:16
  37.4 0.0 copy-done.1
  37.4 1.7 slice.34
  39.1 1.9 %collective-permute-start = (bf16[384,3584]{1,0:T(8,128)(2,1)}, bf16[384,3584]{1,0:T(8,128)(2,1)}, u32[]{:S(2)}, u32[]{:S(2)}) collective-permute-start(bf16[384,3584]{1,0:T(8,128)(2,1)} %slice.34), channel_id=1, source_target_pairs={{0,4},{4,0},{1,5},{5,1},{2,6},{6,2},{3,7},{7,3},{8,12},{12,8},{9,1... | collective-permute-start | bytes 8257544 | tf_op jit(solution)/shard_map/ppermute | solution.py:20
  41.1 5.4 %collective-permute-done.3 = bf16[192,896]{1,0:T(8,128)(2,1)S(1)} collective-permute-done((bf16[192,896]{1,0:T(8,128)(2,1)S(1)}, bf16[192,896]{1,0:T(8,128)(2,1)S(1)}, u32[]{:S(2)}, u32[]{:S(2)}) %collective-permute-start.3) | collective-permute-done | bytes 344096 | tf_op jit(solution)/shard_map/ppermute | solution.py:16
  46.6 27.1 %collective-permute-done.2 = bf16[192,896]{1,0:T(8,128)(2,1)S(1)} collective-permute-done((bf16[192,896]{1,0:T(8,128)(2,1)S(1)}, bf16[192,896]{1,0:T(8,128)(2,1)S(1)}, u32[]{:S(2)}, u32[]{:S(2)}) %collective-permute-start.2) | collective-permute-done | bytes 344096 | tf_op jit(solution)/shard_map/ppermute | solution.py:16
  73.7 0.0 collective-permute-done.1
  73.7 0.2 pad_maximum_fusion.1
  73.9 0.1 constant_dynamic-slice_fusion.2
  74.0 0.0 copy-start.3
  74.0 0.0 copy-start.5
  74.1 1.4 pad_maximum_fusion.2
  75.4 0.0 copy-done.3
  75.4 0.0 copy-done.5
  75.4 1.9 %collective-permute-start.4 = (bf16[4,192,896]{2,1,0:T(8,128)(2,1)}, bf16[4,192,896]{2,1,0:T(8,128)(2,1)}, u32[]{:S(2)}, u32[]{:S(2)}) collective-permute-start(bf16[4,192,896]{2,1,0:T(8,128)(2,1)} %pad_maximum_fusion.2), channel_id=1, source_target_pairs={{0,4},{4,0},{1,5},{5,1},{2,6},{6,2},{3,7},{7,3},{8,12},{12,8},{9,1... | collective-permute-start | bytes 4128776 | tf_op jit(solution)/shard_map/ppermute | solution.py:20
  77.3 0.0 all-to-all-done
  77.3 0.2 fusion.27
  77.5 20.0 %all-gather.1 = bf16[32,4,3584]{2,1,0:T(4,128)(2,1)S(1)} all-gather(bf16[8,4,3584]{2,1,0:T(4,128)(2,1)S(1)} %get-tuple-element.16), channel_id=3, replica_groups=mesh['x'=4,'zb'=4,'zi'=4,'c'=2,'dp'=4] {'zi'}, dimensions={0}, use_global_device_ids=true | all-gather | bytes 1146880 | tf_op jit(solution)/shard_map/all_gather | solution.py:69
  97.5 19.9 %all-gather = bf16[32,4,3584]{2,1,0:T(4,128)(2,1)S(1)} all-gather(bf16[8,4,3584]{2,1,0:T(4,128)(2,1)S(1)} %get-tuple-element.15), channel_id=2, replica_groups=mesh['x'=4,'zb'=4,'zi'=4,'c'=2,'dp'=4] {'zi'}, dimensions={0}, use_global_device_ids=true | all-gather | bytes 1146880 | tf_op jit(solution)/shard_map/all_gather | solution.py:68
  117.4 1.2 pad_maximum_fusion
  118.6 1.5 reshape.47
  120.1 0.0 copy-start.2
  120.1 3.6 %fusion.25 = f32[256,384]{1,0:T(8,128)S(1)} fusion(bf16[256,3584]{1,0:T(8,128)(2,1)} %reshape.47, bf16[576,3584]{1,0:T(8,128)(2,1)} %bitcast.56), kind=kOutput, calls=%fused_computation.47 | convolution fusion | flops 704643072 | bytes 4980736 | tf_op jit(solution)/shard_map/dot_general | solution.py:24
  123.7 0.1 fusion.18
  123.8 0.0 collective-permute-done
  123.8 0.0 copy-done.2
  123.9 2.9 %fusion.28 = f32[256,384]{1,0:T(8,128)S(1)} fusion(bf16[256,3584]{1,0:T(8,128)(2,1)S(1)} %copy-done.2, bf16[384,3584]{1,0:T(8,128)(2,1)} %collective-permute-done), kind=kOutput, calls=%fused_computation.50 | convolution fusion | flops 704643072 | bytes 4980736 | tf_op jit(solution)/shard_map/dot_general | solution.py:24
  126.8 0.0 copy-start.4
  126.8 0.0 copy-start.6
  126.8 0.1 fusion.17
  126.9 0.1 pad_maximum_fusion.3
  127.0 17.4 %all-gather.2 = bf16[1024,384]{1,0:T(8,128)(2,1)S(1)} all-gather(bf16[256,384]{1,0:T(8,128)(2,1)S(1)} %pad_maximum_fusion.3), channel_id=4, replica_groups=mesh['x'=4,'zb'=4,'zi'=4,'c'=2,'dp'=4] {'zi'}, dimensions={0}, use_global_device_ids=true | all-gather | bytes 983040 | tf_op jit(solution)/shard_map/all_gather | solution.py:74
  144.4 0.0 collective-permute-done.4
  144.4 0.0 copy-done.4
  144.4 0.0 copy-done.6
  144.4 2.3 %fusion.13 = bf16[256,896]{1,0:T(8,128)(2,1)S(1)} fusion(bf16[4,256,384]{2,1,0:T(8,128)(2,1)S(1)} %bitcast.63, bf16[4,192,896]{2,1,0:T(8,128)(2,1)} %collective-permute-done.4, bf16[1,192,896]{2,1,0:T(8,128)(2,1)S(1)} %get-tuple-element.8, bf16[1,192,896]{2,1,0:T(8,128)(2,1)S(1)} %copy-done.4, bf16[1,192,896]{2,1,0:T(8,128)(2,1)S(1)} %copy-done.6, ...), kind=kOutput, calls=%fused_computation.15 | convolution fusion | flops 718635008 | bytes 3997696 | tf_op jit(solution)/shard_map/zrh,zhd->rd/dot_general | solution.py:75
  146.8 0.1 reshape.49
  146.9 40.1 %all_to_all.10 = bf16[64,4,896]{2,1,0:T(4,128)(2,1)S(1)} all-to-all(bf16[64,4,896]{2,1,0:T(4,128)(2,1)S(1)} %reshape.49), channel_id=1, replica_groups=mesh['x'=4,'zb'=4,'zi'=4,'c'=2,'dp'=4] {'zi','x','zb'}, dimensions={0} | all-to-all | bytes 917504 | tf_op jit(solution)/shard_map/all_to_all | solution.py:77
  187.1 1.0 fusion.16
  (8 shorter events, 0.3 us)
Async XLA Ops:
  0.0 3.3 %copy-start = (bf16[2,8,3584]{2,1,0:T(8,128)(2,1)S(1)}, bf16[2,8,3584]{2,1,0:T(8,128)(2,1)}, u32[]{:S(2)}) copy-start(bf16[2,8,3584]{2,1,0:T(8,128)(2,1)} %param.4) | copy-start | bytes 344068
  4.8 72.6 %all-to-all-start = ((bf16[16,4,3584]{2,1,0:T(4,128)(2,1)}), bf16[16,4,3584]{2,1,0:T(4,128)(2,1)S(1)}, u32[]{:S(2)}, u32[]{:S(2)}) async-start(bf16[16,4,3584]{2,1,0:T(4,128)(2,1)} %copy.39), calls=%async_computation | async-start | bytes 917504 | tf_op jit(solution)/shard_map/all_to_all | solution.py:66
  24.2 13.2 %copy-start.1 = (bf16[1,3584,576]{1,2,0:T(8,128)(2,1)S(1)}, bf16[1,3584,576]{1,2,0:T(8,128)(2,1)}, u32[]{:S(2)}) copy-start(bf16[1,3584,576]{1,2,0:T(8,128)(2,1)} %param.7) | copy-start | bytes 12386308
  27.2 19.4 %collective-permute-start.3 = (bf16[192,896]{1,0:T(8,128)(2,1)S(1)}, bf16[192,896]{1,0:T(8,128)(2,1)S(1)}, u32[]{:S(2)}, u32[]{:S(2)}) collective-permute-start(bf16[192,896]{1,0:T(8,128)(2,1)S(1)} %bitcast.64), channel_id=1, source_target_pairs={{0,24},{8,16},{16,8},{24,0},{1,25},{9,17},{17,9},{25,1},{2,26},{10... | collective-permute-start | bytes 1032200 | tf_op jit(solution)/shard_map/ppermute | solution.py:16
  31.1 42.6 %collective-permute-start.2 = (bf16[192,896]{1,0:T(8,128)(2,1)S(1)}, bf16[192,896]{1,0:T(8,128)(2,1)S(1)}, u32[]{:S(2)}, u32[]{:S(2)}) collective-permute-start(bf16[192,896]{1,0:T(8,128)(2,1)S(1)} %bitcast.65), channel_id=1, source_target_pairs={{0,16},{8,24},{16,0},{24,8},{1,17},{9,25},{17,1},{25,9},{2,18},{10... | collective-permute-start | bytes 1032200 | tf_op jit(solution)/shard_map/ppermute | solution.py:16
  33.6 40.1 %collective-permute-start.1 = (bf16[192,896]{1,0:T(8,128)(2,1)S(1)}, bf16[192,896]{1,0:T(8,128)(2,1)S(1)}, u32[]{:S(2)}, u32[]{:S(2)}) collective-permute-start(bf16[192,896]{1,0:T(8,128)(2,1)S(1)} %bitcast.66), channel_id=1, source_target_pairs={{0,8},{8,0},{16,24},{24,16},{1,9},{9,1},{17,25},{25,17},{2,10},{10... | collective-permute-start | bytes 1032200 | tf_op jit(solution)/shard_map/ppermute | solution.py:16
  39.1 84.7 %collective-permute-start = (bf16[384,3584]{1,0:T(8,128)(2,1)}, bf16[384,3584]{1,0:T(8,128)(2,1)}, u32[]{:S(2)}, u32[]{:S(2)}) collective-permute-start(bf16[384,3584]{1,0:T(8,128)(2,1)} %slice.34), channel_id=1, source_target_pairs={{0,4},{4,0},{1,5},{5,1},{2,6},{6,2},{3,7},{7,3},{8,12},{12,8},{9,1... | collective-permute-start | bytes 8257544 | tf_op jit(solution)/shard_map/ppermute | solution.py:20
  74.0 1.4 copy-start.3
  74.0 1.4 copy-start.5
  75.4 69.0 %collective-permute-start.4 = (bf16[4,192,896]{2,1,0:T(8,128)(2,1)}, bf16[4,192,896]{2,1,0:T(8,128)(2,1)}, u32[]{:S(2)}, u32[]{:S(2)}) collective-permute-start(bf16[4,192,896]{2,1,0:T(8,128)(2,1)} %pad_maximum_fusion.2), channel_id=1, source_target_pairs={{0,4},{4,0},{1,5},{5,1},{2,6},{6,2},{3,7},{7,3},{8,12},{12,8},{9,1... | collective-permute-start | bytes 4128776 | tf_op jit(solution)/shard_map/ppermute | solution.py:20
  120.1 3.8 %copy-start.2 = (bf16[256,3584]{1,0:T(8,128)(2,1)S(1)}, bf16[256,3584]{1,0:T(8,128)(2,1)}, u32[]{:S(2)}) copy-start(bf16[256,3584]{1,0:T(8,128)(2,1)} %reshape.47) | copy-start | bytes 5505028
  126.8 17.7 %copy-start.4 = (bf16[1,192,896]{2,1,0:T(8,128)(2,1)S(1)}, bf16[1,192,896]{2,1,0:T(8,128)(2,1)}, u32[]{:S(2)}) copy-start(bf16[1,192,896]{2,1,0:T(8,128)(2,1)} %copy-done.3) | copy-start | bytes 1032196
  126.8 17.7 %copy-start.6 = (bf16[1,192,896]{2,1,0:T(8,128)(2,1)S(1)}, bf16[1,192,896]{2,1,0:T(8,128)(2,1)}, u32[]{:S(2)}) copy-start(bf16[1,192,896]{2,1,0:T(8,128)(2,1)} %copy-done.5) | copy-start | bytes 1032196

commit v4 on v3

--- a/solution.py
+++ b/solution.py
@@ -35,8 +35,10 @@
     turned = expert_weights[0].T
     units = turned.shape[0] // 3
     up = turned[: 2 * units]
-    down = turned[2 * units :].reshape(units, line, columns)
     place = lax.axis_index("zi")
+    share = units // lax.axis_size("dp")
+    down = lax.dynamic_slice_in_dim(turned, 2 * units + share * lax.axis_index("dp"), share, 0)
+    down = down.reshape(share, line, columns)
 
     def for_place(at):
         return lax.dynamic_index_in_dim(down, at, 1, keepdims=False)
@@ -46,6 +48,7 @@
     pieces = jnp.stack(
         [lax.dynamic_index_in_dim(pieces, place ^ k, 0, keepdims=False) for k in range(line)]
     )
+    pieces = lax.all_gather(pieces, "dp", axis=1).reshape(line, units, columns)
     other_up = swap(up)
     down_all = jnp.concatenate([pieces, swap(pieces)], axis=1)
 

time: 190 us -> 181 us (0.953)
  waiting for transfers between devices: 32.6 us -> 11 us
  between operations: 0.33 us -> 13.7 us
  blocking collectives: 97.4 us -> 101 us
    ppermute x3, waiting for transfers between devices: 32.6 us -> 11 us  [exchange(): return lax.ppermute(array, 'zi', [(i, i ^ step) for i in range(size)])]
    all_gather x1, blocking collectives: 20 us -> 23.3 us  [on_device(): second = lax.all_gather(arrived[half:], 'zi', axis=0)]
    dynamic_slice x1, local copies, waits for them, and re-layouts: 2.84 us -> 0.72 us  [for_place(): return lax.dynamic_index_in_dim(down, at, 1, keepdims=False)]
  transfers between devices with their start and end apart: 6 -> 7, of which waited for: 2 -> 2; matrix products, arithmetic and copies ran while one was open for 10% -> 9% of each run, Pallas kernels for 0% -> 0%
where the time goes in v4:
time: 181 us; the launch traced here: 180 us
  blocking collectives  101 us (56%)
  starting transfers between devices  31.8 us (18%)
  between operations  13.7 us (8%)
  waiting for transfers between devices  11 us (6%)
  matrix products  8.78 us (5%)
  local copies, waits for them, and re-layouts  8.44 us (5%)
  other arithmetic  5.67 us (3%)
    all_to_all x1, blocking collectives, on_device(): lax.all_to_all(done, HOME, split_axis=0, concat_axis=0, tiled=True)  41 us
    all_gather x1, blocking collectives, on_device(): second = lax.all_gather(arrived[half:], 'zi', axis=0)  23.3 us
    all_gather x1, blocking collectives, on_device(): first = lax.all_gather(arrived[:half], 'zi', axis=0)  18.3 us
    all_gather x1, blocking collectives, on_device(): gathered = lax.all_gather(hidden, 'zi', axis=0)  17.9 us
    all_to_all x1, starting transfers between devices, on_device(): lax.all_to_all(packed, ROWS_OF, split_axis=0, concat_axis=0, tiled=True)  17.7 us
    ppermute x3, waiting for transfers between devices, exchange(): return lax.ppermute(array, 'zi', [(i, i ^ step) for i in range(size)])  11 us
    ppermute x3, starting transfers between devices, exchange(): return lax.ppermute(array, 'zi', [(i, i ^ step) for i in range(size)])  10.1 us
    dot_general x2, matrix products, hidden_of(): projected = lax.dot_general(rows, weights, NT, preferred_element_type=F32)  6.45 us
  transfers between devices with their start and end apart: 7, of which 2 were waited for; matrix products, arithmetic and copies ran while one was open for 9% of the time, Pallas kernels for 0%

profile of v4, /device:TPU:24, one launch (start us, length us, event | category | flops | bytes accessed | tf_op | source)
XLA Modules:
  0.0 179.9 jit_solution(13136659828392222265)
XLA Ops:
  6.5 0.0 copy-start
  6.5 0.8 convert_reduce_fusion
  7.3 0.8 iota_compare_fusion
  8.1 0.9 select_reduce_fusion
  9.0 0.8 fusion.14
  9.8 0.0 copy-done
  9.8 0.3 convolution_convert_fusion
  10.1 1.2 copy.29
  11.3 17.7 %all-to-all-start = ((bf16[16,4,3584]{2,1,0:T(4,128)(2,1)}), bf16[16,4,3584]{2,1,0:T(4,128)(2,1)S(1)}, u32[]{:S(2)}, u32[]{:S(2)}) async-start(bf16[16,4,3584]{2,1,0:T(4,128)(2,1)} %copy.29), calls=%async_computation | async-start | bytes 917504 | tf_op jit(solution)/shard_map/all_to_all | solution.py:69
  29.0 0.0 all-gather.6.cloned.1.call-start
  29.0 1.0 dynamic-slice_bitcast_fusion
  30.0 0.1 reshape.55
  30.1 0.7 constant_dynamic-slice_fusion.6
  30.9 3.8 %collective-permute-start.3 = (bf16[48,896]{1,0:T(8,128)(2,1)S(1)}, bf16[48,896]{1,0:T(8,128)(2,1)S(1)}, u32[]{:S(2)}, u32[]{:S(2)}) collective-permute-start(bf16[48,896]{1,0:T(8,128)(2,1)S(1)} %bitcast.67), channel_id=1, source_target_pairs={{0,24},{8,16},{16,8},{24,0},{1,25},{9,17},{17,9},{25,1},{2,26},{10... | collective-permute-start | bytes 258056 | tf_op jit(solution)/shard_map/ppermute | solution.py:16
  34.8 2.5 %collective-permute-start.2 = (bf16[48,896]{1,0:T(8,128)(2,1)S(1)}, bf16[48,896]{1,0:T(8,128)(2,1)S(1)}, u32[]{:S(2)}, u32[]{:S(2)}) collective-permute-start(bf16[48,896]{1,0:T(8,128)(2,1)S(1)} %bitcast.68), channel_id=1, source_target_pairs={{0,16},{8,24},{16,0},{24,8},{1,17},{9,25},{17,1},{25,9},{2,18},{10... | collective-permute-start | bytes 258056 | tf_op jit(solution)/shard_map/ppermute | solution.py:16
  37.3 3.8 %collective-permute-start.1 = (bf16[48,896]{1,0:T(8,128)(2,1)S(1)}, bf16[48,896]{1,0:T(8,128)(2,1)S(1)}, u32[]{:S(2)}, u32[]{:S(2)}) collective-permute-start(bf16[48,896]{1,0:T(8,128)(2,1)S(1)} %bitcast.69), channel_id=1, source_target_pairs={{0,8},{8,0},{16,24},{24,16},{1,9},{9,1},{17,25},{25,17},{2,10},{10... | collective-permute-start | bytes 258056 | tf_op jit(solution)/shard_map/ppermute | solution.py:16
  41.1 3.5 %slice.30 = bf16[384,3584]{1,0:T(8,128)(2,1)} slice(bf16[576,3584]{1,0:T(8,128)(2,1)} %bitcast.61), slice={[0:384], [0:3584]} | slice | bytes 5505024 | tf_op jit(solution)/shard_map/slice | solution.py:37
  44.6 1.9 %collective-permute-start = (bf16[384,3584]{1,0:T(8,128)(2,1)}, bf16[384,3584]{1,0:T(8,128)(2,1)}, u32[]{:S(2)}, u32[]{:S(2)}) collective-permute-start(bf16[384,3584]{1,0:T(8,128)(2,1)} %slice.30), channel_id=1, source_target_pairs={{0,4},{4,0},{1,5},{5,1},{2,6},{6,2},{3,7},{7,3},{8,12},{12,8},{9,1... | collective-permute-start | bytes 8257544 | tf_op jit(solution)/shard_map/ppermute | solution.py:20
  46.5 1.4 collective-permute-done.3
  48.0 9.5 %collective-permute-done.2 = bf16[48,896]{1,0:T(8,128)(2,1)S(1)} collective-permute-done((bf16[48,896]{1,0:T(8,128)(2,1)S(1)}, bf16[48,896]{1,0:T(8,128)(2,1)S(1)}, u32[]{:S(2)}, u32[]{:S(2)}) %collective-permute-start.2) | collective-permute-done | bytes 86048 | tf_op jit(solution)/shard_map/ppermute | solution.py:16
  57.5 0.0 collective-permute-done.1
  57.5 0.1 pad_maximum_fusion.1
  57.6 0.8 pad_maximum_fusion.2
  58.4 0.0 all-gather.6.cloned.1.call-update
  58.4 0.0 all-to-all-done
  58.5 0.2 fusion.21
  58.6 23.3 %all-gather.1 = bf16[32,4,3584]{2,1,0:T(4,128)(2,1)S(1)} all-gather(bf16[8,4,3584]{2,1,0:T(4,128)(2,1)S(1)} %get-tuple-element.8), channel_id=3, replica_groups=mesh['x'=4,'zb'=4,'zi'=4,'c'=2,'dp'=4] {'zi'}, dimensions={0}, use_global_device_ids=true | all-gather | bytes 1146880 | tf_op jit(solution)/shard_map/all_gather | solution.py:72
  82.0 18.3 %all-gather = bf16[32,4,3584]{2,1,0:T(4,128)(2,1)S(1)} all-gather(bf16[8,4,3584]{2,1,0:T(4,128)(2,1)S(1)} %get-tuple-element.7), channel_id=2, replica_groups=mesh['x'=4,'zb'=4,'zi'=4,'c'=2,'dp'=4] {'zi'}, dimensions={0}, use_global_device_ids=true | all-gather | bytes 1146880 | tf_op jit(solution)/shard_map/all_gather | solution.py:71
  100.3 1.2 pad_maximum_fusion
  101.5 1.5 reshape.53
  103.0 0.0 copy-start.1
  103.0 0.0 all-gather.6.cloned.1.call-done
  103.0 2.0 %collective-permute-start.4 = (bf16[4,192,896]{2,1,0:T(8,128)(2,1)}, bf16[4,192,896]{2,1,0:T(8,128)(2,1)S(1)}, u32[]{:S(2)}, u32[]{:S(2)}) collective-permute-start(bf16[4,192,896]{2,1,0:T(8,128)(2,1)} %all-gather.6.cloned.1.call-done), channel_id=1, source_target_pairs={{0,4},{4,0},{1,5},{5,1},{2,6},{6,2},{3,7},{7,3},{8,12},{12,8},{9,1... | collective-permute-start | bytes 4128776 | tf_op jit(solution)/shard_map/ppermute | solution.py:20
  105.0 3.5 %fusion.19 = f32[256,384]{1,0:T(8,128)S(1)} fusion(bf16[256,3584]{1,0:T(8,128)(2,1)} %reshape.53, bf16[576,3584]{1,0:T(8,128)(2,1)} %bitcast.62), kind=kOutput, calls=%fused_computation.42 | convolution fusion | flops 704643072 | bytes 4980736 | tf_op jit(solution)/shard_map/dot_general | solution.py:24
  108.5 0.1 fusion.12
  108.6 0.0 copy-start.2
  108.6 0.0 collective-permute-done
  108.6 0.0 copy-done.1
  108.6 3.0 %fusion.22 = f32[256,384]{1,0:T(8,128)S(1)} fusion(bf16[256,3584]{1,0:T(8,128)(2,1)S(1)} %copy-done.1, bf16[384,3584]{1,0:T(8,128)(2,1)} %collective-permute-done), kind=kOutput, calls=%fused_computation.45 | convolution fusion | flops 704643072 | bytes 4980736 | tf_op jit(solution)/shard_map/dot_general | solution.py:24
  111.7 0.1 fusion.11
  111.8 0.1 pad_maximum_fusion.3
  111.9 17.9 %all-gather.2 = bf16[1024,384]{1,0:T(8,128)(2,1)S(1)} all-gather(bf16[256,384]{1,0:T(8,128)(2,1)S(1)} %pad_maximum_fusion.3), channel_id=4, replica_groups=mesh['x'=4,'zb'=4,'zi'=4,'c'=2,'dp'=4] {'zi'}, dimensions={0}, use_global_device_ids=true | all-gather | bytes 983040 | tf_op jit(solution)/shard_map/all_gather | solution.py:77
  129.8 0.0 collective-permute-done.4
  129.8 0.0 copy-done.2
  129.8 1.0 fusion.7
  130.8 0.1 reshape.57
  131.0 41.0 %all_to_all.10 = bf16[64,4,896]{2,1,0:T(4,128)(2,1)S(1)} all-to-all(bf16[64,4,896]{2,1,0:T(4,128)(2,1)S(1)} %reshape.57), channel_id=1, replica_groups=mesh['x'=4,'zb'=4,'zi'=4,'c'=2,'dp'=4] {'zi','x','zb'}, dimensions={0} | all-to-all | bytes 917504 | tf_op jit(solution)/shard_map/all_to_all | solution.py:80
  172.0 1.0 fusion.10
  (9 shorter events, 0.2 us)
Async XLA Ops:
  6.5 3.3 %copy-start = (bf16[2,8,3584]{2,1,0:T(8,128)(2,1)S(1)}, bf16[2,8,3584]{2,1,0:T(8,128)(2,1)}, u32[]{:S(2)}) copy-start(bf16[2,8,3584]{2,1,0:T(8,128)(2,1)} %param.4) | copy-start | bytes 344068
  11.3 47.1 %all-to-all-start = ((bf16[16,4,3584]{2,1,0:T(4,128)(2,1)}), bf16[16,4,3584]{2,1,0:T(4,128)(2,1)S(1)}, u32[]{:S(2)}, u32[]{:S(2)}) async-start(bf16[16,4,3584]{2,1,0:T(4,128)(2,1)} %copy.29), calls=%async_computation | async-start | bytes 917504 | tf_op jit(solution)/shard_map/all_to_all | solution.py:69
  29.0 74.0 %all-gather.6.cloned.1.call-start = ((), (), s32[]{:S(2)}) async-start(), calls=%async_computation.2 | async-start | bytes 1720320 | tf_op jit(solution)/shard_map/all_gather | solution.py:51
  30.9 17.1 %collective-permute-start.3 = (bf16[48,896]{1,0:T(8,128)(2,1)S(1)}, bf16[48,896]{1,0:T(8,128)(2,1)S(1)}, u32[]{:S(2)}, u32[]{:S(2)}) collective-permute-start(bf16[48,896]{1,0:T(8,128)(2,1)S(1)} %bitcast.67), channel_id=1, source_target_pairs={{0,24},{8,16},{16,8},{24,0},{1,25},{9,17},{17,9},{25,1},{2,26},{10... | collective-permute-start | bytes 258056 | tf_op jit(solution)/shard_map/ppermute | solution.py:16
  34.8 22.7 %collective-permute-start.2 = (bf16[48,896]{1,0:T(8,128)(2,1)S(1)}, bf16[48,896]{1,0:T(8,128)(2,1)S(1)}, u32[]{:S(2)}, u32[]{:S(2)}) collective-permute-start(bf16[48,896]{1,0:T(8,128)(2,1)S(1)} %bitcast.68), channel_id=1, source_target_pairs={{0,16},{8,24},{16,0},{24,8},{1,17},{9,25},{17,1},{25,9},{2,18},{10... | collective-permute-start | bytes 258056 | tf_op jit(solution)/shard_map/ppermute | solution.py:16
  37.3 20.2 %collective-permute-start.1 = (bf16[48,896]{1,0:T(8,128)(2,1)S(1)}, bf16[48,896]{1,0:T(8,128)(2,1)S(1)}, u32[]{:S(2)}, u32[]{:S(2)}) collective-permute-start(bf16[48,896]{1,0:T(8,128)(2,1)S(1)} %bitcast.69), channel_id=1, source_target_pairs={{0,8},{8,0},{16,24},{24,16},{1,9},{9,1},{17,25},{25,17},{2,10},{10... | collective-permute-start | bytes 258056 | tf_op jit(solution)/shard_map/ppermute | solution.py:16
  44.6 64.0 %collective-permute-start = (bf16[384,3584]{1,0:T(8,128)(2,1)}, bf16[384,3584]{1,0:T(8,128)(2,1)}, u32[]{:S(2)}, u32[]{:S(2)}) collective-permute-start(bf16[384,3584]{1,0:T(8,128)(2,1)} %slice.30), channel_id=1, source_target_pairs={{0,4},{4,0},{1,5},{5,1},{2,6},{6,2},{3,7},{7,3},{8,12},{12,8},{9,1... | collective-permute-start | bytes 8257544 | tf_op jit(solution)/shard_map/ppermute | solution.py:20
  103.0 5.7 %copy-start.1 = (bf16[256,3584]{1,0:T(8,128)(2,1)S(1)}, bf16[256,3584]{1,0:T(8,128)(2,1)}, u32[]{:S(2)}) copy-start(bf16[256,3584]{1,0:T(8,128)(2,1)} %reshape.53) | copy-start | bytes 5505028
  103.0 26.9 %collective-permute-start.4 = (bf16[4,192,896]{2,1,0:T(8,128)(2,1)}, bf16[4,192,896]{2,1,0:T(8,128)(2,1)S(1)}, u32[]{:S(2)}, u32[]{:S(2)}) collective-permute-start(bf16[4,192,896]{2,1,0:T(8,128)(2,1)} %all-gather.6.cloned.1.call-done), channel_id=1, source_target_pairs={{0,4},{4,0},{1,5},{5,1},{2,6},{6,2},{3,7},{7,3},{8,12},{12,8},{9,1... | collective-permute-start | bytes 4128776 | tf_op jit(solution)/shard_map/ppermute | solution.py:20
  108.6 21.2 %copy-start.2 = (bf16[4,192,896]{2,1,0:T(8,128)(2,1)S(1)}, bf16[4,192,896]{2,1,0:T(8,128)(2,1)}, u32[]{:S(2)}) copy-start(bf16[4,192,896]{2,1,0:T(8,128)(2,1)} %all-gather.6.cloned.1.call-done) | copy-start | bytes 4128772
Sparse Core Ops, SparseCore 0:
  58.6 32.3 all-gather.5

commit v5 on v4

v5 whole, which is shorter than its diff:
```python
import jax
import jax.numpy as jnp
from jax import lax
from jax.experimental import pallas as pl
from jax.experimental.pallas import tpu as pltpu
from jax.sharding import Mesh, PartitionSpec as P

FF = 1536
BF = jnp.bfloat16
F32 = jnp.float32
ROWS_OF = ("x", "zb")
HOME = ("x", "zb", "zi")
NT = (((1,), (1,)), ((), ()))


def exchange(array, axis, step):
    size = lax.axis_size(axis)
    return lax.ppermute(array, axis, [(i, i ^ step) for i in range(size)])


def swap(array):
    return lax.ppermute(array, "c", [(0, 1), (1, 0)])


def up_kernel(first_ref, second_ref, own_ref, other_ref, out_ref, gate_ref, value_ref):
    step = pl.program_id(0)
    units = own_ref.shape[0] // 2
    half = first_ref.shape[0]

    @pl.when(step == 0)
    def _():
        gate_ref[...] = jnp.zeros_like(gate_ref)
        value_ref[...] = jnp.zeros_like(value_ref)

    gates = jnp.concatenate([own_ref[:units], other_ref[:units]], axis=0)
    values = jnp.concatenate([own_ref[units:], other_ref[units:]], axis=0)
    for at, rows_ref in ((0, first_ref), (half, second_ref)):
        rows = rows_ref[...]
        here = pl.ds(at, half)
        gate_ref[here] += lax.dot_general(rows, gates, NT, preferred_element_type=F32)
        value_ref[here] += lax.dot_general(rows, values, NT, preferred_element_type=F32)

    @pl.when(step == pl.num_programs(0) - 1)
    def _():
        gate = gate_ref[...]
        out_ref[...] = (gate / (1.0 + jnp.exp(-gate)) * value_ref[...]).astype(BF)


def hidden_of(first, second, own, other):
    half, width = first.shape
    both = other.shape[0]
    chunk = 512
    rows = pl.BlockSpec((half, chunk), lambda i: (0, i))
    weights = pl.BlockSpec((both, chunk), lambda i: (0, i))
    return pl.pallas_call(
        up_kernel,
        grid=(width // chunk,),
        in_specs=[rows, rows, weights, weights],
        out_specs=pl.BlockSpec((2 * half, both), lambda i: (0, 0)),
        out_shape=jax.ShapeDtypeStruct((2 * half, both), BF),
        scratch_shapes=[pltpu.VMEM((2 * half, both), F32), pltpu.VMEM((2 * half, both), F32)],
        compiler_params=pltpu.CompilerParams(
            dimension_semantics=("arbitrary",), vmem_limit_bytes=32 << 20
        ),
    )(first, second, own, other)


def down_kernel(place_ref, hidden_ref, own_ref, other_ref, out_ref):
    shares, line = own_ref.shape[:2]
    total = jnp.zeros(out_ref.shape, F32)
    for at in range(line):
        k = place_ref[0] ^ at
        weights = [ref[place_ref[1] ^ y, k] for ref in (own_ref, other_ref) for y in range(shares)]
        weights = jnp.concatenate(weights, axis=0)
        total += jnp.dot(hidden_ref[at], weights, preferred_element_type=F32)
    out_ref[...] = total.astype(BF)


def outputs_of(place, hidden, own, other):
    vmem = pl.BlockSpec(memory_space=pltpu.VMEM)
    return pl.pallas_call(
        down_kernel,
        in_specs=[pl.BlockSpec(memory_space=pltpu.SMEM), vmem, vmem, vmem],
        out_specs=vmem,
        out_shape=jax.ShapeDtypeStruct((hidden.shape[1], own.shape[3]), BF),
        compiler_params=pltpu.CompilerParams(vmem_limit_bytes=32 << 20),
    )(place, hidden, own, other)


def on_device(tokens, expert_ids, gate_scores, expert_weights):
    batches, row_count, width = tokens.shape
    experts = lax.axis_size("x") * lax.axis_size("zb")
    line = lax.axis_size("zi")
    capacity = 2
    slots = batches * capacity
    columns = width // line
    turned = expert_weights[0].T
    units = turned.shape[0] // 3
    up = turned[: 2 * units]
    place = lax.axis_index("zi")
    share = units // lax.axis_size("dp")
    down = lax.dynamic_slice_in_dim(turned, 2 * units + share * lax.axis_index("dp"), share, 0)
    down = down.reshape(share, line, columns)

    def for_place(at):
        return lax.dynamic_index_in_dim(down, at, 1, keepdims=False)

    pieces = [for_place(place)] + [exchange(for_place(place ^ k), "zi", k) for k in range(1, line)]
    pieces = jnp.stack(pieces)
    shares = [pieces] + [exchange(pieces, "dp", k) for k in range(1, lax.axis_size("dp"))]
    shares = jnp.stack(shares)
    other_shares = swap(shares)
    other_up = swap(up)

    matches = (expert_ids[..., None] == jnp.arange(experts, dtype=jnp.int32)).astype(jnp.int32)
    present = jnp.sum(matches, axis=2)
    before = jnp.cumsum(present, axis=1) - present
    occurrence = jnp.sum(matches * before[:, :, None, :], axis=3)
    slot = jnp.arange(capacity, dtype=jnp.int32)
    landing = (
        (expert_ids[..., None, None] == jnp.arange(experts, dtype=jnp.int32)[:, None])
        & (occurrence[..., None, None] == slot)
    ).astype(F32)
    selector = jnp.sum(landing, axis=2)
    weighting = jnp.sum(landing * gate_scores[..., None, None], axis=2)
    packed = jnp.einsum("mres,mrd->emsd", selector.astype(BF), tokens, preferred_element_type=F32)
    packed = packed.astype(BF).reshape(experts, slots, width)

    arrived = lax.all_to_all(packed, ROWS_OF, split_axis=0, concat_axis=0, tiled=True)
    half = experts // 2
    first = lax.all_gather(arrived[:half], "zi", axis=0).reshape(-1, width)
    second = lax.all_gather(arrived[half:], "zi", axis=0).reshape(-1, width)
    hidden = hidden_of(first, second, turned, other_up)
    gathered = lax.all_gather(hidden, "zi", axis=0)
    done = outputs_of(
        jnp.stack([place, lax.axis_index("dp")]).astype(jnp.int32), gathered, shares, other_shares
    )
    done = done.reshape(2, line, half, slots, columns).transpose(0, 2, 1, 3, 4)
    done = done.reshape(experts * line, slots, columns)
    returned = lax.all_to_all(done, HOME, split_axis=0, concat_axis=0, tiled=True)
    returned = returned.reshape(experts, line, batches, capacity, columns).astype(F32)
    mixed = jnp.einsum("mres,ezmsd->mrzd", weighting, returned, precision=lax.Precision.HIGHEST)
    return mixed.astype(BF).reshape(batches, row_count, width)


def solution(mesh):
    fine = Mesh(mesh.devices.reshape(4, 4, 4, 2, 4), ("x", "zb", "zi", "c", "dp"))
    ep = ("x", "zb", "zi", "c")
    by_row = P(None, ("dp",) + ep, None)
    return jax.shard_map(
        on_device,
        mesh=fine,
        in_specs=(by_row, by_row, by_row, P(ep, None, None)),
        out_specs=by_row,
        check_vma=False,
    )
```

time: 181 us -> 191 us (1.055)
  between operations: 13.7 us -> 0.28 us
  waiting for transfers between devices: 11 us -> 23.4 us
  starting transfers between devices: 31.8 us -> 41.4 us
  Pallas kernels: 0 us -> 9.38 us
  matrix products: 8.78 us -> 1.33 us
  local copies, waits for them, and re-layouts: 8.44 us -> 11.8 us
  blocking collectives: 101 us -> 98.3 us
  other arithmetic: 5.67 us -> 3.59 us
    ppermute x3 -> x6, waiting for transfers between devices: 11 us -> 23.4 us  [exchange(): return lax.ppermute(array, axis, [(i, i ^ step) for i in range(size)])]
    ppermute x3 -> x6, starting transfers between devices: 10.1 us -> 19.9 us  [exchange(): return lax.ppermute(array, axis, [(i, i ^ step) for i in range(size)])]
    pallas_call x0 -> x2, Pallas kernels: none -> 9.38 us  [the longest x1 6.83 us: hidden_of(): pl.pallas_call(up_kernel, grid=(width // chunk,), in_specs=[rows, rows, w...]
    dot_general x4 -> x1, matrix products: 8.46 us -> 1.02 us  [on_device(): jnp.einsum('mres,ezmsd->mrzd', weighting, returned, precision=lax.Precisi...]
    unnamed x10 -> x8, local copies, waits for them, and re-layouts: 0.07 us -> 2.22 us
  transfers between devices with their start and end apart: 7 -> 9, of which waited for: 2 -> 4; matrix products, arithmetic and copies ran while one was open for 9% -> 4% of each run, Pallas kernels for 0% -> 4%
where the time goes in v5:
time: 191 us; the launch traced here: 190 us
  blocking collectives  98.3 us (51%)
  starting transfers between devices  41.4 us (22%)
  waiting for transfers between devices  23.4 us (12%)
  local copies, waits for them, and re-layouts  11.8 us (6%)
  Pallas kernels  9.38 us (5%)
  other arithmetic  3.59 us (2%)
    all_to_all x1, blocking collectives, on_device(): lax.all_to_all(done, HOME, split_axis=0, concat_axis=0, tiled=True)  39.2 us
    ppermute x6, waiting for transfers between devices, exchange(): return lax.ppermute(array, axis, [(i, i ^ step) for i in range(size)])  23.4 us
    all_gather x1, blocking collectives, on_device(): second = lax.all_gather(arrived[half:], 'zi', axis=0).reshape(-1, width)  21 us
    all_gather x1, blocking collectives, on_device(): first = lax.all_gather(arrived[:half], 'zi', axis=0).reshape(-1, width)  20 us
    ppermute x6, starting transfers between devices, exchange(): return lax.ppermute(array, axis, [(i, i ^ step) for i in range(size)])  19.9 us
    all_gather x1, blocking collectives, on_device(): gathered = lax.all_gather(hidden, 'zi', axis=0)  18.2 us
    all_to_all x1, starting transfers between devices, on_device(): lax.all_to_all(packed, ROWS_OF, split_axis=0, concat_axis=0, tiled=True)  17.7 us
    pallas_call x1, Pallas kernels, hidden_of(): pl.pallas_call(up_kernel, grid=(width // chunk,), in_specs=[rows, rows, w...  6.83 us
  transfers between devices with their start and end apart: 9, of which 4 were waited for; matrix products, arithmetic and copies ran while one was open for 4% of the time, Pallas kernels for 4%

profile of v5, /device:TPU:24, one launch (start us, length us, event | category | flops | bytes accessed | tf_op | source)
XLA Modules:
  0.0 189.6 jit_solution(5062721704215611961)
XLA Ops:
  0.0 0.0 copy-start
  0.0 0.8 convert_reduce_fusion
  0.8 0.8 iota_compare_fusion
  1.6 0.9 select_reduce_fusion
  2.5 0.8 fusion.3
  3.3 0.0 copy-done
  3.3 0.3 convolution_convert_fusion
  3.6 1.1 copy.26
  4.7 17.7 %all-to-all-start = ((bf16[16,4,3584]{2,1,0:T(4,128)(2,1)}), bf16[16,4,3584]{2,1,0:T(4,128)(2,1)S(1)}, u32[]{:S(2)}, u32[]{:S(2)}) async-start(bf16[16,4,3584]{2,1,0:T(4,128)(2,1)} %copy.26), calls=%async_computation | async-start | bytes 917504 | tf_op jit(solution)/shard_map/all_to_all | solution.py:129
  22.4 3.5 %slice.14 = bf16[384,3584]{1,0:T(8,128)(2,1)} slice(bf16[576,3584]{1,0:T(8,128)(2,1)} %bitcast.53), slice={[0:384], [0:3584]} | slice | bytes 5505024 | tf_op jit(solution)/shard_map/slice | solution.py:99
  25.9 1.9 %collective-permute-start = (bf16[384,3584]{1,0:T(8,128)(2,1)}, bf16[384,3584]{1,0:T(8,128)(2,1)}, u32[]{:S(2)}, u32[]{:S(2)}) collective-permute-start(bf16[384,3584]{1,0:T(8,128)(2,1)} %slice.14), channel_id=1, source_target_pairs={{0,4},{4,0},{1,5},{5,1},{2,6},{6,2},{3,7},{7,3},{8,12},{12,8},{9,1... | collective-permute-start | bytes 8257544 | tf_op jit(solution)/shard_map/ppermute | solution.py:22
  27.8 1.0 dynamic-slice_bitcast_fusion
  28.8 0.1 reshape.59
  29.0 0.7 constant_dynamic-slice_fusion.3
  29.7 3.8 %collective-permute-start.3 = (bf16[48,896]{1,0:T(8,128)(2,1)S(1)}, bf16[48,896]{1,0:T(8,128)(2,1)S(1)}, u32[]{:S(2)}, u32[]{:S(2)}) collective-permute-start(bf16[48,896]{1,0:T(8,128)(2,1)S(1)} %bitcast.62), channel_id=1, source_target_pairs={{0,24},{8,16},{16,8},{24,0},{1,25},{9,17},{17,9},{25,1},{2,26},{10... | collective-permute-start | bytes 258056 | tf_op jit(solution)/shard_map/ppermute | solution.py:18
  33.6 2.5 %collective-permute-start.2 = (bf16[48,896]{1,0:T(8,128)(2,1)S(1)}, bf16[48,896]{1,0:T(8,128)(2,1)S(1)}, u32[]{:S(2)}, u32[]{:S(2)}) collective-permute-start(bf16[48,896]{1,0:T(8,128)(2,1)S(1)} %bitcast.63), channel_id=1, source_target_pairs={{0,16},{8,24},{16,0},{24,8},{1,17},{9,25},{17,1},{25,9},{2,18},{10... | collective-permute-start | bytes 258056 | tf_op jit(solution)/shard_map/ppermute | solution.py:18
  36.1 3.8 %collective-permute-start.1 = (bf16[48,896]{1,0:T(8,128)(2,1)S(1)}, bf16[48,896]{1,0:T(8,128)(2,1)S(1)}, u32[]{:S(2)}, u32[]{:S(2)}) collective-permute-start(bf16[48,896]{1,0:T(8,128)(2,1)S(1)} %bitcast.64), channel_id=1, source_target_pairs={{0,8},{8,0},{16,24},{24,16},{1,9},{9,1},{17,25},{25,17},{2,10},{10... | collective-permute-start | bytes 258056 | tf_op jit(solution)/shard_map/ppermute | solution.py:18
  39.9 3.3 %collective-permute-done.3 = bf16[48,896]{1,0:T(8,128)(2,1)S(1)} collective-permute-done((bf16[48,896]{1,0:T(8,128)(2,1)S(1)}, bf16[48,896]{1,0:T(8,128)(2,1)S(1)}, u32[]{:S(2)}, u32[]{:S(2)}) %collective-permute-start.3) | collective-permute-done | bytes 86048 | tf_op jit(solution)/shard_map/ppermute | solution.py:18
  43.3 7.7 %collective-permute-done.2 = bf16[48,896]{1,0:T(8,128)(2,1)S(1)} collective-permute-done((bf16[48,896]{1,0:T(8,128)(2,1)S(1)}, bf16[48,896]{1,0:T(8,128)(2,1)S(1)}, u32[]{:S(2)}, u32[]{:S(2)}) %collective-permute-start.2) | collective-permute-done | bytes 86048 | tf_op jit(solution)/shard_map/ppermute | solution.py:18
  50.9 0.0 collective-permute-done.1
  50.9 0.1 fusion.7
  51.0 2.1 %collective-permute-start.6 = (bf16[4,48,896]{2,1,0:T(8,128)(2,1)S(1)}, bf16[4,48,896]{2,1,0:T(8,128)(2,1)S(1)}, u32[]{:S(2)}, u32[]{:S(2)}) collective-permute-start(bf16[4,48,896]{2,1,0:T(8,128)(2,1)S(1)} %get-tuple-element.10), channel_id=1, source_target_pairs={{0,3},{1,2},{2,1},{3,0},{4,7},{5,6},{6,5},{7,4},{8,11},{9,10},{10,... | collective-permute-start | bytes 1032200 | tf_op jit(solution)/shard_map/ppermute | solution.py:18
  53.1 4.5 %collective-permute-start.5 = (bf16[4,48,896]{2,1,0:T(8,128)(2,1)S(1)}, bf16[4,48,896]{2,1,0:T(8,128)(2,1)S(1)}, u32[]{:S(2)}, u32[]{:S(2)}) collective-permute-start(bf16[4,48,896]{2,1,0:T(8,128)(2,1)S(1)} %get-tuple-element.10), channel_id=1, source_target_pairs={{0,2},{1,3},{2,0},{3,1},{4,6},{5,7},{6,4},{7,5},{8,10},{9,11},{10,... | collective-permute-start | bytes 1032200 | tf_op jit(solution)/shard_map/ppermute | solution.py:18
  57.7 3.2 %collective-permute-start.4 = (bf16[4,48,896]{2,1,0:T(8,128)(2,1)S(1)}, bf16[4,48,896]{2,1,0:T(8,128)(2,1)S(1)}, u32[]{:S(2)}, u32[]{:S(2)}) collective-permute-start(bf16[4,48,896]{2,1,0:T(8,128)(2,1)S(1)} %get-tuple-element.10), channel_id=1, source_target_pairs={{0,1},{1,0},{2,3},{3,2},{4,5},{5,4},{6,7},{7,6},{8,9},{9,8},{10,11... | collective-permute-start | bytes 1032200 | tf_op jit(solution)/shard_map/ppermute | solution.py:18
  60.9 0.1 pad_add_fusion.place_ref
  60.9 9.8 %collective-permute-done.6 = bf16[4,48,896]{2,1,0:T(8,128)(2,1)S(1)} collective-permute-done((bf16[4,48,896]{2,1,0:T(8,128)(2,1)S(1)}, bf16[4,48,896]{2,1,0:T(8,128)(2,1)S(1)}, u32[]{:S(2)}, u32[]{:S(2)}) %collective-permute-start.6) | collective-permute-done | bytes 344096 | tf_op jit(solution)/shard_map/ppermute | solution.py:18
  70.8 0.0 collective-permute-done.5
  70.8 2.5 %collective-permute-done.4 = bf16[4,48,896]{2,1,0:T(8,128)(2,1)S(1)} collective-permute-done((bf16[4,48,896]{2,1,0:T(8,128)(2,1)S(1)}, bf16[4,48,896]{2,1,0:T(8,128)(2,1)S(1)}, u32[]{:S(2)}, u32[]{:S(2)}) %collective-permute-start.4) | collective-permute-done | bytes 344096 | tf_op jit(solution)/shard_map/ppermute | solution.py:18
  73.3 0.2 pad_maximum_fusion.own_ref
  73.5 1.9 %collective-permute-start.7 = (bf16[4,4,48,896]{3,2,1,0:T(8,128)(2,1)S(1)}, bf16[4,4,48,896]{3,2,1,0:T(8,128)(2,1)}, u32[]{:S(2)}, u32[]{:S(2)}) collective-permute-start(bf16[4,4,48,896]{3,2,1,0:T(8,128)(2,1)S(1)} %pad_maximum_fusion.own_ref), channel_id=1, source_target_pairs={{0,4},{4,0},{1,5},{5,1},{2,6},{6,2},{3,7},{7,3},{8,12},{12,8},{9,1... | collective-permute-start | bytes 4128776 | tf_op jit(solution)/shard_map/ppermute | solution.py:22
  75.4 0.0 all-to-all-done
  75.4 0.8 fusion.8
  76.3 20.0 %all-gather = bf16[32,4,3584]{2,1,0:T(4,128)(2,1)S(1)} all-gather(bf16[8,4,3584]{2,1,0:T(4,128)(2,1)S(1)} %get-tuple-element.8), channel_id=2, replica_groups=mesh['x'=4,'zb'=4,'zi'=4,'c'=2,'dp'=4] {'zi'}, dimensions={0}, use_global_device_ids=true | all-gather | bytes 1146880 | tf_op jit(solution)/shard_map/all_gather | solution.py:131
  96.3 0.2 reshape.56.first_ref
  96.5 21.0 %all-gather.1 = bf16[32,4,3584]{2,1,0:T(4,128)(2,1)} all-gather(bf16[8,4,3584]{2,1,0:T(4,128)(2,1)} %get-tuple-element.7), channel_id=3, replica_groups=mesh['x'=4,'zb'=4,'zi'=4,'c'=2,'dp'=4] {'zi'}, dimensions={0}, use_global_device_ids=true | all-gather | bytes 1146880 | tf_op jit(solution)/shard_map/all_gather | solution.py:132
  117.4 1.7 reshape.57.second_ref
  119.1 0.0 collective-permute-done.other_ref
  119.1 0.0 copy-start.1
  119.1 2.2 %copy-done.1 = bf16[1,3584,576]{1,2,0:T(8,128)(2,1)S(1)} copy-done((bf16[1,3584,576]{1,2,0:T(8,128)(2,1)S(1)}, bf16[1,3584,576]{1,2,0:T(8,128)(2,1)}, u32[]{:S(2)}) %copy-start.1) | copy-done | bytes 4128792
  121.3 6.8 %shard_map.46 = bf16[256,384]{1,0:T(8,128)(2,1)S(1)} custom-call(bf16[128,3584]{1,0:T(8,128)(2,1)S(1)} %reshape.56.first_ref, bf16[128,3584]{1,0:T(8,128)(2,1)S(1)} %reshape.57.second_ref, bf16[576,3584]{1,0:T(8,128)(2,1)S(1)} %bitcast.54, bf16[384,3584]{1,0:T(8,128)(2,1)} %collective-permute-done.other_ref), custom_call_target="tpu_custom_call" | custom-call | tf_op jit(solution)/shard_map/pallas_call | solution.py:55
  128.1 18.2 %all-gather.2 = bf16[1024,384]{1,0:T(8,128)(2,1)S(1)} all-gather(bf16[256,384]{1,0:T(8,128)(2,1)S(1)} %shard_map.46), channel_id=4, replica_groups=mesh['x'=4,'zb'=4,'zi'=4,'c'=2,'dp'=4] {'zi'}, dimensions={0}, use_global_device_ids=true | all-gather | bytes 983040 | tf_op jit(solution)/shard_map/all_gather | solution.py:134
  146.3 0.0 collective-permute-done.7.other_ref
  146.3 2.5 %shard_map.47 = bf16[256,896]{1,0:T(8,128)(2,1)S(1)} custom-call(s32[2]{0:T(128)S(1)} %pad_add_fusion.place_ref, bf16[4,256,384]{2,1,0:T(8,128)(2,1)S(1)} %bitcast.55, bf16[4,4,48,896]{3,2,1,0:T(8,128)(2,1)S(1)} %pad_maximum_fusion.own_ref, bf16[4,4,48,896]{3,2,1,0:T(8,128)(2,1)} %collective-permute-done.7.other_ref), custom_call_target="tpu_custom_call" | custom-call | tf_op jit(solution)/shard_map/pallas_call | solution.py:81
  148.9 0.1 reshape.60
  149.0 0.2 copy.27
  149.1 39.2 %all_to_all.10 = bf16[64,4,896]{2,1,0:T(4,128)(2,1)S(1)} all-to-all(bf16[64,4,896]{2,1,0:T(4,128)(2,1)S(1)} %bitcast.57), channel_id=1, replica_groups=mesh['x'=4,'zb'=4,'zi'=4,'c'=2,'dp'=4] {'x','zb','zi'}, dimensions={0} | all-to-all | bytes 917504 | tf_op jit(solution)/shard_map/all_to_all | solution.py:140
  188.4 0.2 reshape.72
  188.5 1.0 fusion
  (7 shorter events, 0.1 us)
Async XLA Ops:
  0.0 3.3 %copy-start = (bf16[2,8,3584]{2,1,0:T(8,128)(2,1)S(1)}, bf16[2,8,3584]{2,1,0:T(8,128)(2,1)}, u32[]{:S(2)}) copy-start(bf16[2,8,3584]{2,1,0:T(8,128)(2,1)} %param.4) | copy-start | bytes 344068
  4.7 70.7 %all-to-all-start = ((bf16[16,4,3584]{2,1,0:T(4,128)(2,1)}), bf16[16,4,3584]{2,1,0:T(4,128)(2,1)S(1)}, u32[]{:S(2)}, u32[]{:S(2)}) async-start(bf16[16,4,3584]{2,1,0:T(4,128)(2,1)} %copy.26), calls=%async_computation | async-start | bytes 917504 | tf_op jit(solution)/shard_map/all_to_all | solution.py:129
  25.9 93.2 %collective-permute-start = (bf16[384,3584]{1,0:T(8,128)(2,1)}, bf16[384,3584]{1,0:T(8,128)(2,1)}, u32[]{:S(2)}, u32[]{:S(2)}) collective-permute-start(bf16[384,3584]{1,0:T(8,128)(2,1)} %slice.14), channel_id=1, source_target_pairs={{0,4},{4,0},{1,5},{5,1},{2,6},{6,2},{3,7},{7,3},{8,12},{12,8},{9,1... | collective-permute-start | bytes 8257544 | tf_op jit(solution)/shard_map/ppermute | solution.py:22
  29.7 13.5 %collective-permute-start.3 = (bf16[48,896]{1,0:T(8,128)(2,1)S(1)}, bf16[48,896]{1,0:T(8,128)(2,1)S(1)}, u32[]{:S(2)}, u32[]{:S(2)}) collective-permute-start(bf16[48,896]{1,0:T(8,128)(2,1)S(1)} %bitcast.62), channel_id=1, source_target_pairs={{0,24},{8,16},{16,8},{24,0},{1,25},{9,17},{17,9},{25,1},{2,26},{10... | collective-permute-start | bytes 258056 | tf_op jit(solution)/shard_map/ppermute | solution.py:18
  33.6 17.4 %collective-permute-start.2 = (bf16[48,896]{1,0:T(8,128)(2,1)S(1)}, bf16[48,896]{1,0:T(8,128)(2,1)S(1)}, u32[]{:S(2)}, u32[]{:S(2)}) collective-permute-start(bf16[48,896]{1,0:T(8,128)(2,1)S(1)} %bitcast.63), channel_id=1, source_target_pairs={{0,16},{8,24},{16,0},{24,8},{1,17},{9,25},{17,1},{25,9},{2,18},{10... | collective-permute-start | bytes 258056 | tf_op jit(solution)/shard_map/ppermute | solution.py:18
  36.1 14.9 %collective-permute-start.1 = (bf16[48,896]{1,0:T(8,128)(2,1)S(1)}, bf16[48,896]{1,0:T(8,128)(2,1)S(1)}, u32[]{:S(2)}, u32[]{:S(2)}) collective-permute-start(bf16[48,896]{1,0:T(8,128)(2,1)S(1)} %bitcast.64), channel_id=1, source_target_pairs={{0,8},{8,0},{16,24},{24,16},{1,9},{9,1},{17,25},{25,17},{2,10},{10... | collective-permute-start | bytes 258056 | tf_op jit(solution)/shard_map/ppermute | solution.py:18
  51.0 19.7 %collective-permute-start.6 = (bf16[4,48,896]{2,1,0:T(8,128)(2,1)S(1)}, bf16[4,48,896]{2,1,0:T(8,128)(2,1)S(1)}, u32[]{:S(2)}, u32[]{:S(2)}) collective-permute-start(bf16[4,48,896]{2,1,0:T(8,128)(2,1)S(1)} %get-tuple-element.10), channel_id=1, source_target_pairs={{0,3},{1,2},{2,1},{3,0},{4,7},{5,6},{6,5},{7,4},{8,11},{9,10},{10,... | collective-permute-start | bytes 1032200 | tf_op jit(solution)/shard_map/ppermute | solution.py:18
  53.1 17.6 %collective-permute-start.5 = (bf16[4,48,896]{2,1,0:T(8,128)(2,1)S(1)}, bf16[4,48,896]{2,1,0:T(8,128)(2,1)S(1)}, u32[]{:S(2)}, u32[]{:S(2)}) collective-permute-start(bf16[4,48,896]{2,1,0:T(8,128)(2,1)S(1)} %get-tuple-element.10), channel_id=1, source_target_pairs={{0,2},{1,3},{2,0},{3,1},{4,6},{5,7},{6,4},{7,5},{8,10},{9,11},{10,... | collective-permute-start | bytes 1032200 | tf_op jit(solution)/shard_map/ppermute | solution.py:18
  57.7 15.6 %collective-permute-start.4 = (bf16[4,48,896]{2,1,0:T(8,128)(2,1)S(1)}, bf16[4,48,896]{2,1,0:T(8,128)(2,1)S(1)}, u32[]{:S(2)}, u32[]{:S(2)}) collective-permute-start(bf16[4,48,896]{2,1,0:T(8,128)(2,1)S(1)} %get-tuple-element.10), channel_id=1, source_target_pairs={{0,1},{1,0},{2,3},{3,2},{4,5},{5,4},{6,7},{7,6},{8,9},{9,8},{10,11... | collective-permute-start | bytes 1032200 | tf_op jit(solution)/shard_map/ppermute | solution.py:18
  73.5 72.8 %collective-permute-start.7 = (bf16[4,4,48,896]{3,2,1,0:T(8,128)(2,1)S(1)}, bf16[4,4,48,896]{3,2,1,0:T(8,128)(2,1)}, u32[]{:S(2)}, u32[]{:S(2)}) collective-permute-start(bf16[4,4,48,896]{3,2,1,0:T(8,128)(2,1)S(1)} %pad_maximum_fusion.own_ref), channel_id=1, source_target_pairs={{0,4},{4,0},{1,5},{5,1},{2,6},{6,2},{3,7},{7,3},{8,12},{12,8},{9,1... | collective-permute-start | bytes 4128776 | tf_op jit(solution)/shard_map/ppermute | solution.py:22
  119.1 2.2 %copy-start.1 = (bf16[1,3584,576]{1,2,0:T(8,128)(2,1)S(1)}, bf16[1,3584,576]{1,2,0:T(8,128)(2,1)}, u32[]{:S(2)}) copy-start(bf16[1,3584,576]{1,2,0:T(8,128)(2,1)} %param.7) | copy-start | bytes 12386308

commit v6 on v5

v6 whole, which is shorter than its diff:
```python
import jax
import jax.numpy as jnp
from jax import lax
from jax.experimental import pallas as pl
from jax.experimental.pallas import tpu as pltpu
from jax.sharding import Mesh, PartitionSpec as P

FF = 1536
BF = jnp.bfloat16
F32 = jnp.float32
ROWS_OF = ("x", "zb")
HOME = ("x", "zb", "zi")
NT = (((1,), (1,)), ((), ()))


def exchange(array, axis, step):
    size = lax.axis_size(axis)
    return lax.ppermute(array, axis, [(i, i ^ step) for i in range(size)])


def swap(array):
    return lax.ppermute(array, "c", [(0, 1), (1, 0)])


def pack_kernel(ids_ref, tokens_ref, out_ref):
    batches, picks, rows = ids_ref.shape
    experts, slots, width = out_ref.shape
    capacity = slots // batches
    count = experts * slots
    expert = lax.broadcasted_iota(jnp.int32, (experts, rows), 0)
    row = lax.broadcasted_iota(jnp.int32, (rows, rows), 0)
    earlier = (row < lax.broadcasted_iota(jnp.int32, (rows, rows), 1)).astype(F32)
    owner = lax.broadcasted_iota(jnp.int32, (count, experts), 0) // slots
    spread = (owner == lax.broadcasted_iota(jnp.int32, (count, experts), 1)).astype(F32)
    slot = lax.broadcasted_iota(jnp.int32, (count, rows), 0) % slots
    total = jnp.zeros((count, width), F32)
    for m in range(batches):
        ids = ids_ref[m]
        named = jnp.zeros((experts, rows), jnp.bool_)
        for k in range(picks):
            named = named | (ids[k : k + 1] == expert)
        named = named.astype(F32)
        before = jnp.dot(named, earlier, preferred_element_type=F32)
        named = jnp.dot(spread, named, preferred_element_type=F32)
        before = jnp.dot(spread, before, preferred_element_type=F32)
        here = (slot // capacity == m) & (before == (slot % capacity).astype(F32))
        pick = ((named > 0.5) & here).astype(BF)
        total += jnp.dot(pick, tokens_ref[m], preferred_element_type=F32)
    out_ref[...] = total.astype(BF).reshape(out_ref.shape)


def whole(count):
    return [pl.BlockSpec(memory_space=pltpu.VMEM)] * count


def packed_of(expert_ids, tokens, experts, slots):
    return pl.pallas_call(
        pack_kernel,
        in_specs=whole(2),
        out_specs=whole(1)[0],
        out_shape=jax.ShapeDtypeStruct((experts, slots, tokens.shape[2]), BF),
        compiler_params=pltpu.CompilerParams(vmem_limit_bytes=32 << 20),
    )(expert_ids.transpose(0, 2, 1), tokens)


def up_kernel(first_ref, second_ref, own_ref, other_ref, out_ref):
    units = own_ref.shape[0] // 3
    width = own_ref.shape[1]
    rows = [ref[...].reshape(-1, width) for ref in (first_ref, second_ref)]
    rows = jnp.concatenate(rows, axis=0)
    hidden = []
    for ref in (own_ref, other_ref):
        both = lax.dot_general(ref[: 2 * units], rows, NT, preferred_element_type=F32)
        gate = both[:units]
        hidden.append(gate / (1.0 + jnp.exp(-gate)) * both[units:])
    out_ref[...] = jnp.concatenate(hidden, axis=0).T.astype(BF)


def hidden_of(first, second, own, other):
    count = 2 * first.shape[0] * first.shape[1]
    return pl.pallas_call(
        up_kernel,
        in_specs=whole(4),
        out_specs=whole(1)[0],
        out_shape=jax.ShapeDtypeStruct((count, own.shape[0] // 3 * 2), BF),
        compiler_params=pltpu.CompilerParams(vmem_limit_bytes=48 << 20),
    )(first, second, own, other)


def down_kernel(place_ref, hidden_ref, own_ref, other_ref, out_ref):
    shares, line = own_ref.shape[:2]
    total = jnp.zeros((hidden_ref.shape[1], out_ref.shape[3]), F32)
    for at in range(line):
        k = place_ref[0] ^ at
        weights = [ref[place_ref[1] ^ y, k] for ref in (own_ref, other_ref) for y in range(shares)]
        weights = jnp.concatenate(weights, axis=0)
        total += jnp.dot(hidden_ref[at], weights, preferred_element_type=F32)
    half, slots, columns = out_ref.shape[0] // 2, out_ref.shape[2], out_ref.shape[3]
    total = total.astype(BF).reshape(2, line, half, slots, columns)
    for part in range(2):
        for at in range(line):
            out_ref[part * half : (part + 1) * half, at] = total[part, at]


def outputs_of(place, hidden, own, other, experts, slots):
    return pl.pallas_call(
        down_kernel,
        in_specs=[pl.BlockSpec(memory_space=pltpu.SMEM)] + whole(3),
        out_specs=whole(1)[0],
        out_shape=jax.ShapeDtypeStruct((experts, hidden.shape[0], slots, own.shape[3]), BF),
        compiler_params=pltpu.CompilerParams(vmem_limit_bytes=32 << 20),
    )(place, hidden, own, other)


def on_device(tokens, expert_ids, gate_scores, expert_weights):
    batches, row_count, width = tokens.shape
    experts = lax.axis_size("x") * lax.axis_size("zb")
    line = lax.axis_size("zi")
    capacity = 2
    slots = batches * capacity
    columns = width // line
    turned = expert_weights[0].T
    units = turned.shape[0] // 3
    place = lax.axis_index("zi")
    share = units // lax.axis_size("dp")
    down = lax.dynamic_slice_in_dim(turned, 2 * units + share * lax.axis_index("dp"), share, 0)
    down = down.reshape(share, line, columns)

    def for_place(at):
        return lax.dynamic_index_in_dim(down, at, 1, keepdims=False)

    pieces = [for_place(place)] + [exchange(for_place(place ^ k), "zi", k) for k in range(1, line)]
    pieces = jnp.stack(pieces)
    shares = [pieces] + [exchange(pieces, "dp", k) for k in range(1, lax.axis_size("dp"))]
    other = swap(turned)

    matches = (expert_ids[..., None] == jnp.arange(experts, dtype=jnp.int32)).astype(jnp.int32)
    present = jnp.sum(matches, axis=2)
    before = jnp.cumsum(present, axis=1) - present
    occurrence = jnp.sum(matches * before[:, :, None, :], axis=3)
    slot = jnp.arange(capacity, dtype=jnp.int32)
    landing = (
        (expert_ids[..., None, None] == jnp.arange(experts, dtype=jnp.int32)[:, None])
        & (occurrence[..., None, None] == slot)
    ).astype(F32)
    weighting = jnp.sum(landing * gate_scores[..., None, None], axis=2)
    packed = packed_of(expert_ids, tokens, experts, slots)
    arrived = lax.all_to_all(packed, ROWS_OF, split_axis=0, concat_axis=0, tiled=True)
    half = experts // 2
    first = lax.all_gather(arrived[:half], "zi", axis=0, tiled=True)
    second = lax.all_gather(arrived[half:], "zi", axis=0, tiled=True)
    mark = second[0, 0, 0]
    shares = jnp.where(mark == mark, jnp.stack(shares), jnp.zeros((), BF))
    other_shares = swap(shares)
    hidden = hidden_of(first, second, turned, other)
    gathered = lax.all_gather(hidden, "zi", axis=0)
    position = jnp.stack([place, lax.axis_index("dp")]).astype(jnp.int32)
    done = outputs_of(position, gathered, shares, other_shares, experts, slots)
    done = done.reshape(experts * line, slots, columns)
    returned = lax.all_to_all(done, HOME, split_axis=0, concat_axis=0, tiled=True)
    returned = returned.reshape(experts, line, batches, capacity, columns).astype(F32)
    mixed = jnp.einsum("mres,ezmsd->mrzd", weighting, returned, precision=lax.Precision.HIGHEST)
    return mixed.astype(BF).reshape(batches, row_count, width)


def solution(mesh):
    fine = Mesh(mesh.devices.reshape(4, 4, 4, 2, 4), ("x", "zb", "zi", "c", "dp"))
    ep = ("x", "zb", "zi", "c")
    by_row = P(None, ("dp",) + ep, None)
    return jax.shard_map(
        on_device,
        mesh=fine,
        in_specs=(by_row, by_row, by_row, P(ep, None, None)),
        out_specs=by_row,
        check_vma=False,
    )
```

time: 191 us -> 170 us (0.89)
  blocking collectives: 98.3 us -> 57.5 us
  waiting for transfers between devices: 23.4 us -> 39.2 us
  starting transfers between devices: 41.4 us -> 56.1 us
  local copies, waits for them, and re-layouts: 11.8 us -> 4.36 us
  other arithmetic: 3.59 us -> 0.88 us
    all_to_all x1 -> x0, blocking collectives: 39.2 us -> none  [on_device(): lax.all_to_all(done, HOME, split_axis=0, concat_axis=0, tiled=True)]
    all_to_all x0 -> x1, waiting for transfers between devices: none -> 24.6 us  [on_device(): lax.all_to_all(done, HOME, split_axis=0, concat_axis=0, tiled=True)]
    all_to_all x0 -> x1, starting transfers between devices: none -> 14.7 us  [on_device(): lax.all_to_all(done, HOME, split_axis=0, concat_axis=0, tiled=True)]
    ppermute x6, waiting for transfers between devices: 23.4 us -> 14.5 us  [exchange(): return lax.ppermute(array, axis, [(i, i ^ step) for i in range(size)])]
    slice x2, local copies, waits for them, and re-layouts: 4.35 us -> 0.74 us  [the longest x1 0.58 us: on_device(): mark = second[0, 0, 0]]
    reshape x5 -> x0, local copies, waits for them, and re-layouts: 3.27 us -> none  [the longest x1 1.66 us: on_device(): second = lax.all_gather(arrived[half:], 'zi', axis=0).reshape(-1, width)]
    pallas_call x1 -> x2, Pallas kernels: 6.83 us -> 5.27 us  [the longest x1 3.89 us: hidden_of(): pl.pallas_call(up_kernel, in_specs=whole(4), out_specs=whole(1)[0], out_s...]
  transfers between devices with their start and end apart: 9 -> 10, of which waited for: 4 -> 3; matrix products, arithmetic and copies ran while one was open for 4% -> 2% of each run, Pallas kernels for 4% -> 2%
where the time goes in v6:
time: 170 us; the launch traced here: 169 us
  blocking collectives  57.5 us (34%)
  starting transfers between devices  56.1 us (33%)
  waiting for transfers between devices  39.2 us (23%)
  Pallas kernels  7.79 us (5%)
  local copies, waits for them, and re-layouts  4.36 us (3%)
    all_to_all x1, waiting for transfers between devices, on_device(): lax.all_to_all(done, HOME, split_axis=0, concat_axis=0, tiled=True)  24.6 us
    all_gather x1, blocking collectives, on_device(): first = lax.all_gather(arrived[:half], 'zi', axis=0, tiled=True)  20 us
    ppermute x6, starting transfers between devices, exchange(): return lax.ppermute(array, axis, [(i, i ^ step) for i in range(size)])  19.9 us
    all_gather x1, blocking collectives, on_device(): second = lax.all_gather(arrived[half:], 'zi', axis=0, tiled=True)  19.2 us
    all_gather x1, blocking collectives, on_device(): gathered = lax.all_gather(hidden, 'zi', axis=0)  18.4 us
    all_to_all x1, starting transfers between devices, on_device(): lax.all_to_all(packed, ROWS_OF, split_axis=0, concat_axis=0, tiled=True)  17.7 us
    all_to_all x1, starting transfers between devices, on_device(): lax.all_to_all(done, HOME, split_axis=0, concat_axis=0, tiled=True)  14.7 us
    ppermute x6, waiting for transfers between devices, exchange(): return lax.ppermute(array, axis, [(i, i ^ step) for i in range(size)])  14.5 us
  transfers between devices with their start and end apart: 10, of which 3 were waited for; matrix products, arithmetic and copies ran while one was open for 2% of the time, Pallas kernels for 2%

profile of v6, /device:TPU:24, one launch (start us, length us, event | category | flops | bytes accessed | tf_op | source)
XLA Modules:
  0.0 168.5 jit_solution(912210608269055371)
XLA Ops:
  0.0 0.0 copy-start.1
  0.0 0.9 copy-done.1
  0.9 0.0 copy-start.2
  0.9 0.7 copy-done.2
  1.6 1.4 shard_map.46
  3.0 17.7 %all-to-all-start = ((bf16[16,4,3584]{2,1,0:T(4,128)(2,1)}), bf16[16,4,3584]{2,1,0:T(4,128)(2,1)S(1)}, u32[]{:S(2)}, u32[]{:S(2)}) async-start(bf16[16,4,3584]{2,1,0:T(4,128)(2,1)} %shard_map.46), calls=%async_computation | async-start | bytes 917504 | tf_op jit(solution)/shard_map/all_to_all | solution.py:148
  20.6 1.9 %collective-permute-start = (bf16[576,3584]{1,0:T(8,128)(2,1)}, bf16[576,3584]{1,0:T(8,128)(2,1)}, u32[]{:S(2)}, u32[]{:S(2)}) collective-permute-start(bf16[576,3584]{1,0:T(8,128)(2,1)} %bitcast.44), channel_id=1, source_target_pairs={{0,4},{4,0},{1,5},{5,1},{2,6},{6,2},{3,7},{7,3},{8,12},{12,8},{9,1... | collective-permute-start | bytes 12386312 | tf_op jit(solution)/shard_map/ppermute | solution.py:22
  22.6 1.0 dynamic-slice_bitcast_fusion
  23.6 0.1 reshape.45
  23.7 0.7 constant_dynamic-slice_fusion.3
  24.4 3.8 %collective-permute-start.3 = (bf16[48,896]{1,0:T(8,128)(2,1)S(1)}, bf16[48,896]{1,0:T(8,128)(2,1)S(1)}, u32[]{:S(2)}, u32[]{:S(2)}) collective-permute-start(bf16[48,896]{1,0:T(8,128)(2,1)S(1)} %bitcast.52), channel_id=1, source_target_pairs={{0,24},{8,16},{16,8},{24,0},{1,25},{9,17},{17,9},{25,1},{2,26},{10... | collective-permute-start | bytes 258056 | tf_op jit(solution)/shard_map/ppermute | solution.py:18
  28.3 2.5 %collective-permute-start.2 = (bf16[48,896]{1,0:T(8,128)(2,1)S(1)}, bf16[48,896]{1,0:T(8,128)(2,1)S(1)}, u32[]{:S(2)}, u32[]{:S(2)}) collective-permute-start(bf16[48,896]{1,0:T(8,128)(2,1)S(1)} %bitcast.53), channel_id=1, source_target_pairs={{0,16},{8,24},{16,0},{24,8},{1,17},{9,25},{17,1},{25,9},{2,18},{10... | collective-permute-start | bytes 258056 | tf_op jit(solution)/shard_map/ppermute | solution.py:18
  30.8 3.8 %collective-permute-start.1 = (bf16[48,896]{1,0:T(8,128)(2,1)S(1)}, bf16[48,896]{1,0:T(8,128)(2,1)S(1)}, u32[]{:S(2)}, u32[]{:S(2)}) collective-permute-start(bf16[48,896]{1,0:T(8,128)(2,1)S(1)} %bitcast.54), channel_id=1, source_target_pairs={{0,8},{8,0},{16,24},{24,16},{1,9},{9,1},{17,25},{25,17},{2,10},{10... | collective-permute-start | bytes 258056 | tf_op jit(solution)/shard_map/ppermute | solution.py:18
  34.6 0.9 collective-permute-done.3
  35.6 13.6 %collective-permute-done.2 = bf16[48,896]{1,0:T(8,128)(2,1)S(1)} collective-permute-done((bf16[48,896]{1,0:T(8,128)(2,1)S(1)}, bf16[48,896]{1,0:T(8,128)(2,1)S(1)}, u32[]{:S(2)}, u32[]{:S(2)}) %collective-permute-start.2) | collective-permute-done | bytes 86048 | tf_op jit(solution)/shard_map/ppermute | solution.py:18
  49.2 0.0 collective-permute-done.1
  49.2 0.1 fusion.3
  49.2 2.1 %collective-permute-start.6 = (bf16[4,48,896]{2,1,0:T(8,128)(2,1)S(1)}, bf16[4,48,896]{2,1,0:T(8,128)(2,1)S(1)}, u32[]{:S(2)}, u32[]{:S(2)}) collective-permute-start(bf16[4,48,896]{2,1,0:T(8,128)(2,1)S(1)} %get-tuple-element.8), channel_id=1, source_target_pairs={{0,3},{1,2},{2,1},{3,0},{4,7},{5,6},{6,5},{7,4},{8,11},{9,10},{10,... | collective-permute-start | bytes 1032200 | tf_op jit(solution)/shard_map/ppermute | solution.py:18
  51.4 4.5 %collective-permute-start.5 = (bf16[4,48,896]{2,1,0:T(8,128)(2,1)S(1)}, bf16[4,48,896]{2,1,0:T(8,128)(2,1)S(1)}, u32[]{:S(2)}, u32[]{:S(2)}) collective-permute-start(bf16[4,48,896]{2,1,0:T(8,128)(2,1)S(1)} %get-tuple-element.8), channel_id=1, source_target_pairs={{0,2},{1,3},{2,0},{3,1},{4,6},{5,7},{6,4},{7,5},{8,10},{9,11},{10,... | collective-permute-start | bytes 1032200 | tf_op jit(solution)/shard_map/ppermute | solution.py:18
  55.9 3.2 %collective-permute-start.4 = (bf16[4,48,896]{2,1,0:T(8,128)(2,1)S(1)}, bf16[4,48,896]{2,1,0:T(8,128)(2,1)S(1)}, u32[]{:S(2)}, u32[]{:S(2)}) collective-permute-start(bf16[4,48,896]{2,1,0:T(8,128)(2,1)S(1)} %get-tuple-element.8), channel_id=1, source_target_pairs={{0,1},{1,0},{2,3},{3,2},{4,5},{5,4},{6,7},{7,6},{8,9},{9,8},{10,11... | collective-permute-start | bytes 1032200 | tf_op jit(solution)/shard_map/ppermute | solution.py:18
  59.1 0.0 all-to-all-done
  59.1 0.2 fusion.4
  59.3 0.0 copy-start
  59.3 19.2 %all_gather.13.second_ref = bf16[32,4,3584]{2,1,0:T(4,128)(2,1)S(1)} all-gather(bf16[8,4,3584]{2,1,0:T(4,128)(2,1)S(1)} %get-tuple-element.5), channel_id=1, replica_groups=mesh['x'=4,'zb'=4,'zi'=4,'c'=2,'dp'=4] {'zi'}, dimensions={0}, use_global_device_ids=true | all-gather | bytes 1146880 | tf_op jit(solution)/shard_map/all_gather | solution.py:151
  78.4 0.6 slice.14
  80.4 0.0 collective-permute-done.6
  80.4 0.0 collective-permute-done.5
  80.4 0.0 collective-permute-done.4
  80.4 0.3 maximum_select_fusion.own_ref
  80.7 1.9 %collective-permute-start.7 = (bf16[4,4,48,896]{3,2,1,0:T(8,128)(2,1)S(1)}, bf16[4,4,48,896]{3,2,1,0:T(8,128)(2,1)S(1)}, u32[]{:S(2)}, u32[]{:S(2)}) collective-permute-start(bf16[4,4,48,896]{3,2,1,0:T(8,128)(2,1)S(1)} %maximum_select_fusion.own_ref), channel_id=1, source_target_pairs={{0,4},{4,0},{1,5},{5,1},{2,6},{6,2},{3,7},{7,3},{8,12},{12,8},{9,1... | collective-permute-start | bytes 4128776 | tf_op jit(solution)/shard_map/ppermute | solution.py:22
  82.6 0.1 pad_add_fusion.place_ref
  82.7 20.0 %all_gather.12.first_ref = bf16[32,4,3584]{2,1,0:T(4,128)(2,1)S(1)} all-gather(bf16[8,4,3584]{2,1,0:T(4,128)(2,1)S(1)} %get-tuple-element.6), channel_id=1, replica_groups=mesh['x'=4,'zb'=4,'zi'=4,'c'=2,'dp'=4] {'zi'}, dimensions={0}, use_global_device_ids=true | all-gather | bytes 1146880 | tf_op jit(solution)/shard_map/all_gather | solution.py:150
  102.6 0.0 collective-permute-done.other_ref
  102.6 0.0 copy-done
  102.6 3.9 %shard_map.47 = bf16[256,384]{1,0:T(8,128)(2,1)S(1)} custom-call(bf16[32,4,3584]{2,1,0:T(4,128)(2,1)S(1)} %all_gather.12.first_ref, bf16[32,4,3584]{2,1,0:T(4,128)(2,1)S(1)} %all_gather.13.second_ref, bf16[576,3584]{1,0:T(8,128)(2,1)S(1)} %bitcast.45, bf16[576,3584]{1,0:T(8,128)(2,1)} %collective-permute-done.other_ref), custom_call_target="tpu_custom_call" | custom-call | tf_op jit(solution)/shard_map/pallas_call | solution.py:81
  106.5 18.4 %all-gather = bf16[1024,384]{1,0:T(8,128)(2,1)S(1)} all-gather(bf16[256,384]{1,0:T(8,128)(2,1)S(1)} %shard_map.47), channel_id=2, replica_groups=mesh['x'=4,'zb'=4,'zi'=4,'c'=2,'dp'=4] {'zi'}, dimensions={0}, use_global_device_ids=true | all-gather | bytes 983040 | tf_op jit(solution)/shard_map/all_gather | solution.py:156
  125.0 0.0 collective-permute-done.7.other_ref
  125.0 0.0 copy-start.3
  125.0 0.0 copy-start.4
  125.0 2.5 %shard_map.48 = bf16[16,4,4,896]{3,2,1,0:T(4,128)(2,1)} custom-call(s32[2]{0:T(128)S(1)} %pad_add_fusion.place_ref, bf16[4,256,384]{2,1,0:T(8,128)(2,1)S(1)} %bitcast.46, bf16[4,4,48,896]{3,2,1,0:T(8,128)(2,1)S(1)} %maximum_select_fusion.own_ref, bf16[4,4,48,896]{3,2,1,0:T(8,128)(2,1)S(1)} %collective-permute-done.7.other_ref), custom_call_target="tpu_custom_call" | custom-call | tf_op jit(solution)/shard_map/pallas_call | solution.py:106
  127.5 14.7 %all-to-all-start.1 = ((bf16[64,4,896]{2,1,0:T(4,128)(2,1)}), bf16[64,4,896]{2,1,0:T(4,128)(2,1)S(1)}, u32[]{:S(2)}, u32[]{:S(2)}) async-start(bf16[64,4,896]{2,1,0:T(4,128)(2,1)} %bitcast.19), calls=%async_computation.1 | async-start | bytes 917504 | tf_op jit(solution)/shard_map/all_to_all | solution.py:160
  142.2 0.0 copy-done.3
  142.2 0.1 convert_reduce_fusion
  142.3 0.2 select_reduce_fusion.1
  142.5 0.1 iota_compare_fusion
  142.6 0.0 copy-done.4
  142.6 0.1 select_reduce_fusion
  142.7 24.6 %all-to-all-done.1 = bf16[64,4,896]{2,1,0:T(4,128)(2,1)S(1)} async-done(((bf16[64,4,896]{2,1,0:T(4,128)(2,1)}), bf16[64,4,896]{2,1,0:T(4,128)(2,1)S(1)}, u32[]{:S(2)}, u32[]{:S(2)}) %all-to-all-start.1) | async-done | bytes 458784 | tf_op jit(solution)/shard_map/all_to_all | solution.py:160
  167.3 0.2 reshape.52
  167.5 1.0 fusion
  (7 shorter events, 0.1 us)
Async XLA Ops:
  0.0 0.9 copy-start.1
  0.9 0.7 copy-start.2
  3.0 56.1 %all-to-all-start = ((bf16[16,4,3584]{2,1,0:T(4,128)(2,1)}), bf16[16,4,3584]{2,1,0:T(4,128)(2,1)S(1)}, u32[]{:S(2)}, u32[]{:S(2)}) async-start(bf16[16,4,3584]{2,1,0:T(4,128)(2,1)} %shard_map.46), calls=%async_computation | async-start | bytes 917504 | tf_op jit(solution)/shard_map/all_to_all | solution.py:148
  20.6 82.0 %collective-permute-start = (bf16[576,3584]{1,0:T(8,128)(2,1)}, bf16[576,3584]{1,0:T(8,128)(2,1)}, u32[]{:S(2)}, u32[]{:S(2)}) collective-permute-start(bf16[576,3584]{1,0:T(8,128)(2,1)} %bitcast.44), channel_id=1, source_target_pairs={{0,4},{4,0},{1,5},{5,1},{2,6},{6,2},{3,7},{7,3},{8,12},{12,8},{9,1... | collective-permute-start | bytes 12386312 | tf_op jit(solution)/shard_map/ppermute | solution.py:22
  24.4 11.1 %collective-permute-start.3 = (bf16[48,896]{1,0:T(8,128)(2,1)S(1)}, bf16[48,896]{1,0:T(8,128)(2,1)S(1)}, u32[]{:S(2)}, u32[]{:S(2)}) collective-permute-start(bf16[48,896]{1,0:T(8,128)(2,1)S(1)} %bitcast.52), channel_id=1, source_target_pairs={{0,24},{8,16},{16,8},{24,0},{1,25},{9,17},{17,9},{25,1},{2,26},{10... | collective-permute-start | bytes 258056 | tf_op jit(solution)/shard_map/ppermute | solution.py:18
  28.3 20.9 %collective-permute-start.2 = (bf16[48,896]{1,0:T(8,128)(2,1)S(1)}, bf16[48,896]{1,0:T(8,128)(2,1)S(1)}, u32[]{:S(2)}, u32[]{:S(2)}) collective-permute-start(bf16[48,896]{1,0:T(8,128)(2,1)S(1)} %bitcast.53), channel_id=1, source_target_pairs={{0,16},{8,24},{16,0},{24,8},{1,17},{9,25},{17,1},{25,9},{2,18},{10... | collective-permute-start | bytes 258056 | tf_op jit(solution)/shard_map/ppermute | solution.py:18
  30.8 18.4 %collective-permute-start.1 = (bf16[48,896]{1,0:T(8,128)(2,1)S(1)}, bf16[48,896]{1,0:T(8,128)(2,1)S(1)}, u32[]{:S(2)}, u32[]{:S(2)}) collective-permute-start(bf16[48,896]{1,0:T(8,128)(2,1)S(1)} %bitcast.54), channel_id=1, source_target_pairs={{0,8},{8,0},{16,24},{24,16},{1,9},{9,1},{17,25},{25,17},{2,10},{10... | collective-permute-start | bytes 258056 | tf_op jit(solution)/shard_map/ppermute | solution.py:18
  49.2 31.1 %collective-permute-start.6 = (bf16[4,48,896]{2,1,0:T(8,128)(2,1)S(1)}, bf16[4,48,896]{2,1,0:T(8,128)(2,1)S(1)}, u32[]{:S(2)}, u32[]{:S(2)}) collective-permute-start(bf16[4,48,896]{2,1,0:T(8,128)(2,1)S(1)} %get-tuple-element.8), channel_id=1, source_target_pairs={{0,3},{1,2},{2,1},{3,0},{4,7},{5,6},{6,5},{7,4},{8,11},{9,10},{10,... | collective-permute-start | bytes 1032200 | tf_op jit(solution)/shard_map/ppermute | solution.py:18
  51.4 29.0 %collective-permute-start.5 = (bf16[4,48,896]{2,1,0:T(8,128)(2,1)S(1)}, bf16[4,48,896]{2,1,0:T(8,128)(2,1)S(1)}, u32[]{:S(2)}, u32[]{:S(2)}) collective-permute-start(bf16[4,48,896]{2,1,0:T(8,128)(2,1)S(1)} %get-tuple-element.8), channel_id=1, source_target_pairs={{0,2},{1,3},{2,0},{3,1},{4,6},{5,7},{6,4},{7,5},{8,10},{9,11},{10,... | collective-permute-start | bytes 1032200 | tf_op jit(solution)/shard_map/ppermute | solution.py:18
  55.9 24.5 %collective-permute-start.4 = (bf16[4,48,896]{2,1,0:T(8,128)(2,1)S(1)}, bf16[4,48,896]{2,1,0:T(8,128)(2,1)S(1)}, u32[]{:S(2)}, u32[]{:S(2)}) collective-permute-start(bf16[4,48,896]{2,1,0:T(8,128)(2,1)S(1)} %get-tuple-element.8), channel_id=1, source_target_pairs={{0,1},{1,0},{2,3},{3,2},{4,5},{5,4},{6,7},{7,6},{8,9},{9,8},{10,11... | collective-permute-start | bytes 1032200 | tf_op jit(solution)/shard_map/ppermute | solution.py:18
  59.3 43.4 %copy-start = (bf16[1,3584,576]{1,2,0:T(8,128)(2,1)S(1)}, bf16[1,3584,576]{1,2,0:T(8,128)(2,1)}, u32[]{:S(2)}) copy-start(bf16[1,3584,576]{1,2,0:T(8,128)(2,1)} %param.7) | copy-start | bytes 12386308
  80.7 44.3 %collective-permute-start.7 = (bf16[4,4,48,896]{3,2,1,0:T(8,128)(2,1)S(1)}, bf16[4,4,48,896]{3,2,1,0:T(8,128)(2,1)S(1)}, u32[]{:S(2)}, u32[]{:S(2)}) collective-permute-start(bf16[4,4,48,896]{3,2,1,0:T(8,128)(2,1)S(1)} %maximum_select_fusion.own_ref), channel_id=1, source_target_pairs={{0,4},{4,0},{1,5},{5,1},{2,6},{6,2},{3,7},{7,3},{8,12},{12,8},{9,1... | collective-permute-start | bytes 4128776 | tf_op jit(solution)/shard_map/ppermute | solution.py:22
  125.0 17.2 %copy-start.3 = (s32[2,8,2]{1,2,0:T(2,128)S(1)}, s32[2,8,2]{1,2,0:T(2,128)}, u32[]{:S(2)}) copy-start(s32[2,8,2]{1,2,0:T(2,128)} %param.5) | copy-start | bytes 388
  125.0 17.6 %copy-start.4 = (f32[2,8,2]{1,2,0:T(2,128)S(1)}, f32[2,8,2]{1,2,0:T(2,128)}, u32[]{:S(2)}) copy-start(f32[2,8,2]{1,2,0:T(2,128)} %param.6) | copy-start | bytes 388
  127.5 39.8 %all-to-all-start.1 = ((bf16[64,4,896]{2,1,0:T(4,128)(2,1)}), bf16[64,4,896]{2,1,0:T(4,128)(2,1)S(1)}, u32[]{:S(2)}, u32[]{:S(2)}) async-start(bf16[64,4,896]{2,1,0:T(4,128)(2,1)} %bitcast.19), calls=%async_computation.1 | async-start | bytes 917504 | tf_op jit(solution)/shard_map/all_to_all | solution.py:160

commit v7 on v6

--- a/solution.py
+++ b/solution.py
@@ -16,6 +16,11 @@
 def exchange(array, axis, step):
     size = lax.axis_size(axis)
     return lax.ppermute(array, axis, [(i, i ^ step) for i in range(size)])
+
+
+def after(first, then):
+    mark = first[(0,) * first.ndim]
+    return jnp.where(mark == mark, then, jnp.zeros((), then.dtype))
 
 
 def swap(array):
@@ -63,43 +68,40 @@
     )(expert_ids.transpose(0, 2, 1), tokens)
 
 
-def up_kernel(first_ref, second_ref, own_ref, other_ref, out_ref):
-    units = own_ref.shape[0] // 3
-    width = own_ref.shape[1]
-    rows = [ref[...].reshape(-1, width) for ref in (first_ref, second_ref)]
-    rows = jnp.concatenate(rows, axis=0)
+def up_kernel(rows_ref, own_ref, other_ref, out_ref):
+    units = own_ref.shape[0] // 2
+    rows = rows_ref[...].reshape(-1, own_ref.shape[1])
     hidden = []
     for ref in (own_ref, other_ref):
-        both = lax.dot_general(ref[: 2 * units], rows, NT, preferred_element_type=F32)
+        both = lax.dot_general(ref[...], rows, NT, preferred_element_type=F32)
         gate = both[:units]
         hidden.append(gate / (1.0 + jnp.exp(-gate)) * both[units:])
     out_ref[...] = jnp.concatenate(hidden, axis=0).T.astype(BF)
 
 
-def hidden_of(first, second, own, other):
-    count = 2 * first.shape[0] * first.shape[1]
+def hidden_of(rows, own, other):
+    count = rows.shape[0] * rows.shape[1]
     return pl.pallas_call(
         up_kernel,
-        in_specs=whole(4),
+        in_specs=whole(3),
         out_specs=whole(1)[0],
-        out_shape=jax.ShapeDtypeStruct((count, own.shape[0] // 3 * 2), BF),
+        out_shape=jax.ShapeDtypeStruct((count, own.shape[0]), BF),
         compiler_params=pltpu.CompilerParams(vmem_limit_bytes=48 << 20),
-    )(first, second, own, other)
+    )(rows, own, other)
 
 
 def down_kernel(place_ref, hidden_ref, own_ref, other_ref, out_ref):
     shares, line = own_ref.shape[:2]
-    total = jnp.zeros((hidden_ref.shape[1], out_ref.shape[3]), F32)
+    experts, _, slots, columns = out_ref.shape
+    total = jnp.zeros((line * experts * slots, columns), F32)
     for at in range(line):
         k = place_ref[0] ^ at
         weights = [ref[place_ref[1] ^ y, k] for ref in (own_ref, other_ref) for y in range(shares)]
         weights = jnp.concatenate(weights, axis=0)
         total += jnp.dot(hidden_ref[at], weights, preferred_element_type=F32)
-    half, slots, columns = out_ref.shape[0] // 2, out_ref.shape[2], out_ref.shape[3]
-    total = total.astype(BF).reshape(2, line, half, slots, columns)
-    for part in range(2):
-        for at in range(line):
-            out_ref[part * half : (part + 1) * half, at] = total[part, at]
+    total = total.astype(BF).reshape(line, experts, slots, columns)
+    for p in range(line):
+        out_ref[:, p] = total[p]
 
 
 def outputs_of(place, hidden, own, other, experts, slots):
@@ -130,8 +132,6 @@
         return lax.dynamic_index_in_dim(down, at, 1, keepdims=False)
 
     pieces = [for_place(place)] + [exchange(for_place(place ^ k), "zi", k) for k in range(1, line)]
-    pieces = jnp.stack(pieces)
-    shares = [pieces] + [exchange(pieces, "dp", k) for k in range(1, lax.axis_size("dp"))]
     other = swap(turned)
 
     matches = (expert_ids[..., None] == jnp.arange(experts, dtype=jnp.int32)).astype(jnp.int32)
@@ -146,13 +146,19 @@
     weighting = jnp.sum(landing * gate_scores[..., None, None], axis=2)
     packed = packed_of(expert_ids, tokens, experts, slots)
     arrived = lax.all_to_all(packed, ROWS_OF, split_axis=0, concat_axis=0, tiled=True)
-    half = experts // 2
-    first = lax.all_gather(arrived[:half], "zi", axis=0, tiled=True)
-    second = lax.all_gather(arrived[half:], "zi", axis=0, tiled=True)
-    mark = second[0, 0, 0]
-    shares = jnp.where(mark == mark, jnp.stack(shares), jnp.zeros((), BF))
+    for piece in pieces[1:]:
+        arrived = after(piece, arrived)
+    pieces = jnp.stack(pieces)
+    rows = jnp.broadcast_to(arrived[None], (line,) + arrived.shape)
+    rows = lax.all_to_all(rows, "zi", split_axis=0, concat_axis=0, tiled=True)
+    rows = rows.reshape(line * experts, slots, width)
+    pieces = after(arrived, pieces)
+    shares = [pieces] + [exchange(pieces, "dp", k) for k in range(1, lax.axis_size("dp"))]
+    shares = jnp.stack(shares)
     other_shares = swap(shares)
-    hidden = hidden_of(first, second, turned, other)
+    up = after(arrived, turned[: 2 * units])
+    other_up = after(arrived, other[: 2 * units])
+    hidden = hidden_of(rows, up, other_up)
     gathered = lax.all_gather(hidden, "zi", axis=0)
     position = jnp.stack([place, lax.axis_index("dp")]).astype(jnp.int32)
     done = outputs_of(position, gathered, shares, other_shares, experts, slots)

time: 170 us -> 168 us (0.988)
  blocking collectives: 57.5 us -> 18.2 us
  waiting for transfers between devices: 39.2 us -> 61.1 us
  starting transfers between devices: 56.1 us -> 60.3 us
  between operations: 1.64 us -> 5.31 us
  other arithmetic: 0.88 us -> 4.15 us
  local copies, waits for them, and re-layouts: 4.36 us -> 7.55 us
    all_gather x2 -> x0, blocking collectives: 39.1 us -> none  [the longest x1 20 us: on_device(): first = lax.all_gather(arrived[:half], 'zi', axis=0, tiled=True)]
    ppermute x6, waiting for transfers between devices: 14.5 us -> 27.6 us  [exchange(): return lax.ppermute(array, axis, [(i, i ^ step) for i in range(size)])]
    all_to_all x0 -> x1, waiting for transfers between devices: none -> 8.53 us  [on_device(): rows = lax.all_to_all(rows, 'zi', split_axis=0, concat_axis=0, tiled=True)]
    all_to_all x0 -> x1, starting transfers between devices: none -> 5.66 us  [on_device(): rows = lax.all_to_all(rows, 'zi', split_axis=0, concat_axis=0, tiled=True)]
    select_n x1 -> x5, other arithmetic: 0.25 us -> 2.31 us  [after(): return jnp.where(mark == mark, then, jnp.zeros((), then.dtype))]
    broadcast_in_dim x0 -> x1, local copies, waits for them, and re-layouts: none -> 1.75 us  [on_device(): rows = jnp.broadcast_to(arrived[None], (line,) + arrived.shape)]
    all_to_all x1, starting transfers between devices: 14.7 us -> 12.9 us  [on_device(): lax.all_to_all(done, HOME, split_axis=0, concat_axis=0, tiled=True)]
  transfers between devices with their start and end apart: 10 -> 11, of which waited for: 3 -> 5; matrix products, arithmetic and copies ran while one was open for 2% -> 5% of each run, Pallas kernels for 2% -> 2%
where the time goes in v7:
time: 168 us; the launch traced here: 167 us
  waiting for transfers between devices  61.1 us (36%)
  starting transfers between devices  60.3 us (36%)
  blocking collectives  18.2 us (11%)
  Pallas kernels  9.18 us (5%)
  local copies, waits for them, and re-layouts  7.55 us (4%)
  between operations  5.31 us (3%)
  other arithmetic  4.15 us (2%)
    ppermute x6, waiting for transfers between devices, exchange(): return lax.ppermute(array, axis, [(i, i ^ step) for i in range(size)])  27.6 us
    all_to_all x1, waiting for transfers between devices, on_device(): lax.all_to_all(done, HOME, split_axis=0, concat_axis=0, tiled=True)  25 us
    ppermute x6, starting transfers between devices, exchange(): return lax.ppermute(array, axis, [(i, i ^ step) for i in range(size)])  19.9 us
    all_gather x1, blocking collectives, on_device(): gathered = lax.all_gather(hidden, 'zi', axis=0)  18.2 us
    all_to_all x1, starting transfers between devices, on_device(): lax.all_to_all(packed, ROWS_OF, split_axis=0, concat_axis=0, tiled=True)  17.7 us
    all_to_all x1, starting transfers between devices, on_device(): lax.all_to_all(done, HOME, split_axis=0, concat_axis=0, tiled=True)  12.9 us
    all_to_all x1, waiting for transfers between devices, on_device(): rows = lax.all_to_all(rows, 'zi', split_axis=0, concat_axis=0, tiled=True)  8.53 us
    all_to_all x1, starting transfers between devices, on_device(): rows = lax.all_to_all(rows, 'zi', split_axis=0, concat_axis=0, tiled=True)  5.66 us
  transfers between devices with their start and end apart: 11, of which 5 were waited for; matrix products, arithmetic and copies ran while one was open for 5% of the time, Pallas kernels for 2%

profile of v7, /device:TPU:24, one launch (start us, length us, event | category | flops | bytes accessed | tf_op | source)
XLA Modules:
  0.0 166.8 jit_solution(2796262475650837597)
XLA Ops:
  0.0 0.0 copy-start
  0.0 0.9 copy-done
  0.9 0.0 copy-start.1
  0.9 0.7 copy-done.1
  1.6 1.4 shard_map.46
  3.0 17.7 %all-to-all-start = ((bf16[16,4,3584]{2,1,0:T(4,128)(2,1)}), bf16[16,4,3584]{2,1,0:T(4,128)(2,1)S(1)}, u32[]{:S(2)}, u32[]{:S(2)}) async-start(bf16[16,4,3584]{2,1,0:T(4,128)(2,1)} %shard_map.46), calls=%async_computation | async-start | bytes 917504 | tf_op jit(solution)/shard_map/all_to_all | solution.py:148
  20.6 1.0 dynamic-slice_bitcast_fusion
  21.7 0.1 reshape.111
  21.8 0.7 constant_dynamic-slice_fusion
  22.5 2.9 %collective-permute-start.2 = (bf16[48,896]{1,0:T(8,128)(2,1)S(1)}, bf16[48,896]{1,0:T(8,128)(2,1)S(1)}, u32[]{:S(2)}, u32[]{:S(2)}) collective-permute-start(bf16[48,896]{1,0:T(8,128)(2,1)S(1)} %bitcast.68), channel_id=1, source_target_pairs={{0,8},{8,0},{16,24},{24,16},{1,9},{9,1},{17,25},{25,17},{2,10},{10... | collective-permute-start | bytes 258056 | tf_op jit(solution)/shard_map/ppermute | solution.py:18
  25.5 3.4 %collective-permute-start.1 = (bf16[48,896]{1,0:T(8,128)(2,1)S(1)}, bf16[48,896]{1,0:T(8,128)(2,1)S(1)}, u32[]{:S(2)}, u32[]{:S(2)}) collective-permute-start(bf16[48,896]{1,0:T(8,128)(2,1)S(1)} %bitcast.67), channel_id=1, source_target_pairs={{0,16},{8,24},{16,0},{24,8},{1,17},{9,25},{17,1},{25,9},{2,18},{10... | collective-permute-start | bytes 258056 | tf_op jit(solution)/shard_map/ppermute | solution.py:18
  28.9 3.8 %collective-permute-start = (bf16[48,896]{1,0:T(8,128)(2,1)S(1)}, bf16[48,896]{1,0:T(8,128)(2,1)S(1)}, u32[]{:S(2)}, u32[]{:S(2)}) collective-permute-start(bf16[48,896]{1,0:T(8,128)(2,1)S(1)} %bitcast.66), channel_id=1, source_target_pairs={{0,24},{8,16},{16,8},{24,0},{1,25},{9,17},{17,9},{25,1},{2,26},{10... | collective-permute-start | bytes 258056 | tf_op jit(solution)/shard_map/ppermute | solution.py:18
  32.7 14.1 %collective-permute-done.2 = bf16[48,896]{1,0:T(8,128)(2,1)S(1)} collective-permute-done((bf16[48,896]{1,0:T(8,128)(2,1)S(1)}, bf16[48,896]{1,0:T(8,128)(2,1)S(1)}, u32[]{:S(2)}, u32[]{:S(2)}) %collective-permute-start.2) | collective-permute-done | bytes 86048 | tf_op jit(solution)/shard_map/ppermute | solution.py:18
  46.8 0.5 slice.28
  48.4 0.0 collective-permute-done.1
  48.5 0.5 slice.27
  50.2 0.0 collective-permute-done
  50.2 0.6 slice.26
  52.1 0.0 all-to-all-done
  52.1 0.3 select_select_fusion
  52.3 1.8 %broadcast_in_dim.31 = bf16[4,16,4,3584]{3,2,1,0:T(4,128)(2,1)} broadcast(bf16[16,4,3584]{2,1,0:T(4,128)(2,1)S(1)} %select_select_fusion), dimensions={1,2,3} | broadcast | bytes 2293760 | tf_op jit(solution)/shard_map/broadcast_in_dim | solution.py:152
  54.1 5.7 %all-to-all-start.1 = ((bf16[4,16,4,3584]{3,2,1,0:T(4,128)(2,1)}), bf16[4,16,4,3584]{3,2,1,0:T(4,128)(2,1)}, u32[]{:S(2)}, u32[]{:S(2)}) async-start(bf16[4,16,4,3584]{3,2,1,0:T(4,128)(2,1)} %broadcast_in_dim.31), calls=%async_computation.1 | async-start | bytes 3670016 | tf_op jit(solution)/shard_map/all_to_all | solution.py:153
  59.8 0.0 copy-start.3
  59.8 2.2 %collective-permute-start.3 = (bf16[576,3584]{1,0:T(8,128)(2,1)}, bf16[576,3584]{1,0:T(8,128)(2,1)S(1)}, u32[]{:S(2)}, u32[]{:S(2)}) collective-permute-start(bf16[576,3584]{1,0:T(8,128)(2,1)} %bitcast.53), channel_id=1, source_target_pairs={{0,4},{4,0},{1,5},{5,1},{2,6},{6,2},{3,7},{7,3},{8,12},{12,8},{9,1... | collective-permute-start | bytes 12386312 | tf_op jit(solution)/shard_map/ppermute | solution.py:27
  62.0 0.6 slice.29
  63.9 0.1 maximum_select_fusion.1
  64.0 2.1 %collective-permute-start.6 = (bf16[4,48,896]{2,1,0:T(8,128)(2,1)S(1)}, bf16[4,48,896]{2,1,0:T(8,128)(2,1)S(1)}, u32[]{:S(2)}, u32[]{:S(2)}) collective-permute-start(bf16[4,48,896]{2,1,0:T(8,128)(2,1)S(1)} %maximum_select_fusion.1), channel_id=1, source_target_pairs={{0,3},{1,2},{2,1},{3,0},{4,7},{5,6},{6,5},{7,4},{8,11},{9,10},{10,... | collective-permute-start | bytes 1032200 | tf_op jit(solution)/shard_map/ppermute | solution.py:18
  66.1 4.5 %collective-permute-start.5 = (bf16[4,48,896]{2,1,0:T(8,128)(2,1)S(1)}, bf16[4,48,896]{2,1,0:T(8,128)(2,1)S(1)}, u32[]{:S(2)}, u32[]{:S(2)}) collective-permute-start(bf16[4,48,896]{2,1,0:T(8,128)(2,1)S(1)} %maximum_select_fusion.1), channel_id=1, source_target_pairs={{0,2},{1,3},{2,0},{3,1},{4,6},{5,7},{6,4},{7,5},{8,10},{9,11},{10,... | collective-permute-start | bytes 1032200 | tf_op jit(solution)/shard_map/ppermute | solution.py:18
  70.6 3.2 %collective-permute-start.4 = (bf16[4,48,896]{2,1,0:T(8,128)(2,1)S(1)}, bf16[4,48,896]{2,1,0:T(8,128)(2,1)S(1)}, u32[]{:S(2)}, u32[]{:S(2)}) collective-permute-start(bf16[4,48,896]{2,1,0:T(8,128)(2,1)S(1)} %maximum_select_fusion.1), channel_id=1, source_target_pairs={{0,1},{1,0},{2,3},{3,2},{4,5},{5,4},{6,7},{7,6},{8,9},{9,8},{10,11... | collective-permute-start | bytes 1032200 | tf_op jit(solution)/shard_map/ppermute | solution.py:18
  73.8 0.1 pad_add_fusion.place_ref
  73.9 0.1 maximum_select_fusion
  74.0 11.0 %collective-permute-done.6 = bf16[4,48,896]{2,1,0:T(8,128)(2,1)S(1)} collective-permute-done((bf16[4,48,896]{2,1,0:T(8,128)(2,1)S(1)}, bf16[4,48,896]{2,1,0:T(8,128)(2,1)S(1)}, u32[]{:S(2)}, u32[]{:S(2)}) %collective-permute-start.6) | collective-permute-done | bytes 344096 | tf_op jit(solution)/shard_map/ppermute | solution.py:18
  84.9 0.0 collective-permute-done.5
  84.9 2.5 %collective-permute-done.4 = bf16[4,48,896]{2,1,0:T(8,128)(2,1)S(1)} collective-permute-done((bf16[4,48,896]{2,1,0:T(8,128)(2,1)S(1)}, bf16[4,48,896]{2,1,0:T(8,128)(2,1)S(1)}, u32[]{:S(2)}, u32[]{:S(2)}) %collective-permute-start.4) | collective-permute-done | bytes 344096 | tf_op jit(solution)/shard_map/ppermute | solution.py:18
  87.5 1.3 pad_maximum_fusion.own_ref
  88.7 1.9 %collective-permute-start.7 = (bf16[4,4,48,896]{3,2,1,0:T(8,128)(2,1)}, bf16[4,4,48,896]{3,2,1,0:T(8,128)(2,1)}, u32[]{:S(2)}, u32[]{:S(2)}) collective-permute-start(bf16[4,4,48,896]{3,2,1,0:T(8,128)(2,1)} %pad_maximum_fusion.own_ref), channel_id=1, source_target_pairs={{0,4},{4,0},{1,5},{5,1},{2,6},{6,2},{3,7},{7,3},{8,12},{12,8},{9,1... | collective-permute-start | bytes 4128776 | tf_op jit(solution)/shard_map/ppermute | solution.py:27
  90.7 0.0 copy-done.3
  90.7 0.2 slice_select_fusion.1.own_ref
  90.9 0.0 collective-permute-done.3
  90.9 1.7 %slice_select_fusion.other_ref = bf16[384,3584]{1,0:T(8,128)(2,1)} fusion(bf16[576,3584]{1,0:T(8,128)(2,1)S(1)} %collective-permute-done.3, pred[]{:T(512)} %bitcast.11), kind=kLoop, calls=%fused_computation | loop fusion | flops 1376256 | bytes 5505025 | tf_op jit(solution)/shard_map/jit(_where)/select_n | solution.py:23
  92.6 8.5 %all-to-all-done.1 = bf16[4,16,4,3584]{3,2,1,0:T(4,128)(2,1)} async-done(((bf16[4,16,4,3584]{3,2,1,0:T(4,128)(2,1)}), bf16[4,16,4,3584]{3,2,1,0:T(4,128)(2,1)}, u32[]{:S(2)}, u32[]{:S(2)}) %all-to-all-start.1) | async-done | bytes 1835040 | tf_op jit(solution)/shard_map/all_to_all | solution.py:153
  101.1 4.1 %shard_map.47 = bf16[256,384]{1,0:T(8,128)(2,1)S(1)} custom-call(bf16[64,4,3584]{2,1,0:T(4,128)(2,1)} %bitcast.10.rows_ref, bf16[384,3584]{1,0:T(8,128)(2,1)S(1)} %slice_select_fusion.1.own_ref, bf16[384,3584]{1,0:T(8,128)(2,1)} %slice_select_fusion.other_ref), custom_call_target="tpu_custom_call" | custom-call | tf_op jit(solution)/shard_map/pallas_call | solution.py:84
  105.2 0.0 copy-start.2
  105.2 0.0 copy-start.4
  105.2 18.2 %all-gather = bf16[1024,384]{1,0:T(8,128)(2,1)S(1)} all-gather(bf16[256,384]{1,0:T(8,128)(2,1)S(1)} %shard_map.47), channel_id=2, replica_groups=mesh['x'=4,'zb'=4,'zi'=4,'c'=2,'dp'=4] {'zi'}, dimensions={0}, use_global_device_ids=true | all-gather | bytes 983040 | tf_op jit(solution)/shard_map/all_gather | solution.py:162
  123.4 0.0 collective-permute-done.7.other_ref
  123.4 3.7 %shard_map.48 = bf16[16,4,4,896]{3,2,1,0:T(4,128)(2,1)} custom-call(s32[2]{0:T(128)S(1)} %pad_add_fusion.place_ref, bf16[4,256,384]{2,1,0:T(8,128)(2,1)S(1)} %bitcast.51, bf16[4,4,48,896]{3,2,1,0:T(8,128)(2,1)} %pad_maximum_fusion.own_ref, bf16[4,4,48,896]{3,2,1,0:T(8,128)(2,1)} %collective-permute-done.7.other_ref), custom_call_target="tpu_custom_call" | custom-call | tf_op jit(solution)/shard_map/pallas_call | solution.py:108
  127.1 12.9 %all-to-all-start.2 = ((bf16[64,4,896]{2,1,0:T(4,128)(2,1)}), bf16[64,4,896]{2,1,0:T(4,128)(2,1)S(1)}, u32[]{:S(2)}, u32[]{:S(2)}) async-start(bf16[64,4,896]{2,1,0:T(4,128)(2,1)} %bitcast.25), calls=%async_computation.2 | async-start | bytes 917504 | tf_op jit(solution)/shard_map/all_to_all | solution.py:166
  140.1 0.0 copy-done.2
  140.1 0.1 convert_reduce_fusion
  140.2 0.2 select_reduce_fusion.1
  140.4 0.1 iota_compare_fusion
  140.5 0.0 copy-done.4
  140.5 0.1 select_reduce_fusion
  140.6 25.0 %all-to-all-done.2 = bf16[64,4,896]{2,1,0:T(4,128)(2,1)S(1)} async-done(((bf16[64,4,896]{2,1,0:T(4,128)(2,1)}), bf16[64,4,896]{2,1,0:T(4,128)(2,1)S(1)}, u32[]{:S(2)}, u32[]{:S(2)}) %all-to-all-start.2) | async-done | bytes 458784 | tf_op jit(solution)/shard_map/all_to_all | solution.py:166
  165.6 0.2 reshape.119
  165.8 1.0 fusion
  (7 shorter events, 0.1 us)
Async XLA Ops:
  0.0 0.9 copy-start
  0.9 0.7 copy-start.1
  3.0 49.1 %all-to-all-start = ((bf16[16,4,3584]{2,1,0:T(4,128)(2,1)}), bf16[16,4,3584]{2,1,0:T(4,128)(2,1)S(1)}, u32[]{:S(2)}, u32[]{:S(2)}) async-start(bf16[16,4,3584]{2,1,0:T(4,128)(2,1)} %shard_map.46), calls=%async_computation | async-start | bytes 917504 | tf_op jit(solution)/shard_map/all_to_all | solution.py:148
  22.5 24.3 %collective-permute-start.2 = (bf16[48,896]{1,0:T(8,128)(2,1)S(1)}, bf16[48,896]{1,0:T(8,128)(2,1)S(1)}, u32[]{:S(2)}, u32[]{:S(2)}) collective-permute-start(bf16[48,896]{1,0:T(8,128)(2,1)S(1)} %bitcast.68), channel_id=1, source_target_pairs={{0,8},{8,0},{16,24},{24,16},{1,9},{9,1},{17,25},{25,17},{2,10},{10... | collective-permute-start | bytes 258056 | tf_op jit(solution)/shard_map/ppermute | solution.py:18
  25.5 23.0 %collective-permute-start.1 = (bf16[48,896]{1,0:T(8,128)(2,1)S(1)}, bf16[48,896]{1,0:T(8,128)(2,1)S(1)}, u32[]{:S(2)}, u32[]{:S(2)}) collective-permute-start(bf16[48,896]{1,0:T(8,128)(2,1)S(1)} %bitcast.67), channel_id=1, source_target_pairs={{0,16},{8,24},{16,0},{24,8},{1,17},{9,25},{17,1},{25,9},{2,18},{10... | collective-permute-start | bytes 258056 | tf_op jit(solution)/shard_map/ppermute | solution.py:18
  28.9 21.4 %collective-permute-start = (bf16[48,896]{1,0:T(8,128)(2,1)S(1)}, bf16[48,896]{1,0:T(8,128)(2,1)S(1)}, u32[]{:S(2)}, u32[]{:S(2)}) collective-permute-start(bf16[48,896]{1,0:T(8,128)(2,1)S(1)} %bitcast.66), channel_id=1, source_target_pairs={{0,24},{8,16},{16,8},{24,0},{1,25},{9,17},{17,9},{25,1},{2,26},{10... | collective-permute-start | bytes 258056 | tf_op jit(solution)/shard_map/ppermute | solution.py:18
  54.1 47.0 %all-to-all-start.1 = ((bf16[4,16,4,3584]{3,2,1,0:T(4,128)(2,1)}), bf16[4,16,4,3584]{3,2,1,0:T(4,128)(2,1)}, u32[]{:S(2)}, u32[]{:S(2)}) async-start(bf16[4,16,4,3584]{3,2,1,0:T(4,128)(2,1)} %broadcast_in_dim.31), calls=%async_computation.1 | async-start | bytes 3670016 | tf_op jit(solution)/shard_map/all_to_all | solution.py:153
  59.8 30.9 %copy-start.3 = (bf16[1,3584,576]{1,2,0:T(8,128)(2,1)S(1)}, bf16[1,3584,576]{1,2,0:T(8,128)(2,1)}, u32[]{:S(2)}) copy-start(bf16[1,3584,576]{1,2,0:T(8,128)(2,1)} %param.7) | copy-start | bytes 12386308
  59.8 31.1 %collective-permute-start.3 = (bf16[576,3584]{1,0:T(8,128)(2,1)}, bf16[576,3584]{1,0:T(8,128)(2,1)S(1)}, u32[]{:S(2)}, u32[]{:S(2)}) collective-permute-start(bf16[576,3584]{1,0:T(8,128)(2,1)} %bitcast.53), channel_id=1, source_target_pairs={{0,4},{4,0},{1,5},{5,1},{2,6},{6,2},{3,7},{7,3},{8,12},{12,8},{9,1... | collective-permute-start | bytes 12386312 | tf_op jit(solution)/shard_map/ppermute | solution.py:27
  64.0 20.9 %collective-permute-start.6 = (bf16[4,48,896]{2,1,0:T(8,128)(2,1)S(1)}, bf16[4,48,896]{2,1,0:T(8,128)(2,1)S(1)}, u32[]{:S(2)}, u32[]{:S(2)}) collective-permute-start(bf16[4,48,896]{2,1,0:T(8,128)(2,1)S(1)} %maximum_select_fusion.1), channel_id=1, source_target_pairs={{0,3},{1,2},{2,1},{3,0},{4,7},{5,6},{6,5},{7,4},{8,11},{9,10},{10,... | collective-permute-start | bytes 1032200 | tf_op jit(solution)/shard_map/ppermute | solution.py:18
  66.1 18.8 %collective-permute-start.5 = (bf16[4,48,896]{2,1,0:T(8,128)(2,1)S(1)}, bf16[4,48,896]{2,1,0:T(8,128)(2,1)S(1)}, u32[]{:S(2)}, u32[]{:S(2)}) collective-permute-start(bf16[4,48,896]{2,1,0:T(8,128)(2,1)S(1)} %maximum_select_fusion.1), channel_id=1, source_target_pairs={{0,2},{1,3},{2,0},{3,1},{4,6},{5,7},{6,4},{7,5},{8,10},{9,11},{10,... | collective-permute-start | bytes 1032200 | tf_op jit(solution)/shard_map/ppermute | solution.py:18
  70.6 16.8 %collective-permute-start.4 = (bf16[4,48,896]{2,1,0:T(8,128)(2,1)S(1)}, bf16[4,48,896]{2,1,0:T(8,128)(2,1)S(1)}, u32[]{:S(2)}, u32[]{:S(2)}) collective-permute-start(bf16[4,48,896]{2,1,0:T(8,128)(2,1)S(1)} %maximum_select_fusion.1), channel_id=1, source_target_pairs={{0,1},{1,0},{2,3},{3,2},{4,5},{5,4},{6,7},{7,6},{8,9},{9,8},{10,11... | collective-permute-start | bytes 1032200 | tf_op jit(solution)/shard_map/ppermute | solution.py:18
  88.7 34.7 %collective-permute-start.7 = (bf16[4,4,48,896]{3,2,1,0:T(8,128)(2,1)}, bf16[4,4,48,896]{3,2,1,0:T(8,128)(2,1)}, u32[]{:S(2)}, u32[]{:S(2)}) collective-permute-start(bf16[4,4,48,896]{3,2,1,0:T(8,128)(2,1)} %pad_maximum_fusion.own_ref), channel_id=1, source_target_pairs={{0,4},{4,0},{1,5},{5,1},{2,6},{6,2},{3,7},{7,3},{8,12},{12,8},{9,1... | collective-permute-start | bytes 4128776 | tf_op jit(solution)/shard_map/ppermute | solution.py:27
  105.2 34.9 %copy-start.2 = (s32[2,8,2]{1,2,0:T(2,128)S(1)}, s32[2,8,2]{1,2,0:T(2,128)}, u32[]{:S(2)}) copy-start(s32[2,8,2]{1,2,0:T(2,128)} %param.5) | copy-start | bytes 388
  105.2 35.3 %copy-start.4 = (f32[2,8,2]{1,2,0:T(2,128)S(1)}, f32[2,8,2]{1,2,0:T(2,128)}, u32[]{:S(2)}) copy-start(f32[2,8,2]{1,2,0:T(2,128)} %param.6) | copy-start | bytes 388
  127.1 38.5 %all-to-all-start.2 = ((bf16[64,4,896]{2,1,0:T(4,128)(2,1)}), bf16[64,4,896]{2,1,0:T(4,128)(2,1)S(1)}, u32[]{:S(2)}, u32[]{:S(2)}) async-start(bf16[64,4,896]{2,1,0:T(4,128)(2,1)} %bitcast.25), calls=%async_computation.2 | async-start | bytes 917504 | tf_op jit(solution)/shard_map/all_to_all | solution.py:166

commit v8 on v6

--- a/solution.py
+++ b/solution.py
@@ -22,7 +22,8 @@
     return lax.ppermute(array, "c", [(0, 1), (1, 0)])
 
 
-def pack_kernel(ids_ref, tokens_ref, out_ref):
+def pack_kernel(ids_ref, tokens_ref, *refs):
+    out_ref = refs[-1]
     batches, picks, rows = ids_ref.shape
     experts, slots, width = out_ref.shape
     capacity = slots // batches
@@ -53,24 +54,24 @@
     return [pl.BlockSpec(memory_space=pltpu.VMEM)] * count
 
 
-def packed_of(expert_ids, tokens, experts, slots):
+def packed_of(expert_ids, tokens, experts, slots, earlier):
     return pl.pallas_call(
         pack_kernel,
-        in_specs=whole(2),
+        in_specs=whole(2) + [pl.BlockSpec(memory_space=pl.ANY)] * len(earlier),
         out_specs=whole(1)[0],
         out_shape=jax.ShapeDtypeStruct((experts, slots, tokens.shape[2]), BF),
         compiler_params=pltpu.CompilerParams(vmem_limit_bytes=32 << 20),
-    )(expert_ids.transpose(0, 2, 1), tokens)
+    )(expert_ids.transpose(0, 2, 1), tokens, *earlier)
 
 
 def up_kernel(first_ref, second_ref, own_ref, other_ref, out_ref):
-    units = own_ref.shape[0] // 3
+    units = own_ref.shape[0] // 2
     width = own_ref.shape[1]
     rows = [ref[...].reshape(-1, width) for ref in (first_ref, second_ref)]
     rows = jnp.concatenate(rows, axis=0)
     hidden = []
     for ref in (own_ref, other_ref):
-        both = lax.dot_general(ref[: 2 * units], rows, NT, preferred_element_type=F32)
+        both = lax.dot_general(ref[...], rows, NT, preferred_element_type=F32)
         gate = both[:units]
         hidden.append(gate / (1.0 + jnp.exp(-gate)) * both[units:])
     out_ref[...] = jnp.concatenate(hidden, axis=0).T.astype(BF)
@@ -80,9 +81,10 @@
     count = 2 * first.shape[0] * first.shape[1]
     return pl.pallas_call(
         up_kernel,
-        in_specs=whole(4),
+        grid=(1,),
+        in_specs=whole(3) + [pl.BlockSpec(own.shape, lambda i: (0, 0))],
         out_specs=whole(1)[0],
-        out_shape=jax.ShapeDtypeStruct((count, own.shape[0] // 3 * 2), BF),
+        out_shape=jax.ShapeDtypeStruct((count, own.shape[0]), BF),
         compiler_params=pltpu.CompilerParams(vmem_limit_bytes=48 << 20),
     )(first, second, own, other)
 
@@ -130,9 +132,12 @@
         return lax.dynamic_index_in_dim(down, at, 1, keepdims=False)
 
     pieces = [for_place(place)] + [exchange(for_place(place ^ k), "zi", k) for k in range(1, line)]
+    moved = pieces[1:]
     pieces = jnp.stack(pieces)
     shares = [pieces] + [exchange(pieces, "dp", k) for k in range(1, lax.axis_size("dp"))]
     other = swap(turned)
+    mark = moved[0][0, 0]
+    up = jnp.where(mark == mark, turned[: 2 * units], jnp.zeros((), BF))
 
     matches = (expert_ids[..., None] == jnp.arange(experts, dtype=jnp.int32)).astype(jnp.int32)
     present = jnp.sum(matches, axis=2)
@@ -144,15 +149,14 @@
         & (occurrence[..., None, None] == slot)
     ).astype(F32)
     weighting = jnp.sum(landing * gate_scores[..., None, None], axis=2)
-    packed = packed_of(expert_ids, tokens, experts, slots)
+    packed = packed_of(expert_ids, tokens, experts, slots, moved)
     arrived = lax.all_to_all(packed, ROWS_OF, split_axis=0, concat_axis=0, tiled=True)
     half = experts // 2
     first = lax.all_gather(arrived[:half], "zi", axis=0, tiled=True)
     second = lax.all_gather(arrived[half:], "zi", axis=0, tiled=True)
-    mark = second[0, 0, 0]
-    shares = jnp.where(mark == mark, jnp.stack(shares), jnp.zeros((), BF))
+    shares = jnp.stack(shares)
     other_shares = swap(shares)
-    hidden = hidden_of(first, second, turned, other)
+    hidden = hidden_of(first, second, up, other)
     gathered = lax.all_gather(hidden, "zi", axis=0)
     position = jnp.stack([place, lax.axis_index("dp")]).astype(jnp.int32)
     done = outputs_of(position, gathered, shares, other_shares, experts, slots)

time: 170 us -> 171 us (level)
  starting transfers between devices: 56.1 us -> 50.2 us
  blocking collectives: 57.5 us -> 62.5 us
  other arithmetic: 0.88 us -> 3.88 us
    all_gather x1, blocking collectives: 20 us -> 25.1 us  [on_device(): first = lax.all_gather(arrived[:half], 'zi', axis=0, tiled=True)]
    all_to_all x1, starting transfers between devices: 14.7 us -> 10.6 us  [on_device(): lax.all_to_all(done, HOME, split_axis=0, concat_axis=0, tiled=True)]
    all_to_all x1, starting transfers between devices: 17.7 us -> 15 us  [on_device(): lax.all_to_all(packed, ROWS_OF, split_axis=0, concat_axis=0, tiled=True)]
  transfers between devices with their start and end apart: 10 -> 10, of which waited for: 3 -> 5; matrix products, arithmetic and copies ran while one was open for 2% -> 4% of each run, Pallas kernels for 2% -> 3%
where the time goes in v8:
time: 171 us; the launch traced here: 170 us
  blocking collectives  62.5 us (37%)
  starting transfers between devices  50.2 us (29%)
  waiting for transfers between devices  39.1 us (23%)
  Pallas kernels  8.66 us (5%)
  other arithmetic  3.88 us (2%)
  local copies, waits for them, and re-layouts  2.72 us (2%)
    all_gather x1, blocking collectives, on_device(): first = lax.all_gather(arrived[:half], 'zi', axis=0, tiled=True)  25.1 us
    all_to_all x1, waiting for transfers between devices, on_device(): lax.all_to_all(done, HOME, split_axis=0, concat_axis=0, tiled=True)  24.9 us
    ppermute x6, starting transfers between devices, exchange(): return lax.ppermute(array, axis, [(i, i ^ step) for i in range(size)])  20.7 us
    all_gather x1, blocking collectives, on_device(): second = lax.all_gather(arrived[half:], 'zi', axis=0, tiled=True)  19.9 us
    all_gather x1, blocking collectives, on_device(): gathered = lax.all_gather(hidden, 'zi', axis=0)  17.5 us
    all_to_all x1, starting transfers between devices, on_device(): lax.all_to_all(packed, ROWS_OF, split_axis=0, concat_axis=0, tiled=True)  15 us
    ppermute x6, waiting for transfers between devices, exchange(): return lax.ppermute(array, axis, [(i, i ^ step) for i in range(size)])  14.2 us
    all_to_all x1, starting transfers between devices, on_device(): lax.all_to_all(done, HOME, split_axis=0, concat_axis=0, tiled=True)  10.6 us
  transfers between devices with their start and end apart: 10, of which 5 were waited for; matrix products, arithmetic and copies ran while one was open for 4% of the time, Pallas kernels for 3%

profile of v8, /device:TPU:24, one launch (start us, length us, event | category | flops | bytes accessed | tf_op | source)
XLA Modules:
  0.0 169.6 jit_solution(15068290601152496400)
XLA Ops:
  0.0 1.9 %collective-permute-start.3 = (bf16[576,3584]{1,0:T(8,128)(2,1)}, bf16[576,3584]{1,0:T(8,128)(2,1)}, u32[]{:S(2)}, u32[]{:S(2)}) collective-permute-start(bf16[576,3584]{1,0:T(8,128)(2,1)} %bitcast.49), channel_id=1, source_target_pairs={{0,4},{4,0},{1,5},{5,1},{2,6},{6,2},{3,7},{7,3},{8,12},{12,8},{9,1... | collective-permute-start | bytes 12386312 | tf_op jit(solution)/shard_map/ppermute | solution.py:22
  1.9 1.0 dynamic-slice_bitcast_fusion
  2.9 0.0 copy-start
  3.0 0.0 copy-start.1
  3.0 0.1 reshape.45
  3.1 0.7 constant_dynamic-slice_fusion
  3.8 3.8 %collective-permute-start = (bf16[48,896]{1,0:T(8,128)(2,1)S(1)}, bf16[48,896]{1,0:T(8,128)(2,1)S(1)}, u32[]{:S(2)}, u32[]{:S(2)}) collective-permute-start(bf16[48,896]{1,0:T(8,128)(2,1)S(1)} %bitcast.55), channel_id=1, source_target_pairs={{0,8},{8,0},{16,24},{24,16},{1,9},{9,1},{17,25},{25,17},{2,10},{10... | collective-permute-start | bytes 258056 | tf_op jit(solution)/shard_map/ppermute | solution.py:18
  7.7 5.2 %collective-permute-start.1 = (bf16[48,896]{1,0:T(8,128)(2,1)S(1)}, bf16[48,896]{1,0:T(8,128)(2,1)S(1)}, u32[]{:S(2)}, u32[]{:S(2)}) collective-permute-start(bf16[48,896]{1,0:T(8,128)(2,1)S(1)} %bitcast.56), channel_id=1, source_target_pairs={{0,16},{8,24},{16,0},{24,8},{1,17},{9,25},{17,1},{25,9},{2,18},{10... | collective-permute-start | bytes 258056 | tf_op jit(solution)/shard_map/ppermute | solution.py:18
  12.9 1.9 %collective-permute-start.2 = (bf16[48,896]{1,0:T(8,128)(2,1)S(1)}, bf16[48,896]{1,0:T(8,128)(2,1)S(1)}, u32[]{:S(2)}, u32[]{:S(2)}) collective-permute-start(bf16[48,896]{1,0:T(8,128)(2,1)S(1)} %bitcast.57), channel_id=1, source_target_pairs={{0,24},{8,16},{16,8},{24,0},{1,25},{9,17},{17,9},{25,1},{2,26},{10... | collective-permute-start | bytes 258056 | tf_op jit(solution)/shard_map/ppermute | solution.py:18
  14.8 0.0 collective-permute-done.refs_0_
  14.8 2.5 %collective-permute-done.1.refs_1_ = bf16[48,896]{1,0:T(8,128)(2,1)S(1)} collective-permute-done((bf16[48,896]{1,0:T(8,128)(2,1)S(1)}, bf16[48,896]{1,0:T(8,128)(2,1)S(1)}, u32[]{:S(2)}, u32[]{:S(2)}) %collective-permute-start.1) | collective-permute-done | bytes 86048 | tf_op jit(solution)/shard_map/ppermute | solution.py:18
  17.4 3.7 %collective-permute-done.2.refs_2_ = bf16[48,896]{1,0:T(8,128)(2,1)S(1)} collective-permute-done((bf16[48,896]{1,0:T(8,128)(2,1)S(1)}, bf16[48,896]{1,0:T(8,128)(2,1)S(1)}, u32[]{:S(2)}, u32[]{:S(2)}) %collective-permute-start.2) | collective-permute-done | bytes 86048 | tf_op jit(solution)/shard_map/ppermute | solution.py:18
  21.1 0.0 copy-done
  21.1 0.0 copy-done.1
  21.1 1.4 shard_map.46
  22.5 15.0 %all-to-all-start = ((bf16[16,4,3584]{2,1,0:T(4,128)(2,1)}), bf16[16,4,3584]{2,1,0:T(4,128)(2,1)S(1)}, u32[]{:S(2)}, u32[]{:S(2)}) async-start(bf16[16,4,3584]{2,1,0:T(4,128)(2,1)} %shard_map.46), calls=%async_computation | async-start | bytes 917504 | tf_op jit(solution)/shard_map/all_to_all | solution.py:153
  37.5 0.1 pad_add_fusion.place_ref
  37.6 0.1 fusion.3
  37.6 2.1 %collective-permute-start.6 = (bf16[4,48,896]{2,1,0:T(8,128)(2,1)S(1)}, bf16[4,48,896]{2,1,0:T(8,128)(2,1)S(1)}, u32[]{:S(2)}, u32[]{:S(2)}) collective-permute-start(bf16[4,48,896]{2,1,0:T(8,128)(2,1)S(1)} %get-tuple-element.8), channel_id=1, source_target_pairs={{0,3},{1,2},{2,1},{3,0},{4,7},{5,6},{6,5},{7,4},{8,11},{9,10},{10,... | collective-permute-start | bytes 1032200 | tf_op jit(solution)/shard_map/ppermute | solution.py:18
  39.8 4.5 %collective-permute-start.5 = (bf16[4,48,896]{2,1,0:T(8,128)(2,1)S(1)}, bf16[4,48,896]{2,1,0:T(8,128)(2,1)S(1)}, u32[]{:S(2)}, u32[]{:S(2)}) collective-permute-start(bf16[4,48,896]{2,1,0:T(8,128)(2,1)S(1)} %get-tuple-element.8), channel_id=1, source_target_pairs={{0,2},{1,3},{2,0},{3,1},{4,6},{5,7},{6,4},{7,5},{8,10},{9,11},{10,... | collective-permute-start | bytes 1032200 | tf_op jit(solution)/shard_map/ppermute | solution.py:18
  44.3 3.2 %collective-permute-start.4 = (bf16[4,48,896]{2,1,0:T(8,128)(2,1)S(1)}, bf16[4,48,896]{2,1,0:T(8,128)(2,1)S(1)}, u32[]{:S(2)}, u32[]{:S(2)}) collective-permute-start(bf16[4,48,896]{2,1,0:T(8,128)(2,1)S(1)} %get-tuple-element.8), channel_id=1, source_target_pairs={{0,1},{1,0},{2,3},{3,2},{4,5},{5,4},{6,7},{7,6},{8,9},{9,8},{10,11... | collective-permute-start | bytes 1032200 | tf_op jit(solution)/shard_map/ppermute | solution.py:18
  47.5 0.5 slice.18
  49.3 2.0 %slice_select_fusion.own_ref = bf16[384,3584]{1,0:T(8,128)(2,1)S(1)} fusion(bf16[576,3584]{1,0:T(8,128)(2,1)} %bitcast.50, pred[]{:T(512)} %bitcast.7), kind=kLoop, calls=%fused_computation | loop fusion | flops 1376256 | bytes 5505025 | tf_op jit(solution)/shard_map/jit(_where)/select_n | solution.py:140
  51.3 5.4 %collective-permute-done.6 = bf16[4,48,896]{2,1,0:T(8,128)(2,1)S(1)} collective-permute-done((bf16[4,48,896]{2,1,0:T(8,128)(2,1)S(1)}, bf16[4,48,896]{2,1,0:T(8,128)(2,1)S(1)}, u32[]{:S(2)}, u32[]{:S(2)}) %collective-permute-start.6) | collective-permute-done | bytes 344096 | tf_op jit(solution)/shard_map/ppermute | solution.py:18
  56.7 0.0 collective-permute-done.5
  56.7 2.5 %collective-permute-done.4 = bf16[4,48,896]{2,1,0:T(8,128)(2,1)S(1)} collective-permute-done((bf16[4,48,896]{2,1,0:T(8,128)(2,1)S(1)}, bf16[4,48,896]{2,1,0:T(8,128)(2,1)S(1)}, u32[]{:S(2)}, u32[]{:S(2)}) %collective-permute-start.4) | collective-permute-done | bytes 344096 | tf_op jit(solution)/shard_map/ppermute | solution.py:18
  59.2 1.3 pad_maximum_fusion.own_ref
  60.5 1.9 %collective-permute-start.7 = (bf16[4,4,48,896]{3,2,1,0:T(8,128)(2,1)}, bf16[4,4,48,896]{3,2,1,0:T(8,128)(2,1)}, u32[]{:S(2)}, u32[]{:S(2)}) collective-permute-start(bf16[4,4,48,896]{3,2,1,0:T(8,128)(2,1)} %pad_maximum_fusion.own_ref), channel_id=1, source_target_pairs={{0,4},{4,0},{1,5},{5,1},{2,6},{6,2},{3,7},{7,3},{8,12},{12,8},{9,1... | collective-permute-start | bytes 4128776 | tf_op jit(solution)/shard_map/ppermute | solution.py:22
  62.4 0.0 all-to-all-done
  62.4 0.2 fusion.4
  62.6 25.1 %all_gather.12.first_ref = bf16[32,4,3584]{2,1,0:T(4,128)(2,1)S(1)} all-gather(bf16[8,4,3584]{2,1,0:T(4,128)(2,1)S(1)} %get-tuple-element.6), channel_id=1, replica_groups=mesh['x'=4,'zb'=4,'zi'=4,'c'=2,'dp'=4] {'zi'}, dimensions={0}, use_global_device_ids=true | all-gather | bytes 1146880 | tf_op jit(solution)/shard_map/all_gather | solution.py:155
  87.7 19.9 %all_gather.13.second_ref = bf16[32,4,3584]{2,1,0:T(4,128)(2,1)S(1)} all-gather(bf16[8,4,3584]{2,1,0:T(4,128)(2,1)S(1)} %get-tuple-element.5), channel_id=1, replica_groups=mesh['x'=4,'zb'=4,'zi'=4,'c'=2,'dp'=4] {'zi'}, dimensions={0}, use_global_device_ids=true | all-gather | bytes 1146880 | tf_op jit(solution)/shard_map/all_gather | solution.py:156
  107.6 0.0 collective-permute-done.3.other_ref
  107.6 3.5 %shard_map.47 = bf16[256,384]{1,0:T(8,128)(2,1)S(1)} custom-call(bf16[32,4,3584]{2,1,0:T(4,128)(2,1)S(1)} %all_gather.12.first_ref, bf16[32,4,3584]{2,1,0:T(4,128)(2,1)S(1)} %all_gather.13.second_ref, bf16[384,3584]{1,0:T(8,128)(2,1)S(1)} %slice_select_fusion.own_ref, bf16[576,3584]{1,0:T(8,128)(2,1)} %collective-permute-done.3.other_ref), custom_call_target="tpu_custom_call" | custom-call | tf_op jit(solution)/shard_map/pallas_call | solution.py:82
  111.1 17.5 %all-gather = bf16[1024,384]{1,0:T(8,128)(2,1)S(1)} all-gather(bf16[256,384]{1,0:T(8,128)(2,1)S(1)} %shard_map.47), channel_id=2, replica_groups=mesh['x'=4,'zb'=4,'zi'=4,'c'=2,'dp'=4] {'zi'}, dimensions={0}, use_global_device_ids=true | all-gather | bytes 983040 | tf_op jit(solution)/shard_map/all_gather | solution.py:160
  128.6 0.0 collective-permute-done.7.other_ref
  128.6 0.0 copy-start.2
  128.6 3.8 %shard_map.48 = bf16[16,4,4,896]{3,2,1,0:T(4,128)(2,1)} custom-call(s32[2]{0:T(128)S(1)} %pad_add_fusion.place_ref, bf16[4,256,384]{2,1,0:T(8,128)(2,1)S(1)} %bitcast.44, bf16[4,4,48,896]{3,2,1,0:T(8,128)(2,1)} %pad_maximum_fusion.own_ref, bf16[4,4,48,896]{3,2,1,0:T(8,128)(2,1)} %collective-permute-done.7.other_ref), custom_call_target="tpu_custom_call" | custom-call | tf_op jit(solution)/shard_map/pallas_call | solution.py:108
  132.4 10.6 %all-to-all-start.1 = ((bf16[64,4,896]{2,1,0:T(4,128)(2,1)}), bf16[64,4,896]{2,1,0:T(4,128)(2,1)S(1)}, u32[]{:S(2)}, u32[]{:S(2)}) async-start(bf16[64,4,896]{2,1,0:T(4,128)(2,1)} %bitcast.19), calls=%async_computation.1 | async-start | bytes 917504 | tf_op jit(solution)/shard_map/all_to_all | solution.py:164
  143.0 0.1 convert_reduce_fusion
  143.1 0.2 select_reduce_fusion.1
  143.3 0.1 iota_compare_fusion
  143.4 0.0 copy-done.2
  143.4 0.1 select_reduce_fusion
  143.5 24.9 %all-to-all-done.1 = bf16[64,4,896]{2,1,0:T(4,128)(2,1)S(1)} async-done(((bf16[64,4,896]{2,1,0:T(4,128)(2,1)}), bf16[64,4,896]{2,1,0:T(4,128)(2,1)S(1)}, u32[]{:S(2)}, u32[]{:S(2)}) %all-to-all-start.1) | async-done | bytes 458784 | tf_op jit(solution)/shard_map/all_to_all | solution.py:164
  168.4 0.2 reshape.52
  168.6 1.0 fusion
  (7 shorter events, 0.1 us)
Async XLA Ops:
  0.0 107.6 %collective-permute-start.3 = (bf16[576,3584]{1,0:T(8,128)(2,1)}, bf16[576,3584]{1,0:T(8,128)(2,1)}, u32[]{:S(2)}, u32[]{:S(2)}) collective-permute-start(bf16[576,3584]{1,0:T(8,128)(2,1)} %bitcast.49), channel_id=1, source_target_pairs={{0,4},{4,0},{1,5},{5,1},{2,6},{6,2},{3,7},{7,3},{8,12},{12,8},{9,1... | collective-permute-start | bytes 12386312 | tf_op jit(solution)/shard_map/ppermute | solution.py:22
  2.9 18.1 %copy-start = (bf16[2,8,3584]{2,1,0:T(8,128)(2,1)S(1)}, bf16[2,8,3584]{2,1,0:T(8,128)(2,1)}, u32[]{:S(2)}) copy-start(bf16[2,8,3584]{2,1,0:T(8,128)(2,1)} %tokens_ref.1) | copy-start | bytes 344068
  3.0 18.1 %copy-start.1 = (s32[2,8,2]{1,2,0:T(2,128)S(1)}, s32[2,8,2]{1,2,0:T(2,128)}, u32[]{:S(2)}) copy-start(s32[2,8,2]{1,2,0:T(2,128)} %param.5) | copy-start | bytes 388
  3.8 11.0 %collective-permute-start = (bf16[48,896]{1,0:T(8,128)(2,1)S(1)}, bf16[48,896]{1,0:T(8,128)(2,1)S(1)}, u32[]{:S(2)}, u32[]{:S(2)}) collective-permute-start(bf16[48,896]{1,0:T(8,128)(2,1)S(1)} %bitcast.55), channel_id=1, source_target_pairs={{0,8},{8,0},{16,24},{24,16},{1,9},{9,1},{17,25},{25,17},{2,10},{10... | collective-permute-start | bytes 258056 | tf_op jit(solution)/shard_map/ppermute | solution.py:18
  7.7 9.7 %collective-permute-start.1 = (bf16[48,896]{1,0:T(8,128)(2,1)S(1)}, bf16[48,896]{1,0:T(8,128)(2,1)S(1)}, u32[]{:S(2)}, u32[]{:S(2)}) collective-permute-start(bf16[48,896]{1,0:T(8,128)(2,1)S(1)} %bitcast.56), channel_id=1, source_target_pairs={{0,16},{8,24},{16,0},{24,8},{1,17},{9,25},{17,1},{25,9},{2,18},{10... | collective-permute-start | bytes 258056 | tf_op jit(solution)/shard_map/ppermute | solution.py:18
  12.9 8.2 %collective-permute-start.2 = (bf16[48,896]{1,0:T(8,128)(2,1)S(1)}, bf16[48,896]{1,0:T(8,128)(2,1)S(1)}, u32[]{:S(2)}, u32[]{:S(2)}) collective-permute-start(bf16[48,896]{1,0:T(8,128)(2,1)S(1)} %bitcast.57), channel_id=1, source_target_pairs={{0,24},{8,16},{16,8},{24,0},{1,25},{9,17},{17,9},{25,1},{2,26},{10... | collective-permute-start | bytes 258056 | tf_op jit(solution)/shard_map/ppermute | solution.py:18
  22.5 39.9 %all-to-all-start = ((bf16[16,4,3584]{2,1,0:T(4,128)(2,1)}), bf16[16,4,3584]{2,1,0:T(4,128)(2,1)S(1)}, u32[]{:S(2)}, u32[]{:S(2)}) async-start(bf16[16,4,3584]{2,1,0:T(4,128)(2,1)} %shard_map.46), calls=%async_computation | async-start | bytes 917504 | tf_op jit(solution)/shard_map/all_to_all | solution.py:153
  37.6 19.0 %collective-permute-start.6 = (bf16[4,48,896]{2,1,0:T(8,128)(2,1)S(1)}, bf16[4,48,896]{2,1,0:T(8,128)(2,1)S(1)}, u32[]{:S(2)}, u32[]{:S(2)}) collective-permute-start(bf16[4,48,896]{2,1,0:T(8,128)(2,1)S(1)} %get-tuple-element.8), channel_id=1, source_target_pairs={{0,3},{1,2},{2,1},{3,0},{4,7},{5,6},{6,5},{7,4},{8,11},{9,10},{10,... | collective-permute-start | bytes 1032200 | tf_op jit(solution)/shard_map/ppermute | solution.py:18
  39.8 16.9 %collective-permute-start.5 = (bf16[4,48,896]{2,1,0:T(8,128)(2,1)S(1)}, bf16[4,48,896]{2,1,0:T(8,128)(2,1)S(1)}, u32[]{:S(2)}, u32[]{:S(2)}) collective-permute-start(bf16[4,48,896]{2,1,0:T(8,128)(2,1)S(1)} %get-tuple-element.8), channel_id=1, source_target_pairs={{0,2},{1,3},{2,0},{3,1},{4,6},{5,7},{6,4},{7,5},{8,10},{9,11},{10,... | collective-permute-start | bytes 1032200 | tf_op jit(solution)/shard_map/ppermute | solution.py:18
  44.3 14.9 %collective-permute-start.4 = (bf16[4,48,896]{2,1,0:T(8,128)(2,1)S(1)}, bf16[4,48,896]{2,1,0:T(8,128)(2,1)S(1)}, u32[]{:S(2)}, u32[]{:S(2)}) collective-permute-start(bf16[4,48,896]{2,1,0:T(8,128)(2,1)S(1)} %get-tuple-element.8), channel_id=1, source_target_pairs={{0,1},{1,0},{2,3},{3,2},{4,5},{5,4},{6,7},{7,6},{8,9},{9,8},{10,11... | collective-permute-start | bytes 1032200 | tf_op jit(solution)/shard_map/ppermute | solution.py:18
  60.5 68.1 %collective-permute-start.7 = (bf16[4,4,48,896]{3,2,1,0:T(8,128)(2,1)}, bf16[4,4,48,896]{3,2,1,0:T(8,128)(2,1)}, u32[]{:S(2)}, u32[]{:S(2)}) collective-permute-start(bf16[4,4,48,896]{3,2,1,0:T(8,128)(2,1)} %pad_maximum_fusion.own_ref), channel_id=1, source_target_pairs={{0,4},{4,0},{1,5},{5,1},{2,6},{6,2},{3,7},{7,3},{8,12},{12,8},{9,1... | collective-permute-start | bytes 4128776 | tf_op jit(solution)/shard_map/ppermute | solution.py:22
  128.6 14.8 %copy-start.2 = (f32[2,8,2]{1,2,0:T(2,128)S(1)}, f32[2,8,2]{1,2,0:T(2,128)}, u32[]{:S(2)}) copy-start(f32[2,8,2]{1,2,0:T(2,128)} %param.6) | copy-start | bytes 388
  132.4 36.1 %all-to-all-start.1 = ((bf16[64,4,896]{2,1,0:T(4,128)(2,1)}), bf16[64,4,896]{2,1,0:T(4,128)(2,1)S(1)}, u32[]{:S(2)}, u32[]{:S(2)}) async-start(bf16[64,4,896]{2,1,0:T(4,128)(2,1)} %bitcast.19), calls=%async_computation.1 | async-start | bytes 917504 | tf_op jit(solution)/shard_map/all_to_all | solution.py:164

commit v9 on v8

--- a/solution.py
+++ b/solution.py
@@ -60,7 +60,7 @@
         in_specs=whole(2) + [pl.BlockSpec(memory_space=pl.ANY)] * len(earlier),
         out_specs=whole(1)[0],
         out_shape=jax.ShapeDtypeStruct((experts, slots, tokens.shape[2]), BF),
-        compiler_params=pltpu.CompilerParams(vmem_limit_bytes=32 << 20),
+        compiler_params=pltpu.CompilerParams(vmem_limit_bytes=16 << 20),
     )(expert_ids.transpose(0, 2, 1), tokens, *earlier)
 
 
@@ -85,7 +85,7 @@
         in_specs=whole(3) + [pl.BlockSpec(own.shape, lambda i: (0, 0))],
         out_specs=whole(1)[0],
         out_shape=jax.ShapeDtypeStruct((count, own.shape[0]), BF),
-        compiler_params=pltpu.CompilerParams(vmem_limit_bytes=48 << 20),
+        compiler_params=pltpu.CompilerParams(vmem_limit_bytes=24 << 20),
     )(first, second, own, other)
 
 
@@ -93,8 +93,7 @@
     shares, line = own_ref.shape[:2]
     total = jnp.zeros((hidden_ref.shape[1], out_ref.shape[3]), F32)
     for at in range(line):
-        k = place_ref[0] ^ at
-        weights = [ref[place_ref[1] ^ y, k] for ref in (own_ref, other_ref) for y in range(shares)]
+        weights = [ref[place_ref[0] ^ y, at] for ref in (own_ref, other_ref) for y in range(shares)]
         weights = jnp.concatenate(weights, axis=0)
         total += jnp.dot(hidden_ref[at], weights, preferred_element_type=F32)
     half, slots, columns = out_ref.shape[0] // 2, out_ref.shape[2], out_ref.shape[3]
@@ -110,7 +109,7 @@
         in_specs=[pl.BlockSpec(memory_space=pltpu.SMEM)] + whole(3),
         out_specs=whole(1)[0],
         out_shape=jax.ShapeDtypeStruct((experts, hidden.shape[0], slots, own.shape[3]), BF),
-        compiler_params=pltpu.CompilerParams(vmem_limit_bytes=32 << 20),
+        compiler_params=pltpu.CompilerParams(vmem_limit_bytes=16 << 20),
     )(place, hidden, own, other)
 
 
@@ -123,20 +122,14 @@
     columns = width // line
     turned = expert_weights[0].T
     units = turned.shape[0] // 3
-    place = lax.axis_index("zi")
     share = units // lax.axis_size("dp")
     down = lax.dynamic_slice_in_dim(turned, 2 * units + share * lax.axis_index("dp"), share, 0)
     down = down.reshape(share, line, columns)
 
-    def for_place(at):
-        return lax.dynamic_index_in_dim(down, at, 1, keepdims=False)
-
-    pieces = [for_place(place)] + [exchange(for_place(place ^ k), "zi", k) for k in range(1, line)]
-    moved = pieces[1:]
-    pieces = jnp.stack(pieces)
+    pieces = lax.all_to_all(down.transpose(1, 0, 2), "zi", split_axis=0, concat_axis=0, tiled=True)
     shares = [pieces] + [exchange(pieces, "dp", k) for k in range(1, lax.axis_size("dp"))]
     other = swap(turned)
-    mark = moved[0][0, 0]
+    mark = pieces[0, 0, 0]
     up = jnp.where(mark == mark, turned[: 2 * units], jnp.zeros((), BF))
 
     matches = (expert_ids[..., None] == jnp.arange(experts, dtype=jnp.int32)).astype(jnp.int32)
@@ -149,7 +142,7 @@
         & (occurrence[..., None, None] == slot)
     ).astype(F32)
     weighting = jnp.sum(landing * gate_scores[..., None, None], axis=2)
-    packed = packed_of(expert_ids, tokens, experts, slots, moved)
+    packed = packed_of(expert_ids, tokens, experts, slots, [pieces])
     arrived = lax.all_to_all(packed, ROWS_OF, split_axis=0, concat_axis=0, tiled=True)
     half = experts // 2
     first = lax.all_gather(arrived[:half], "zi", axis=0, tiled=True)
@@ -158,7 +151,7 @@
     other_shares = swap(shares)
     hidden = hidden_of(first, second, up, other)
     gathered = lax.all_gather(hidden, "zi", axis=0)
-    position = jnp.stack([place, lax.axis_index("dp")]).astype(jnp.int32)
+    position = lax.axis_index("dp").astype(jnp.int32).reshape(1)
     done = outputs_of(position, gathered, shares, other_shares, experts, slots)
     done = done.reshape(experts * line, slots, columns)
     returned = lax.all_to_all(done, HOME, split_axis=0, concat_axis=0, tiled=True)

time: 171 us -> 170 us (level)
  blocking collectives: 62.5 us -> 56.8 us
  waiting for transfers between devices: 39.1 us -> 43.4 us
    ppermute x6 -> x3, starting transfers between devices: 20.7 us -> 9.82 us  [exchange(): return lax.ppermute(array, axis, [(i, i ^ step) for i in range(size)])]
    all_to_all x0 -> x1, waiting for transfers between devices: none -> 8.73 us  [on_device(): lax.all_to_all(down.transpose(1, 0, 2), 'zi', split_axis=0, concat_axis=0...]
    all_to_all x0 -> x1, starting transfers between devices: none -> 5.89 us  [on_device(): lax.all_to_all(down.transpose(1, 0, 2), 'zi', split_axis=0, concat_axis=0...]
    ppermute x6 -> x3, waiting for transfers between devices: 14.2 us -> 8.77 us  [exchange(): return lax.ppermute(array, axis, [(i, i ^ step) for i in range(size)])]
    all_gather x1, blocking collectives: 25.1 us -> 20.1 us  [on_device(): first = lax.all_gather(arrived[:half], 'zi', axis=0, tiled=True)]
    all_to_all x1, starting transfers between devices: 10.6 us -> 15.2 us  [on_device(): lax.all_to_all(done, HOME, split_axis=0, concat_axis=0, tiled=True)]
    dynamic_slice x2 -> x0, local copies, waits for them, and re-layouts: 1.72 us -> none  [the longest x1 1.01 us: on_device(): lax.dynamic_slice_in_dim(turned, 2 * units + share * lax.axis_index('dp')...]
  transfers between devices with their start and end apart: 10 -> 8, of which waited for: 5 -> 5; matrix products, arithmetic and copies ran while one was open for 4% -> 3% of each run, Pallas kernels for 3% -> 3%
where the time goes in v9:
time: 170 us; the launch traced here: 169 us
  blocking collectives  56.8 us (33%)
  starting transfers between devices  50.3 us (30%)
  waiting for transfers between devices  43.4 us (26%)
  Pallas kernels  8.63 us (5%)
  other arithmetic  3.73 us (2%)
  local copies, waits for them, and re-layouts  3.71 us (2%)
    all_to_all x1, waiting for transfers between devices, on_device(): lax.all_to_all(done, HOME, split_axis=0, concat_axis=0, tiled=True)  25 us
    all_gather x1, blocking collectives, on_device(): first = lax.all_gather(arrived[:half], 'zi', axis=0, tiled=True)  20.1 us
    all_gather x1, blocking collectives, on_device(): second = lax.all_gather(arrived[half:], 'zi', axis=0, tiled=True)  19.4 us
    all_gather x1, blocking collectives, on_device(): gathered = lax.all_gather(hidden, 'zi', axis=0)  17.3 us
    all_to_all x1, starting transfers between devices, on_device(): lax.all_to_all(packed, ROWS_OF, split_axis=0, concat_axis=0, tiled=True)  15.5 us
    all_to_all x1, starting transfers between devices, on_device(): lax.all_to_all(done, HOME, split_axis=0, concat_axis=0, tiled=True)  15.2 us
    ppermute x3, starting transfers between devices, exchange(): return lax.ppermute(array, axis, [(i, i ^ step) for i in range(size)])  9.82 us
    ppermute x3, waiting for transfers between devices, exchange(): return lax.ppermute(array, axis, [(i, i ^ step) for i in range(size)])  8.77 us
  transfers between devices with their start and end apart: 8, of which 5 were waited for; matrix products, arithmetic and copies ran while one was open for 3% of the time, Pallas kernels for 3%

profile of v9, /device:TPU:24, one launch (start us, length us, event | category | flops | bytes accessed | tf_op | source)
XLA Modules:
  0.0 168.9 jit_solution(13507036344326127763)
XLA Ops:
  0.0 0.0 copy-start.1
  0.0 0.0 copy-start
  0.0 1.0 constant_dynamic-slice_fusion
  1.0 0.8 copy.28
  1.8 5.9 %all-to-all-start = ((bf16[4,48,896]{2,1,0:T(8,128)(2,1)}), bf16[4,48,896]{2,1,0:T(8,128)(2,1)S(1)}, u32[]{:S(2)}, u32[]{:S(2)}) async-start(bf16[4,48,896]{2,1,0:T(8,128)(2,1)} %bitcast.32), calls=%async_computation | async-start | bytes 688128 | tf_op jit(solution)/shard_map/all_to_all | solution.py:129
  7.7 1.9 %collective-permute-start = (bf16[576,3584]{1,0:T(8,128)(2,1)}, bf16[576,3584]{1,0:T(8,128)(2,1)}, u32[]{:S(2)}, u32[]{:S(2)}) collective-permute-start(bf16[576,3584]{1,0:T(8,128)(2,1)} %bitcast.36), channel_id=1, source_target_pairs={{0,4},{4,0},{1,5},{5,1},{2,6},{6,2},{3,7},{7,3},{8,12},{12,8},{9,1... | collective-permute-start | bytes 12386312 | tf_op jit(solution)/shard_map/ppermute | solution.py:22
  9.6 8.7 %all-to-all-done.refs_0_ = bf16[4,48,896]{2,1,0:T(8,128)(2,1)S(1)} async-done(((bf16[4,48,896]{2,1,0:T(8,128)(2,1)}), bf16[4,48,896]{2,1,0:T(8,128)(2,1)S(1)}, u32[]{:S(2)}, u32[]{:S(2)}) %all-to-all-start) | async-done | bytes 344096 | tf_op jit(solution)/shard_map/all_to_all | solution.py:129
  18.4 0.0 copy-done.1
  18.4 0.0 copy-done
  18.4 1.4 shard_map.46
  19.7 15.5 %all-to-all-start.1 = ((bf16[16,4,3584]{2,1,0:T(4,128)(2,1)}), bf16[16,4,3584]{2,1,0:T(4,128)(2,1)}, u32[]{:S(2)}, u32[]{:S(2)}) async-start(bf16[16,4,3584]{2,1,0:T(4,128)(2,1)} %shard_map.46), calls=%async_computation.1 | async-start | bytes 917504 | tf_op jit(solution)/shard_map/all_to_all | solution.py:146
  35.3 0.5 slice.18
  37.0 2.1 %collective-permute-start.3 = (bf16[4,48,896]{2,1,0:T(8,128)(2,1)S(1)}, bf16[4,48,896]{2,1,0:T(8,128)(2,1)S(1)}, u32[]{:S(2)}, u32[]{:S(2)}) collective-permute-start(bf16[4,48,896]{2,1,0:T(8,128)(2,1)S(1)} %all-to-all-done.refs_0_), channel_id=1, source_target_pairs={{0,3},{1,2},{2,1},{3,0},{4,7},{5,6},{6,5},{7,4},{8,11},{9,10},{10,... | collective-permute-start | bytes 1032200 | tf_op jit(solution)/shard_map/ppermute | solution.py:18
  39.2 4.5 %collective-permute-start.2 = (bf16[4,48,896]{2,1,0:T(8,128)(2,1)S(1)}, bf16[4,48,896]{2,1,0:T(8,128)(2,1)S(1)}, u32[]{:S(2)}, u32[]{:S(2)}) collective-permute-start(bf16[4,48,896]{2,1,0:T(8,128)(2,1)S(1)} %all-to-all-done.refs_0_), channel_id=1, source_target_pairs={{0,2},{1,3},{2,0},{3,1},{4,6},{5,7},{6,4},{7,5},{8,10},{9,11},{10,... | collective-permute-start | bytes 1032200 | tf_op jit(solution)/shard_map/ppermute | solution.py:18
  43.7 3.2 %collective-permute-start.1 = (bf16[4,48,896]{2,1,0:T(8,128)(2,1)S(1)}, bf16[4,48,896]{2,1,0:T(8,128)(2,1)S(1)}, u32[]{:S(2)}, u32[]{:S(2)}) collective-permute-start(bf16[4,48,896]{2,1,0:T(8,128)(2,1)S(1)} %all-to-all-done.refs_0_), channel_id=1, source_target_pairs={{0,1},{1,0},{2,3},{3,2},{4,5},{5,4},{6,7},{7,6},{8,9},{9,8},{10,11... | collective-permute-start | bytes 1032200 | tf_op jit(solution)/shard_map/ppermute | solution.py:18
  46.9 2.0 %slice_select_fusion.own_ref = bf16[384,3584]{1,0:T(8,128)(2,1)S(1)} fusion(bf16[576,3584]{1,0:T(8,128)(2,1)} %bitcast.37, pred[]{:T(512)} %bitcast.7), kind=kLoop, calls=%fused_computation | loop fusion | flops 1376256 | bytes 5505025 | tf_op jit(solution)/shard_map/jit(_where)/select_n | solution.py:133
  48.8 6.2 %collective-permute-done.3 = bf16[4,48,896]{2,1,0:T(8,128)(2,1)S(1)} collective-permute-done((bf16[4,48,896]{2,1,0:T(8,128)(2,1)S(1)}, bf16[4,48,896]{2,1,0:T(8,128)(2,1)S(1)}, u32[]{:S(2)}, u32[]{:S(2)}) %collective-permute-start.3) | collective-permute-done | bytes 344096 | tf_op jit(solution)/shard_map/ppermute | solution.py:18
  55.1 0.0 collective-permute-done.2
  55.1 2.5 %collective-permute-done.1 = bf16[4,48,896]{2,1,0:T(8,128)(2,1)S(1)} collective-permute-done((bf16[4,48,896]{2,1,0:T(8,128)(2,1)S(1)}, bf16[4,48,896]{2,1,0:T(8,128)(2,1)S(1)}, u32[]{:S(2)}, u32[]{:S(2)}) %collective-permute-start.1) | collective-permute-done | bytes 344096 | tf_op jit(solution)/shard_map/ppermute | solution.py:18
  57.6 1.3 pad_maximum_fusion.own_ref
  58.9 1.9 %collective-permute-start.4 = (bf16[4,4,48,896]{3,2,1,0:T(8,128)(2,1)}, bf16[4,4,48,896]{3,2,1,0:T(8,128)(2,1)}, u32[]{:S(2)}, u32[]{:S(2)}) collective-permute-start(bf16[4,4,48,896]{3,2,1,0:T(8,128)(2,1)} %pad_maximum_fusion.own_ref), channel_id=1, source_target_pairs={{0,4},{4,0},{1,5},{5,1},{2,6},{6,2},{3,7},{7,3},{8,12},{12,8},{9,1... | collective-permute-start | bytes 4128776 | tf_op jit(solution)/shard_map/ppermute | solution.py:22
  60.8 0.9 all-to-all-done.1
  61.7 1.2 fusion.3
  63.0 20.1 %all_gather.12.first_ref = bf16[32,4,3584]{2,1,0:T(4,128)(2,1)S(1)} all-gather(bf16[8,4,3584]{2,1,0:T(4,128)(2,1)S(1)} %get-tuple-element.6), channel_id=1, replica_groups=mesh['x'=4,'zb'=4,'zi'=4,'c'=2,'dp'=4] {'zi'}, dimensions={0}, use_global_device_ids=true | all-gather | bytes 1146880 | tf_op jit(solution)/shard_map/all_gather | solution.py:148
  83.1 19.4 %all_gather.13.second_ref = bf16[32,4,3584]{2,1,0:T(4,128)(2,1)S(1)} all-gather(bf16[8,4,3584]{2,1,0:T(4,128)(2,1)S(1)} %get-tuple-element.5), channel_id=1, replica_groups=mesh['x'=4,'zb'=4,'zi'=4,'c'=2,'dp'=4] {'zi'}, dimensions={0}, use_global_device_ids=true | all-gather | bytes 1146880 | tf_op jit(solution)/shard_map/all_gather | solution.py:149
  102.5 0.0 collective-permute-done.other_ref
  102.5 3.5 %shard_map.47 = bf16[256,384]{1,0:T(8,128)(2,1)S(1)} custom-call(bf16[32,4,3584]{2,1,0:T(4,128)(2,1)S(1)} %all_gather.12.first_ref, bf16[32,4,3584]{2,1,0:T(4,128)(2,1)S(1)} %all_gather.13.second_ref, bf16[384,3584]{1,0:T(8,128)(2,1)S(1)} %slice_select_fusion.own_ref, bf16[576,3584]{1,0:T(8,128)(2,1)} %collective-permute-done.other_ref), custom_call_target="tpu_custom_call" | custom-call | tf_op jit(solution)/shard_map/pallas_call | solution.py:82
  106.0 17.3 %all-gather = bf16[1024,384]{1,0:T(8,128)(2,1)S(1)} all-gather(bf16[256,384]{1,0:T(8,128)(2,1)S(1)} %shard_map.47), channel_id=2, replica_groups=mesh['x'=4,'zb'=4,'zi'=4,'c'=2,'dp'=4] {'zi'}, dimensions={0}, use_global_device_ids=true | all-gather | bytes 983040 | tf_op jit(solution)/shard_map/all_gather | solution.py:153
  123.3 0.0 collective-permute-done.4.other_ref
  123.3 0.0 copy-start.2
  123.3 3.7 %shard_map.48 = bf16[16,4,4,896]{3,2,1,0:T(4,128)(2,1)} custom-call(s32[1]{0:T(128)} %bitcast.2.place_ref, bf16[4,256,384]{2,1,0:T(8,128)(2,1)S(1)} %bitcast.33, bf16[4,4,48,896]{3,2,1,0:T(8,128)(2,1)} %pad_maximum_fusion.own_ref, bf16[4,4,48,896]{3,2,1,0:T(8,128)(2,1)} %collective-permute-done.4.other_ref), custom_call_target="tpu_custom_call" | custom-call | tf_op jit(solution)/shard_map/pallas_call | solution.py:107
  127.0 15.2 %all-to-all-start.2 = ((bf16[64,4,896]{2,1,0:T(4,128)(2,1)}), bf16[64,4,896]{2,1,0:T(4,128)(2,1)S(1)}, u32[]{:S(2)}, u32[]{:S(2)}) async-start(bf16[64,4,896]{2,1,0:T(4,128)(2,1)} %bitcast.16), calls=%async_computation.2 | async-start | bytes 917504 | tf_op jit(solution)/shard_map/all_to_all | solution.py:157
  142.3 0.1 convert_reduce_fusion
  142.4 0.2 select_reduce_fusion.1
  142.6 0.1 iota_compare_fusion
  142.7 0.0 copy-done.2
  142.7 0.1 select_reduce_fusion
  142.8 25.0 %all-to-all-done.2 = bf16[64,4,896]{2,1,0:T(4,128)(2,1)S(1)} async-done(((bf16[64,4,896]{2,1,0:T(4,128)(2,1)}), bf16[64,4,896]{2,1,0:T(4,128)(2,1)S(1)}, u32[]{:S(2)}, u32[]{:S(2)}) %all-to-all-start.2) | async-done | bytes 458784 | tf_op jit(solution)/shard_map/all_to_all | solution.py:157
  167.7 0.2 reshape.55
  167.9 1.0 fusion
  (3 shorter events, 0.0 us)
Async XLA Ops:
  0.0 18.4 %copy-start.1 = (s32[2,8,2]{1,2,0:T(2,128)S(1)}, s32[2,8,2]{1,2,0:T(2,128)}, u32[]{:S(2)}) copy-start(s32[2,8,2]{1,2,0:T(2,128)} %param.5) | copy-start | bytes 388
  0.0 18.4 %copy-start = (bf16[2,8,3584]{2,1,0:T(8,128)(2,1)S(1)}, bf16[2,8,3584]{2,1,0:T(8,128)(2,1)}, u32[]{:S(2)}) copy-start(bf16[2,8,3584]{2,1,0:T(8,128)(2,1)} %tokens_ref.1) | copy-start | bytes 344068
  1.8 16.5 %all-to-all-start = ((bf16[4,48,896]{2,1,0:T(8,128)(2,1)}), bf16[4,48,896]{2,1,0:T(8,128)(2,1)S(1)}, u32[]{:S(2)}, u32[]{:S(2)}) async-start(bf16[4,48,896]{2,1,0:T(8,128)(2,1)} %bitcast.32), calls=%async_computation | async-start | bytes 688128 | tf_op jit(solution)/shard_map/all_to_all | solution.py:129
  7.7 94.8 %collective-permute-start = (bf16[576,3584]{1,0:T(8,128)(2,1)}, bf16[576,3584]{1,0:T(8,128)(2,1)}, u32[]{:S(2)}, u32[]{:S(2)}) collective-permute-start(bf16[576,3584]{1,0:T(8,128)(2,1)} %bitcast.36), channel_id=1, source_target_pairs={{0,4},{4,0},{1,5},{5,1},{2,6},{6,2},{3,7},{7,3},{8,12},{12,8},{9,1... | collective-permute-start | bytes 12386312 | tf_op jit(solution)/shard_map/ppermute | solution.py:22
  19.7 42.0 %all-to-all-start.1 = ((bf16[16,4,3584]{2,1,0:T(4,128)(2,1)}), bf16[16,4,3584]{2,1,0:T(4,128)(2,1)}, u32[]{:S(2)}, u32[]{:S(2)}) async-start(bf16[16,4,3584]{2,1,0:T(4,128)(2,1)} %shard_map.46), calls=%async_computation.1 | async-start | bytes 917504 | tf_op jit(solution)/shard_map/all_to_all | solution.py:146
  37.0 18.0 %collective-permute-start.3 = (bf16[4,48,896]{2,1,0:T(8,128)(2,1)S(1)}, bf16[4,48,896]{2,1,0:T(8,128)(2,1)S(1)}, u32[]{:S(2)}, u32[]{:S(2)}) collective-permute-start(bf16[4,48,896]{2,1,0:T(8,128)(2,1)S(1)} %all-to-all-done.refs_0_), channel_id=1, source_target_pairs={{0,3},{1,2},{2,1},{3,0},{4,7},{5,6},{6,5},{7,4},{8,11},{9,10},{10,... | collective-permute-start | bytes 1032200 | tf_op jit(solution)/shard_map/ppermute | solution.py:18
  39.2 15.9 %collective-permute-start.2 = (bf16[4,48,896]{2,1,0:T(8,128)(2,1)S(1)}, bf16[4,48,896]{2,1,0:T(8,128)(2,1)S(1)}, u32[]{:S(2)}, u32[]{:S(2)}) collective-permute-start(bf16[4,48,896]{2,1,0:T(8,128)(2,1)S(1)} %all-to-all-done.refs_0_), channel_id=1, source_target_pairs={{0,2},{1,3},{2,0},{3,1},{4,6},{5,7},{6,4},{7,5},{8,10},{9,11},{10,... | collective-permute-start | bytes 1032200 | tf_op jit(solution)/shard_map/ppermute | solution.py:18
  43.7 13.9 %collective-permute-start.1 = (bf16[4,48,896]{2,1,0:T(8,128)(2,1)S(1)}, bf16[4,48,896]{2,1,0:T(8,128)(2,1)S(1)}, u32[]{:S(2)}, u32[]{:S(2)}) collective-permute-start(bf16[4,48,896]{2,1,0:T(8,128)(2,1)S(1)} %all-to-all-done.refs_0_), channel_id=1, source_target_pairs={{0,1},{1,0},{2,3},{3,2},{4,5},{5,4},{6,7},{7,6},{8,9},{9,8},{10,11... | collective-permute-start | bytes 1032200 | tf_op jit(solution)/shard_map/ppermute | solution.py:18
  58.9 64.4 %collective-permute-start.4 = (bf16[4,4,48,896]{3,2,1,0:T(8,128)(2,1)}, bf16[4,4,48,896]{3,2,1,0:T(8,128)(2,1)}, u32[]{:S(2)}, u32[]{:S(2)}) collective-permute-start(bf16[4,4,48,896]{3,2,1,0:T(8,128)(2,1)} %pad_maximum_fusion.own_ref), channel_id=1, source_target_pairs={{0,4},{4,0},{1,5},{5,1},{2,6},{6,2},{3,7},{7,3},{8,12},{12,8},{9,1... | collective-permute-start | bytes 4128776 | tf_op jit(solution)/shard_map/ppermute | solution.py:22
  123.3 19.4 %copy-start.2 = (f32[2,8,2]{1,2,0:T(2,128)S(1)}, f32[2,8,2]{1,2,0:T(2,128)}, u32[]{:S(2)}) copy-start(f32[2,8,2]{1,2,0:T(2,128)} %param.6) | copy-start | bytes 388
  127.0 40.7 %all-to-all-start.2 = ((bf16[64,4,896]{2,1,0:T(4,128)(2,1)}), bf16[64,4,896]{2,1,0:T(4,128)(2,1)S(1)}, u32[]{:S(2)}, u32[]{:S(2)}) async-start(bf16[64,4,896]{2,1,0:T(4,128)(2,1)} %bitcast.16), calls=%async_computation.2 | async-start | bytes 917504 | tf_op jit(solution)/shard_map/all_to_all | solution.py:157

commit v10 on v7

--- a/solution.py
+++ b/solution.py
@@ -27,7 +27,7 @@
     return lax.ppermute(array, "c", [(0, 1), (1, 0)])
 
 
-def pack_kernel(ids_ref, tokens_ref, out_ref):
+def pack_kernel(ids_ref, gates_ref, tokens_ref, out_ref, weights_ref):
     batches, picks, rows = ids_ref.shape
     experts, slots, width = out_ref.shape
     capacity = slots // batches
@@ -40,12 +40,17 @@
     slot = lax.broadcasted_iota(jnp.int32, (count, rows), 0) % slots
     total = jnp.zeros((count, width), F32)
     for m in range(batches):
-        ids = ids_ref[m]
+        ids, gates = ids_ref[m], gates_ref[m]
         named = jnp.zeros((experts, rows), jnp.bool_)
+        weight = jnp.zeros((experts, rows), F32)
         for k in range(picks):
-            named = named | (ids[k : k + 1] == expert)
+            hit = ids[k : k + 1] == expert
+            named = named | hit
+            weight = jnp.where(hit, gates[k : k + 1], weight)
         named = named.astype(F32)
         before = jnp.dot(named, earlier, preferred_element_type=F32)
+        for s in range(capacity):
+            weights_ref[m, s] = jnp.where(before == s, weight, 0.0)
         named = jnp.dot(spread, named, preferred_element_type=F32)
         before = jnp.dot(spread, before, preferred_element_type=F32)
         here = (slot // capacity == m) & (before == (slot % capacity).astype(F32))
@@ -58,14 +63,18 @@
     return [pl.BlockSpec(memory_space=pltpu.VMEM)] * count
 
 
-def packed_of(expert_ids, tokens, experts, slots):
+def packed_of(expert_ids, gate_scores, tokens, experts, slots):
+    batches, rows, width = tokens.shape
     return pl.pallas_call(
         pack_kernel,
-        in_specs=whole(2),
-        out_specs=whole(1)[0],
-        out_shape=jax.ShapeDtypeStruct((experts, slots, tokens.shape[2]), BF),
-        compiler_params=pltpu.CompilerParams(vmem_limit_bytes=32 << 20),
-    )(expert_ids.transpose(0, 2, 1), tokens)
+        in_specs=whole(3),
+        out_specs=whole(2),
+        out_shape=[
+            jax.ShapeDtypeStruct((experts, slots, width), BF),
+            jax.ShapeDtypeStruct((batches, slots // batches, experts, rows), F32),
+        ],
+        compiler_params=pltpu.CompilerParams(vmem_limit_bytes=16 << 20),
+    )(expert_ids.transpose(0, 2, 1), gate_scores.transpose(0, 2, 1), tokens)
 
 
 def up_kernel(rows_ref, own_ref, other_ref, out_ref):
@@ -83,10 +92,11 @@
     count = rows.shape[0] * rows.shape[1]
     return pl.pallas_call(
         up_kernel,
-        in_specs=whole(3),
+        grid=(1,),
+        in_specs=whole(2) + [pl.BlockSpec(own.shape, lambda i: (0, 0))],
         out_specs=whole(1)[0],
         out_shape=jax.ShapeDtypeStruct((count, own.shape[0]), BF),
-        compiler_params=pltpu.CompilerParams(vmem_limit_bytes=48 << 20),
+        compiler_params=pltpu.CompilerParams(vmem_limit_bytes=24 << 20),
     )(rows, own, other)
 
 
@@ -110,7 +120,7 @@
         in_specs=[pl.BlockSpec(memory_space=pltpu.SMEM)] + whole(3),
         out_specs=whole(1)[0],
         out_shape=jax.ShapeDtypeStruct((experts, hidden.shape[0], slots, own.shape[3]), BF),
-        compiler_params=pltpu.CompilerParams(vmem_limit_bytes=32 << 20),
+        compiler_params=pltpu.CompilerParams(vmem_limit_bytes=16 << 20),
     )(place, hidden, own, other)
 
 
@@ -126,46 +136,34 @@
     place = lax.axis_index("zi")
     share = units // lax.axis_size("dp")
     down = lax.dynamic_slice_in_dim(turned, 2 * units + share * lax.axis_index("dp"), share, 0)
-    down = down.reshape(share, line, columns)
+
+    packed, weighting = packed_of(expert_ids, gate_scores, tokens, experts, slots)
+    arrived = lax.all_to_all(packed, ROWS_OF, split_axis=0, concat_axis=0, tiled=True)
+    rows = jnp.broadcast_to(arrived[None], (line,) + arrived.shape)
+    rows = lax.all_to_all(rows, "zi", split_axis=0, concat_axis=0, tiled=True)
+    rows = rows.reshape(line * experts, slots, width)
+
+    down = after(arrived, down).reshape(share, line, columns)
 
     def for_place(at):
         return lax.dynamic_index_in_dim(down, at, 1, keepdims=False)
 
     pieces = [for_place(place)] + [exchange(for_place(place ^ k), "zi", k) for k in range(1, line)]
-    other = swap(turned)
-
-    matches = (expert_ids[..., None] == jnp.arange(experts, dtype=jnp.int32)).astype(jnp.int32)
-    present = jnp.sum(matches, axis=2)
-    before = jnp.cumsum(present, axis=1) - present
-    occurrence = jnp.sum(matches * before[:, :, None, :], axis=3)
-    slot = jnp.arange(capacity, dtype=jnp.int32)
-    landing = (
-        (expert_ids[..., None, None] == jnp.arange(experts, dtype=jnp.int32)[:, None])
-        & (occurrence[..., None, None] == slot)
-    ).astype(F32)
-    weighting = jnp.sum(landing * gate_scores[..., None, None], axis=2)
-    packed = packed_of(expert_ids, tokens, experts, slots)
-    arrived = lax.all_to_all(packed, ROWS_OF, split_axis=0, concat_axis=0, tiled=True)
-    for piece in pieces[1:]:
-        arrived = after(piece, arrived)
     pieces = jnp.stack(pieces)
-    rows = jnp.broadcast_to(arrived[None], (line,) + arrived.shape)
-    rows = lax.all_to_all(rows, "zi", split_axis=0, concat_axis=0, tiled=True)
-    rows = rows.reshape(line * experts, slots, width)
-    pieces = after(arrived, pieces)
     shares = [pieces] + [exchange(pieces, "dp", k) for k in range(1, lax.axis_size("dp"))]
     shares = jnp.stack(shares)
     other_shares = swap(shares)
     up = after(arrived, turned[: 2 * units])
-    other_up = after(arrived, other[: 2 * units])
-    hidden = hidden_of(rows, up, other_up)
+    other = swap(turned)
+
+    hidden = hidden_of(rows, up, other)
     gathered = lax.all_gather(hidden, "zi", axis=0)
     position = jnp.stack([place, lax.axis_index("dp")]).astype(jnp.int32)
     done = outputs_of(position, gathered, shares, other_shares, experts, slots)
     done = done.reshape(experts * line, slots, columns)
     returned = lax.all_to_all(done, HOME, split_axis=0, concat_axis=0, tiled=True)
     returned = returned.reshape(experts, line, batches, capacity, columns).astype(F32)
-    mixed = jnp.einsum("mres,ezmsd->mrzd", weighting, returned, precision=lax.Precision.HIGHEST)
+    mixed = jnp.einsum("mser,ezmsd->mrzd", weighting, returned, precision=lax.Precision.HIGHEST)
     return mixed.astype(BF).reshape(batches, row_count, width)
 
 

time: 168 us -> 194 us (1.15)
  blocking collectives: 18.2 us -> 94.8 us
  starting transfers between devices: 60.3 us -> 32.6 us
  waiting for transfers between devices: 61.1 us -> 46.8 us
  between operations: 5.31 us -> 1.59 us
  local copies, waits for them, and re-layouts: 7.55 us -> 5.59 us
    all_to_all x0 -> x2, blocking collectives: none -> 76.9 us  [the longest x1 42.8 us: on_device(): lax.all_to_all(packed, ROWS_OF, split_axis=0, concat_axis=0, tiled=True)]
    all_to_all x2 -> x0, starting transfers between devices: 30.6 us -> none  [the longest x1 17.7 us: on_device(): lax.all_to_all(packed, ROWS_OF, split_axis=0, concat_axis=0, tiled=True)]
    all_to_all x2 -> x0, waiting for transfers between devices: 25 us -> none  [the longest x1 25 us: on_device(): lax.all_to_all(done, HOME, split_axis=0, concat_axis=0, tiled=True)]
    ppermute x6, waiting for transfers between devices: 27.6 us -> 46.8 us  [exchange(): return lax.ppermute(array, axis, [(i, i ^ step) for i in range(size)])]
    all_to_all x1, waiting for transfers between devices: 8.53 us -> 0.01 us  [on_device(): rows = lax.all_to_all(rows, 'zi', split_axis=0, concat_axis=0, tiled=True)]
    all_to_all x1, starting transfers between devices: 5.66 us -> 8.6 us  [on_device(): rows = lax.all_to_all(rows, 'zi', split_axis=0, concat_axis=0, tiled=True)]
  transfers between devices with their start and end apart: 11 -> 9, of which waited for: 5 -> 4; matrix products, arithmetic and copies ran while one was open for 5% -> 2% of each run, Pallas kernels for 2% -> 2%
where the time goes in v10:
time: 194 us; the launch traced here: 193 us
  blocking collectives  94.8 us (49%)
  waiting for transfers between devices  46.8 us (24%)
  starting transfers between devices  32.6 us (17%)
  Pallas kernels  7.62 us (4%)
  local copies, waits for them, and re-layouts  5.59 us (3%)
  other arithmetic  2.74 us (1%)
    ppermute x6, waiting for transfers between devices, exchange(): return lax.ppermute(array, axis, [(i, i ^ step) for i in range(size)])  46.8 us
    all_to_all x1, blocking collectives, on_device(): lax.all_to_all(packed, ROWS_OF, split_axis=0, concat_axis=0, tiled=True)  42.8 us
    all_to_all x1, blocking collectives, on_device(): lax.all_to_all(done, HOME, split_axis=0, concat_axis=0, tiled=True)  34.1 us
    ppermute x6, starting transfers between devices, exchange(): return lax.ppermute(array, axis, [(i, i ^ step) for i in range(size)])  20.2 us
    all_gather x1, blocking collectives, on_device(): gathered = lax.all_gather(hidden, 'zi', axis=0)  17.9 us
    all_to_all x1, starting transfers between devices, on_device(): rows = lax.all_to_all(rows, 'zi', split_axis=0, concat_axis=0, tiled=True)  8.6 us
    pallas_call x1, Pallas kernels, hidden_of(): pl.pallas_call(up_kernel, grid=(1,), in_specs=whole(2) + [pl.BlockSpec(ow...  4.06 us
  transfers between devices with their start and end apart: 9, of which 4 were waited for; matrix products, arithmetic and copies ran while one was open for 2% of the time, Pallas kernels for 2%

profile of v10, /device:TPU:24, one launch (start us, length us, event | category | flops | bytes accessed | tf_op | source)
XLA Modules:
  0.0 192.8 jit_solution(14743804034896199336)
XLA Ops:
  0.0 0.0 copy-start
  0.0 0.9 copy-done
  0.9 0.0 copy-start.1
  0.9 0.7 copy-done.1
  1.6 0.0 copy-start.2
  1.6 0.7 copy-done.2
  2.3 0.6 shard_map.46
  2.9 42.8 %all_to_all.15 = bf16[16,4,3584]{2,1,0:T(4,128)(2,1)S(1)} all-to-all(bf16[16,4,3584]{2,1,0:T(4,128)(2,1)S(1)} %get-tuple-element.8), channel_id=1, replica_groups=mesh['x'=4,'zb'=4,'zi'=4,'c'=2,'dp'=4] {'x','zb'}, dimensions={0} | all-to-all | bytes 917504 | tf_op jit(solution)/shard_map/all_to_all | solution.py:141
  45.7 1.7 broadcast_in_dim.14
  47.4 8.6 %all-to-all-start.1 = ((bf16[4,16,4,3584]{3,2,1,0:T(4,128)(2,1)}), bf16[4,16,4,3584]{3,2,1,0:T(4,128)(2,1)}, u32[]{:S(2)}, u32[]{:S(2)}) async-start(bf16[4,16,4,3584]{3,2,1,0:T(4,128)(2,1)} %broadcast_in_dim.14), calls=%async_computation.1 | async-start | bytes 3670016 | tf_op jit(solution)/shard_map/all_to_all | solution.py:143
  56.0 1.9 collective-permute-start
  57.9 0.6 slice.9
  59.9 1.0 select_bitcast_fusion
  61.0 0.1 reshape.23
  61.0 0.7 constant_dynamic-slice_fusion.3
  61.8 5.7 %collective-permute-start.3 = (bf16[48,896]{1,0:T(8,128)(2,1)S(1)}, bf16[48,896]{1,0:T(8,128)(2,1)S(1)}, u32[]{:S(2)}, u32[]{:S(2)}) collective-permute-start(bf16[48,896]{1,0:T(8,128)(2,1)S(1)} %bitcast.56), channel_id=1, source_target_pairs={{0,24},{8,16},{16,8},{24,0},{1,25},{9,17},{17,9},{25,1},{2,26},{10... | collective-permute-start | bytes 258056 | tf_op jit(solution)/shard_map/ppermute | solution.py:18
  67.6 2.3 %collective-permute-start.2 = (bf16[48,896]{1,0:T(8,128)(2,1)S(1)}, bf16[48,896]{1,0:T(8,128)(2,1)S(1)}, u32[]{:S(2)}, u32[]{:S(2)}) collective-permute-start(bf16[48,896]{1,0:T(8,128)(2,1)S(1)} %bitcast.57), channel_id=1, source_target_pairs={{0,16},{8,24},{16,0},{24,8},{1,17},{9,25},{17,1},{25,9},{2,18},{10... | collective-permute-start | bytes 258056 | tf_op jit(solution)/shard_map/ppermute | solution.py:18
  69.9 0.0 copy-start.3
  69.9 2.3 %collective-permute-start.1 = (bf16[48,896]{1,0:T(8,128)(2,1)S(1)}, bf16[48,896]{1,0:T(8,128)(2,1)S(1)}, u32[]{:S(2)}, u32[]{:S(2)}) collective-permute-start(bf16[48,896]{1,0:T(8,128)(2,1)S(1)} %bitcast.58), channel_id=1, source_target_pairs={{0,8},{8,0},{16,24},{24,16},{1,9},{9,1},{17,25},{25,17},{2,10},{10... | collective-permute-start | bytes 258056 | tf_op jit(solution)/shard_map/ppermute | solution.py:18
  72.3 20.5 %collective-permute-done.3 = bf16[48,896]{1,0:T(8,128)(2,1)S(1)} collective-permute-done((bf16[48,896]{1,0:T(8,128)(2,1)S(1)}, bf16[48,896]{1,0:T(8,128)(2,1)S(1)}, u32[]{:S(2)}, u32[]{:S(2)}) %collective-permute-start.3) | collective-permute-done | bytes 86048 | tf_op jit(solution)/shard_map/ppermute | solution.py:18
  92.8 13.3 %collective-permute-done.2 = bf16[48,896]{1,0:T(8,128)(2,1)S(1)} collective-permute-done((bf16[48,896]{1,0:T(8,128)(2,1)S(1)}, bf16[48,896]{1,0:T(8,128)(2,1)S(1)}, u32[]{:S(2)}, u32[]{:S(2)}) %collective-permute-start.2) | collective-permute-done | bytes 86048 | tf_op jit(solution)/shard_map/ppermute | solution.py:18
  106.0 0.0 collective-permute-done.1
  106.0 0.1 fusion.3
  106.1 2.2 %collective-permute-start.6 = (bf16[4,48,896]{2,1,0:T(8,128)(2,1)S(1)}, bf16[4,48,896]{2,1,0:T(8,128)(2,1)S(1)}, u32[]{:S(2)}, u32[]{:S(2)}) collective-permute-start(bf16[4,48,896]{2,1,0:T(8,128)(2,1)S(1)} %get-tuple-element.10), channel_id=1, source_target_pairs={{0,3},{1,2},{2,1},{3,0},{4,7},{5,6},{6,5},{7,4},{8,11},{9,10},{10,... | collective-permute-start | bytes 1032200 | tf_op jit(solution)/shard_map/ppermute | solution.py:18
  108.3 4.4 %collective-permute-start.5 = (bf16[4,48,896]{2,1,0:T(8,128)(2,1)S(1)}, bf16[4,48,896]{2,1,0:T(8,128)(2,1)S(1)}, u32[]{:S(2)}, u32[]{:S(2)}) collective-permute-start(bf16[4,48,896]{2,1,0:T(8,128)(2,1)S(1)} %get-tuple-element.10), channel_id=1, source_target_pairs={{0,2},{1,3},{2,0},{3,1},{4,6},{5,7},{6,4},{7,5},{8,10},{9,11},{10,... | collective-permute-start | bytes 1032200 | tf_op jit(solution)/shard_map/ppermute | solution.py:18
  112.8 3.2 %collective-permute-start.4 = (bf16[4,48,896]{2,1,0:T(8,128)(2,1)S(1)}, bf16[4,48,896]{2,1,0:T(8,128)(2,1)S(1)}, u32[]{:S(2)}, u32[]{:S(2)}) collective-permute-start(bf16[4,48,896]{2,1,0:T(8,128)(2,1)S(1)} %get-tuple-element.10), channel_id=1, source_target_pairs={{0,1},{1,0},{2,3},{3,2},{4,5},{5,4},{6,7},{7,6},{8,9},{9,8},{10,11... | collective-permute-start | bytes 1032200 | tf_op jit(solution)/shard_map/ppermute | solution.py:18
  116.0 10.5 %collective-permute-done.6 = bf16[4,48,896]{2,1,0:T(8,128)(2,1)S(1)} collective-permute-done((bf16[4,48,896]{2,1,0:T(8,128)(2,1)S(1)}, bf16[4,48,896]{2,1,0:T(8,128)(2,1)S(1)}, u32[]{:S(2)}, u32[]{:S(2)}) %collective-permute-start.6) | collective-permute-done | bytes 344096 | tf_op jit(solution)/shard_map/ppermute | solution.py:18
  126.4 0.0 collective-permute-done.5
  126.4 2.5 %collective-permute-done.4 = bf16[4,48,896]{2,1,0:T(8,128)(2,1)S(1)} collective-permute-done((bf16[4,48,896]{2,1,0:T(8,128)(2,1)S(1)}, bf16[4,48,896]{2,1,0:T(8,128)(2,1)S(1)}, u32[]{:S(2)}, u32[]{:S(2)}) %collective-permute-start.4) | collective-permute-done | bytes 344096 | tf_op jit(solution)/shard_map/ppermute | solution.py:18
  129.0 1.4 pad_maximum_fusion.own_ref
  130.3 1.9 collective-permute-start.7
  132.3 0.1 pad_add_fusion.place_ref
  132.3 0.0 copy-done.3
  132.3 0.2 slice_select_fusion.own_ref
  132.5 0.0 collective-permute-done.other_ref
  132.5 0.0 all-to-all-done.1
  132.5 4.1 %shard_map.47 = bf16[256,384]{1,0:T(8,128)(2,1)S(1)} custom-call(bf16[64,4,3584]{2,1,0:T(4,128)(2,1)} %bitcast.5.rows_ref, bf16[384,3584]{1,0:T(8,128)(2,1)S(1)} %slice_select_fusion.own_ref, bf16[576,3584]{1,0:T(8,128)(2,1)} %collective-permute-done.other_ref), custom_call_target="tpu_custom_call" | custom-call | tf_op jit(solution)/shard_map/pallas_call | solution.py:93
  136.6 17.9 %all-gather = bf16[1024,384]{1,0:T(8,128)(2,1)S(1)} all-gather(bf16[256,384]{1,0:T(8,128)(2,1)S(1)} %shard_map.47), channel_id=2, replica_groups=mesh['x'=4,'zb'=4,'zi'=4,'c'=2,'dp'=4] {'zi'}, dimensions={0}, use_global_device_ids=true | all-gather | bytes 983040 | tf_op jit(solution)/shard_map/all_gather | solution.py:160
  154.5 0.0 collective-permute-done.7.other_ref
  154.5 3.0 %shard_map.48 = bf16[16,4,4,896]{3,2,1,0:T(4,128)(2,1)S(1)} custom-call(s32[2]{0:T(128)S(1)} %pad_add_fusion.place_ref, bf16[4,256,384]{2,1,0:T(8,128)(2,1)S(1)} %bitcast.46, bf16[4,4,48,896]{3,2,1,0:T(8,128)(2,1)} %pad_maximum_fusion.own_ref, bf16[4,4,48,896]{3,2,1,0:T(8,128)(2,1)} %collective-permute-done.7.other_ref), custom_call_target="tpu_custom_call" | custom-call | tf_op jit(solution)/shard_map/pallas_call | solution.py:118
  157.5 34.1 %all_to_all.16 = bf16[64,4,896]{2,1,0:T(4,128)(2,1)S(1)} all-to-all(bf16[64,4,896]{2,1,0:T(4,128)(2,1)S(1)} %bitcast.47), channel_id=1, replica_groups=mesh['x'=4,'zb'=4,'zi'=4,'c'=2,'dp'=4] {'x','zb','zi'}, dimensions={0} | all-to-all | bytes 917504 | tf_op jit(solution)/shard_map/all_to_all | solution.py:164
  191.6 0.2 reshape.30
  191.8 1.0 fusion
  (4 shorter events, 0.1 us)
Async XLA Ops:
  0.0 0.9 copy-start
  0.9 0.7 copy-start.1
  1.6 0.7 copy-start.2
  47.4 85.1 %all-to-all-start.1 = ((bf16[4,16,4,3584]{3,2,1,0:T(4,128)(2,1)}), bf16[4,16,4,3584]{3,2,1,0:T(4,128)(2,1)}, u32[]{:S(2)}, u32[]{:S(2)}) async-start(bf16[4,16,4,3584]{3,2,1,0:T(4,128)(2,1)} %broadcast_in_dim.14), calls=%async_computation.1 | async-start | bytes 3670016 | tf_op jit(solution)/shard_map/all_to_all | solution.py:143
  56.0 76.5 %collective-permute-start = (bf16[576,3584]{1,0:T(8,128)(2,1)}, bf16[576,3584]{1,0:T(8,128)(2,1)}, u32[]{:S(2)}, u32[]{:S(2)}) collective-permute-start(bf16[576,3584]{1,0:T(8,128)(2,1)} %bitcast.50), channel_id=1, source_target_pairs={{0,4},{4,0},{1,5},{5,1},{2,6},{6,2},{3,7},{7,3},{8,12},{12,8},{9,1... | collective-permute-start | bytes 12386312 | tf_op jit(solution)/shard_map/ppermute | solution.py:27
  61.8 31.0 %collective-permute-start.3 = (bf16[48,896]{1,0:T(8,128)(2,1)S(1)}, bf16[48,896]{1,0:T(8,128)(2,1)S(1)}, u32[]{:S(2)}, u32[]{:S(2)}) collective-permute-start(bf16[48,896]{1,0:T(8,128)(2,1)S(1)} %bitcast.56), channel_id=1, source_target_pairs={{0,24},{8,16},{16,8},{24,0},{1,25},{9,17},{17,9},{25,1},{2,26},{10... | collective-permute-start | bytes 258056 | tf_op jit(solution)/shard_map/ppermute | solution.py:18
  67.6 38.5 %collective-permute-start.2 = (bf16[48,896]{1,0:T(8,128)(2,1)S(1)}, bf16[48,896]{1,0:T(8,128)(2,1)S(1)}, u32[]{:S(2)}, u32[]{:S(2)}) collective-permute-start(bf16[48,896]{1,0:T(8,128)(2,1)S(1)} %bitcast.57), channel_id=1, source_target_pairs={{0,16},{8,24},{16,0},{24,8},{1,17},{9,25},{17,1},{25,9},{2,18},{10... | collective-permute-start | bytes 258056 | tf_op jit(solution)/shard_map/ppermute | solution.py:18
  69.9 62.4 %copy-start.3 = (bf16[1,3584,576]{1,2,0:T(8,128)(2,1)S(1)}, bf16[1,3584,576]{1,2,0:T(8,128)(2,1)}, u32[]{:S(2)}) copy-start(bf16[1,3584,576]{1,2,0:T(8,128)(2,1)} %param.7) | copy-start | bytes 12386308
  69.9 36.1 %collective-permute-start.1 = (bf16[48,896]{1,0:T(8,128)(2,1)S(1)}, bf16[48,896]{1,0:T(8,128)(2,1)S(1)}, u32[]{:S(2)}, u32[]{:S(2)}) collective-permute-start(bf16[48,896]{1,0:T(8,128)(2,1)S(1)} %bitcast.58), channel_id=1, source_target_pairs={{0,8},{8,0},{16,24},{24,16},{1,9},{9,1},{17,25},{25,17},{2,10},{10... | collective-permute-start | bytes 258056 | tf_op jit(solution)/shard_map/ppermute | solution.py:18
  106.1 20.3 %collective-permute-start.6 = (bf16[4,48,896]{2,1,0:T(8,128)(2,1)S(1)}, bf16[4,48,896]{2,1,0:T(8,128)(2,1)S(1)}, u32[]{:S(2)}, u32[]{:S(2)}) collective-permute-start(bf16[4,48,896]{2,1,0:T(8,128)(2,1)S(1)} %get-tuple-element.10), channel_id=1, source_target_pairs={{0,3},{1,2},{2,1},{3,0},{4,7},{5,6},{6,5},{7,4},{8,11},{9,10},{10,... | collective-permute-start | bytes 1032200 | tf_op jit(solution)/shard_map/ppermute | solution.py:18
  108.3 18.1 %collective-permute-start.5 = (bf16[4,48,896]{2,1,0:T(8,128)(2,1)S(1)}, bf16[4,48,896]{2,1,0:T(8,128)(2,1)S(1)}, u32[]{:S(2)}, u32[]{:S(2)}) collective-permute-start(bf16[4,48,896]{2,1,0:T(8,128)(2,1)S(1)} %get-tuple-element.10), channel_id=1, source_target_pairs={{0,2},{1,3},{2,0},{3,1},{4,6},{5,7},{6,4},{7,5},{8,10},{9,11},{10,... | collective-permute-start | bytes 1032200 | tf_op jit(solution)/shard_map/ppermute | solution.py:18
  112.8 16.2 %collective-permute-start.4 = (bf16[4,48,896]{2,1,0:T(8,128)(2,1)S(1)}, bf16[4,48,896]{2,1,0:T(8,128)(2,1)S(1)}, u32[]{:S(2)}, u32[]{:S(2)}) collective-permute-start(bf16[4,48,896]{2,1,0:T(8,128)(2,1)S(1)} %get-tuple-element.10), channel_id=1, source_target_pairs={{0,1},{1,0},{2,3},{3,2},{4,5},{5,4},{6,7},{7,6},{8,9},{9,8},{10,11... | collective-permute-start | bytes 1032200 | tf_op jit(solution)/shard_map/ppermute | solution.py:18
  130.3 24.2 %collective-permute-start.7 = (bf16[4,4,48,896]{3,2,1,0:T(8,128)(2,1)}, bf16[4,4,48,896]{3,2,1,0:T(8,128)(2,1)}, u32[]{:S(2)}, u32[]{:S(2)}) collective-permute-start(bf16[4,4,48,896]{3,2,1,0:T(8,128)(2,1)} %pad_maximum_fusion.own_ref), channel_id=1, source_target_pairs={{0,4},{4,0},{1,5},{5,1},{2,6},{6,2},{3,7},{7,3},{8,12},{12,8},{9,1... | collective-permute-start | bytes 4128776 | tf_op jit(solution)/shard_map/ppermute | solution.py:27

commit v11 on v9

--- a/solution.py
+++ b/solution.py
@@ -8,8 +8,8 @@
 FF = 1536
 BF = jnp.bfloat16
 F32 = jnp.float32
-ROWS_OF = ("x", "zb")
 HOME = ("x", "zb", "zi")
+ANYWHERE = pl.BlockSpec(memory_space=pl.ANY)
 NT = (((1,), (1,)), ((), ()))
 
 
@@ -22,56 +22,70 @@
     return lax.ppermute(array, "c", [(0, 1), (1, 0)])
 
 
-def pack_kernel(ids_ref, tokens_ref, *refs):
-    out_ref = refs[-1]
-    batches, picks, rows = ids_ref.shape
-    experts, slots, width = out_ref.shape
-    capacity = slots // batches
+def pack_kernel(block_ref, _, *refs):
+    rows_refs, out_ref = refs[:-1], refs[-1]
+    experts, blocks, slots, width = out_ref.shape
+    capacity = 2
+    rows = rows_refs[0].shape[0]
+    per_batch = rows * capacity // slots
     count = experts * slots
-    expert = lax.broadcasted_iota(jnp.int32, (experts, rows), 0)
-    row = lax.broadcasted_iota(jnp.int32, (rows, rows), 0)
-    earlier = (row < lax.broadcasted_iota(jnp.int32, (rows, rows), 1)).astype(F32)
-    owner = lax.broadcasted_iota(jnp.int32, (count, experts), 0) // slots
-    spread = (owner == lax.broadcasted_iota(jnp.int32, (count, experts), 1)).astype(F32)
-    slot = lax.broadcasted_iota(jnp.int32, (count, rows), 0) % slots
-    total = jnp.zeros((count, width), F32)
-    for m in range(batches):
-        ids = ids_ref[m]
-        named = jnp.zeros((experts, rows), jnp.bool_)
-        for k in range(picks):
-            named = named | (ids[k : k + 1] == expert)
-        named = named.astype(F32)
-        before = jnp.dot(named, earlier, preferred_element_type=F32)
-        named = jnp.dot(spread, named, preferred_element_type=F32)
-        before = jnp.dot(spread, before, preferred_element_type=F32)
-        here = (slot // capacity == m) & (before == (slot % capacity).astype(F32))
-        pick = ((named > 0.5) & here).astype(BF)
-        total += jnp.dot(pick, tokens_ref[m], preferred_element_type=F32)
-    out_ref[...] = total.astype(BF).reshape(out_ref.shape)
+    own = block_ref[0]
+
+    def grid(shape, axis):
+        return lax.broadcasted_iota(jnp.int32, shape, axis)
+
+    row, other = grid((rows, rows), 0), grid((rows, rows), 1)
+    earlier = ((other < row) & (other // per_batch == row // per_batch)).astype(F32)
+    at, slot = grid((rows, count), 0), grid((rows, count), 1)
+    expert = ((slot // slots) * blocks + own).astype(F32)
+    of_batch = slot % slots // capacity == at // per_batch
+    nth = (slot % capacity).astype(F32)
+    for k, ref in enumerate(rows_refs):
+        ids = ref[:, width:].astype(F32)
+        hit = ((ids[:, 0:1] == expert) | (ids[:, 1:2] == expert)).astype(F32)
+        before = jnp.dot(earlier, hit, preferred_element_type=F32)
+        pick = jnp.where(of_batch & (before == nth), hit, 0.0).T.astype(BF)
+        packed = jnp.dot(pick, ref[:, :width], preferred_element_type=F32)
+        out_ref[:, (own + blocks - k) % blocks] = packed.astype(BF).reshape(experts, slots, width)
 
 
 def whole(count):
     return [pl.BlockSpec(memory_space=pltpu.VMEM)] * count
 
 
-def packed_of(expert_ids, tokens, experts, slots, earlier):
+def packed_of(block, earlier, rows, experts, slots, width):
     return pl.pallas_call(
         pack_kernel,
-        in_specs=whole(2) + [pl.BlockSpec(memory_space=pl.ANY)] * len(earlier),
+        in_specs=[pl.BlockSpec(memory_space=pltpu.SMEM), ANYWHERE] + whole(len(rows)),
         out_specs=whole(1)[0],
-        out_shape=jax.ShapeDtypeStruct((experts, slots, tokens.shape[2]), BF),
+        out_shape=jax.ShapeDtypeStruct((experts, len(rows), slots, width), BF),
         compiler_params=pltpu.CompilerParams(vmem_limit_bytes=16 << 20),
-    )(expert_ids.transpose(0, 2, 1), tokens, *earlier)
+    )(block, earlier, *rows)
+
+
+def stack_kernel(_, *refs):
+    for k, ref in enumerate(refs[:-1]):
+        refs[-1][k] = ref[...]
+
+
+def stack_after(earlier, arrays):
+    return pl.pallas_call(
+        stack_kernel,
+        in_specs=[ANYWHERE] + whole(len(arrays)),
+        out_specs=whole(1)[0],
+        out_shape=jax.ShapeDtypeStruct((len(arrays),) + arrays[0].shape, arrays[0].dtype),
+        compiler_params=pltpu.CompilerParams(vmem_limit_bytes=16 << 20),
+    )(earlier, *arrays)
 
 
 def up_kernel(first_ref, second_ref, own_ref, other_ref, out_ref):
-    units = own_ref.shape[0] // 2
+    units = own_ref.shape[0] // 3
     width = own_ref.shape[1]
     rows = [ref[...].reshape(-1, width) for ref in (first_ref, second_ref)]
     rows = jnp.concatenate(rows, axis=0)
     hidden = []
     for ref in (own_ref, other_ref):
-        both = lax.dot_general(ref[...], rows, NT, preferred_element_type=F32)
+        both = lax.dot_general(ref[: 2 * units], rows, NT, preferred_element_type=F32)
         gate = both[:units]
         hidden.append(gate / (1.0 + jnp.exp(-gate)) * both[units:])
     out_ref[...] = jnp.concatenate(hidden, axis=0).T.astype(BF)
@@ -79,12 +93,13 @@
 
 def hidden_of(first, second, own, other):
     count = 2 * first.shape[0] * first.shape[1]
+    both = own.shape[0] // 3 * 2
     return pl.pallas_call(
         up_kernel,
         grid=(1,),
-        in_specs=whole(3) + [pl.BlockSpec(own.shape, lambda i: (0, 0))],
+        in_specs=whole(3) + [pl.BlockSpec((both, own.shape[1]), lambda i: (0, 0))],
         out_specs=whole(1)[0],
-        out_shape=jax.ShapeDtypeStruct((count, own.shape[0]), BF),
+        out_shape=jax.ShapeDtypeStruct((count, both), BF),
         compiler_params=pltpu.CompilerParams(vmem_limit_bytes=24 << 20),
     )(first, second, own, other)
 
@@ -129,8 +144,6 @@
     pieces = lax.all_to_all(down.transpose(1, 0, 2), "zi", split_axis=0, concat_axis=0, tiled=True)
     shares = [pieces] + [exchange(pieces, "dp", k) for k in range(1, lax.axis_size("dp"))]
     other = swap(turned)
-    mark = pieces[0, 0, 0]
-    up = jnp.where(mark == mark, turned[: 2 * units], jnp.zeros((), BF))
 
     matches = (expert_ids[..., None] == jnp.arange(experts, dtype=jnp.int32)).astype(jnp.int32)
     present = jnp.sum(matches, axis=2)
@@ -142,14 +155,23 @@
         & (occurrence[..., None, None] == slot)
     ).astype(F32)
     weighting = jnp.sum(landing * gate_scores[..., None, None], axis=2)
-    packed = packed_of(expert_ids, tokens, experts, slots, [pieces])
-    arrived = lax.all_to_all(packed, ROWS_OF, split_axis=0, concat_axis=0, tiled=True)
+    blocks = lax.axis_size("zb")
+    named = jnp.pad(expert_ids.reshape(-1, 2).astype(BF), ((0, 0), (0, 126)))
+    sent = jnp.concatenate([tokens.reshape(-1, width), named], axis=1)
+    rows = [sent] + [
+        lax.ppermute(sent, "zb", [(i, (i + k) % blocks) for i in range(blocks)])
+        for k in range(1, blocks)
+    ]
+    block = lax.axis_index("zb").astype(jnp.int32).reshape(1)
+    packed = packed_of(block, pieces, rows, experts // blocks, slots, width)
+    arrived = lax.all_to_all(packed, "x", split_axis=0, concat_axis=0, tiled=True)
+    arrived = arrived.reshape(experts, slots, width)
     half = experts // 2
     first = lax.all_gather(arrived[:half], "zi", axis=0, tiled=True)
     second = lax.all_gather(arrived[half:], "zi", axis=0, tiled=True)
-    shares = jnp.stack(shares)
+    shares = stack_after(second, shares)
     other_shares = swap(shares)
-    hidden = hidden_of(first, second, up, other)
+    hidden = hidden_of(first, second, turned, other)
     gathered = lax.all_gather(hidden, "zi", axis=0)
     position = lax.axis_index("dp").astype(jnp.int32).reshape(1)
     done = outputs_of(position, gathered, shares, other_shares, experts, slots)

time: 170 us -> 175 us (1.029)
  starting transfers between devices: 50.3 us -> 61.2 us
  waiting for transfers between devices: 43.4 us -> 40.9 us
  blocking collectives: 56.8 us -> 58.9 us
    ppermute x0 -> x3, starting transfers between devices: none -> 23 us  [on_device(): lax.ppermute(sent, 'zb', [(i, (i + k) % blocks) for i in range(blocks)])]
    ppermute x0 -> x3, waiting for transfers between devices: none -> 16.2 us  [on_device(): lax.ppermute(sent, 'zb', [(i, (i + k) % blocks) for i in range(blocks)])]
    all_to_all x1, starting transfers between devices: 15.5 us -> 4.29 us  [on_device(): lax.all_to_all(packed, 'x', split_axis=0, concat_axis=0, tiled=True)]
    ppermute x3, waiting for transfers between devices: 8.77 us -> 0.01 us  [exchange(): return lax.ppermute(array, axis, [(i, i ^ step) for i in range(size)])]
    all_to_all x1, waiting for transfers between devices: 8.73 us -> 0.01 us  [on_device(): lax.all_to_all(down.transpose(1, 0, 2), 'zi', split_axis=0, concat_axis=0...]
    select_n x1 -> x0, other arithmetic: 1.96 us -> none  [on_device(): up = jnp.where(mark == mark, turned[:2 * units], jnp.zeros((), BF))]
    pallas_call x1, Pallas kernels: 3.73 us -> 1.96 us  [outputs_of(): pl.pallas_call(down_kernel, in_specs=[pl.BlockSpec(memory_space=pltpu.SME...]
    pallas_call x2 -> x3, Pallas kernels: 4.9 us -> 5.49 us  [the longest x1 3.5 us: hidden_of(): pl.pallas_call(up_kernel, grid=(1,), in_specs=whole(3) + [pl.BlockSpec((b...]
  transfers between devices with their start and end apart: 8 -> 11, of which waited for: 5 -> 3; matrix products, arithmetic and copies ran while one was open for 3% -> 2% of each run, Pallas kernels for 3% -> 3%
where the time goes in v11:
time: 175 us; the launch traced here: 174 us
  starting transfers between devices  61.2 us (35%)
  blocking collectives  58.9 us (34%)
  waiting for transfers between devices  40.9 us (23%)
  Pallas kernels  7.44 us (4%)
  local copies, waits for them, and re-layouts  2.22 us (1%)
  other arithmetic  2.08 us (1%)
    all_to_all x1, waiting for transfers between devices, on_device(): lax.all_to_all(done, HOME, split_axis=0, concat_axis=0, tiled=True)  24.7 us
    ppermute x3, starting transfers between devices, on_device(): lax.ppermute(sent, 'zb', [(i, (i + k) % blocks) for i in range(blocks)])  23 us
    all_gather x1, blocking collectives, on_device(): first = lax.all_gather(arrived[:half], 'zi', axis=0, tiled=True)  20 us
    all_gather x1, blocking collectives, on_device(): second = lax.all_gather(arrived[half:], 'zi', axis=0, tiled=True)  20 us
    all_gather x1, blocking collectives, on_device(): gathered = lax.all_gather(hidden, 'zi', axis=0)  19 us
    ppermute x3, waiting for transfers between devices, on_device(): lax.ppermute(sent, 'zb', [(i, (i + k) % blocks) for i in range(blocks)])  16.2 us
    all_to_all x1, starting transfers between devices, on_device(): lax.all_to_all(done, HOME, split_axis=0, concat_axis=0, tiled=True)  13.8 us
    ppermute x3, starting transfers between devices, exchange(): return lax.ppermute(array, axis, [(i, i ^ step) for i in range(size)])  10.4 us
  transfers between devices with their start and end apart: 11, of which 3 were waited for; matrix products, arithmetic and copies ran while one was open for 2% of the time, Pallas kernels for 3%

profile of v11, /device:TPU:24, one launch (start us, length us, event | category | flops | bytes accessed | tf_op | source)
XLA Modules:
  0.0 174.1 jit_solution(628607731057034237)
XLA Ops:
  0.0 1.9 %collective-permute-start.3 = (bf16[576,3584]{1,0:T(8,128)(2,1)}, bf16[576,3584]{1,0:T(8,128)(2,1)}, u32[]{:S(2)}, u32[]{:S(2)}) collective-permute-start(bf16[576,3584]{1,0:T(8,128)(2,1)} %bitcast.32), channel_id=1, source_target_pairs={{0,4},{4,0},{1,5},{5,1},{2,6},{6,2},{3,7},{7,3},{8,12},{12,8},{9,1... | collective-permute-start | bytes 12386312 | tf_op jit(solution)/shard_map/ppermute | solution.py:22
  1.9 1.0 constant_dynamic-slice_fusion
  2.9 0.8 copy.38
  3.7 5.9 %all-to-all-start = ((bf16[4,48,896]{2,1,0:T(8,128)(2,1)}), bf16[4,48,896]{2,1,0:T(8,128)(2,1)S(1)}, u32[]{:S(2)}, u32[]{:S(2)}) async-start(bf16[4,48,896]{2,1,0:T(8,128)(2,1)} %bitcast.31), calls=%async_computation | async-start | bytes 688128 | tf_op jit(solution)/shard_map/all_to_all | solution.py:144
  9.6 0.7 convert_element_type.17
  10.3 0.1 copy.30
  10.4 0.9 fusion.3.refs_0_
  11.3 9.1 %collective-permute-start = (bf16[16,3712]{1,0:T(8,128)(2,1)S(1)}, bf16[16,3712]{1,0:T(8,128)(2,1)S(1)}, u32[]{:S(2)}, u32[]{:S(2)}) collective-permute-start(bf16[16,3712]{1,0:T(8,128)(2,1)S(1)} %fusion.3.refs_0_), channel_id=1, source_target_pairs={{0,32},{32,64},{64,96},{96,0},{1,33},{33,65},{65,97},{97,1},{2,34}... | collective-permute-start | bytes 356360 | tf_op jit(solution)/shard_map/ppermute | solution.py:162
  20.4 8.5 %collective-permute-start.1 = (bf16[16,3712]{1,0:T(8,128)(2,1)S(1)}, bf16[16,3712]{1,0:T(8,128)(2,1)S(1)}, u32[]{:S(2)}, u32[]{:S(2)}) collective-permute-start(bf16[16,3712]{1,0:T(8,128)(2,1)S(1)} %fusion.3.refs_0_), channel_id=1, source_target_pairs={{0,64},{32,96},{64,0},{96,32},{1,65},{33,97},{65,1},{97,33},{2,66}... | collective-permute-start | bytes 356360 | tf_op jit(solution)/shard_map/ppermute | solution.py:162
  28.9 5.5 %collective-permute-start.2 = (bf16[16,3712]{1,0:T(8,128)(2,1)S(1)}, bf16[16,3712]{1,0:T(8,128)(2,1)S(1)}, u32[]{:S(2)}, u32[]{:S(2)}) collective-permute-start(bf16[16,3712]{1,0:T(8,128)(2,1)S(1)} %fusion.3.refs_0_), channel_id=1, source_target_pairs={{0,96},{32,0},{64,32},{96,64},{1,97},{33,1},{65,33},{97,65},{2,98}... | collective-permute-start | bytes 356360 | tf_op jit(solution)/shard_map/ppermute | solution.py:162
  34.4 0.0 collective-permute-done.refs_1_
  34.4 9.6 %collective-permute-done.1.refs_2_ = bf16[16,3712]{1,0:T(8,128)(2,1)S(1)} collective-permute-done((bf16[16,3712]{1,0:T(8,128)(2,1)S(1)}, bf16[16,3712]{1,0:T(8,128)(2,1)S(1)}, u32[]{:S(2)}, u32[]{:S(2)}) %collective-permute-start.1) | collective-permute-done | bytes 118816 | tf_op jit(solution)/shard_map/ppermute | solution.py:162
  43.9 6.6 %collective-permute-done.2.refs_3_ = bf16[16,3712]{1,0:T(8,128)(2,1)S(1)} collective-permute-done((bf16[16,3712]{1,0:T(8,128)(2,1)S(1)}, bf16[16,3712]{1,0:T(8,128)(2,1)S(1)}, u32[]{:S(2)}, u32[]{:S(2)}) %collective-permute-start.2) | collective-permute-done | bytes 118816 | tf_op jit(solution)/shard_map/ppermute | solution.py:162
  50.5 0.0 all-to-all-done._.refs_0_
  50.5 1.9 %shard_map.46 = bf16[4,4,4,3584]{3,2,1,0:T(4,128)(2,1)} custom-call(s32[1]{0:T(128)} %bitcast.3.block_ref, bf16[4,48,896]{2,1,0:T(8,128)(2,1)S(1)} %all-to-all-done._.refs_0_, bf16[16,3712]{1,0:T(8,128)(2,1)S(1)} %fusion.3.refs_0_, bf16[16,3712]{1,0:T(8,128)(2,1)S(1)} %collective-permute-done.refs_1_, bf16[16,3712]{1,0:T(8,128)(2,1)S(1)} %collective-permute-done.1.refs_2_, ...), custom_call_target="tpu_custom_call" | custom-call | tf_op jit(solution)/shard_map/pallas_call | solution.py:57
  52.4 4.3 %all-to-all-start.1 = ((bf16[4,4,4,3584]{3,2,1,0:T(4,128)(2,1)}), bf16[4,4,4,3584]{3,2,1,0:T(4,128)(2,1)S(1)}, u32[]{:S(2)}, u32[]{:S(2)}) async-start(bf16[4,4,4,3584]{3,2,1,0:T(4,128)(2,1)} %shard_map.46), calls=%async_computation.1 | async-start | bytes 917504 | tf_op jit(solution)/shard_map/all_to_all | solution.py:167
  56.7 2.6 %collective-permute-start.4 = (bf16[4,48,896]{2,1,0:T(8,128)(2,1)S(1)}, bf16[4,48,896]{2,1,0:T(8,128)(2,1)S(1)}, u32[]{:S(2)}, u32[]{:S(2)}) collective-permute-start(bf16[4,48,896]{2,1,0:T(8,128)(2,1)S(1)} %all-to-all-done._.refs_0_), channel_id=1, source_target_pairs={{0,1},{1,0},{2,3},{3,2},{4,5},{5,4},{6,7},{7,6},{8,9},{9,8},{10,11... | collective-permute-start | bytes 1032200 | tf_op jit(solution)/shard_map/ppermute | solution.py:18
  59.4 2.8 %collective-permute-start.5 = (bf16[4,48,896]{2,1,0:T(8,128)(2,1)S(1)}, bf16[4,48,896]{2,1,0:T(8,128)(2,1)S(1)}, u32[]{:S(2)}, u32[]{:S(2)}) collective-permute-start(bf16[4,48,896]{2,1,0:T(8,128)(2,1)S(1)} %all-to-all-done._.refs_0_), channel_id=1, source_target_pairs={{0,2},{1,3},{2,0},{3,1},{4,6},{5,7},{6,4},{7,5},{8,10},{9,11},{10,... | collective-permute-start | bytes 1032200 | tf_op jit(solution)/shard_map/ppermute | solution.py:18
  62.2 4.9 %collective-permute-start.6 = (bf16[4,48,896]{2,1,0:T(8,128)(2,1)S(1)}, bf16[4,48,896]{2,1,0:T(8,128)(2,1)S(1)}, u32[]{:S(2)}, u32[]{:S(2)}) collective-permute-start(bf16[4,48,896]{2,1,0:T(8,128)(2,1)S(1)} %all-to-all-done._.refs_0_), channel_id=1, source_target_pairs={{0,3},{1,2},{2,1},{3,0},{4,7},{5,6},{6,5},{7,4},{8,11},{9,10},{10,... | collective-permute-start | bytes 1032200 | tf_op jit(solution)/shard_map/ppermute | solution.py:18
  67.1 0.0 all-to-all-done.1
  67.2 0.0 copy-start
  67.2 0.2 fusion.5
  67.3 20.0 %all_gather.13.second_ref._ = bf16[32,4,3584]{2,1,0:T(4,128)(2,1)S(1)} all-gather(bf16[8,4,3584]{2,1,0:T(4,128)(2,1)S(1)} %bitcast.37), channel_id=1, replica_groups=mesh['x'=4,'zb'=4,'zi'=4,'c'=2,'dp'=4] {'zi'}, dimensions={0}, use_global_device_ids=true | all-gather | bytes 1146880 | tf_op jit(solution)/shard_map/all_gather | solution.py:171
  87.3 0.0 collective-permute-done.4.refs_1_
  87.3 0.0 collective-permute-done.5.refs_2_
  87.3 0.0 collective-permute-done.6.refs_3_
  87.3 0.1 shard_map.48.own_ref
  87.4 1.9 %collective-permute-start.7 = (bf16[4,4,48,896]{3,2,1,0:T(8,128)(2,1)S(1)}, bf16[4,4,48,896]{3,2,1,0:T(8,128)(2,1)S(1)}, u32[]{:S(2)}, u32[]{:S(2)}) collective-permute-start(bf16[4,4,48,896]{3,2,1,0:T(8,128)(2,1)S(1)} %shard_map.48.own_ref), channel_id=1, source_target_pairs={{0,4},{4,0},{1,5},{5,1},{2,6},{6,2},{3,7},{7,3},{8,12},{12,8},{9,1... | collective-permute-start | bytes 4128776 | tf_op jit(solution)/shard_map/ppermute | solution.py:22
  89.4 20.0 %all_gather.12.first_ref = bf16[32,4,3584]{2,1,0:T(4,128)(2,1)S(1)} all-gather(bf16[8,4,3584]{2,1,0:T(4,128)(2,1)S(1)} %bitcast.36), channel_id=1, replica_groups=mesh['x'=4,'zb'=4,'zi'=4,'c'=2,'dp'=4] {'zi'}, dimensions={0}, use_global_device_ids=true | all-gather | bytes 1146880 | tf_op jit(solution)/shard_map/all_gather | solution.py:170
  109.4 0.0 collective-permute-done.3.other_ref
  109.4 0.0 copy-done
  109.4 3.5 %shard_map.47 = bf16[256,384]{1,0:T(8,128)(2,1)S(1)} custom-call(bf16[32,4,3584]{2,1,0:T(4,128)(2,1)S(1)} %all_gather.12.first_ref, bf16[32,4,3584]{2,1,0:T(4,128)(2,1)S(1)} %all_gather.13.second_ref._, bf16[576,3584]{1,0:T(8,128)(2,1)S(1)} %bitcast.33, bf16[576,3584]{1,0:T(8,128)(2,1)} %collective-permute-done.3.other_ref), custom_call_target="tpu_custom_call" | custom-call | tf_op jit(solution)/shard_map/pallas_call | solution.py:97
  112.9 0.0 copy-start.1
  112.9 0.0 copy-start.2
  112.9 19.0 %all-gather = bf16[1024,384]{1,0:T(8,128)(2,1)S(1)} all-gather(bf16[256,384]{1,0:T(8,128)(2,1)S(1)} %shard_map.47), channel_id=2, replica_groups=mesh['x'=4,'zb'=4,'zi'=4,'c'=2,'dp'=4] {'zi'}, dimensions={0}, use_global_device_ids=true | all-gather | bytes 983040 | tf_op jit(solution)/shard_map/all_gather | solution.py:175
  131.9 0.0 collective-permute-done.7.other_ref
  131.9 2.0 %shard_map.49 = bf16[16,4,4,896]{3,2,1,0:T(4,128)(2,1)} custom-call(s32[1]{0:T(128)} %bitcast.2.place_ref, bf16[4,256,384]{2,1,0:T(8,128)(2,1)S(1)} %bitcast.34, bf16[4,4,48,896]{3,2,1,0:T(8,128)(2,1)S(1)} %shard_map.48.own_ref, bf16[4,4,48,896]{3,2,1,0:T(8,128)(2,1)S(1)} %collective-permute-done.7.other_ref), custom_call_target="tpu_custom_call" | custom-call | tf_op jit(solution)/shard_map/pallas_call | solution.py:122
  133.8 13.8 %all-to-all-start.2 = ((bf16[64,4,896]{2,1,0:T(4,128)(2,1)}), bf16[64,4,896]{2,1,0:T(4,128)(2,1)S(1)}, u32[]{:S(2)}, u32[]{:S(2)}) async-start(bf16[64,4,896]{2,1,0:T(4,128)(2,1)} %bitcast.15), calls=%async_computation.2 | async-start | bytes 917504 | tf_op jit(solution)/shard_map/all_to_all | solution.py:179
  147.6 0.0 copy-done.1
  147.6 0.1 convert_reduce_fusion
  147.7 0.2 select_reduce_fusion.1
  148.0 0.1 iota_compare_fusion.1
  148.0 0.0 copy-done.2
  148.0 0.1 select_reduce_fusion
  148.1 24.7 %all-to-all-done.2 = bf16[64,4,896]{2,1,0:T(4,128)(2,1)S(1)} async-done(((bf16[64,4,896]{2,1,0:T(4,128)(2,1)}), bf16[64,4,896]{2,1,0:T(4,128)(2,1)S(1)}, u32[]{:S(2)}, u32[]{:S(2)}) %all-to-all-start.2) | async-done | bytes 458784 | tf_op jit(solution)/shard_map/all_to_all | solution.py:179
  172.9 0.2 reshape.67
  173.0 1.0 fusion
  (3 shorter events, 0.0 us)
Async XLA Ops:
  0.0 109.4 %collective-permute-start.3 = (bf16[576,3584]{1,0:T(8,128)(2,1)}, bf16[576,3584]{1,0:T(8,128)(2,1)}, u32[]{:S(2)}, u32[]{:S(2)}) collective-permute-start(bf16[576,3584]{1,0:T(8,128)(2,1)} %bitcast.32), channel_id=1, source_target_pairs={{0,4},{4,0},{1,5},{5,1},{2,6},{6,2},{3,7},{7,3},{8,12},{12,8},{9,1... | collective-permute-start | bytes 12386312 | tf_op jit(solution)/shard_map/ppermute | solution.py:22
  3.7 46.8 %all-to-all-start = ((bf16[4,48,896]{2,1,0:T(8,128)(2,1)}), bf16[4,48,896]{2,1,0:T(8,128)(2,1)S(1)}, u32[]{:S(2)}, u32[]{:S(2)}) async-start(bf16[4,48,896]{2,1,0:T(8,128)(2,1)} %bitcast.31), calls=%async_computation | async-start | bytes 688128 | tf_op jit(solution)/shard_map/all_to_all | solution.py:144
  11.3 23.1 %collective-permute-start = (bf16[16,3712]{1,0:T(8,128)(2,1)S(1)}, bf16[16,3712]{1,0:T(8,128)(2,1)S(1)}, u32[]{:S(2)}, u32[]{:S(2)}) collective-permute-start(bf16[16,3712]{1,0:T(8,128)(2,1)S(1)} %fusion.3.refs_0_), channel_id=1, source_target_pairs={{0,32},{32,64},{64,96},{96,0},{1,33},{33,65},{65,97},{97,1},{2,34}... | collective-permute-start | bytes 356360 | tf_op jit(solution)/shard_map/ppermute | solution.py:162
  20.4 23.5 %collective-permute-start.1 = (bf16[16,3712]{1,0:T(8,128)(2,1)S(1)}, bf16[16,3712]{1,0:T(8,128)(2,1)S(1)}, u32[]{:S(2)}, u32[]{:S(2)}) collective-permute-start(bf16[16,3712]{1,0:T(8,128)(2,1)S(1)} %fusion.3.refs_0_), channel_id=1, source_target_pairs={{0,64},{32,96},{64,0},{96,32},{1,65},{33,97},{65,1},{97,33},{2,66}... | collective-permute-start | bytes 356360 | tf_op jit(solution)/shard_map/ppermute | solution.py:162
  28.9 21.6 %collective-permute-start.2 = (bf16[16,3712]{1,0:T(8,128)(2,1)S(1)}, bf16[16,3712]{1,0:T(8,128)(2,1)S(1)}, u32[]{:S(2)}, u32[]{:S(2)}) collective-permute-start(bf16[16,3712]{1,0:T(8,128)(2,1)S(1)} %fusion.3.refs_0_), channel_id=1, source_target_pairs={{0,96},{32,0},{64,32},{96,64},{1,97},{33,1},{65,33},{97,65},{2,98}... | collective-permute-start | bytes 356360 | tf_op jit(solution)/shard_map/ppermute | solution.py:162
  52.4 14.7 %all-to-all-start.1 = ((bf16[4,4,4,3584]{3,2,1,0:T(4,128)(2,1)}), bf16[4,4,4,3584]{3,2,1,0:T(4,128)(2,1)S(1)}, u32[]{:S(2)}, u32[]{:S(2)}) async-start(bf16[4,4,4,3584]{3,2,1,0:T(4,128)(2,1)} %shard_map.46), calls=%async_computation.1 | async-start | bytes 917504 | tf_op jit(solution)/shard_map/all_to_all | solution.py:167
  56.7 30.6 %collective-permute-start.4 = (bf16[4,48,896]{2,1,0:T(8,128)(2,1)S(1)}, bf16[4,48,896]{2,1,0:T(8,128)(2,1)S(1)}, u32[]{:S(2)}, u32[]{:S(2)}) collective-permute-start(bf16[4,48,896]{2,1,0:T(8,128)(2,1)S(1)} %all-to-all-done._.refs_0_), channel_id=1, source_target_pairs={{0,1},{1,0},{2,3},{3,2},{4,5},{5,4},{6,7},{7,6},{8,9},{9,8},{10,11... | collective-permute-start | bytes 1032200 | tf_op jit(solution)/shard_map/ppermute | solution.py:18
  59.4 28.0 %collective-permute-start.5 = (bf16[4,48,896]{2,1,0:T(8,128)(2,1)S(1)}, bf16[4,48,896]{2,1,0:T(8,128)(2,1)S(1)}, u32[]{:S(2)}, u32[]{:S(2)}) collective-permute-start(bf16[4,48,896]{2,1,0:T(8,128)(2,1)S(1)} %all-to-all-done._.refs_0_), channel_id=1, source_target_pairs={{0,2},{1,3},{2,0},{3,1},{4,6},{5,7},{6,4},{7,5},{8,10},{9,11},{10,... | collective-permute-start | bytes 1032200 | tf_op jit(solution)/shard_map/ppermute | solution.py:18
  62.2 25.1 %collective-permute-start.6 = (bf16[4,48,896]{2,1,0:T(8,128)(2,1)S(1)}, bf16[4,48,896]{2,1,0:T(8,128)(2,1)S(1)}, u32[]{:S(2)}, u32[]{:S(2)}) collective-permute-start(bf16[4,48,896]{2,1,0:T(8,128)(2,1)S(1)} %all-to-all-done._.refs_0_), channel_id=1, source_target_pairs={{0,3},{1,2},{2,1},{3,0},{4,7},{5,6},{6,5},{7,4},{8,11},{9,10},{10,... | collective-permute-start | bytes 1032200 | tf_op jit(solution)/shard_map/ppermute | solution.py:18
  67.2 42.2 %copy-start = (bf16[1,3584,576]{1,2,0:T(8,128)(2,1)S(1)}, bf16[1,3584,576]{1,2,0:T(8,128)(2,1)}, u32[]{:S(2)}) copy-start(bf16[1,3584,576]{1,2,0:T(8,128)(2,1)} %param.7) | copy-start | bytes 12386308
  87.4 44.4 %collective-permute-start.7 = (bf16[4,4,48,896]{3,2,1,0:T(8,128)(2,1)S(1)}, bf16[4,4,48,896]{3,2,1,0:T(8,128)(2,1)S(1)}, u32[]{:S(2)}, u32[]{:S(2)}) collective-permute-start(bf16[4,4,48,896]{3,2,1,0:T(8,128)(2,1)S(1)} %shard_map.48.own_ref), channel_id=1, source_target_pairs={{0,4},{4,0},{1,5},{5,1},{2,6},{6,2},{3,7},{7,3},{8,12},{12,8},{9,1... | collective-permute-start | bytes 4128776 | tf_op jit(solution)/shard_map/ppermute | solution.py:22
  112.9 34.7 %copy-start.1 = (s32[2,8,2]{1,2,0:T(2,128)S(1)}, s32[2,8,2]{1,2,0:T(2,128)}, u32[]{:S(2)}) copy-start(s32[2,8,2]{1,2,0:T(2,128)} %param.5) | copy-start | bytes 388
  112.9 35.1 %copy-start.2 = (f32[2,8,2]{1,2,0:T(2,128)S(1)}, f32[2,8,2]{1,2,0:T(2,128)}, u32[]{:S(2)}) copy-start(f32[2,8,2]{1,2,0:T(2,128)} %param.6) | copy-start | bytes 388
  133.8 39.0 %all-to-all-start.2 = ((bf16[64,4,896]{2,1,0:T(4,128)(2,1)}), bf16[64,4,896]{2,1,0:T(4,128)(2,1)S(1)}, u32[]{:S(2)}, u32[]{:S(2)}) async-start(bf16[64,4,896]{2,1,0:T(4,128)(2,1)} %bitcast.15), calls=%async_computation.2 | async-start | bytes 917504 | tf_op jit(solution)/shard_map/all_to_all | solution.py:179

commit v12 on v7

--- a/solution.py
+++ b/solution.py
@@ -10,6 +10,7 @@
 F32 = jnp.float32
 ROWS_OF = ("x", "zb")
 HOME = ("x", "zb", "zi")
+ANYWHERE = pl.BlockSpec(memory_space=pl.ANY)
 NT = (((1,), (1,)), ((), ()))
 
 
@@ -64,15 +65,49 @@
         in_specs=whole(2),
         out_specs=whole(1)[0],
         out_shape=jax.ShapeDtypeStruct((experts, slots, tokens.shape[2]), BF),
-        compiler_params=pltpu.CompilerParams(vmem_limit_bytes=32 << 20),
+        compiler_params=pltpu.CompilerParams(vmem_limit_bytes=16 << 20),
     )(expert_ids.transpose(0, 2, 1), tokens)
 
 
-def up_kernel(rows_ref, own_ref, other_ref, out_ref):
+def repeat_kernel(rows_ref, *refs):
+    for k in range(refs[-1].shape[0]):
+        refs[-1][k] = rows_ref[...]
+
+
+def repeat_after(earlier, rows, times):
+    return pl.pallas_call(
+        repeat_kernel,
+        in_specs=whole(1) + [ANYWHERE] * len(earlier),
+        out_specs=whole(1)[0],
+        out_shape=jax.ShapeDtypeStruct((times,) + rows.shape, rows.dtype),
+        compiler_params=pltpu.CompilerParams(vmem_limit_bytes=16 << 20),
+    )(rows, *earlier)
+
+
+def stack_kernel(_, *refs):
+    for k, ref in enumerate(refs[:-1]):
+        refs[-1][k] = ref[...]
+
+
+def stack_after(earlier, arrays):
+    return pl.pallas_call(
+        stack_kernel,
+        in_specs=[ANYWHERE] + whole(len(arrays)),
+        out_specs=whole(1)[0],
+        out_shape=jax.ShapeDtypeStruct((len(arrays),) + arrays[0].shape, arrays[0].dtype),
+        compiler_params=pltpu.CompilerParams(vmem_limit_bytes=16 << 20),
+    )(earlier, *arrays)
+
+
+def up_kernel(rows_ref, own_ref, other_ref, out_ref, held_ref, arrival):
     units = own_ref.shape[0] // 2
+    copy = pltpu.make_async_copy(other_ref.at[pl.ds(0, 2 * units)], held_ref, arrival)
+    copy.start()
     rows = rows_ref[...].reshape(-1, own_ref.shape[1])
     hidden = []
-    for ref in (own_ref, other_ref):
+    for ref in (own_ref, held_ref):
+        if ref is held_ref:
+            copy.wait()
         both = lax.dot_general(ref[...], rows, NT, preferred_element_type=F32)
         gate = both[:units]
         hidden.append(gate / (1.0 + jnp.exp(-gate)) * both[units:])
@@ -83,20 +118,30 @@
     count = rows.shape[0] * rows.shape[1]
     return pl.pallas_call(
         up_kernel,
-        in_specs=whole(3),
+        in_specs=whole(2) + [ANYWHERE],
         out_specs=whole(1)[0],
         out_shape=jax.ShapeDtypeStruct((count, own.shape[0]), BF),
+        scratch_shapes=[pltpu.VMEM(own.shape, BF), pltpu.SemaphoreType.DMA(())],
         compiler_params=pltpu.CompilerParams(vmem_limit_bytes=48 << 20),
     )(rows, own, other)
 
 
-def down_kernel(place_ref, hidden_ref, own_ref, other_ref, out_ref):
-    shares, line = own_ref.shape[:2]
-    experts, _, slots, columns = out_ref.shape
+def down_kernel(place_ref, hidden_ref, own_ref, other_ref, out_ref, held_ref, arrivals):
+    shares, line, share, columns = own_ref.shape
+    experts, _, slots, _ = out_ref.shape
+    copies = []
+    for at in range(line):
+        for i, ref in enumerate((own_ref, other_ref)):
+            source = ref.at[:, place_ref[0] ^ at]
+            copies.append(pltpu.make_async_copy(source, held_ref.at[at, i], arrivals.at[at, i]))
+    for copy in copies:
+        copy.start()
     total = jnp.zeros((line * experts * slots, columns), F32)
     for at in range(line):
-        k = place_ref[0] ^ at
-        weights = [ref[place_ref[1] ^ y, k] for ref in (own_ref, other_ref) for y in range(shares)]
+        weights = []
+        for i in range(2):
+            copies[2 * at + i].wait()
+            weights += [held_ref[at, i, place_ref[1] ^ y] for y in range(shares)]
         weights = jnp.concatenate(weights, axis=0)
         total += jnp.dot(hidden_ref[at], weights, preferred_element_type=F32)
     total = total.astype(BF).reshape(line, experts, slots, columns)
@@ -105,12 +150,17 @@
 
 
 def outputs_of(place, hidden, own, other, experts, slots):
+    shares, line, share, columns = own.shape
     return pl.pallas_call(
         down_kernel,
-        in_specs=[pl.BlockSpec(memory_space=pltpu.SMEM)] + whole(3),
-        out_specs=whole(1)[0],
-        out_shape=jax.ShapeDtypeStruct((experts, hidden.shape[0], slots, own.shape[3]), BF),
-        compiler_params=pltpu.CompilerParams(vmem_limit_bytes=32 << 20),
+        in_specs=[pl.BlockSpec(memory_space=pltpu.SMEM)] + whole(1) + [ANYWHERE] * 2,
+        out_specs=whole(1)[0],
+        out_shape=jax.ShapeDtypeStruct((experts, line, slots, columns), BF),
+        scratch_shapes=[
+            pltpu.VMEM((line, 2, shares, share, columns), BF),
+            pltpu.SemaphoreType.DMA((line, 2)),
+        ],
+        compiler_params=pltpu.CompilerParams(vmem_limit_bytes=16 << 20),
     )(place, hidden, own, other)
 
 
@@ -146,19 +196,15 @@
     weighting = jnp.sum(landing * gate_scores[..., None, None], axis=2)
     packed = packed_of(expert_ids, tokens, experts, slots)
     arrived = lax.all_to_all(packed, ROWS_OF, split_axis=0, concat_axis=0, tiled=True)
-    for piece in pieces[1:]:
-        arrived = after(piece, arrived)
-    pieces = jnp.stack(pieces)
-    rows = jnp.broadcast_to(arrived[None], (line,) + arrived.shape)
-    rows = lax.all_to_all(rows, "zi", split_axis=0, concat_axis=0, tiled=True)
+    sent = repeat_after(pieces[1:], arrived, line)
+    rows = lax.all_to_all(sent, "zi", split_axis=0, concat_axis=0, tiled=True)
     rows = rows.reshape(line * experts, slots, width)
-    pieces = after(arrived, pieces)
+    pieces = stack_after(sent, pieces)
     shares = [pieces] + [exchange(pieces, "dp", k) for k in range(1, lax.axis_size("dp"))]
     shares = jnp.stack(shares)
     other_shares = swap(shares)
-    up = after(arrived, turned[: 2 * units])
-    other_up = after(arrived, other[: 2 * units])
-    hidden = hidden_of(rows, up, other_up)
+    up = after(sent, turned[: 2 * units])
+    hidden = hidden_of(rows, up, after(sent, other[: 2 * units]))
     gathered = lax.all_gather(hidden, "zi", axis=0)
     position = jnp.stack([place, lax.axis_index("dp")]).astype(jnp.int32)
     done = outputs_of(position, gathered, shares, other_shares, experts, slots)

time: 168 us -> 169 us (level)
  Pallas kernels: 9.18 us -> 13.4 us
  between operations: 5.31 us -> 1.59 us
  waiting for transfers between devices: 61.1 us -> 64.6 us
  local copies, waits for them, and re-layouts: 7.55 us -> 4.81 us
    pallas_call x1 -> x3, Pallas kernels: 4.06 us -> 7.84 us  [the longest x1 6.42 us: hidden_of(): pl.pallas_call(up_kernel, in_specs=whole(2) + [ANYWHERE], out_specs=whole...]
    all_to_all x1, starting transfers between devices: 5.66 us -> 8.39 us  [on_device(): rows = lax.all_to_all(sent, 'zi', split_axis=0, concat_axis=0, tiled=True)]
    all_to_all x1, starting transfers between devices: 12.9 us -> 10.3 us  [on_device(): lax.all_to_all(done, HOME, split_axis=0, concat_axis=0, tiled=True)]
    all_to_all x1, waiting for transfers between devices: 0.01 us -> 2.54 us  [on_device(): lax.all_to_all(packed, ROWS_OF, split_axis=0, concat_axis=0, tiled=True)]
    all_to_all x1, waiting for transfers between devices: 25 us -> 27 us  [on_device(): lax.all_to_all(done, HOME, split_axis=0, concat_axis=0, tiled=True)]
    broadcast_in_dim x1 -> x0, local copies, waits for them, and re-layouts: 1.75 us -> none  [on_device(): rows = jnp.broadcast_to(arrived[None], (line,) + arrived.shape)]
  transfers between devices with their start and end apart: 11 -> 11, of which waited for: 5 -> 6; matrix products, arithmetic and copies ran while one was open for 5% -> 4% of each run, Pallas kernels for 2% -> 4%
where the time goes in v12:
time: 169 us; the launch traced here: 168 us
  waiting for transfers between devices  64.6 us (38%)
  starting transfers between devices  60.9 us (36%)
  blocking collectives  17.6 us (10%)
  Pallas kernels  13.4 us (8%)
  local copies, waits for them, and re-layouts  4.81 us (3%)
  other arithmetic  3.74 us (2%)
    ppermute x6, waiting for transfers between devices, exchange(): return lax.ppermute(array, axis, [(i, i ^ step) for i in range(size)])  27.1 us
    all_to_all x1, waiting for transfers between devices, on_device(): lax.all_to_all(done, HOME, split_axis=0, concat_axis=0, tiled=True)  27 us
    ppermute x6, starting transfers between devices, exchange(): return lax.ppermute(array, axis, [(i, i ^ step) for i in range(size)])  20.8 us
    all_to_all x1, starting transfers between devices, on_device(): lax.all_to_all(packed, ROWS_OF, split_axis=0, concat_axis=0, tiled=True)  17.7 us
    all_gather x1, blocking collectives, on_device(): gathered = lax.all_gather(hidden, 'zi', axis=0)  17.6 us
    all_to_all x1, starting transfers between devices, on_device(): lax.all_to_all(done, HOME, split_axis=0, concat_axis=0, tiled=True)  10.3 us
    all_to_all x1, starting transfers between devices, on_device(): rows = lax.all_to_all(sent, 'zi', split_axis=0, concat_axis=0, tiled=True)  8.39 us
    all_to_all x1, waiting for transfers between devices, on_device(): rows = lax.all_to_all(sent, 'zi', split_axis=0, concat_axis=0, tiled=True)  7.98 us
  transfers between devices with their start and end apart: 11, of which 6 were waited for; matrix products, arithmetic and copies ran while one was open for 4% of the time, Pallas kernels for 4%

profile of v12, /device:TPU:24, one launch (start us, length us, event | category | flops | bytes accessed | tf_op | source)
XLA Modules:
  0.0 167.7 jit_solution(6434702649689908921)
XLA Ops:
  0.0 0.0 copy-start
  0.0 0.9 copy-done
  0.9 0.0 copy-start.1
  0.9 0.7 copy-done.1
  1.6 1.4 shard_map.46
  3.0 17.7 %all-to-all-start = ((bf16[16,4,3584]{2,1,0:T(4,128)(2,1)}), bf16[16,4,3584]{2,1,0:T(4,128)(2,1)S(1)}, u32[]{:S(2)}, u32[]{:S(2)}) async-start(bf16[16,4,3584]{2,1,0:T(4,128)(2,1)} %shard_map.46), calls=%async_computation | async-start | bytes 917504 | tf_op jit(solution)/shard_map/all_to_all | solution.py:198
  20.6 1.0 dynamic-slice_bitcast_fusion
  21.7 0.1 reshape.47
  21.8 0.7 constant_dynamic-slice_fusion
  22.5 2.9 %collective-permute-start = (bf16[48,896]{1,0:T(8,128)(2,1)S(1)}, bf16[48,896]{1,0:T(8,128)(2,1)S(1)}, u32[]{:S(2)}, u32[]{:S(2)}) collective-permute-start(bf16[48,896]{1,0:T(8,128)(2,1)S(1)} %bitcast.50), channel_id=1, source_target_pairs={{0,8},{8,0},{16,24},{24,16},{1,9},{9,1},{17,25},{25,17},{2,10},{10... | collective-permute-start | bytes 258056 | tf_op jit(solution)/shard_map/ppermute | solution.py:19
  25.5 3.4 %collective-permute-start.1 = (bf16[48,896]{1,0:T(8,128)(2,1)S(1)}, bf16[48,896]{1,0:T(8,128)(2,1)S(1)}, u32[]{:S(2)}, u32[]{:S(2)}) collective-permute-start(bf16[48,896]{1,0:T(8,128)(2,1)S(1)} %bitcast.51), channel_id=1, source_target_pairs={{0,16},{8,24},{16,0},{24,8},{1,17},{9,25},{17,1},{25,9},{2,18},{10... | collective-permute-start | bytes 258056 | tf_op jit(solution)/shard_map/ppermute | solution.py:19
  28.9 3.8 %collective-permute-start.2 = (bf16[48,896]{1,0:T(8,128)(2,1)S(1)}, bf16[48,896]{1,0:T(8,128)(2,1)S(1)}, u32[]{:S(2)}, u32[]{:S(2)}) collective-permute-start(bf16[48,896]{1,0:T(8,128)(2,1)S(1)} %bitcast.52), channel_id=1, source_target_pairs={{0,24},{8,16},{16,8},{24,0},{1,25},{9,17},{17,9},{25,1},{2,26},{10... | collective-permute-start | bytes 258056 | tf_op jit(solution)/shard_map/ppermute | solution.py:19
  32.7 14.1 %collective-permute-done.refs_0_.refs_1_ = bf16[48,896]{1,0:T(8,128)(2,1)S(1)} collective-permute-done((bf16[48,896]{1,0:T(8,128)(2,1)S(1)}, bf16[48,896]{1,0:T(8,128)(2,1)S(1)}, u32[]{:S(2)}, u32[]{:S(2)}) %collective-permute-start) | collective-permute-done | bytes 86048 | tf_op jit(solution)/shard_map/ppermute | solution.py:19
  46.8 0.0 collective-permute-done.1.refs_1_.refs_2_
  46.8 0.0 collective-permute-done.2.refs_2_.refs_3_
  46.8 2.5 %all-to-all-done.rows_ref = bf16[16,4,3584]{2,1,0:T(4,128)(2,1)S(1)} async-done(((bf16[16,4,3584]{2,1,0:T(4,128)(2,1)}), bf16[16,4,3584]{2,1,0:T(4,128)(2,1)S(1)}, u32[]{:S(2)}, u32[]{:S(2)}) %all-to-all-start) | async-done | bytes 458784 | tf_op jit(solution)/shard_map/all_to_all | solution.py:198
  49.3 1.4 shard_map.47._
  50.7 8.4 %all-to-all-start.1 = ((bf16[4,16,4,3584]{3,2,1,0:T(4,128)(2,1)}), bf16[4,16,4,3584]{3,2,1,0:T(4,128)(2,1)}, u32[]{:S(2)}, u32[]{:S(2)}) async-start(bf16[4,16,4,3584]{3,2,1,0:T(4,128)(2,1)} %shard_map.47._), calls=%async_computation.1 | async-start | bytes 3670016 | tf_op jit(solution)/shard_map/all_to_all | solution.py:200
  59.1 1.9 %collective-permute-start.3 = (bf16[576,3584]{1,0:T(8,128)(2,1)}, bf16[576,3584]{1,0:T(8,128)(2,1)S(1)}, u32[]{:S(2)}, u32[]{:S(2)}) collective-permute-start(bf16[576,3584]{1,0:T(8,128)(2,1)} %bitcast.45), channel_id=1, source_target_pairs={{0,4},{4,0},{1,5},{5,1},{2,6},{6,2},{3,7},{7,3},{8,12},{12,8},{9,1... | collective-permute-start | bytes 12386312 | tf_op jit(solution)/shard_map/ppermute | solution.py:28
  61.0 0.0 copy-start.3
  61.1 2.9 %collective-permute-start.4 = (bf16[4,48,896]{2,1,0:T(8,128)(2,1)S(1)}, bf16[4,48,896]{2,1,0:T(8,128)(2,1)S(1)}, u32[]{:S(2)}, u32[]{:S(2)}) collective-permute-start(bf16[4,48,896]{2,1,0:T(8,128)(2,1)S(1)} %shard_map.49), channel_id=1, source_target_pairs={{0,1},{1,0},{2,3},{3,2},{4,5},{5,4},{6,7},{7,6},{8,9},{9,8},{10,11... | collective-permute-start | bytes 1032200 | tf_op jit(solution)/shard_map/ppermute | solution.py:19
  64.0 2.8 %collective-permute-start.5 = (bf16[4,48,896]{2,1,0:T(8,128)(2,1)S(1)}, bf16[4,48,896]{2,1,0:T(8,128)(2,1)S(1)}, u32[]{:S(2)}, u32[]{:S(2)}) collective-permute-start(bf16[4,48,896]{2,1,0:T(8,128)(2,1)S(1)} %shard_map.49), channel_id=1, source_target_pairs={{0,2},{1,3},{2,0},{3,1},{4,6},{5,7},{6,4},{7,5},{8,10},{9,11},{10,... | collective-permute-start | bytes 1032200 | tf_op jit(solution)/shard_map/ppermute | solution.py:19
  66.9 5.0 %collective-permute-start.6 = (bf16[4,48,896]{2,1,0:T(8,128)(2,1)S(1)}, bf16[4,48,896]{2,1,0:T(8,128)(2,1)S(1)}, u32[]{:S(2)}, u32[]{:S(2)}) collective-permute-start(bf16[4,48,896]{2,1,0:T(8,128)(2,1)S(1)} %shard_map.49), channel_id=1, source_target_pairs={{0,3},{1,2},{2,1},{3,0},{4,7},{5,6},{6,5},{7,4},{8,11},{9,10},{10,... | collective-permute-start | bytes 1032200 | tf_op jit(solution)/shard_map/ppermute | solution.py:19
  71.8 0.1 pad_add_fusion.place_ref
  71.9 1.2 slice.13
  74.4 0.0 collective-permute-done.4
  74.4 6.5 %collective-permute-done.5 = bf16[4,48,896]{2,1,0:T(8,128)(2,1)S(1)} collective-permute-done((bf16[4,48,896]{2,1,0:T(8,128)(2,1)S(1)}, bf16[4,48,896]{2,1,0:T(8,128)(2,1)S(1)}, u32[]{:S(2)}, u32[]{:S(2)}) %collective-permute-start.5) | collective-permute-done | bytes 344096 | tf_op jit(solution)/shard_map/ppermute | solution.py:19
  80.8 6.5 %collective-permute-done.6 = bf16[4,48,896]{2,1,0:T(8,128)(2,1)S(1)} collective-permute-done((bf16[4,48,896]{2,1,0:T(8,128)(2,1)S(1)}, bf16[4,48,896]{2,1,0:T(8,128)(2,1)S(1)}, u32[]{:S(2)}, u32[]{:S(2)}) %collective-permute-start.6) | collective-permute-done | bytes 344096 | tf_op jit(solution)/shard_map/ppermute | solution.py:19
  87.3 1.3 pad_maximum_fusion.own_ref
  88.6 1.9 %collective-permute-start.7 = (bf16[4,4,48,896]{3,2,1,0:T(8,128)(2,1)}, bf16[4,4,48,896]{3,2,1,0:T(8,128)(2,1)}, u32[]{:S(2)}, u32[]{:S(2)}) collective-permute-start(bf16[4,4,48,896]{3,2,1,0:T(8,128)(2,1)} %pad_maximum_fusion.own_ref), channel_id=1, source_target_pairs={{0,4},{4,0},{1,5},{5,1},{2,6},{6,2},{3,7},{7,3},{8,12},{12,8},{9,1... | collective-permute-start | bytes 4128776 | tf_op jit(solution)/shard_map/ppermute | solution.py:28
  90.5 0.0 copy-done.3
  90.5 0.2 slice_select_fusion.1.own_ref
  90.7 0.0 collective-permute-done.3
  90.8 1.7 %slice_select_fusion.other_ref = bf16[384,3584]{1,0:T(8,128)(2,1)} fusion(bf16[576,3584]{1,0:T(8,128)(2,1)S(1)} %collective-permute-done.3, pred[]{:T(512)} %bitcast.8), kind=kLoop, calls=%fused_computation | loop fusion | flops 1376256 | bytes 5505025 | tf_op jit(solution)/shard_map/jit(_where)/select_n | solution.py:24
  92.5 8.0 %all-to-all-done.1 = bf16[4,16,4,3584]{3,2,1,0:T(4,128)(2,1)} async-done(((bf16[4,16,4,3584]{3,2,1,0:T(4,128)(2,1)}), bf16[4,16,4,3584]{3,2,1,0:T(4,128)(2,1)}, u32[]{:S(2)}, u32[]{:S(2)}) %all-to-all-start.1) | async-done | bytes 1835040 | tf_op jit(solution)/shard_map/all_to_all | solution.py:200
  100.5 6.4 %shard_map.48 = bf16[256,384]{1,0:T(8,128)(2,1)S(1)} custom-call(bf16[64,4,3584]{2,1,0:T(4,128)(2,1)} %bitcast.7.rows_ref, bf16[384,3584]{1,0:T(8,128)(2,1)S(1)} %slice_select_fusion.1.own_ref, bf16[384,3584]{1,0:T(8,128)(2,1)} %slice_select_fusion.other_ref), custom_call_target="tpu_custom_call" | custom-call | tf_op jit(solution)/shard_map/pallas_call | solution.py:119
  106.9 0.0 copy-start.2
  106.9 0.0 copy-start.4
  106.9 17.6 %all-gather = bf16[1024,384]{1,0:T(8,128)(2,1)S(1)} all-gather(bf16[256,384]{1,0:T(8,128)(2,1)S(1)} %shard_map.48), channel_id=2, replica_groups=mesh['x'=4,'zb'=4,'zi'=4,'c'=2,'dp'=4] {'zi'}, dimensions={0}, use_global_device_ids=true | all-gather | bytes 983040 | tf_op jit(solution)/shard_map/all_gather | solution.py:208
  124.5 0.0 collective-permute-done.7.other_ref
  124.5 4.2 %shard_map.50 = bf16[16,4,4,896]{3,2,1,0:T(4,128)(2,1)} custom-call(s32[2]{0:T(128)S(1)} %pad_add_fusion.place_ref, bf16[4,256,384]{2,1,0:T(8,128)(2,1)S(1)} %bitcast.41, bf16[4,4,48,896]{3,2,1,0:T(8,128)(2,1)} %pad_maximum_fusion.own_ref, bf16[4,4,48,896]{3,2,1,0:T(8,128)(2,1)} %collective-permute-done.7.other_ref), custom_call_target="tpu_custom_call" | custom-call | tf_op jit(solution)/shard_map/pallas_call | solution.py:154
  128.7 10.3 %all-to-all-start.2 = ((bf16[64,4,896]{2,1,0:T(4,128)(2,1)}), bf16[64,4,896]{2,1,0:T(4,128)(2,1)S(1)}, u32[]{:S(2)}, u32[]{:S(2)}) async-start(bf16[64,4,896]{2,1,0:T(4,128)(2,1)} %bitcast.17), calls=%async_computation.2 | async-start | bytes 917504 | tf_op jit(solution)/shard_map/all_to_all | solution.py:212
  139.0 0.0 copy-done.2
  139.0 0.1 convert_reduce_fusion
  139.1 0.2 select_reduce_fusion.1
  139.3 0.1 iota_compare_fusion
  139.4 0.0 copy-done.4
  139.4 0.1 select_reduce_fusion
  139.5 27.0 %all-to-all-done.2 = bf16[64,4,896]{2,1,0:T(4,128)(2,1)S(1)} async-done(((bf16[64,4,896]{2,1,0:T(4,128)(2,1)}), bf16[64,4,896]{2,1,0:T(4,128)(2,1)S(1)}, u32[]{:S(2)}, u32[]{:S(2)}) %all-to-all-start.2) | async-done | bytes 458784 | tf_op jit(solution)/shard_map/all_to_all | solution.py:212
  166.5 0.2 reshape.55
  166.7 1.0 fusion
  (8 shorter events, 0.1 us)
Async XLA Ops:
  0.0 0.9 copy-start
  0.9 0.7 copy-start.1
  3.0 46.4 %all-to-all-start = ((bf16[16,4,3584]{2,1,0:T(4,128)(2,1)}), bf16[16,4,3584]{2,1,0:T(4,128)(2,1)S(1)}, u32[]{:S(2)}, u32[]{:S(2)}) async-start(bf16[16,4,3584]{2,1,0:T(4,128)(2,1)} %shard_map.46), calls=%async_computation | async-start | bytes 917504 | tf_op jit(solution)/shard_map/all_to_all | solution.py:198
  22.5 24.3 %collective-permute-start = (bf16[48,896]{1,0:T(8,128)(2,1)S(1)}, bf16[48,896]{1,0:T(8,128)(2,1)S(1)}, u32[]{:S(2)}, u32[]{:S(2)}) collective-permute-start(bf16[48,896]{1,0:T(8,128)(2,1)S(1)} %bitcast.50), channel_id=1, source_target_pairs={{0,8},{8,0},{16,24},{24,16},{1,9},{9,1},{17,25},{25,17},{2,10},{10... | collective-permute-start | bytes 258056 | tf_op jit(solution)/shard_map/ppermute | solution.py:19
  25.5 21.3 %collective-permute-start.1 = (bf16[48,896]{1,0:T(8,128)(2,1)S(1)}, bf16[48,896]{1,0:T(8,128)(2,1)S(1)}, u32[]{:S(2)}, u32[]{:S(2)}) collective-permute-start(bf16[48,896]{1,0:T(8,128)(2,1)S(1)} %bitcast.51), channel_id=1, source_target_pairs={{0,16},{8,24},{16,0},{24,8},{1,17},{9,25},{17,1},{25,9},{2,18},{10... | collective-permute-start | bytes 258056 | tf_op jit(solution)/shard_map/ppermute | solution.py:19
  28.9 17.9 %collective-permute-start.2 = (bf16[48,896]{1,0:T(8,128)(2,1)S(1)}, bf16[48,896]{1,0:T(8,128)(2,1)S(1)}, u32[]{:S(2)}, u32[]{:S(2)}) collective-permute-start(bf16[48,896]{1,0:T(8,128)(2,1)S(1)} %bitcast.52), channel_id=1, source_target_pairs={{0,24},{8,16},{16,8},{24,0},{1,25},{9,17},{17,9},{25,1},{2,26},{10... | collective-permute-start | bytes 258056 | tf_op jit(solution)/shard_map/ppermute | solution.py:19
  50.7 49.7 %all-to-all-start.1 = ((bf16[4,16,4,3584]{3,2,1,0:T(4,128)(2,1)}), bf16[4,16,4,3584]{3,2,1,0:T(4,128)(2,1)}, u32[]{:S(2)}, u32[]{:S(2)}) async-start(bf16[4,16,4,3584]{3,2,1,0:T(4,128)(2,1)} %shard_map.47._), calls=%async_computation.1 | async-start | bytes 3670016 | tf_op jit(solution)/shard_map/all_to_all | solution.py:200
  59.1 31.6 %collective-permute-start.3 = (bf16[576,3584]{1,0:T(8,128)(2,1)}, bf16[576,3584]{1,0:T(8,128)(2,1)S(1)}, u32[]{:S(2)}, u32[]{:S(2)}) collective-permute-start(bf16[576,3584]{1,0:T(8,128)(2,1)} %bitcast.45), channel_id=1, source_target_pairs={{0,4},{4,0},{1,5},{5,1},{2,6},{6,2},{3,7},{7,3},{8,12},{12,8},{9,1... | collective-permute-start | bytes 12386312 | tf_op jit(solution)/shard_map/ppermute | solution.py:28
  61.0 29.5 %copy-start.3 = (bf16[1,3584,576]{1,2,0:T(8,128)(2,1)S(1)}, bf16[1,3584,576]{1,2,0:T(8,128)(2,1)}, u32[]{:S(2)}) copy-start(bf16[1,3584,576]{1,2,0:T(8,128)(2,1)} %param.7) | copy-start | bytes 12386308
  61.1 13.3 %collective-permute-start.4 = (bf16[4,48,896]{2,1,0:T(8,128)(2,1)S(1)}, bf16[4,48,896]{2,1,0:T(8,128)(2,1)S(1)}, u32[]{:S(2)}, u32[]{:S(2)}) collective-permute-start(bf16[4,48,896]{2,1,0:T(8,128)(2,1)S(1)} %shard_map.49), channel_id=1, source_target_pairs={{0,1},{1,0},{2,3},{3,2},{4,5},{5,4},{6,7},{7,6},{8,9},{9,8},{10,11... | collective-permute-start | bytes 1032200 | tf_op jit(solution)/shard_map/ppermute | solution.py:19
  64.0 16.8 %collective-permute-start.5 = (bf16[4,48,896]{2,1,0:T(8,128)(2,1)S(1)}, bf16[4,48,896]{2,1,0:T(8,128)(2,1)S(1)}, u32[]{:S(2)}, u32[]{:S(2)}) collective-permute-start(bf16[4,48,896]{2,1,0:T(8,128)(2,1)S(1)} %shard_map.49), channel_id=1, source_target_pairs={{0,2},{1,3},{2,0},{3,1},{4,6},{5,7},{6,4},{7,5},{8,10},{9,11},{10,... | collective-permute-start | bytes 1032200 | tf_op jit(solution)/shard_map/ppermute | solution.py:19
  66.9 20.5 %collective-permute-start.6 = (bf16[4,48,896]{2,1,0:T(8,128)(2,1)S(1)}, bf16[4,48,896]{2,1,0:T(8,128)(2,1)S(1)}, u32[]{:S(2)}, u32[]{:S(2)}) collective-permute-start(bf16[4,48,896]{2,1,0:T(8,128)(2,1)S(1)} %shard_map.49), channel_id=1, source_target_pairs={{0,3},{1,2},{2,1},{3,0},{4,7},{5,6},{6,5},{7,4},{8,11},{9,10},{10,... | collective-permute-start | bytes 1032200 | tf_op jit(solution)/shard_map/ppermute | solution.py:19
  88.6 35.9 %collective-permute-start.7 = (bf16[4,4,48,896]{3,2,1,0:T(8,128)(2,1)}, bf16[4,4,48,896]{3,2,1,0:T(8,128)(2,1)}, u32[]{:S(2)}, u32[]{:S(2)}) collective-permute-start(bf16[4,4,48,896]{3,2,1,0:T(8,128)(2,1)} %pad_maximum_fusion.own_ref), channel_id=1, source_target_pairs={{0,4},{4,0},{1,5},{5,1},{2,6},{6,2},{3,7},{7,3},{8,12},{12,8},{9,1... | collective-permute-start | bytes 4128776 | tf_op jit(solution)/shard_map/ppermute | solution.py:28
  106.9 32.1 %copy-start.2 = (s32[2,8,2]{1,2,0:T(2,128)S(1)}, s32[2,8,2]{1,2,0:T(2,128)}, u32[]{:S(2)}) copy-start(s32[2,8,2]{1,2,0:T(2,128)} %param.5) | copy-start | bytes 388
  106.9 32.5 %copy-start.4 = (f32[2,8,2]{1,2,0:T(2,128)S(1)}, f32[2,8,2]{1,2,0:T(2,128)}, u32[]{:S(2)}) copy-start(f32[2,8,2]{1,2,0:T(2,128)} %param.6) | copy-start | bytes 388
  128.7 37.8 %all-to-all-start.2 = ((bf16[64,4,896]{2,1,0:T(4,128)(2,1)}), bf16[64,4,896]{2,1,0:T(4,128)(2,1)S(1)}, u32[]{:S(2)}, u32[]{:S(2)}) async-start(bf16[64,4,896]{2,1,0:T(4,128)(2,1)} %bitcast.17), calls=%async_computation.2 | async-start | bytes 917504 | tf_op jit(solution)/shard_map/all_to_all | solution.py:212

commit v13 on v12

--- a/solution.py
+++ b/solution.py
@@ -99,15 +99,11 @@
     )(earlier, *arrays)
 
 
-def up_kernel(rows_ref, own_ref, other_ref, out_ref, held_ref, arrival):
+def up_kernel(rows_ref, own_ref, other_ref, out_ref):
     units = own_ref.shape[0] // 2
-    copy = pltpu.make_async_copy(other_ref.at[pl.ds(0, 2 * units)], held_ref, arrival)
-    copy.start()
     rows = rows_ref[...].reshape(-1, own_ref.shape[1])
     hidden = []
-    for ref in (own_ref, held_ref):
-        if ref is held_ref:
-            copy.wait()
+    for ref in (own_ref, other_ref):
         both = lax.dot_general(ref[...], rows, NT, preferred_element_type=F32)
         gate = both[:units]
         hidden.append(gate / (1.0 + jnp.exp(-gate)) * both[units:])
@@ -118,30 +114,21 @@
     count = rows.shape[0] * rows.shape[1]
     return pl.pallas_call(
         up_kernel,
-        in_specs=whole(2) + [ANYWHERE],
+        grid=(1,),
+        in_specs=whole(2) + [pl.BlockSpec(own.shape, lambda i: (0, 0))],
         out_specs=whole(1)[0],
         out_shape=jax.ShapeDtypeStruct((count, own.shape[0]), BF),
-        scratch_shapes=[pltpu.VMEM(own.shape, BF), pltpu.SemaphoreType.DMA(())],
         compiler_params=pltpu.CompilerParams(vmem_limit_bytes=48 << 20),
     )(rows, own, other)
 
 
-def down_kernel(place_ref, hidden_ref, own_ref, other_ref, out_ref, held_ref, arrivals):
-    shares, line, share, columns = own_ref.shape
-    experts, _, slots, _ = out_ref.shape
-    copies = []
-    for at in range(line):
-        for i, ref in enumerate((own_ref, other_ref)):
-            source = ref.at[:, place_ref[0] ^ at]
-            copies.append(pltpu.make_async_copy(source, held_ref.at[at, i], arrivals.at[at, i]))
-    for copy in copies:
-        copy.start()
+def down_kernel(place_ref, hidden_ref, own_ref, other_ref, out_ref):
+    shares, line = own_ref.shape[:2]
+    experts, _, slots, columns = out_ref.shape
     total = jnp.zeros((line * experts * slots, columns), F32)
     for at in range(line):
-        weights = []
-        for i in range(2):
-            copies[2 * at + i].wait()
-            weights += [held_ref[at, i, place_ref[1] ^ y] for y in range(shares)]
+        k = place_ref[0] ^ at
+        weights = [ref[place_ref[1] ^ y, k] for ref in (own_ref, other_ref) for y in range(shares)]
         weights = jnp.concatenate(weights, axis=0)
         total += jnp.dot(hidden_ref[at], weights, preferred_element_type=F32)
     total = total.astype(BF).reshape(line, experts, slots, columns)
@@ -150,16 +137,11 @@
 
 
 def outputs_of(place, hidden, own, other, experts, slots):
-    shares, line, share, columns = own.shape
     return pl.pallas_call(
         down_kernel,
-        in_specs=[pl.BlockSpec(memory_space=pltpu.SMEM)] + whole(1) + [ANYWHERE] * 2,
-        out_specs=whole(1)[0],
-        out_shape=jax.ShapeDtypeStruct((experts, line, slots, columns), BF),
-        scratch_shapes=[
-            pltpu.VMEM((line, 2, shares, share, columns), BF),
-            pltpu.SemaphoreType.DMA((line, 2)),
-        ],
+        in_specs=[pl.BlockSpec(memory_space=pltpu.SMEM)] + whole(3),
+        out_specs=whole(1)[0],
+        out_shape=jax.ShapeDtypeStruct((experts, hidden.shape[0], slots, own.shape[3]), BF),
         compiler_params=pltpu.CompilerParams(vmem_limit_bytes=16 << 20),
     )(place, hidden, own, other)
 
@@ -204,7 +186,7 @@
     shares = jnp.stack(shares)
     other_shares = swap(shares)
     up = after(sent, turned[: 2 * units])
-    hidden = hidden_of(rows, up, after(sent, other[: 2 * units]))
+    hidden = hidden_of(rows, up, other)
     gathered = lax.all_gather(hidden, "zi", axis=0)
     position = jnp.stack([place, lax.axis_index("dp")]).astype(jnp.int32)
     done = outputs_of(position, gathered, shares, other_shares, experts, slots)

time: 169 us -> 166 us (0.982)
  Pallas kernels: 13.4 us -> 10.6 us
  waiting for transfers between devices: 64.6 us -> 66.8 us
    pallas_call x1, Pallas kernels: 6.42 us -> 4.05 us  [hidden_of(): pl.pallas_call(up_kernel, grid=(1,), in_specs=whole(2) + [pl.BlockSpec(ow...]
    select_n x2 -> x1, other arithmetic: 1.9 us -> 0.18 us  [after(): return jnp.where(mark == mark, then, jnp.zeros((), then.dtype))]
  transfers between devices with their start and end apart: 11 -> 11, of which waited for: 6 -> 6; matrix products, arithmetic and copies ran while one was open for 4% -> 3% of each run, Pallas kernels for 4% -> 2%
where the time goes in v13:
time: 166 us; the launch traced here: 165 us
  waiting for transfers between devices  66.8 us (40%)
  starting transfers between devices  60.3 us (36%)
  blocking collectives  17.7 us (11%)
  Pallas kernels  10.6 us (6%)
  local copies, waits for them, and re-layouts  4.77 us (3%)
  other arithmetic  2.11 us (1%)
    ppermute x6, waiting for transfers between devices, exchange(): return lax.ppermute(array, axis, [(i, i ^ step) for i in range(size)])  27.7 us
    all_to_all x1, waiting for transfers between devices, on_device(): lax.all_to_all(done, HOME, split_axis=0, concat_axis=0, tiled=True)  27 us
    ppermute x6, starting transfers between devices, exchange(): return lax.ppermute(array, axis, [(i, i ^ step) for i in range(size)])  20.2 us
    all_gather x1, blocking collectives, on_device(): gathered = lax.all_gather(hidden, 'zi', axis=0)  17.7 us
    all_to_all x1, starting transfers between devices, on_device(): lax.all_to_all(packed, ROWS_OF, split_axis=0, concat_axis=0, tiled=True)  17.7 us
    all_to_all x1, starting transfers between devices, on_device(): lax.all_to_all(done, HOME, split_axis=0, concat_axis=0, tiled=True)  10.3 us
    all_to_all x1, waiting for transfers between devices, on_device(): rows = lax.all_to_all(sent, 'zi', split_axis=0, concat_axis=0, tiled=True)  9.58 us
    all_to_all x1, starting transfers between devices, on_device(): rows = lax.all_to_all(sent, 'zi', split_axis=0, concat_axis=0, tiled=True)  8.39 us
  transfers between devices with their start and end apart: 11, of which 6 were waited for; matrix products, arithmetic and copies ran while one was open for 3% of the time, Pallas kernels for 2%

profile of v13, /device:TPU:24, one launch (start us, length us, event | category | flops | bytes accessed | tf_op | source)
XLA Modules:
  0.0 164.9 jit_solution(8021924928046287504)
XLA Ops:
  0.0 0.0 copy-start
  0.0 0.9 copy-done
  0.9 0.0 copy-start.1
  0.9 0.7 copy-done.1
  1.6 1.4 shard_map.46
  3.0 17.7 %all-to-all-start = ((bf16[16,4,3584]{2,1,0:T(4,128)(2,1)}), bf16[16,4,3584]{2,1,0:T(4,128)(2,1)S(1)}, u32[]{:S(2)}, u32[]{:S(2)}) async-start(bf16[16,4,3584]{2,1,0:T(4,128)(2,1)} %shard_map.46), calls=%async_computation | async-start | bytes 917504 | tf_op jit(solution)/shard_map/all_to_all | solution.py:180
  20.6 1.0 dynamic-slice_bitcast_fusion
  21.7 0.1 reshape.47
  21.8 0.7 constant_dynamic-slice_fusion
  22.5 2.9 %collective-permute-start = (bf16[48,896]{1,0:T(8,128)(2,1)S(1)}, bf16[48,896]{1,0:T(8,128)(2,1)S(1)}, u32[]{:S(2)}, u32[]{:S(2)}) collective-permute-start(bf16[48,896]{1,0:T(8,128)(2,1)S(1)} %bitcast.50), channel_id=1, source_target_pairs={{0,8},{8,0},{16,24},{24,16},{1,9},{9,1},{17,25},{25,17},{2,10},{10... | collective-permute-start | bytes 258056 | tf_op jit(solution)/shard_map/ppermute | solution.py:19
  25.5 3.4 %collective-permute-start.1 = (bf16[48,896]{1,0:T(8,128)(2,1)S(1)}, bf16[48,896]{1,0:T(8,128)(2,1)S(1)}, u32[]{:S(2)}, u32[]{:S(2)}) collective-permute-start(bf16[48,896]{1,0:T(8,128)(2,1)S(1)} %bitcast.51), channel_id=1, source_target_pairs={{0,16},{8,24},{16,0},{24,8},{1,17},{9,25},{17,1},{25,9},{2,18},{10... | collective-permute-start | bytes 258056 | tf_op jit(solution)/shard_map/ppermute | solution.py:19
  28.9 3.8 %collective-permute-start.2 = (bf16[48,896]{1,0:T(8,128)(2,1)S(1)}, bf16[48,896]{1,0:T(8,128)(2,1)S(1)}, u32[]{:S(2)}, u32[]{:S(2)}) collective-permute-start(bf16[48,896]{1,0:T(8,128)(2,1)S(1)} %bitcast.52), channel_id=1, source_target_pairs={{0,24},{8,16},{16,8},{24,0},{1,25},{9,17},{17,9},{25,1},{2,26},{10... | collective-permute-start | bytes 258056 | tf_op jit(solution)/shard_map/ppermute | solution.py:19
  32.7 14.1 %collective-permute-done.refs_0_.refs_1_ = bf16[48,896]{1,0:T(8,128)(2,1)S(1)} collective-permute-done((bf16[48,896]{1,0:T(8,128)(2,1)S(1)}, bf16[48,896]{1,0:T(8,128)(2,1)S(1)}, u32[]{:S(2)}, u32[]{:S(2)}) %collective-permute-start) | collective-permute-done | bytes 86048 | tf_op jit(solution)/shard_map/ppermute | solution.py:19
  46.8 0.0 collective-permute-done.1.refs_1_.refs_2_
  46.8 0.0 collective-permute-done.2.refs_2_.refs_3_
  46.8 2.5 %all-to-all-done.rows_ref = bf16[16,4,3584]{2,1,0:T(4,128)(2,1)S(1)} async-done(((bf16[16,4,3584]{2,1,0:T(4,128)(2,1)}), bf16[16,4,3584]{2,1,0:T(4,128)(2,1)S(1)}, u32[]{:S(2)}, u32[]{:S(2)}) %all-to-all-start) | async-done | bytes 458784 | tf_op jit(solution)/shard_map/all_to_all | solution.py:180
  49.3 1.4 shard_map.47._
  50.7 8.4 %all-to-all-start.1 = ((bf16[4,16,4,3584]{3,2,1,0:T(4,128)(2,1)}), bf16[4,16,4,3584]{3,2,1,0:T(4,128)(2,1)}, u32[]{:S(2)}, u32[]{:S(2)}) async-start(bf16[4,16,4,3584]{3,2,1,0:T(4,128)(2,1)} %shard_map.47._), calls=%async_computation.1 | async-start | bytes 3670016 | tf_op jit(solution)/shard_map/all_to_all | solution.py:182
  59.1 1.9 %collective-permute-start.3 = (bf16[576,3584]{1,0:T(8,128)(2,1)}, bf16[576,3584]{1,0:T(8,128)(2,1)}, u32[]{:S(2)}, u32[]{:S(2)}) collective-permute-start(bf16[576,3584]{1,0:T(8,128)(2,1)} %bitcast.45), channel_id=1, source_target_pairs={{0,4},{4,0},{1,5},{5,1},{2,6},{6,2},{3,7},{7,3},{8,12},{12,8},{9,1... | collective-permute-start | bytes 12386312 | tf_op jit(solution)/shard_map/ppermute | solution.py:28
  61.0 0.0 copy-start.3
  61.1 2.4 %collective-permute-start.6 = (bf16[4,48,896]{2,1,0:T(8,128)(2,1)S(1)}, bf16[4,48,896]{2,1,0:T(8,128)(2,1)S(1)}, u32[]{:S(2)}, u32[]{:S(2)}) collective-permute-start(bf16[4,48,896]{2,1,0:T(8,128)(2,1)S(1)} %shard_map.49), channel_id=1, source_target_pairs={{0,3},{1,2},{2,1},{3,0},{4,7},{5,6},{6,5},{7,4},{8,11},{9,10},{10,... | collective-permute-start | bytes 1032200 | tf_op jit(solution)/shard_map/ppermute | solution.py:19
  63.5 4.5 %collective-permute-start.5 = (bf16[4,48,896]{2,1,0:T(8,128)(2,1)S(1)}, bf16[4,48,896]{2,1,0:T(8,128)(2,1)S(1)}, u32[]{:S(2)}, u32[]{:S(2)}) collective-permute-start(bf16[4,48,896]{2,1,0:T(8,128)(2,1)S(1)} %shard_map.49), channel_id=1, source_target_pairs={{0,2},{1,3},{2,0},{3,1},{4,6},{5,7},{6,4},{7,5},{8,10},{9,11},{10,... | collective-permute-start | bytes 1032200 | tf_op jit(solution)/shard_map/ppermute | solution.py:19
  68.0 3.2 %collective-permute-start.4 = (bf16[4,48,896]{2,1,0:T(8,128)(2,1)S(1)}, bf16[4,48,896]{2,1,0:T(8,128)(2,1)S(1)}, u32[]{:S(2)}, u32[]{:S(2)}) collective-permute-start(bf16[4,48,896]{2,1,0:T(8,128)(2,1)S(1)} %shard_map.49), channel_id=1, source_target_pairs={{0,1},{1,0},{2,3},{3,2},{4,5},{5,4},{6,7},{7,6},{8,9},{9,8},{10,11... | collective-permute-start | bytes 1032200 | tf_op jit(solution)/shard_map/ppermute | solution.py:19
  71.2 11.1 %collective-permute-done.6 = bf16[4,48,896]{2,1,0:T(8,128)(2,1)S(1)} collective-permute-done((bf16[4,48,896]{2,1,0:T(8,128)(2,1)S(1)}, bf16[4,48,896]{2,1,0:T(8,128)(2,1)S(1)}, u32[]{:S(2)}, u32[]{:S(2)}) %collective-permute-start.6) | collective-permute-done | bytes 344096 | tf_op jit(solution)/shard_map/ppermute | solution.py:19
  82.3 0.0 collective-permute-done.5
  82.3 2.5 %collective-permute-done.4 = bf16[4,48,896]{2,1,0:T(8,128)(2,1)S(1)} collective-permute-done((bf16[4,48,896]{2,1,0:T(8,128)(2,1)S(1)}, bf16[4,48,896]{2,1,0:T(8,128)(2,1)S(1)}, u32[]{:S(2)}, u32[]{:S(2)}) %collective-permute-start.4) | collective-permute-done | bytes 344096 | tf_op jit(solution)/shard_map/ppermute | solution.py:19
  84.8 1.4 pad_maximum_fusion.own_ref
  86.2 1.9 %collective-permute-start.7 = (bf16[4,4,48,896]{3,2,1,0:T(8,128)(2,1)}, bf16[4,4,48,896]{3,2,1,0:T(8,128)(2,1)}, u32[]{:S(2)}, u32[]{:S(2)}) collective-permute-start(bf16[4,4,48,896]{3,2,1,0:T(8,128)(2,1)} %pad_maximum_fusion.own_ref), channel_id=1, source_target_pairs={{0,4},{4,0},{1,5},{5,1},{2,6},{6,2},{3,7},{7,3},{8,12},{12,8},{9,1... | collective-permute-start | bytes 4128776 | tf_op jit(solution)/shard_map/ppermute | solution.py:28
  88.1 0.1 pad_add_fusion.place_ref
  88.2 1.1 slice.8
  90.6 0.0 copy-done.3
  90.6 0.2 slice_select_fusion.own_ref
  90.8 0.0 collective-permute-done.3.other_ref
  90.8 9.6 %all-to-all-done.1 = bf16[4,16,4,3584]{3,2,1,0:T(4,128)(2,1)} async-done(((bf16[4,16,4,3584]{3,2,1,0:T(4,128)(2,1)}), bf16[4,16,4,3584]{3,2,1,0:T(4,128)(2,1)}, u32[]{:S(2)}, u32[]{:S(2)}) %all-to-all-start.1) | async-done | bytes 1835040 | tf_op jit(solution)/shard_map/all_to_all | solution.py:182
  100.4 4.1 %shard_map.48 = bf16[256,384]{1,0:T(8,128)(2,1)S(1)} custom-call(bf16[64,4,3584]{2,1,0:T(4,128)(2,1)} %bitcast.7.rows_ref, bf16[384,3584]{1,0:T(8,128)(2,1)S(1)} %slice_select_fusion.own_ref, bf16[576,3584]{1,0:T(8,128)(2,1)} %collective-permute-done.3.other_ref), custom_call_target="tpu_custom_call" | custom-call | tf_op jit(solution)/shard_map/pallas_call | solution.py:115
  104.5 17.7 %all-gather = bf16[1024,384]{1,0:T(8,128)(2,1)S(1)} all-gather(bf16[256,384]{1,0:T(8,128)(2,1)S(1)} %shard_map.48), channel_id=2, replica_groups=mesh['x'=4,'zb'=4,'zi'=4,'c'=2,'dp'=4] {'zi'}, dimensions={0}, use_global_device_ids=true | all-gather | bytes 983040 | tf_op jit(solution)/shard_map/all_gather | solution.py:190
  122.1 0.0 collective-permute-done.7.other_ref
  122.1 0.0 copy-start.2
  122.2 0.0 copy-start.4
  122.2 3.8 %shard_map.50 = bf16[16,4,4,896]{3,2,1,0:T(4,128)(2,1)} custom-call(s32[2]{0:T(128)S(1)} %pad_add_fusion.place_ref, bf16[4,256,384]{2,1,0:T(8,128)(2,1)S(1)} %bitcast.41, bf16[4,4,48,896]{3,2,1,0:T(8,128)(2,1)} %pad_maximum_fusion.own_ref, bf16[4,4,48,896]{3,2,1,0:T(8,128)(2,1)} %collective-permute-done.7.other_ref), custom_call_target="tpu_custom_call" | custom-call | tf_op jit(solution)/shard_map/pallas_call | solution.py:140
  125.9 10.3 %all-to-all-start.2 = ((bf16[64,4,896]{2,1,0:T(4,128)(2,1)}), bf16[64,4,896]{2,1,0:T(4,128)(2,1)S(1)}, u32[]{:S(2)}, u32[]{:S(2)}) async-start(bf16[64,4,896]{2,1,0:T(4,128)(2,1)} %bitcast.17), calls=%async_computation.2 | async-start | bytes 917504 | tf_op jit(solution)/shard_map/all_to_all | solution.py:194
  136.2 0.0 copy-done.2
  136.2 0.1 convert_reduce_fusion
  136.3 0.2 select_reduce_fusion.1
  136.5 0.1 iota_compare_fusion
  136.6 0.0 copy-done.4
  136.6 0.1 select_reduce_fusion
  136.7 27.0 %all-to-all-done.2 = bf16[64,4,896]{2,1,0:T(4,128)(2,1)S(1)} async-done(((bf16[64,4,896]{2,1,0:T(4,128)(2,1)}), bf16[64,4,896]{2,1,0:T(4,128)(2,1)S(1)}, u32[]{:S(2)}, u32[]{:S(2)}) %all-to-all-start.2) | async-done | bytes 458784 | tf_op jit(solution)/shard_map/all_to_all | solution.py:194
  163.7 0.2 reshape.55
  163.8 1.0 fusion
  (8 shorter events, 0.1 us)
Async XLA Ops:
  0.0 0.9 copy-start
  0.9 0.7 copy-start.1
  3.0 46.4 %all-to-all-start = ((bf16[16,4,3584]{2,1,0:T(4,128)(2,1)}), bf16[16,4,3584]{2,1,0:T(4,128)(2,1)S(1)}, u32[]{:S(2)}, u32[]{:S(2)}) async-start(bf16[16,4,3584]{2,1,0:T(4,128)(2,1)} %shard_map.46), calls=%async_computation | async-start | bytes 917504 | tf_op jit(solution)/shard_map/all_to_all | solution.py:180
  22.5 24.3 %collective-permute-start = (bf16[48,896]{1,0:T(8,128)(2,1)S(1)}, bf16[48,896]{1,0:T(8,128)(2,1)S(1)}, u32[]{:S(2)}, u32[]{:S(2)}) collective-permute-start(bf16[48,896]{1,0:T(8,128)(2,1)S(1)} %bitcast.50), channel_id=1, source_target_pairs={{0,8},{8,0},{16,24},{24,16},{1,9},{9,1},{17,25},{25,17},{2,10},{10... | collective-permute-start | bytes 258056 | tf_op jit(solution)/shard_map/ppermute | solution.py:19
  25.5 21.3 %collective-permute-start.1 = (bf16[48,896]{1,0:T(8,128)(2,1)S(1)}, bf16[48,896]{1,0:T(8,128)(2,1)S(1)}, u32[]{:S(2)}, u32[]{:S(2)}) collective-permute-start(bf16[48,896]{1,0:T(8,128)(2,1)S(1)} %bitcast.51), channel_id=1, source_target_pairs={{0,16},{8,24},{16,0},{24,8},{1,17},{9,25},{17,1},{25,9},{2,18},{10... | collective-permute-start | bytes 258056 | tf_op jit(solution)/shard_map/ppermute | solution.py:19
  28.9 17.9 %collective-permute-start.2 = (bf16[48,896]{1,0:T(8,128)(2,1)S(1)}, bf16[48,896]{1,0:T(8,128)(2,1)S(1)}, u32[]{:S(2)}, u32[]{:S(2)}) collective-permute-start(bf16[48,896]{1,0:T(8,128)(2,1)S(1)} %bitcast.52), channel_id=1, source_target_pairs={{0,24},{8,16},{16,8},{24,0},{1,25},{9,17},{17,9},{25,1},{2,26},{10... | collective-permute-start | bytes 258056 | tf_op jit(solution)/shard_map/ppermute | solution.py:19
  50.7 49.7 %all-to-all-start.1 = ((bf16[4,16,4,3584]{3,2,1,0:T(4,128)(2,1)}), bf16[4,16,4,3584]{3,2,1,0:T(4,128)(2,1)}, u32[]{:S(2)}, u32[]{:S(2)}) async-start(bf16[4,16,4,3584]{3,2,1,0:T(4,128)(2,1)} %shard_map.47._), calls=%async_computation.1 | async-start | bytes 3670016 | tf_op jit(solution)/shard_map/all_to_all | solution.py:182
  59.1 31.8 %collective-permute-start.3 = (bf16[576,3584]{1,0:T(8,128)(2,1)}, bf16[576,3584]{1,0:T(8,128)(2,1)}, u32[]{:S(2)}, u32[]{:S(2)}) collective-permute-start(bf16[576,3584]{1,0:T(8,128)(2,1)} %bitcast.45), channel_id=1, source_target_pairs={{0,4},{4,0},{1,5},{5,1},{2,6},{6,2},{3,7},{7,3},{8,12},{12,8},{9,1... | collective-permute-start | bytes 12386312 | tf_op jit(solution)/shard_map/ppermute | solution.py:28
  61.0 29.6 %copy-start.3 = (bf16[1,3584,576]{1,2,0:T(8,128)(2,1)S(1)}, bf16[1,3584,576]{1,2,0:T(8,128)(2,1)}, u32[]{:S(2)}) copy-start(bf16[1,3584,576]{1,2,0:T(8,128)(2,1)} %param.7) | copy-start | bytes 12386308
  61.1 21.2 %collective-permute-start.6 = (bf16[4,48,896]{2,1,0:T(8,128)(2,1)S(1)}, bf16[4,48,896]{2,1,0:T(8,128)(2,1)S(1)}, u32[]{:S(2)}, u32[]{:S(2)}) collective-permute-start(bf16[4,48,896]{2,1,0:T(8,128)(2,1)S(1)} %shard_map.49), channel_id=1, source_target_pairs={{0,3},{1,2},{2,1},{3,0},{4,7},{5,6},{6,5},{7,4},{8,11},{9,10},{10,... | collective-permute-start | bytes 1032200 | tf_op jit(solution)/shard_map/ppermute | solution.py:19
  63.5 18.8 %collective-permute-start.5 = (bf16[4,48,896]{2,1,0:T(8,128)(2,1)S(1)}, bf16[4,48,896]{2,1,0:T(8,128)(2,1)S(1)}, u32[]{:S(2)}, u32[]{:S(2)}) collective-permute-start(bf16[4,48,896]{2,1,0:T(8,128)(2,1)S(1)} %shard_map.49), channel_id=1, source_target_pairs={{0,2},{1,3},{2,0},{3,1},{4,6},{5,7},{6,4},{7,5},{8,10},{9,11},{10,... | collective-permute-start | bytes 1032200 | tf_op jit(solution)/shard_map/ppermute | solution.py:19
  68.0 16.8 %collective-permute-start.4 = (bf16[4,48,896]{2,1,0:T(8,128)(2,1)S(1)}, bf16[4,48,896]{2,1,0:T(8,128)(2,1)S(1)}, u32[]{:S(2)}, u32[]{:S(2)}) collective-permute-start(bf16[4,48,896]{2,1,0:T(8,128)(2,1)S(1)} %shard_map.49), channel_id=1, source_target_pairs={{0,1},{1,0},{2,3},{3,2},{4,5},{5,4},{6,7},{7,6},{8,9},{9,8},{10,11... | collective-permute-start | bytes 1032200 | tf_op jit(solution)/shard_map/ppermute | solution.py:19
  86.2 36.0 %collective-permute-start.7 = (bf16[4,4,48,896]{3,2,1,0:T(8,128)(2,1)}, bf16[4,4,48,896]{3,2,1,0:T(8,128)(2,1)}, u32[]{:S(2)}, u32[]{:S(2)}) collective-permute-start(bf16[4,4,48,896]{3,2,1,0:T(8,128)(2,1)} %pad_maximum_fusion.own_ref), channel_id=1, source_target_pairs={{0,4},{4,0},{1,5},{5,1},{2,6},{6,2},{3,7},{7,3},{8,12},{12,8},{9,1... | collective-permute-start | bytes 4128776 | tf_op jit(solution)/shard_map/ppermute | solution.py:28
  122.1 14.0 %copy-start.2 = (s32[2,8,2]{1,2,0:T(2,128)S(1)}, s32[2,8,2]{1,2,0:T(2,128)}, u32[]{:S(2)}) copy-start(s32[2,8,2]{1,2,0:T(2,128)} %param.5) | copy-start | bytes 388
  122.2 14.5 %copy-start.4 = (f32[2,8,2]{1,2,0:T(2,128)S(1)}, f32[2,8,2]{1,2,0:T(2,128)}, u32[]{:S(2)}) copy-start(f32[2,8,2]{1,2,0:T(2,128)} %param.6) | copy-start | bytes 388
  125.9 37.8 %all-to-all-start.2 = ((bf16[64,4,896]{2,1,0:T(4,128)(2,1)}), bf16[64,4,896]{2,1,0:T(4,128)(2,1)S(1)}, u32[]{:S(2)}, u32[]{:S(2)}) async-start(bf16[64,4,896]{2,1,0:T(4,128)(2,1)} %bitcast.17), calls=%async_computation.2 | async-start | bytes 917504 | tf_op jit(solution)/shard_map/all_to_all | solution.py:194

commit v14 on v10

--- a/solution.py
+++ b/solution.py
@@ -10,17 +10,13 @@
 F32 = jnp.float32
 ROWS_OF = ("x", "zb")
 HOME = ("x", "zb", "zi")
+ANYWHERE = pl.BlockSpec(memory_space=pl.ANY)
 NT = (((1,), (1,)), ((), ()))
 
 
 def exchange(array, axis, step):
     size = lax.axis_size(axis)
     return lax.ppermute(array, axis, [(i, i ^ step) for i in range(size)])
-
-
-def after(first, then):
-    mark = first[(0,) * first.ndim]
-    return jnp.where(mark == mark, then, jnp.zeros((), then.dtype))
 
 
 def swap(array):
@@ -77,27 +73,68 @@
     )(expert_ids.transpose(0, 2, 1), gate_scores.transpose(0, 2, 1), tokens)
 
 
-def up_kernel(rows_ref, own_ref, other_ref, out_ref):
-    units = own_ref.shape[0] // 2
-    rows = rows_ref[...].reshape(-1, own_ref.shape[1])
+def repeat_kernel(_, *refs):
+    arrays, out_ref, done = refs[:-2], refs[-2], refs[-1]
+    copies = [
+        pltpu.make_async_copy(ref, out_ref.at[copy, k], done.at[copy, k])
+        for copy in range(out_ref.shape[0])
+        for k, ref in enumerate(arrays)
+    ]
+    for copy in copies:
+        copy.start()
+    for copy in copies:
+        copy.wait()
+
+
+def repeat_after(earlier, arrays, times):
+    return pl.pallas_call(
+        repeat_kernel,
+        in_specs=[ANYWHERE] + whole(len(arrays)),
+        out_specs=pl.BlockSpec(memory_space=pltpu.HBM),
+        out_shape=jax.ShapeDtypeStruct((times, len(arrays)) + arrays[0].shape, BF),
+        scratch_shapes=[pltpu.SemaphoreType.DMA((times, len(arrays)))],
+        compiler_params=pltpu.CompilerParams(vmem_limit_bytes=53 << 20),
+    )(earlier, *arrays)
+
+
+def copy_kernel(_, array_ref, out_ref):
+    out_ref[...] = array_ref[...]
+
+
+def copy_after(earlier, array):
+    return pl.pallas_call(
+        copy_kernel,
+        in_specs=[ANYWHERE] + whole(1),
+        out_specs=whole(1)[0],
+        out_shape=jax.ShapeDtypeStruct(array.shape, array.dtype),
+        compiler_params=pltpu.CompilerParams(vmem_limit_bytes=16 << 20),
+    )(earlier, array)
+
+
+def up_kernel(first_ref, second_ref, own_ref, other_ref, out_ref):
+    units = own_ref.shape[0] // 3
+    width = own_ref.shape[1]
+    rows = [ref[...].reshape(-1, width) for ref in (first_ref, second_ref)]
+    rows = jnp.concatenate(rows, axis=0)
     hidden = []
     for ref in (own_ref, other_ref):
-        both = lax.dot_general(ref[...], rows, NT, preferred_element_type=F32)
+        both = lax.dot_general(ref[: 2 * units], rows, NT, preferred_element_type=F32)
         gate = both[:units]
         hidden.append(gate / (1.0 + jnp.exp(-gate)) * both[units:])
     out_ref[...] = jnp.concatenate(hidden, axis=0).T.astype(BF)
 
 
-def hidden_of(rows, own, other):
-    count = rows.shape[0] * rows.shape[1]
+def hidden_of(first, second, own, other):
+    count = 2 * first.shape[0] * first.shape[1]
+    both = own.shape[0] // 3 * 2
     return pl.pallas_call(
         up_kernel,
         grid=(1,),
-        in_specs=whole(2) + [pl.BlockSpec(own.shape, lambda i: (0, 0))],
+        in_specs=whole(3) + [pl.BlockSpec((both, own.shape[1]), lambda i: (0, 0))],
         out_specs=whole(1)[0],
-        out_shape=jax.ShapeDtypeStruct((count, own.shape[0]), BF),
+        out_shape=jax.ShapeDtypeStruct((count, both), BF),
         compiler_params=pltpu.CompilerParams(vmem_limit_bytes=24 << 20),
-    )(rows, own, other)
+    )(first, second, own, other)
 
 
 def down_kernel(place_ref, hidden_ref, own_ref, other_ref, out_ref):
@@ -106,12 +143,14 @@
     total = jnp.zeros((line * experts * slots, columns), F32)
     for at in range(line):
         k = place_ref[0] ^ at
-        weights = [ref[place_ref[1] ^ y, k] for ref in (own_ref, other_ref) for y in range(shares)]
+        weights = [ref[y, k] for ref in (own_ref, other_ref) for y in range(shares)]
         weights = jnp.concatenate(weights, axis=0)
         total += jnp.dot(hidden_ref[at], weights, preferred_element_type=F32)
-    total = total.astype(BF).reshape(line, experts, slots, columns)
-    for p in range(line):
-        out_ref[:, p] = total[p]
+    half = experts // 2
+    total = total.astype(BF).reshape(2, line, half, slots, columns)
+    for part in range(2):
+        for p in range(line):
+            out_ref[part * half : (part + 1) * half, p] = total[part, p]
 
 
 def outputs_of(place, hidden, own, other, experts, slots):
@@ -136,29 +175,26 @@
     place = lax.axis_index("zi")
     share = units // lax.axis_size("dp")
     down = lax.dynamic_slice_in_dim(turned, 2 * units + share * lax.axis_index("dp"), share, 0)
-
-    packed, weighting = packed_of(expert_ids, gate_scores, tokens, experts, slots)
-    arrived = lax.all_to_all(packed, ROWS_OF, split_axis=0, concat_axis=0, tiled=True)
-    rows = jnp.broadcast_to(arrived[None], (line,) + arrived.shape)
-    rows = lax.all_to_all(rows, "zi", split_axis=0, concat_axis=0, tiled=True)
-    rows = rows.reshape(line * experts, slots, width)
-
-    down = after(arrived, down).reshape(share, line, columns)
+    down = down.reshape(share, line, columns)
 
     def for_place(at):
         return lax.dynamic_index_in_dim(down, at, 1, keepdims=False)
 
     pieces = [for_place(place)] + [exchange(for_place(place ^ k), "zi", k) for k in range(1, line)]
-    pieces = jnp.stack(pieces)
-    shares = [pieces] + [exchange(pieces, "dp", k) for k in range(1, lax.axis_size("dp"))]
-    shares = jnp.stack(shares)
+    packed, weighting = packed_of(expert_ids, gate_scores, tokens, experts, slots)
+    mark = weighting[0, 0, 0, 0]
+    other = swap(jnp.where(mark == mark, turned[: 2 * units], jnp.zeros((), BF)))
+    arrived = lax.all_to_all(packed, ROWS_OF, split_axis=0, concat_axis=0, tiled=True)
+    shares = repeat_after(arrived, pieces, lax.axis_size("dp"))
+    shares = lax.all_to_all(shares, "dp", split_axis=0, concat_axis=0, tiled=True)
+    half = experts // 2
+    first = lax.all_gather(arrived[:half], "zi", axis=0, tiled=True)
+    second = lax.all_gather(arrived[half:], "zi", axis=0, tiled=True)
+    shares = copy_after(second, shares)
     other_shares = swap(shares)
-    up = after(arrived, turned[: 2 * units])
-    other = swap(turned)
-
-    hidden = hidden_of(rows, up, other)
+    hidden = hidden_of(first, second, turned, other)
     gathered = lax.all_gather(hidden, "zi", axis=0)
-    position = jnp.stack([place, lax.axis_index("dp")]).astype(jnp.int32)
+    position = place.astype(jnp.int32).reshape(1)
     done = outputs_of(position, gathered, shares, other_shares, experts, slots)
     done = done.reshape(experts * line, slots, columns)
     returned = lax.all_to_all(done, HOME, split_axis=0, concat_axis=0, tiled=True)

time: 194 us -> 163 us (0.84)
  waiting for transfers between devices: 46.8 us -> 9.98 us
  starting transfers between devices: 32.6 us -> 36.6 us
    all_to_all x1 -> x0, blocking collectives: 42.8 us -> none  [on_device(): lax.all_to_all(packed, ROWS_OF, split_axis=0, concat_axis=0, tiled=True)]
    all_gather x0 -> x2, blocking collectives: none -> 42.8 us  [the longest x1 22.8 us: on_device(): second = lax.all_gather(arrived[half:], 'zi', axis=0, tiled=True)]
    ppermute x6 -> x3, waiting for transfers between devices: 46.8 us -> 9.97 us  [exchange(): return lax.ppermute(array, axis, [(i, i ^ step) for i in range(size)])]
    all_to_all x1 -> x2, starting transfers between devices: 8.6 us -> 22.4 us  [the longest x1 17.7 us: on_device(): lax.all_to_all(packed, ROWS_OF, split_axis=0, concat_axis=0, tiled=True)]
    ppermute x6 -> x3, starting transfers between devices: 20.2 us -> 10.1 us  [exchange(): return lax.ppermute(array, axis, [(i, i ^ step) for i in range(size)])]
    select_n x2 -> x1, other arithmetic: 1.23 us -> 3.49 us  [on_device(): other = swap(jnp.where(mark == mark, turned[:2 * units], jnp.zeros((), BF)))]
    pallas_call x1 -> x3, Pallas kernels: 4.06 us -> 4.83 us  [the longest x1 3.5 us: hidden_of(): pl.pallas_call(up_kernel, grid=(1,), in_specs=whole(3) + [pl.BlockSpec((b...]
  transfers between devices with their start and end apart: 9 -> 7, of which waited for: 4 -> 3; matrix products, arithmetic and copies ran while one was open for 2% -> 4% of each run, Pallas kernels for 2% -> 3%
where the time goes in v14:
time: 163 us; the launch traced here: 162 us
  blocking collectives  96.7 us (59%)
  starting transfers between devices  36.6 us (22%)
  waiting for transfers between devices  9.98 us (6%)
  Pallas kernels  7.41 us (5%)
  local copies, waits for them, and re-layouts  4.97 us (3%)
  other arithmetic  3.49 us (2%)
    all_to_all x1, blocking collectives, on_device(): lax.all_to_all(done, HOME, split_axis=0, concat_axis=0, tiled=True)  35.2 us
    all_gather x1, blocking collectives, on_device(): second = lax.all_gather(arrived[half:], 'zi', axis=0, tiled=True)  22.8 us
    all_gather x1, blocking collectives, on_device(): first = lax.all_gather(arrived[:half], 'zi', axis=0, tiled=True)  20 us
    all_gather x1, blocking collectives, on_device(): gathered = lax.all_gather(hidden, 'zi', axis=0)  18.7 us
    all_to_all x1, starting transfers between devices, on_device(): lax.all_to_all(packed, ROWS_OF, split_axis=0, concat_axis=0, tiled=True)  17.7 us
    ppermute x3, starting transfers between devices, exchange(): return lax.ppermute(array, axis, [(i, i ^ step) for i in range(size)])  10.1 us
    ppermute x3, waiting for transfers between devices, exchange(): return lax.ppermute(array, axis, [(i, i ^ step) for i in range(size)])  9.97 us
    all_to_all x1, starting transfers between devices, on_device(): lax.all_to_all(shares, 'dp', split_axis=0, concat_axis=0, tiled=True)  4.7 us
  transfers between devices with their start and end apart: 7, of which 3 were waited for; matrix products, arithmetic and copies ran while one was open for 4% of the time, Pallas kernels for 3%

profile of v14, /device:TPU:24, one launch (start us, length us, event | category | flops | bytes accessed | tf_op | source)
XLA Modules:
  0.0 161.6 jit_solution(8537024390153042058)
XLA Ops:
  0.0 0.0 copy-start.1
  0.0 0.9 copy-done.1
  0.9 0.0 copy-start.2
  0.9 0.7 copy-done.2
  1.6 0.0 copy-start.3
  1.6 0.7 copy-done.3
  2.3 1.4 shard_map.46
  3.6 17.7 %all-to-all-start = ((bf16[16,4,3584]{2,1,0:T(4,128)(2,1)}), bf16[16,4,3584]{2,1,0:T(4,128)(2,1)S(1)}, u32[]{:S(2)}, u32[]{:S(2)}) async-start(bf16[16,4,3584]{2,1,0:T(4,128)(2,1)} %get-tuple-element.8), calls=%async_computation | async-start | bytes 917504 | tf_op jit(solution)/shard_map/all_to_all | solution.py:187
  21.3 0.5 slice.14
  23.1 3.5 %slice_select_fusion = bf16[384,3584]{1,0:T(8,128)(2,1)} fusion(bf16[576,3584]{1,0:T(8,128)(2,1)} %bitcast.36, pred[]{:T(512)} %bitcast.6), kind=kLoop, calls=%fused_computation | loop fusion | flops 1376256 | bytes 5505025 | tf_op jit(solution)/shard_map/jit(_where)/select_n | solution.py:186
  26.6 1.9 %collective-permute-start = (bf16[384,3584]{1,0:T(8,128)(2,1)}, bf16[384,3584]{1,0:T(8,128)(2,1)}, u32[]{:S(2)}, u32[]{:S(2)}) collective-permute-start(bf16[384,3584]{1,0:T(8,128)(2,1)} %slice_select_fusion), channel_id=1, source_target_pairs={{0,4},{4,0},{1,5},{5,1},{2,6},{6,2},{3,7},{7,3},{8,12},{12,8},{9,1... | collective-permute-start | bytes 8257544 | tf_op jit(solution)/shard_map/ppermute | solution.py:23
  28.6 1.0 dynamic-slice_bitcast_fusion
  29.6 0.1 reshape.21
  29.7 0.7 constant_dynamic-slice_fusion
  30.4 2.9 %collective-permute-start.1 = (bf16[48,896]{1,0:T(8,128)(2,1)S(1)}, bf16[48,896]{1,0:T(8,128)(2,1)S(1)}, u32[]{:S(2)}, u32[]{:S(2)}) collective-permute-start(bf16[48,896]{1,0:T(8,128)(2,1)S(1)} %bitcast.43), channel_id=1, source_target_pairs={{0,8},{8,0},{16,24},{24,16},{1,9},{9,1},{17,25},{25,17},{2,10},{10... | collective-permute-start | bytes 258056 | tf_op jit(solution)/shard_map/ppermute | solution.py:19
  33.4 3.4 %collective-permute-start.2 = (bf16[48,896]{1,0:T(8,128)(2,1)S(1)}, bf16[48,896]{1,0:T(8,128)(2,1)S(1)}, u32[]{:S(2)}, u32[]{:S(2)}) collective-permute-start(bf16[48,896]{1,0:T(8,128)(2,1)S(1)} %bitcast.44), channel_id=1, source_target_pairs={{0,16},{8,24},{16,0},{24,8},{1,17},{9,25},{17,1},{25,9},{2,18},{10... | collective-permute-start | bytes 258056 | tf_op jit(solution)/shard_map/ppermute | solution.py:19
  36.8 3.8 %collective-permute-start.3 = (bf16[48,896]{1,0:T(8,128)(2,1)S(1)}, bf16[48,896]{1,0:T(8,128)(2,1)S(1)}, u32[]{:S(2)}, u32[]{:S(2)}) collective-permute-start(bf16[48,896]{1,0:T(8,128)(2,1)S(1)} %bitcast.45), channel_id=1, source_target_pairs={{0,24},{8,16},{16,8},{24,0},{1,25},{9,17},{17,9},{25,1},{2,26},{10... | collective-permute-start | bytes 258056 | tf_op jit(solution)/shard_map/ppermute | solution.py:19
  40.6 5.3 %collective-permute-done.1.refs_1_ = bf16[48,896]{1,0:T(8,128)(2,1)S(1)} collective-permute-done((bf16[48,896]{1,0:T(8,128)(2,1)S(1)}, bf16[48,896]{1,0:T(8,128)(2,1)S(1)}, u32[]{:S(2)}, u32[]{:S(2)}) %collective-permute-start.1) | collective-permute-done | bytes 86048 | tf_op jit(solution)/shard_map/ppermute | solution.py:19
  45.9 0.8 collective-permute-done.2.refs_2_
  46.7 3.9 %collective-permute-done.3.refs_3_ = bf16[48,896]{1,0:T(8,128)(2,1)S(1)} collective-permute-done((bf16[48,896]{1,0:T(8,128)(2,1)S(1)}, bf16[48,896]{1,0:T(8,128)(2,1)S(1)}, u32[]{:S(2)}, u32[]{:S(2)}) %collective-permute-start.3) | collective-permute-done | bytes 86048 | tf_op jit(solution)/shard_map/ppermute | solution.py:19
  50.6 0.0 all-to-all-done._
  50.6 1.2 shard_map.48
  51.8 4.7 %all-to-all-start.1 = ((bf16[4,4,48,896]{3,2,1,0:T(8,128)(2,1)}), bf16[4,4,48,896]{3,2,1,0:T(8,128)(2,1)S(1)}, u32[]{:S(2)}, u32[]{:S(2)}) async-start(bf16[4,4,48,896]{3,2,1,0:T(8,128)(2,1)} %shard_map.48), calls=%async_computation.1 | async-start | bytes 2752512 | tf_op jit(solution)/shard_map/all_to_all | solution.py:189
  56.5 0.2 fusion.3
  56.7 22.8 %all_gather.13.second_ref._ = bf16[32,4,3584]{2,1,0:T(4,128)(2,1)S(1)} all-gather(bf16[8,4,3584]{2,1,0:T(4,128)(2,1)S(1)} %get-tuple-element.9), channel_id=1, replica_groups=mesh['x'=4,'zb'=4,'zi'=4,'c'=2,'dp'=4] {'zi'}, dimensions={0}, use_global_device_ids=true | all-gather | bytes 1146880 | tf_op jit(solution)/shard_map/all_gather | solution.py:192
  79.5 0.0 all-to-all-done.1.array_ref
  79.5 0.0 copy-start
  79.5 0.1 shard_map.49.own_ref
  79.6 2.2 %collective-permute-start.4 = (bf16[4,4,48,896]{3,2,1,0:T(8,128)(2,1)S(1)}, bf16[4,4,48,896]{3,2,1,0:T(8,128)(2,1)S(1)}, u32[]{:S(2)}, u32[]{:S(2)}) collective-permute-start(bf16[4,4,48,896]{3,2,1,0:T(8,128)(2,1)S(1)} %shard_map.49.own_ref), channel_id=1, source_target_pairs={{0,4},{4,0},{1,5},{5,1},{2,6},{6,2},{3,7},{7,3},{8,12},{12,8},{9,1... | collective-permute-start | bytes 4128776 | tf_op jit(solution)/shard_map/ppermute | solution.py:23
  81.8 20.0 %all_gather.12.first_ref = bf16[32,4,3584]{2,1,0:T(4,128)(2,1)S(1)} all-gather(bf16[8,4,3584]{2,1,0:T(4,128)(2,1)S(1)} %get-tuple-element.10), channel_id=1, replica_groups=mesh['x'=4,'zb'=4,'zi'=4,'c'=2,'dp'=4] {'zi'}, dimensions={0}, use_global_device_ids=true | all-gather | bytes 1146880 | tf_op jit(solution)/shard_map/all_gather | solution.py:191
  101.8 0.0 collective-permute-done.other_ref
  101.8 0.0 copy-done
  101.8 3.5 %shard_map.47 = bf16[256,384]{1,0:T(8,128)(2,1)S(1)} custom-call(bf16[32,4,3584]{2,1,0:T(4,128)(2,1)S(1)} %all_gather.12.first_ref, bf16[32,4,3584]{2,1,0:T(4,128)(2,1)S(1)} %all_gather.13.second_ref._, bf16[576,3584]{1,0:T(8,128)(2,1)S(1)} %bitcast.37, bf16[384,3584]{1,0:T(8,128)(2,1)} %collective-permute-done.other_ref), custom_call_target="tpu_custom_call" | custom-call | tf_op jit(solution)/shard_map/pallas_call | solution.py:130
  105.3 18.7 %all-gather = bf16[1024,384]{1,0:T(8,128)(2,1)S(1)} all-gather(bf16[256,384]{1,0:T(8,128)(2,1)S(1)} %shard_map.47), channel_id=2, replica_groups=mesh['x'=4,'zb'=4,'zi'=4,'c'=2,'dp'=4] {'zi'}, dimensions={0}, use_global_device_ids=true | all-gather | bytes 983040 | tf_op jit(solution)/shard_map/all_gather | solution.py:196
  124.0 0.0 collective-permute-done.4.other_ref
  124.0 1.2 shard_map.50
  125.2 35.2 %all_to_all.15 = bf16[64,4,896]{2,1,0:T(4,128)(2,1)S(1)} all-to-all(bf16[64,4,896]{2,1,0:T(4,128)(2,1)S(1)} %bitcast.39), channel_id=1, replica_groups=mesh['x'=4,'zb'=4,'zi'=4,'c'=2,'dp'=4] {'x','zb','zi'}, dimensions={0} | all-to-all | bytes 917504 | tf_op jit(solution)/shard_map/all_to_all | solution.py:200
  160.4 0.2 reshape.28
  160.6 1.0 fusion
  (4 shorter events, 0.1 us)
Async XLA Ops:
  0.0 0.9 copy-start.1
  0.9 0.7 copy-start.2
  1.6 0.7 copy-start.3
  3.6 47.0 %all-to-all-start = ((bf16[16,4,3584]{2,1,0:T(4,128)(2,1)}), bf16[16,4,3584]{2,1,0:T(4,128)(2,1)S(1)}, u32[]{:S(2)}, u32[]{:S(2)}) async-start(bf16[16,4,3584]{2,1,0:T(4,128)(2,1)} %get-tuple-element.8), calls=%async_computation | async-start | bytes 917504 | tf_op jit(solution)/shard_map/all_to_all | solution.py:187
  26.6 75.1 %collective-permute-start = (bf16[384,3584]{1,0:T(8,128)(2,1)}, bf16[384,3584]{1,0:T(8,128)(2,1)}, u32[]{:S(2)}, u32[]{:S(2)}) collective-permute-start(bf16[384,3584]{1,0:T(8,128)(2,1)} %slice_select_fusion), channel_id=1, source_target_pairs={{0,4},{4,0},{1,5},{5,1},{2,6},{6,2},{3,7},{7,3},{8,12},{12,8},{9,1... | collective-permute-start | bytes 8257544 | tf_op jit(solution)/shard_map/ppermute | solution.py:23
  30.4 15.5 %collective-permute-start.1 = (bf16[48,896]{1,0:T(8,128)(2,1)S(1)}, bf16[48,896]{1,0:T(8,128)(2,1)S(1)}, u32[]{:S(2)}, u32[]{:S(2)}) collective-permute-start(bf16[48,896]{1,0:T(8,128)(2,1)S(1)} %bitcast.43), channel_id=1, source_target_pairs={{0,8},{8,0},{16,24},{24,16},{1,9},{9,1},{17,25},{25,17},{2,10},{10... | collective-permute-start | bytes 258056 | tf_op jit(solution)/shard_map/ppermute | solution.py:19
  33.4 13.3 %collective-permute-start.2 = (bf16[48,896]{1,0:T(8,128)(2,1)S(1)}, bf16[48,896]{1,0:T(8,128)(2,1)S(1)}, u32[]{:S(2)}, u32[]{:S(2)}) collective-permute-start(bf16[48,896]{1,0:T(8,128)(2,1)S(1)} %bitcast.44), channel_id=1, source_target_pairs={{0,16},{8,24},{16,0},{24,8},{1,17},{9,25},{17,1},{25,9},{2,18},{10... | collective-permute-start | bytes 258056 | tf_op jit(solution)/shard_map/ppermute | solution.py:19
  36.8 13.8 %collective-permute-start.3 = (bf16[48,896]{1,0:T(8,128)(2,1)S(1)}, bf16[48,896]{1,0:T(8,128)(2,1)S(1)}, u32[]{:S(2)}, u32[]{:S(2)}) collective-permute-start(bf16[48,896]{1,0:T(8,128)(2,1)S(1)} %bitcast.45), channel_id=1, source_target_pairs={{0,24},{8,16},{16,8},{24,0},{1,25},{9,17},{17,9},{25,1},{2,26},{10... | collective-permute-start | bytes 258056 | tf_op jit(solution)/shard_map/ppermute | solution.py:19
  51.8 27.6 %all-to-all-start.1 = ((bf16[4,4,48,896]{3,2,1,0:T(8,128)(2,1)}), bf16[4,4,48,896]{3,2,1,0:T(8,128)(2,1)S(1)}, u32[]{:S(2)}, u32[]{:S(2)}) async-start(bf16[4,4,48,896]{3,2,1,0:T(8,128)(2,1)} %shard_map.48), calls=%async_computation.1 | async-start | bytes 2752512 | tf_op jit(solution)/shard_map/all_to_all | solution.py:189
  79.5 22.3 %copy-start = (bf16[1,3584,576]{1,2,0:T(8,128)(2,1)S(1)}, bf16[1,3584,576]{1,2,0:T(8,128)(2,1)}, u32[]{:S(2)}) copy-start(bf16[1,3584,576]{1,2,0:T(8,128)(2,1)} %param.7) | copy-start | bytes 12386308
  79.6 44.4 %collective-permute-start.4 = (bf16[4,4,48,896]{3,2,1,0:T(8,128)(2,1)S(1)}, bf16[4,4,48,896]{3,2,1,0:T(8,128)(2,1)S(1)}, u32[]{:S(2)}, u32[]{:S(2)}) collective-permute-start(bf16[4,4,48,896]{3,2,1,0:T(8,128)(2,1)S(1)} %shard_map.49.own_ref), channel_id=1, source_target_pairs={{0,4},{4,0},{1,5},{5,1},{2,6},{6,2},{3,7},{7,3},{8,12},{12,8},{9,1... | collective-permute-start | bytes 4128776 | tf_op jit(solution)/shard_map/ppermute | solution.py:23

commit v15 on v14

--- a/solution.py
+++ b/solution.py
@@ -73,7 +73,7 @@
     )(expert_ids.transpose(0, 2, 1), gate_scores.transpose(0, 2, 1), tokens)
 
 
-def repeat_kernel(_, *refs):
+def repeat_kernel(_, __, *refs):
     arrays, out_ref, done = refs[:-2], refs[-2], refs[-1]
     copies = [
         pltpu.make_async_copy(ref, out_ref.at[copy, k], done.at[copy, k])
@@ -89,30 +89,16 @@
 def repeat_after(earlier, arrays, times):
     return pl.pallas_call(
         repeat_kernel,
-        in_specs=[ANYWHERE] + whole(len(arrays)),
+        in_specs=[ANYWHERE] * 2 + whole(len(arrays)),
         out_specs=pl.BlockSpec(memory_space=pltpu.HBM),
         out_shape=jax.ShapeDtypeStruct((times, len(arrays)) + arrays[0].shape, BF),
         scratch_shapes=[pltpu.SemaphoreType.DMA((times, len(arrays)))],
-        compiler_params=pltpu.CompilerParams(vmem_limit_bytes=53 << 20),
-    )(earlier, *arrays)
-
-
-def copy_kernel(_, array_ref, out_ref):
-    out_ref[...] = array_ref[...]
-
-
-def copy_after(earlier, array):
-    return pl.pallas_call(
-        copy_kernel,
-        in_specs=[ANYWHERE] + whole(1),
-        out_specs=whole(1)[0],
-        out_shape=jax.ShapeDtypeStruct(array.shape, array.dtype),
-        compiler_params=pltpu.CompilerParams(vmem_limit_bytes=16 << 20),
-    )(earlier, array)
+        compiler_params=pltpu.CompilerParams(vmem_limit_bytes=50 << 20),
+    )(*earlier, *arrays)
 
 
 def up_kernel(first_ref, second_ref, own_ref, other_ref, out_ref):
-    units = own_ref.shape[0] // 3
+    units = own_ref.shape[0] // 2
     width = own_ref.shape[1]
     rows = [ref[...].reshape(-1, width) for ref in (first_ref, second_ref)]
     rows = jnp.concatenate(rows, axis=0)
@@ -126,7 +112,7 @@
 
 def hidden_of(first, second, own, other):
     count = 2 * first.shape[0] * first.shape[1]
-    both = own.shape[0] // 3 * 2
+    both = own.shape[0]
     return pl.pallas_call(
         up_kernel,
         grid=(1,),
@@ -137,13 +123,15 @@
     )(first, second, own, other)
 
 
-def down_kernel(place_ref, hidden_ref, own_ref, other_ref, out_ref):
-    shares, line = own_ref.shape[:2]
+def down_kernel(place_ref, hidden_ref, shares_ref, out_ref):
+    shares, cores, line = shares_ref.shape[:3]
     experts, _, slots, columns = out_ref.shape
     total = jnp.zeros((line * experts * slots, columns), F32)
     for at in range(line):
         k = place_ref[0] ^ at
-        weights = [ref[y, k] for ref in (own_ref, other_ref) for y in range(shares)]
+        weights = [
+            shares_ref[y, place_ref[1] ^ core, k] for core in range(cores) for y in range(shares)
+        ]
         weights = jnp.concatenate(weights, axis=0)
         total += jnp.dot(hidden_ref[at], weights, preferred_element_type=F32)
     half = experts // 2
@@ -153,14 +141,14 @@
             out_ref[part * half : (part + 1) * half, p] = total[part, p]
 
 
-def outputs_of(place, hidden, own, other, experts, slots):
+def outputs_of(place, hidden, shares, experts, slots):
     return pl.pallas_call(
         down_kernel,
-        in_specs=[pl.BlockSpec(memory_space=pltpu.SMEM)] + whole(3),
+        in_specs=[pl.BlockSpec(memory_space=pltpu.SMEM)] + whole(2),
         out_specs=whole(1)[0],
-        out_shape=jax.ShapeDtypeStruct((experts, hidden.shape[0], slots, own.shape[3]), BF),
+        out_shape=jax.ShapeDtypeStruct((experts, hidden.shape[0], slots, shares.shape[-1]), BF),
         compiler_params=pltpu.CompilerParams(vmem_limit_bytes=16 << 20),
-    )(place, hidden, own, other)
+    )(place, hidden, shares)
 
 
 def on_device(tokens, expert_ids, gate_scores, expert_weights):
@@ -180,22 +168,23 @@
     def for_place(at):
         return lax.dynamic_index_in_dim(down, at, 1, keepdims=False)
 
+    other = swap(turned)
     pieces = [for_place(place)] + [exchange(for_place(place ^ k), "zi", k) for k in range(1, line)]
     packed, weighting = packed_of(expert_ids, gate_scores, tokens, experts, slots)
-    mark = weighting[0, 0, 0, 0]
-    other = swap(jnp.where(mark == mark, turned[: 2 * units], jnp.zeros((), BF)))
     arrived = lax.all_to_all(packed, ROWS_OF, split_axis=0, concat_axis=0, tiled=True)
-    shares = repeat_after(arrived, pieces, lax.axis_size("dp"))
-    shares = lax.all_to_all(shares, "dp", split_axis=0, concat_axis=0, tiled=True)
+    mark = pieces[1][0, 0]
+    up = jnp.where(mark == mark, turned[: 2 * units], jnp.zeros((), BF))
+    replicas, cores = lax.axis_size("dp"), lax.axis_size("c")
+    shares = repeat_after((arrived, up), pieces, replicas * cores)
+    shares = lax.all_to_all(shares, ("dp", "c"), split_axis=0, concat_axis=0, tiled=True)
+    shares = shares.reshape((replicas, cores) + shares.shape[1:])
     half = experts // 2
     first = lax.all_gather(arrived[:half], "zi", axis=0, tiled=True)
     second = lax.all_gather(arrived[half:], "zi", axis=0, tiled=True)
-    shares = copy_after(second, shares)
-    other_shares = swap(shares)
-    hidden = hidden_of(first, second, turned, other)
+    hidden = hidden_of(first, second, up, other)
     gathered = lax.all_gather(hidden, "zi", axis=0)
-    position = place.astype(jnp.int32).reshape(1)
-    done = outputs_of(position, gathered, shares, other_shares, experts, slots)
+    position = jnp.stack([place, lax.axis_index("c")]).astype(jnp.int32)
+    done = outputs_of(position, gathered, shares, experts, slots)
     done = done.reshape(experts * line, slots, columns)
     returned = lax.all_to_all(done, HOME, split_axis=0, concat_axis=0, tiled=True)
     returned = returned.reshape(experts, line, batches, capacity, columns).astype(F32)

time: 163 us -> 167 us (1.025)
  waiting for transfers between devices: 9.98 us -> 14.8 us
  Pallas kernels: 7.41 us -> 9.68 us
  starting transfers between devices: 36.6 us -> 34.4 us
    ppermute x3, waiting for transfers between devices: 9.97 us -> 14.7 us  [exchange(): return lax.ppermute(array, axis, [(i, i ^ step) for i in range(size)])]
    all_gather x1, blocking collectives: 22.8 us -> 19.9 us  [on_device(): second = lax.all_gather(arrived[half:], 'zi', axis=0, tiled=True)]
    ppermute x2 -> x1, starting transfers between devices: 4.09 us -> 1.91 us  [swap(): return lax.ppermute(array, 'c', [(0, 1), (1, 0)])]
    all_gather x1, blocking collectives: 20 us -> 21.9 us  [on_device(): first = lax.all_gather(arrived[:half], 'zi', axis=0, tiled=True)]
    pallas_call x1, Pallas kernels: 1.19 us -> 2.98 us  [outputs_of(): pl.pallas_call(down_kernel, in_specs=[pl.BlockSpec(memory_space=pltpu.SME...]
  transfers between devices with their start and end apart: 7 -> 6, of which waited for: 3 -> 1; matrix products, arithmetic and copies ran while one was open for 4% -> 4% of each run, Pallas kernels for 3% -> 4%
where the time goes in v15:
time: 167 us; the launch traced here: 166 us
  blocking collectives  95.7 us (57%)
  starting transfers between devices  34.4 us (21%)
  waiting for transfers between devices  14.8 us (9%)
  Pallas kernels  9.68 us (6%)
  local copies, waits for them, and re-layouts  4.96 us (3%)
  other arithmetic  3.58 us (2%)
    all_to_all x1, blocking collectives, on_device(): lax.all_to_all(done, HOME, split_axis=0, concat_axis=0, tiled=True)  36.5 us
    all_gather x1, blocking collectives, on_device(): first = lax.all_gather(arrived[:half], 'zi', axis=0, tiled=True)  21.9 us
    all_gather x1, blocking collectives, on_device(): second = lax.all_gather(arrived[half:], 'zi', axis=0, tiled=True)  19.9 us
    all_to_all x1, starting transfers between devices, on_device(): lax.all_to_all(packed, ROWS_OF, split_axis=0, concat_axis=0, tiled=True)  17.7 us
    all_gather x1, blocking collectives, on_device(): gathered = lax.all_gather(hidden, 'zi', axis=0)  17.5 us
    ppermute x3, waiting for transfers between devices, exchange(): return lax.ppermute(array, axis, [(i, i ^ step) for i in range(size)])  14.7 us
    ppermute x3, starting transfers between devices, exchange(): return lax.ppermute(array, axis, [(i, i ^ step) for i in range(size)])  10.1 us
    all_to_all x1, starting transfers between devices, on_device(): lax.all_to_all(shares, ('dp', 'c'), split_axis=0, concat_axis=0, tiled=True)  4.7 us
  transfers between devices with their start and end apart: 6, of which 1 were waited for; matrix products, arithmetic and copies ran while one was open for 4% of the time, Pallas kernels for 4%

profile of v15, /device:TPU:24, one launch (start us, length us, event | category | flops | bytes accessed | tf_op | source)
XLA Modules:
  0.0 165.6 jit_solution(5511871276598537653)
XLA Ops:
  0.0 1.9 %collective-permute-start.1 = (bf16[576,3584]{1,0:T(8,128)(2,1)}, bf16[576,3584]{1,0:T(8,128)(2,1)}, u32[]{:S(2)}, u32[]{:S(2)}) collective-permute-start(bf16[576,3584]{1,0:T(8,128)(2,1)} %bitcast.43), channel_id=1, source_target_pairs={{0,4},{4,0},{1,5},{5,1},{2,6},{6,2},{3,7},{7,3},{8,12},{12,8},{9,1... | collective-permute-start | bytes 12386312 | tf_op jit(solution)/shard_map/ppermute | solution.py:23
  1.9 0.0 copy-start.1
  1.9 0.9 copy-done.1
  2.8 0.0 copy-start.2
  2.8 0.7 copy-done.2
  3.5 0.0 copy-start.3
  3.5 0.7 copy-done.3
  4.2 1.4 shard_map.46
  5.6 17.7 %all-to-all-start = ((bf16[16,4,3584]{2,1,0:T(4,128)(2,1)}), bf16[16,4,3584]{2,1,0:T(4,128)(2,1)S(1)}, u32[]{:S(2)}, u32[]{:S(2)}) async-start(bf16[16,4,3584]{2,1,0:T(4,128)(2,1)} %get-tuple-element.8), calls=%async_computation | async-start | bytes 917504 | tf_op jit(solution)/shard_map/all_to_all | solution.py:174
  23.3 1.0 dynamic-slice_bitcast_fusion
  24.3 0.1 reshape.20
  24.4 0.7 constant_dynamic-slice_fusion
  25.1 2.9 %collective-permute-start = (bf16[48,896]{1,0:T(8,128)(2,1)S(1)}, bf16[48,896]{1,0:T(8,128)(2,1)S(1)}, u32[]{:S(2)}, u32[]{:S(2)}) collective-permute-start(bf16[48,896]{1,0:T(8,128)(2,1)S(1)} %bitcast.47), channel_id=1, source_target_pairs={{0,8},{8,0},{16,24},{24,16},{1,9},{9,1},{17,25},{25,17},{2,10},{10... | collective-permute-start | bytes 258056 | tf_op jit(solution)/shard_map/ppermute | solution.py:19
  28.1 3.4 %collective-permute-start.2 = (bf16[48,896]{1,0:T(8,128)(2,1)S(1)}, bf16[48,896]{1,0:T(8,128)(2,1)S(1)}, u32[]{:S(2)}, u32[]{:S(2)}) collective-permute-start(bf16[48,896]{1,0:T(8,128)(2,1)S(1)} %bitcast.45), channel_id=1, source_target_pairs={{0,16},{8,24},{16,0},{24,8},{1,17},{9,25},{17,1},{25,9},{2,18},{10... | collective-permute-start | bytes 258056 | tf_op jit(solution)/shard_map/ppermute | solution.py:19
  31.5 3.8 %collective-permute-start.3 = (bf16[48,896]{1,0:T(8,128)(2,1)S(1)}, bf16[48,896]{1,0:T(8,128)(2,1)S(1)}, u32[]{:S(2)}, u32[]{:S(2)}) collective-permute-start(bf16[48,896]{1,0:T(8,128)(2,1)S(1)} %bitcast.46), channel_id=1, source_target_pairs={{0,24},{8,16},{16,8},{24,0},{1,25},{9,17},{17,9},{25,1},{2,26},{10... | collective-permute-start | bytes 258056 | tf_op jit(solution)/shard_map/ppermute | solution.py:19
  35.3 14.7 %collective-permute-done.refs_1_ = bf16[48,896]{1,0:T(8,128)(2,1)S(1)} collective-permute-done((bf16[48,896]{1,0:T(8,128)(2,1)S(1)}, bf16[48,896]{1,0:T(8,128)(2,1)S(1)}, u32[]{:S(2)}, u32[]{:S(2)}) %collective-permute-start) | collective-permute-done | bytes 86048 | tf_op jit(solution)/shard_map/ppermute | solution.py:19
  50.1 0.5 slice.18
  51.9 3.5 %slice_select_fusion.own_ref.__ = bf16[384,3584]{1,0:T(8,128)(2,1)} fusion(bf16[576,3584]{1,0:T(8,128)(2,1)} %bitcast.44, pred[]{:T(512)} %bitcast.7), kind=kLoop, calls=%fused_computation | loop fusion | flops 1376256 | bytes 5505025 | tf_op jit(solution)/shard_map/jit(_where)/select_n | solution.py:176
  55.4 0.0 collective-permute-done.2.refs_2_
  55.4 0.0 collective-permute-done.3.refs_3_
  55.4 0.0 all-to-all-done._
  55.4 1.8 %shard_map.48 = bf16[8,4,48,896]{3,2,1,0:T(8,128)(2,1)} custom-call(bf16[16,4,3584]{2,1,0:T(4,128)(2,1)S(1)} %all-to-all-done._, bf16[384,3584]{1,0:T(8,128)(2,1)} %slice_select_fusion.own_ref.__, bf16[48,896]{1,0:T(8,128)(2,1)S(1)} %bitcast.40, bf16[48,896]{1,0:T(8,128)(2,1)S(1)} %collective-permute-done.refs_1_, ...), custom_call_target="tpu_custom_call" | custom-call | tf_op jit(solution)/shard_map/pallas_call | solution.py:90
  57.2 4.7 %all-to-all-start.1 = ((bf16[8,4,48,896]{3,2,1,0:T(8,128)(2,1)}), bf16[8,4,48,896]{3,2,1,0:T(8,128)(2,1)}, u32[]{:S(2)}, u32[]{:S(2)}) async-start(bf16[8,4,48,896]{3,2,1,0:T(8,128)(2,1)} %shard_map.48), calls=%async_computation.1 | async-start | bytes 5505024 | tf_op jit(solution)/shard_map/all_to_all | solution.py:179
  61.9 0.0 copy-start
  61.9 0.1 pad_add_fusion.place_ref
  62.0 0.2 fusion.3
  62.1 21.9 %all_gather.12.first_ref = bf16[32,4,3584]{2,1,0:T(4,128)(2,1)S(1)} all-gather(bf16[8,4,3584]{2,1,0:T(4,128)(2,1)S(1)} %get-tuple-element.10), channel_id=1, replica_groups=mesh['x'=4,'zb'=4,'zi'=4,'c'=2,'dp'=4] {'zi'}, dimensions={0}, use_global_device_ids=true | all-gather | bytes 1146880 | tf_op jit(solution)/shard_map/all_gather | solution.py:182
  84.0 19.9 %all_gather.13.second_ref = bf16[32,4,3584]{2,1,0:T(4,128)(2,1)S(1)} all-gather(bf16[8,4,3584]{2,1,0:T(4,128)(2,1)S(1)} %get-tuple-element.9), channel_id=1, replica_groups=mesh['x'=4,'zb'=4,'zi'=4,'c'=2,'dp'=4] {'zi'}, dimensions={0}, use_global_device_ids=true | all-gather | bytes 1146880 | tf_op jit(solution)/shard_map/all_gather | solution.py:183
  103.9 0.0 collective-permute-done.1.other_ref
  103.9 0.0 copy-done
  103.9 3.5 %shard_map.47 = bf16[256,384]{1,0:T(8,128)(2,1)S(1)} custom-call(bf16[32,4,3584]{2,1,0:T(4,128)(2,1)S(1)} %all_gather.12.first_ref, bf16[32,4,3584]{2,1,0:T(4,128)(2,1)S(1)} %all_gather.13.second_ref, bf16[384,3584]{1,0:T(8,128)(2,1)S(1)} %copy-done, bf16[576,3584]{1,0:T(8,128)(2,1)} %collective-permute-done.1.other_ref), custom_call_target="tpu_custom_call" | custom-call | tf_op jit(solution)/shard_map/pallas_call | solution.py:116
  107.4 17.5 %all-gather = bf16[1024,384]{1,0:T(8,128)(2,1)S(1)} all-gather(bf16[256,384]{1,0:T(8,128)(2,1)S(1)} %shard_map.47), channel_id=2, replica_groups=mesh['x'=4,'zb'=4,'zi'=4,'c'=2,'dp'=4] {'zi'}, dimensions={0}, use_global_device_ids=true | all-gather | bytes 983040 | tf_op jit(solution)/shard_map/all_gather | solution.py:185
  124.9 0.0 all-to-all-done.1
  124.9 3.0 %shard_map.49 = bf16[16,4,4,896]{3,2,1,0:T(4,128)(2,1)S(1)} custom-call(s32[2]{0:T(128)S(1)} %pad_add_fusion.place_ref, bf16[4,256,384]{2,1,0:T(8,128)(2,1)S(1)} %bitcast.38, bf16[4,2,4,48,896]{4,3,2,1,0:T(8,128)(2,1)} %bitcast.12.shares_ref), custom_call_target="tpu_custom_call" | custom-call | tf_op jit(solution)/shard_map/pallas_call | solution.py:145
  127.9 36.5 %all_to_all.15 = bf16[64,4,896]{2,1,0:T(4,128)(2,1)S(1)} all-to-all(bf16[64,4,896]{2,1,0:T(4,128)(2,1)S(1)} %bitcast.39), channel_id=1, replica_groups=mesh['x'=4,'zb'=4,'zi'=4,'c'=2,'dp'=4] {'x','zb','zi'}, dimensions={0} | all-to-all | bytes 917504 | tf_op jit(solution)/shard_map/all_to_all | solution.py:189
  164.4 0.2 reshape.28
  164.5 1.0 fusion
  (4 shorter events, 0.1 us)
Async XLA Ops:
  0.0 103.9 %collective-permute-start.1 = (bf16[576,3584]{1,0:T(8,128)(2,1)}, bf16[576,3584]{1,0:T(8,128)(2,1)}, u32[]{:S(2)}, u32[]{:S(2)}) collective-permute-start(bf16[576,3584]{1,0:T(8,128)(2,1)} %bitcast.43), channel_id=1, source_target_pairs={{0,4},{4,0},{1,5},{5,1},{2,6},{6,2},{3,7},{7,3},{8,12},{12,8},{9,1... | collective-permute-start | bytes 12386312 | tf_op jit(solution)/shard_map/ppermute | solution.py:23
  1.9 0.9 copy-start.1
  2.8 0.7 copy-start.2
  3.5 0.7 copy-start.3
  5.6 49.8 %all-to-all-start = ((bf16[16,4,3584]{2,1,0:T(4,128)(2,1)}), bf16[16,4,3584]{2,1,0:T(4,128)(2,1)S(1)}, u32[]{:S(2)}, u32[]{:S(2)}) async-start(bf16[16,4,3584]{2,1,0:T(4,128)(2,1)} %get-tuple-element.8), calls=%async_computation | async-start | bytes 917504 | tf_op jit(solution)/shard_map/all_to_all | solution.py:174
  25.1 24.9 %collective-permute-start = (bf16[48,896]{1,0:T(8,128)(2,1)S(1)}, bf16[48,896]{1,0:T(8,128)(2,1)S(1)}, u32[]{:S(2)}, u32[]{:S(2)}) collective-permute-start(bf16[48,896]{1,0:T(8,128)(2,1)S(1)} %bitcast.47), channel_id=1, source_target_pairs={{0,8},{8,0},{16,24},{24,16},{1,9},{9,1},{17,25},{25,17},{2,10},{10... | collective-permute-start | bytes 258056 | tf_op jit(solution)/shard_map/ppermute | solution.py:19
  28.1 27.3 %collective-permute-start.2 = (bf16[48,896]{1,0:T(8,128)(2,1)S(1)}, bf16[48,896]{1,0:T(8,128)(2,1)S(1)}, u32[]{:S(2)}, u32[]{:S(2)}) collective-permute-start(bf16[48,896]{1,0:T(8,128)(2,1)S(1)} %bitcast.45), channel_id=1, source_target_pairs={{0,16},{8,24},{16,0},{24,8},{1,17},{9,25},{17,1},{25,9},{2,18},{10... | collective-permute-start | bytes 258056 | tf_op jit(solution)/shard_map/ppermute | solution.py:19
  31.5 23.9 %collective-permute-start.3 = (bf16[48,896]{1,0:T(8,128)(2,1)S(1)}, bf16[48,896]{1,0:T(8,128)(2,1)S(1)}, u32[]{:S(2)}, u32[]{:S(2)}) collective-permute-start(bf16[48,896]{1,0:T(8,128)(2,1)S(1)} %bitcast.46), channel_id=1, source_target_pairs={{0,24},{8,16},{16,8},{24,0},{1,25},{9,17},{17,9},{25,1},{2,26},{10... | collective-permute-start | bytes 258056 | tf_op jit(solution)/shard_map/ppermute | solution.py:19
  57.2 67.7 %all-to-all-start.1 = ((bf16[8,4,48,896]{3,2,1,0:T(8,128)(2,1)}), bf16[8,4,48,896]{3,2,1,0:T(8,128)(2,1)}, u32[]{:S(2)}, u32[]{:S(2)}) async-start(bf16[8,4,48,896]{3,2,1,0:T(8,128)(2,1)} %shard_map.48), calls=%async_computation.1 | async-start | bytes 5505024 | tf_op jit(solution)/shard_map/all_to_all | solution.py:179
  61.9 42.0 %copy-start = (bf16[384,3584]{1,0:T(8,128)(2,1)S(1)}, bf16[384,3584]{1,0:T(8,128)(2,1)}, u32[]{:S(2)}) copy-start(bf16[384,3584]{1,0:T(8,128)(2,1)} %slice_select_fusion.own_ref.__) | copy-start | bytes 8257540

commit v16 on v15

--- a/solution.py
+++ b/solution.py
@@ -73,7 +73,7 @@
     )(expert_ids.transpose(0, 2, 1), gate_scores.transpose(0, 2, 1), tokens)
 
 
-def repeat_kernel(_, __, *refs):
+def repeat_kernel(_, *refs):
     arrays, out_ref, done = refs[:-2], refs[-2], refs[-1]
     copies = [
         pltpu.make_async_copy(ref, out_ref.at[copy, k], done.at[copy, k])
@@ -89,12 +89,12 @@
 def repeat_after(earlier, arrays, times):
     return pl.pallas_call(
         repeat_kernel,
-        in_specs=[ANYWHERE] * 2 + whole(len(arrays)),
+        in_specs=[ANYWHERE] + whole(len(arrays)),
         out_specs=pl.BlockSpec(memory_space=pltpu.HBM),
         out_shape=jax.ShapeDtypeStruct((times, len(arrays)) + arrays[0].shape, BF),
         scratch_shapes=[pltpu.SemaphoreType.DMA((times, len(arrays)))],
-        compiler_params=pltpu.CompilerParams(vmem_limit_bytes=50 << 20),
-    )(*earlier, *arrays)
+        compiler_params=pltpu.CompilerParams(vmem_limit_bytes=53 << 20),
+    )(earlier, *arrays)
 
 
 def up_kernel(first_ref, second_ref, own_ref, other_ref, out_ref):
@@ -168,14 +168,14 @@
     def for_place(at):
         return lax.dynamic_index_in_dim(down, at, 1, keepdims=False)
 
-    other = swap(turned)
     pieces = [for_place(place)] + [exchange(for_place(place ^ k), "zi", k) for k in range(1, line)]
     packed, weighting = packed_of(expert_ids, gate_scores, tokens, experts, slots)
+    mark = weighting[0, 0, 0, 0]
+    up = jnp.where(mark == mark, turned[: 2 * units], jnp.zeros((), BF))
+    other = swap(up)
     arrived = lax.all_to_all(packed, ROWS_OF, split_axis=0, concat_axis=0, tiled=True)
-    mark = pieces[1][0, 0]
-    up = jnp.where(mark == mark, turned[: 2 * units], jnp.zeros((), BF))
     replicas, cores = lax.axis_size("dp"), lax.axis_size("c")
-    shares = repeat_after((arrived, up), pieces, replicas * cores)
+    shares = repeat_after(arrived, pieces, replicas * cores)
     shares = lax.all_to_all(shares, ("dp", "c"), split_axis=0, concat_axis=0, tiled=True)
     shares = shares.reshape((replicas, cores) + shares.shape[1:])
     half = experts // 2

time: 167 us -> 162 us (0.970)
  waiting for transfers between devices: 14.8 us -> 10.2 us
  local copies, waits for them, and re-layouts: 4.96 us -> 6.75 us
    ppermute x3, waiting for transfers between devices: 14.7 us -> 10.2 us  [exchange(): return lax.ppermute(array, axis, [(i, i ^ step) for i in range(size)])]
    all_to_all x1, blocking collectives: 36.5 us -> 33.3 us  [on_device(): lax.all_to_all(done, HOME, split_axis=0, concat_axis=0, tiled=True)]
    all_gather x1, blocking collectives: 21.9 us -> 23.7 us  [on_device(): first = lax.all_gather(arrived[:half], 'zi', axis=0, tiled=True)]
  transfers between devices with their start and end apart: 6 -> 6, of which waited for: 1 -> 2; matrix products, arithmetic and copies ran while one was open for 4% -> 4% of each run, Pallas kernels for 4% -> 3%
where the time goes in v16:
time: 162 us; the launch traced here: 160 us
  blocking collectives  94.4 us (58%)
  starting transfers between devices  34.4 us (21%)
  waiting for transfers between devices  10.2 us (6%)
  Pallas kernels  9.72 us (6%)
  local copies, waits for them, and re-layouts  6.75 us (4%)
  other arithmetic  2.03 us (1%)
    all_to_all x1, blocking collectives, on_device(): lax.all_to_all(done, HOME, split_axis=0, concat_axis=0, tiled=True)  33.3 us
    all_gather x1, blocking collectives, on_device(): first = lax.all_gather(arrived[:half], 'zi', axis=0, tiled=True)  23.7 us
    all_gather x1, blocking collectives, on_device(): second = lax.all_gather(arrived[half:], 'zi', axis=0, tiled=True)  19.9 us
    all_to_all x1, starting transfers between devices, on_device(): lax.all_to_all(packed, ROWS_OF, split_axis=0, concat_axis=0, tiled=True)  17.7 us
    all_gather x1, blocking collectives, on_device(): gathered = lax.all_gather(hidden, 'zi', axis=0)  17.5 us
    ppermute x3, waiting for transfers between devices, exchange(): return lax.ppermute(array, axis, [(i, i ^ step) for i in range(size)])  10.2 us
    ppermute x3, starting transfers between devices, exchange(): return lax.ppermute(array, axis, [(i, i ^ step) for i in range(size)])  10.1 us
    all_to_all x1, starting transfers between devices, on_device(): lax.all_to_all(shares, ('dp', 'c'), split_axis=0, concat_axis=0, tiled=True)  4.75 us
  transfers between devices with their start and end apart: 6, of which 2 were waited for; matrix products, arithmetic and copies ran while one was open for 4% of the time, Pallas kernels for 3%

profile of v16, /device:TPU:24, one launch (start us, length us, event | category | flops | bytes accessed | tf_op | source)
XLA Modules:
  0.0 160.0 jit_solution(7144897839564467164)
XLA Ops:
  0.0 0.0 copy-start
  0.0 0.9 copy-done
  0.9 0.0 copy-start.3
  0.9 0.7 copy-done.3
  1.6 0.0 copy-start.4
  1.6 0.7 copy-done.4
  2.3 1.4 shard_map.46
  3.6 0.0 copy-start.1
  3.7 17.7 %all-to-all-start = ((bf16[16,4,3584]{2,1,0:T(4,128)(2,1)}), bf16[16,4,3584]{2,1,0:T(4,128)(2,1)S(1)}, u32[]{:S(2)}, u32[]{:S(2)}) async-start(bf16[16,4,3584]{2,1,0:T(4,128)(2,1)} %get-tuple-element.8), calls=%async_computation | async-start | bytes 917504 | tf_op jit(solution)/shard_map/all_to_all | solution.py:176
  21.3 0.6 slice.14
  23.1 0.0 copy-done.1
  23.2 2.0 %slice_select_fusion.own_ref = bf16[384,3584]{1,0:T(8,128)(2,1)S(1)} fusion(bf16[576,3584]{1,0:T(8,128)(2,1)} %bitcast.43, pred[]{:T(512)} %bitcast.5), kind=kLoop, calls=%fused_computation | loop fusion | flops 1376256 | bytes 5505025 | tf_op jit(solution)/shard_map/jit(_where)/select_n | solution.py:174
  25.1 1.9 %collective-permute-start = (bf16[384,3584]{1,0:T(8,128)(2,1)S(1)}, bf16[384,3584]{1,0:T(8,128)(2,1)}, u32[]{:S(2)}, u32[]{:S(2)}) collective-permute-start(bf16[384,3584]{1,0:T(8,128)(2,1)S(1)} %slice_select_fusion.own_ref), channel_id=1, source_target_pairs={{0,4},{4,0},{1,5},{5,1},{2,6},{6,2},{3,7},{7,3},{8,12},{12,8},{9,1... | collective-permute-start | bytes 8257544 | tf_op jit(solution)/shard_map/ppermute | solution.py:23
  27.1 1.7 %dynamic-slice_bitcast_fusion = bf16[48,3584]{1,0:T(8,128)(2,1)} fusion(bf16[1,3584,576]{1,2,0:T(8,128)(2,1)} %param.7, s32[]{:T(128)S(6)} %select_n.26), kind=kLoop, calls=%fused_computation.4 | loop fusion | bytes 688132 | tf_op jit(solution)/shard_map/dynamic_slice | solution.py:165
  28.8 1.1 reshape.20
  29.9 0.7 constant_dynamic-slice_fusion
  30.6 2.9 %collective-permute-start.1 = (bf16[48,896]{1,0:T(8,128)(2,1)S(1)}, bf16[48,896]{1,0:T(8,128)(2,1)S(1)}, u32[]{:S(2)}, u32[]{:S(2)}) collective-permute-start(bf16[48,896]{1,0:T(8,128)(2,1)S(1)} %bitcast.44), channel_id=1, source_target_pairs={{0,8},{8,0},{16,24},{24,16},{1,9},{9,1},{17,25},{25,17},{2,10},{10... | collective-permute-start | bytes 258056 | tf_op jit(solution)/shard_map/ppermute | solution.py:19
  33.6 3.4 %collective-permute-start.2 = (bf16[48,896]{1,0:T(8,128)(2,1)S(1)}, bf16[48,896]{1,0:T(8,128)(2,1)S(1)}, u32[]{:S(2)}, u32[]{:S(2)}) collective-permute-start(bf16[48,896]{1,0:T(8,128)(2,1)S(1)} %bitcast.45), channel_id=1, source_target_pairs={{0,16},{8,24},{16,0},{24,8},{1,17},{9,25},{17,1},{25,9},{2,18},{10... | collective-permute-start | bytes 258056 | tf_op jit(solution)/shard_map/ppermute | solution.py:19
  37.0 3.8 %collective-permute-start.3 = (bf16[48,896]{1,0:T(8,128)(2,1)S(1)}, bf16[48,896]{1,0:T(8,128)(2,1)S(1)}, u32[]{:S(2)}, u32[]{:S(2)}) collective-permute-start(bf16[48,896]{1,0:T(8,128)(2,1)S(1)} %bitcast.46), channel_id=1, source_target_pairs={{0,24},{8,16},{16,8},{24,0},{1,25},{9,17},{17,9},{25,1},{2,26},{10... | collective-permute-start | bytes 258056 | tf_op jit(solution)/shard_map/ppermute | solution.py:19
  40.8 4.9 %collective-permute-done.1.refs_1_ = bf16[48,896]{1,0:T(8,128)(2,1)S(1)} collective-permute-done((bf16[48,896]{1,0:T(8,128)(2,1)S(1)}, bf16[48,896]{1,0:T(8,128)(2,1)S(1)}, u32[]{:S(2)}, u32[]{:S(2)}) %collective-permute-start.1) | collective-permute-done | bytes 86048 | tf_op jit(solution)/shard_map/ppermute | solution.py:19
  45.8 5.3 %collective-permute-done.2.refs_2_ = bf16[48,896]{1,0:T(8,128)(2,1)S(1)} collective-permute-done((bf16[48,896]{1,0:T(8,128)(2,1)S(1)}, bf16[48,896]{1,0:T(8,128)(2,1)S(1)}, u32[]{:S(2)}, u32[]{:S(2)}) %collective-permute-start.2) | collective-permute-done | bytes 86048 | tf_op jit(solution)/shard_map/ppermute | solution.py:19
  51.0 0.0 collective-permute-done.3.refs_3_
  51.0 0.0 all-to-all-done._
  51.0 1.8 %shard_map.48 = bf16[8,4,48,896]{3,2,1,0:T(8,128)(2,1)} custom-call(bf16[16,4,3584]{2,1,0:T(4,128)(2,1)S(1)} %all-to-all-done._, bf16[48,896]{1,0:T(8,128)(2,1)S(1)} %bitcast.40, bf16[48,896]{1,0:T(8,128)(2,1)S(1)} %collective-permute-done.1.refs_1_, bf16[48,896]{1,0:T(8,128)(2,1)S(1)} %collective-permute-done.2.refs_2_, ...), custom_call_target="tpu_custom_call" | custom-call | tf_op jit(solution)/shard_map/pallas_call | solution.py:90
  52.9 4.7 %all-to-all-start.1 = ((bf16[8,4,48,896]{3,2,1,0:T(8,128)(2,1)}), bf16[8,4,48,896]{3,2,1,0:T(8,128)(2,1)}, u32[]{:S(2)}, u32[]{:S(2)}) async-start(bf16[8,4,48,896]{3,2,1,0:T(8,128)(2,1)} %shard_map.48), calls=%async_computation.1 | async-start | bytes 5505024 | tf_op jit(solution)/shard_map/all_to_all | solution.py:179
  57.6 0.1 pad_add_fusion.place_ref
  57.7 0.2 fusion.3
  57.9 23.7 %all_gather.12.first_ref = bf16[32,4,3584]{2,1,0:T(4,128)(2,1)S(1)} all-gather(bf16[8,4,3584]{2,1,0:T(4,128)(2,1)S(1)} %get-tuple-element.10), channel_id=1, replica_groups=mesh['x'=4,'zb'=4,'zi'=4,'c'=2,'dp'=4] {'zi'}, dimensions={0}, use_global_device_ids=true | all-gather | bytes 1146880 | tf_op jit(solution)/shard_map/all_gather | solution.py:182
  81.5 19.9 %all_gather.13.second_ref = bf16[32,4,3584]{2,1,0:T(4,128)(2,1)S(1)} all-gather(bf16[8,4,3584]{2,1,0:T(4,128)(2,1)S(1)} %get-tuple-element.9), channel_id=1, replica_groups=mesh['x'=4,'zb'=4,'zi'=4,'c'=2,'dp'=4] {'zi'}, dimensions={0}, use_global_device_ids=true | all-gather | bytes 1146880 | tf_op jit(solution)/shard_map/all_gather | solution.py:183
  101.5 0.0 collective-permute-done.other_ref
  101.5 3.5 %shard_map.47 = bf16[256,384]{1,0:T(8,128)(2,1)S(1)} custom-call(bf16[32,4,3584]{2,1,0:T(4,128)(2,1)S(1)} %all_gather.12.first_ref, bf16[32,4,3584]{2,1,0:T(4,128)(2,1)S(1)} %all_gather.13.second_ref, bf16[384,3584]{1,0:T(8,128)(2,1)S(1)} %slice_select_fusion.own_ref, bf16[384,3584]{1,0:T(8,128)(2,1)} %collective-permute-done.other_ref), custom_call_target="tpu_custom_call" | custom-call | tf_op jit(solution)/shard_map/pallas_call | solution.py:116
  105.0 17.5 %all-gather = bf16[1024,384]{1,0:T(8,128)(2,1)S(1)} all-gather(bf16[256,384]{1,0:T(8,128)(2,1)S(1)} %shard_map.47), channel_id=2, replica_groups=mesh['x'=4,'zb'=4,'zi'=4,'c'=2,'dp'=4] {'zi'}, dimensions={0}, use_global_device_ids=true | all-gather | bytes 983040 | tf_op jit(solution)/shard_map/all_gather | solution.py:185
  122.5 0.0 all-to-all-done.1
  122.5 0.0 copy-start.2
  122.5 3.0 %shard_map.49 = bf16[16,4,4,896]{3,2,1,0:T(4,128)(2,1)S(1)} custom-call(s32[2]{0:T(128)S(1)} %pad_add_fusion.place_ref, bf16[4,256,384]{2,1,0:T(8,128)(2,1)S(1)} %bitcast.38, bf16[4,2,4,48,896]{4,3,2,1,0:T(8,128)(2,1)} %bitcast.11.shares_ref), custom_call_target="tpu_custom_call" | custom-call | tf_op jit(solution)/shard_map/pallas_call | solution.py:145
  125.5 33.3 %all_to_all.15 = bf16[64,4,896]{2,1,0:T(4,128)(2,1)S(1)} all-to-all(bf16[64,4,896]{2,1,0:T(4,128)(2,1)S(1)} %bitcast.39), channel_id=1, replica_groups=mesh['x'=4,'zb'=4,'zi'=4,'c'=2,'dp'=4] {'x','zb','zi'}, dimensions={0} | all-to-all | bytes 917504 | tf_op jit(solution)/shard_map/all_to_all | solution.py:189
  158.8 0.2 reshape.28
  158.9 0.0 copy-done.2
  158.9 1.0 fusion
  (4 shorter events, 0.1 us)
Async XLA Ops:
  0.0 0.9 copy-start
  0.9 0.7 copy-start.3
  1.6 0.7 copy-start.4
  3.6 19.5 %copy-start.1 = (f32[2,2,16,8]{3,2,1,0:T(8,128)}, f32[2,2,16,8]{3,2,1,0:T(8,128)S(1)}, u32[]{:S(2)}) copy-start(f32[2,2,16,8]{3,2,1,0:T(8,128)S(1)} %get-tuple-element.7) | copy-start | bytes 6148
  3.7 47.4 %all-to-all-start = ((bf16[16,4,3584]{2,1,0:T(4,128)(2,1)}), bf16[16,4,3584]{2,1,0:T(4,128)(2,1)S(1)}, u32[]{:S(2)}, u32[]{:S(2)}) async-start(bf16[16,4,3584]{2,1,0:T(4,128)(2,1)} %get-tuple-element.8), calls=%async_computation | async-start | bytes 917504 | tf_op jit(solution)/shard_map/all_to_all | solution.py:176
  25.1 76.4 %collective-permute-start = (bf16[384,3584]{1,0:T(8,128)(2,1)S(1)}, bf16[384,3584]{1,0:T(8,128)(2,1)}, u32[]{:S(2)}, u32[]{:S(2)}) collective-permute-start(bf16[384,3584]{1,0:T(8,128)(2,1)S(1)} %slice_select_fusion.own_ref), channel_id=1, source_target_pairs={{0,4},{4,0},{1,5},{5,1},{2,6},{6,2},{3,7},{7,3},{8,12},{12,8},{9,1... | collective-permute-start | bytes 8257544 | tf_op jit(solution)/shard_map/ppermute | solution.py:23
  30.6 15.1 %collective-permute-start.1 = (bf16[48,896]{1,0:T(8,128)(2,1)S(1)}, bf16[48,896]{1,0:T(8,128)(2,1)S(1)}, u32[]{:S(2)}, u32[]{:S(2)}) collective-permute-start(bf16[48,896]{1,0:T(8,128)(2,1)S(1)} %bitcast.44), channel_id=1, source_target_pairs={{0,8},{8,0},{16,24},{24,16},{1,9},{9,1},{17,25},{25,17},{2,10},{10... | collective-permute-start | bytes 258056 | tf_op jit(solution)/shard_map/ppermute | solution.py:19
  33.6 17.4 %collective-permute-start.2 = (bf16[48,896]{1,0:T(8,128)(2,1)S(1)}, bf16[48,896]{1,0:T(8,128)(2,1)S(1)}, u32[]{:S(2)}, u32[]{:S(2)}) collective-permute-start(bf16[48,896]{1,0:T(8,128)(2,1)S(1)} %bitcast.45), channel_id=1, source_target_pairs={{0,16},{8,24},{16,0},{24,8},{1,17},{9,25},{17,1},{25,9},{2,18},{10... | collective-permute-start | bytes 258056 | tf_op jit(solution)/shard_map/ppermute | solution.py:19
  37.0 14.0 %collective-permute-start.3 = (bf16[48,896]{1,0:T(8,128)(2,1)S(1)}, bf16[48,896]{1,0:T(8,128)(2,1)S(1)}, u32[]{:S(2)}, u32[]{:S(2)}) collective-permute-start(bf16[48,896]{1,0:T(8,128)(2,1)S(1)} %bitcast.46), channel_id=1, source_target_pairs={{0,24},{8,16},{16,8},{24,0},{1,25},{9,17},{17,9},{25,1},{2,26},{10... | collective-permute-start | bytes 258056 | tf_op jit(solution)/shard_map/ppermute | solution.py:19
  52.9 69.6 %all-to-all-start.1 = ((bf16[8,4,48,896]{3,2,1,0:T(8,128)(2,1)}), bf16[8,4,48,896]{3,2,1,0:T(8,128)(2,1)}, u32[]{:S(2)}, u32[]{:S(2)}) async-start(bf16[8,4,48,896]{3,2,1,0:T(8,128)(2,1)} %shard_map.48), calls=%async_computation.1 | async-start | bytes 5505024 | tf_op jit(solution)/shard_map/all_to_all | solution.py:179
  122.5 36.5 %copy-start.2 = (f32[2,2,16,8]{3,2,1,0:T(8,128)S(1)}, f32[2,2,16,8]{3,2,1,0:T(8,128)}, u32[]{:S(2)}) copy-start(f32[2,2,16,8]{3,2,1,0:T(8,128)} %copy-done.1) | copy-start | bytes 6148

commit v17 on v16

--- a/solution.py
+++ b/solution.py
@@ -116,7 +116,11 @@
     return pl.pallas_call(
         up_kernel,
         grid=(1,),
-        in_specs=whole(3) + [pl.BlockSpec((both, own.shape[1]), lambda i: (0, 0))],
+        in_specs=[
+            pl.BlockSpec(first.shape, lambda i: (0, 0, 0)),
+            *whole(2),
+            pl.BlockSpec((both, own.shape[1]), lambda i: (0, 0)),
+        ],
         out_specs=whole(1)[0],
         out_shape=jax.ShapeDtypeStruct((count, both), BF),
         compiler_params=pltpu.CompilerParams(vmem_limit_bytes=24 << 20),
@@ -174,13 +178,13 @@
     up = jnp.where(mark == mark, turned[: 2 * units], jnp.zeros((), BF))
     other = swap(up)
     arrived = lax.all_to_all(packed, ROWS_OF, split_axis=0, concat_axis=0, tiled=True)
-    replicas, cores = lax.axis_size("dp"), lax.axis_size("c")
-    shares = repeat_after(arrived, pieces, replicas * cores)
-    shares = lax.all_to_all(shares, ("dp", "c"), split_axis=0, concat_axis=0, tiled=True)
-    shares = shares.reshape((replicas, cores) + shares.shape[1:])
     half = experts // 2
     first = lax.all_gather(arrived[:half], "zi", axis=0, tiled=True)
     second = lax.all_gather(arrived[half:], "zi", axis=0, tiled=True)
+    replicas, cores = lax.axis_size("dp"), lax.axis_size("c")
+    shares = repeat_after(first, pieces, replicas * cores)
+    shares = lax.all_to_all(shares, ("dp", "c"), split_axis=0, concat_axis=0, tiled=True)
+    shares = shares.reshape((replicas, cores) + shares.shape[1:])
     hidden = hidden_of(first, second, up, other)
     gathered = lax.all_gather(hidden, "zi", axis=0)
     position = jnp.stack([place, lax.axis_index("c")]).astype(jnp.int32)

time: 162 us -> 162 us (level)
  waiting for transfers between devices: 10.2 us -> 5.69 us
  blocking collectives: 94.4 us -> 98.4 us
    ppermute x3, waiting for transfers between devices: 10.2 us -> 0.01 us  [exchange(): return lax.ppermute(array, axis, [(i, i ^ step) for i in range(size)])]
    all_gather x1, blocking collectives: 23.7 us -> 29.4 us  [on_device(): first = lax.all_gather(arrived[:half], 'zi', axis=0, tiled=True)]
    all_to_all x1, waiting for transfers between devices: 0.01 us -> 5.67 us  [on_device(): lax.all_to_all(packed, ROWS_OF, split_axis=0, concat_axis=0, tiled=True)]
    all_to_all x1, blocking collectives: 33.3 us -> 30.7 us  [on_device(): lax.all_to_all(done, HOME, split_axis=0, concat_axis=0, tiled=True)]
    unnamed x14 -> x12, local copies, waits for them, and re-layouts: 2.32 us -> 4.13 us
  transfers between devices with their start and end apart: 6 -> 6, of which waited for: 2 -> 1; matrix products, arithmetic and copies ran while one was open for 4% -> 4% of each run, Pallas kernels for 3% -> 3%
where the time goes in v17:
time: 162 us; the launch traced here: 161 us
  blocking collectives  98.4 us (61%)
  starting transfers between devices  34.4 us (21%)
  Pallas kernels  9.72 us (6%)
  local copies, waits for them, and re-layouts  7.83 us (5%)
  waiting for transfers between devices  5.69 us (4%)
  other arithmetic  2.03 us (1%)
    all_to_all x1, blocking collectives, on_device(): lax.all_to_all(done, HOME, split_axis=0, concat_axis=0, tiled=True)  30.7 us
    all_gather x1, blocking collectives, on_device(): first = lax.all_gather(arrived[:half], 'zi', axis=0, tiled=True)  29.4 us
    all_gather x1, blocking collectives, on_device(): second = lax.all_gather(arrived[half:], 'zi', axis=0, tiled=True)  19.8 us
    all_gather x1, blocking collectives, on_device(): gathered = lax.all_gather(hidden, 'zi', axis=0)  18.6 us
    all_to_all x1, starting transfers between devices, on_device(): lax.all_to_all(packed, ROWS_OF, split_axis=0, concat_axis=0, tiled=True)  17.7 us
    ppermute x3, starting transfers between devices, exchange(): return lax.ppermute(array, axis, [(i, i ^ step) for i in range(size)])  10.1 us
    all_to_all x1, waiting for transfers between devices, on_device(): lax.all_to_all(packed, ROWS_OF, split_axis=0, concat_axis=0, tiled=True)  5.67 us
    all_to_all x1, starting transfers between devices, on_device(): lax.all_to_all(shares, ('dp', 'c'), split_axis=0, concat_axis=0, tiled=True)  4.7 us
  transfers between devices with their start and end apart: 6, of which 1 were waited for; matrix products, arithmetic and copies ran while one was open for 4% of the time, Pallas kernels for 3%

profile of v17, /device:TPU:24, one launch (start us, length us, event | category | flops | bytes accessed | tf_op | source)
XLA Modules:
  0.0 160.6 jit_solution(7400539869222966256)
XLA Ops:
  0.0 0.0 copy-start.1
  0.0 0.9 copy-done.1
  0.9 0.0 copy-start.2
  0.9 0.7 copy-done.2
  1.6 0.0 copy-start.3
  1.6 0.7 copy-done.3
  2.3 1.4 shard_map.46
  3.7 17.7 %all-to-all-start = ((bf16[16,4,3584]{2,1,0:T(4,128)(2,1)}), bf16[16,4,3584]{2,1,0:T(4,128)(2,1)}, u32[]{:S(2)}, u32[]{:S(2)}) async-start(bf16[16,4,3584]{2,1,0:T(4,128)(2,1)} %get-tuple-element.8), calls=%async_computation | async-start | bytes 917504 | tf_op jit(solution)/shard_map/all_to_all | solution.py:180
  21.4 0.5 slice.14
  23.2 2.0 %slice_select_fusion.own_ref = bf16[384,3584]{1,0:T(8,128)(2,1)S(1)} fusion(bf16[576,3584]{1,0:T(8,128)(2,1)} %bitcast.43, pred[]{:T(512)} %bitcast.5), kind=kLoop, calls=%fused_computation | loop fusion | flops 1376256 | bytes 5505025 | tf_op jit(solution)/shard_map/jit(_where)/select_n | solution.py:178
  25.2 1.9 %collective-permute-start = (bf16[384,3584]{1,0:T(8,128)(2,1)S(1)}, bf16[384,3584]{1,0:T(8,128)(2,1)}, u32[]{:S(2)}, u32[]{:S(2)}) collective-permute-start(bf16[384,3584]{1,0:T(8,128)(2,1)S(1)} %slice_select_fusion.own_ref), channel_id=1, source_target_pairs={{0,4},{4,0},{1,5},{5,1},{2,6},{6,2},{3,7},{7,3},{8,12},{12,8},{9,1... | collective-permute-start | bytes 8257544 | tf_op jit(solution)/shard_map/ppermute | solution.py:23
  27.1 1.0 dynamic-slice_bitcast_fusion
  28.1 0.1 reshape.20
  28.2 0.7 constant_dynamic-slice_fusion
  29.0 2.9 %collective-permute-start.1 = (bf16[48,896]{1,0:T(8,128)(2,1)S(1)}, bf16[48,896]{1,0:T(8,128)(2,1)S(1)}, u32[]{:S(2)}, u32[]{:S(2)}) collective-permute-start(bf16[48,896]{1,0:T(8,128)(2,1)S(1)} %bitcast.44), channel_id=1, source_target_pairs={{0,8},{8,0},{16,24},{24,16},{1,9},{9,1},{17,25},{25,17},{2,10},{10... | collective-permute-start | bytes 258056 | tf_op jit(solution)/shard_map/ppermute | solution.py:19
  31.9 3.4 %collective-permute-start.2 = (bf16[48,896]{1,0:T(8,128)(2,1)S(1)}, bf16[48,896]{1,0:T(8,128)(2,1)S(1)}, u32[]{:S(2)}, u32[]{:S(2)}) collective-permute-start(bf16[48,896]{1,0:T(8,128)(2,1)S(1)} %bitcast.45), channel_id=1, source_target_pairs={{0,16},{8,24},{16,0},{24,8},{1,17},{9,25},{17,1},{25,9},{2,18},{10... | collective-permute-start | bytes 258056 | tf_op jit(solution)/shard_map/ppermute | solution.py:19
  35.3 0.6 copy.31
  36.0 3.8 %collective-permute-start.3 = (bf16[48,896]{1,0:T(8,128)(2,1)}, bf16[48,896]{1,0:T(8,128)(2,1)S(1)}, u32[]{:S(2)}, u32[]{:S(2)}) collective-permute-start(bf16[48,896]{1,0:T(8,128)(2,1)} %bitcast.34), channel_id=1, source_target_pairs={{0,24},{8,16},{16,8},{24,0},{1,25},{9,17},{17,9},{25,1},{2,26},{10... | collective-permute-start | bytes 258056 | tf_op jit(solution)/shard_map/ppermute | solution.py:19
  39.8 5.7 %all-to-all-done = bf16[16,4,3584]{2,1,0:T(4,128)(2,1)} async-done(((bf16[16,4,3584]{2,1,0:T(4,128)(2,1)}), bf16[16,4,3584]{2,1,0:T(4,128)(2,1)}, u32[]{:S(2)}, u32[]{:S(2)}) %all-to-all-start) | async-done | bytes 458784 | tf_op jit(solution)/shard_map/all_to_all | solution.py:180
  45.5 1.2 fusion.3
  46.7 29.4 %all_gather.12.first_ref._ = bf16[32,4,3584]{2,1,0:T(4,128)(2,1)} all-gather(bf16[8,4,3584]{2,1,0:T(4,128)(2,1)S(1)} %get-tuple-element.10), channel_id=1, replica_groups=mesh['x'=4,'zb'=4,'zi'=4,'c'=2,'dp'=4] {'zi'}, dimensions={0}, use_global_device_ids=true | all-gather | bytes 1146880 | tf_op jit(solution)/shard_map/all_gather | solution.py:182
  76.0 0.0 collective-permute-done.1.refs_1_
  76.0 0.0 collective-permute-done.2.refs_2_
  76.0 0.0 collective-permute-done.3.refs_3_
  76.0 1.8 %shard_map.48 = bf16[8,4,48,896]{3,2,1,0:T(8,128)(2,1)} custom-call(bf16[32,4,3584]{2,1,0:T(4,128)(2,1)} %all_gather.12.first_ref._, bf16[48,896]{1,0:T(8,128)(2,1)S(1)} %bitcast.40, bf16[48,896]{1,0:T(8,128)(2,1)S(1)} %collective-permute-done.1.refs_1_, bf16[48,896]{1,0:T(8,128)(2,1)S(1)} %collective-permute-done.2.refs_2_, ...), custom_call_target="tpu_custom_call" | custom-call | tf_op jit(solution)/shard_map/pallas_call | solution.py:90
  77.9 4.7 %all-to-all-start.1 = ((bf16[8,4,48,896]{3,2,1,0:T(8,128)(2,1)}), bf16[8,4,48,896]{3,2,1,0:T(8,128)(2,1)}, u32[]{:S(2)}, u32[]{:S(2)}) async-start(bf16[8,4,48,896]{3,2,1,0:T(8,128)(2,1)} %shard_map.48), calls=%async_computation.1 | async-start | bytes 5505024 | tf_op jit(solution)/shard_map/all_to_all | solution.py:186
  82.6 0.1 pad_add_fusion.place_ref
  82.7 19.8 %all_gather.13.second_ref = bf16[32,4,3584]{2,1,0:T(4,128)(2,1)S(1)} all-gather(bf16[8,4,3584]{2,1,0:T(4,128)(2,1)S(1)} %get-tuple-element.9), channel_id=1, replica_groups=mesh['x'=4,'zb'=4,'zi'=4,'c'=2,'dp'=4] {'zi'}, dimensions={0}, use_global_device_ids=true | all-gather | bytes 1146880 | tf_op jit(solution)/shard_map/all_gather | solution.py:183
  102.5 0.0 collective-permute-done.other_ref
  102.5 0.0 copy-start
  102.5 1.2 copy-done
  103.7 3.5 %shard_map.47 = bf16[256,384]{1,0:T(8,128)(2,1)S(1)} custom-call(bf16[32,4,3584]{2,1,0:T(4,128)(2,1)S(1)} %copy-done, bf16[32,4,3584]{2,1,0:T(4,128)(2,1)S(1)} %all_gather.13.second_ref, bf16[384,3584]{1,0:T(8,128)(2,1)S(1)} %slice_select_fusion.own_ref, bf16[384,3584]{1,0:T(8,128)(2,1)} %collective-permute-done.other_ref), custom_call_target="tpu_custom_call" | custom-call | tf_op jit(solution)/shard_map/pallas_call | solution.py:116
  107.2 18.6 %all-gather = bf16[1024,384]{1,0:T(8,128)(2,1)S(1)} all-gather(bf16[256,384]{1,0:T(8,128)(2,1)S(1)} %shard_map.47), channel_id=2, replica_groups=mesh['x'=4,'zb'=4,'zi'=4,'c'=2,'dp'=4] {'zi'}, dimensions={0}, use_global_device_ids=true | all-gather | bytes 983040 | tf_op jit(solution)/shard_map/all_gather | solution.py:189
  125.7 0.0 all-to-all-done.1
  125.7 3.0 %shard_map.49 = bf16[16,4,4,896]{3,2,1,0:T(4,128)(2,1)S(1)} custom-call(s32[2]{0:T(128)S(1)} %pad_add_fusion.place_ref, bf16[4,256,384]{2,1,0:T(8,128)(2,1)S(1)} %bitcast.38, bf16[4,2,4,48,896]{4,3,2,1,0:T(8,128)(2,1)} %bitcast.11.shares_ref), custom_call_target="tpu_custom_call" | custom-call | tf_op jit(solution)/shard_map/pallas_call | solution.py:149
  128.7 30.7 %all_to_all.15 = bf16[64,4,896]{2,1,0:T(4,128)(2,1)S(1)} all-to-all(bf16[64,4,896]{2,1,0:T(4,128)(2,1)S(1)} %bitcast.39), channel_id=1, replica_groups=mesh['x'=4,'zb'=4,'zi'=4,'c'=2,'dp'=4] {'x','zb','zi'}, dimensions={0} | all-to-all | bytes 917504 | tf_op jit(solution)/shard_map/all_to_all | solution.py:193
  159.4 0.2 reshape.28
  159.6 1.0 fusion
  (3 shorter events, 0.0 us)
Async XLA Ops:
  0.0 0.9 copy-start.1
  0.9 0.7 copy-start.2
  1.6 0.7 copy-start.3
  3.7 41.8 %all-to-all-start = ((bf16[16,4,3584]{2,1,0:T(4,128)(2,1)}), bf16[16,4,3584]{2,1,0:T(4,128)(2,1)}, u32[]{:S(2)}, u32[]{:S(2)}) async-start(bf16[16,4,3584]{2,1,0:T(4,128)(2,1)} %get-tuple-element.8), calls=%async_computation | async-start | bytes 917504 | tf_op jit(solution)/shard_map/all_to_all | solution.py:180
  25.2 77.3 %collective-permute-start = (bf16[384,3584]{1,0:T(8,128)(2,1)S(1)}, bf16[384,3584]{1,0:T(8,128)(2,1)}, u32[]{:S(2)}, u32[]{:S(2)}) collective-permute-start(bf16[384,3584]{1,0:T(8,128)(2,1)S(1)} %slice_select_fusion.own_ref), channel_id=1, source_target_pairs={{0,4},{4,0},{1,5},{5,1},{2,6},{6,2},{3,7},{7,3},{8,12},{12,8},{9,1... | collective-permute-start | bytes 8257544 | tf_op jit(solution)/shard_map/ppermute | solution.py:23
  29.0 47.1 %collective-permute-start.1 = (bf16[48,896]{1,0:T(8,128)(2,1)S(1)}, bf16[48,896]{1,0:T(8,128)(2,1)S(1)}, u32[]{:S(2)}, u32[]{:S(2)}) collective-permute-start(bf16[48,896]{1,0:T(8,128)(2,1)S(1)} %bitcast.44), channel_id=1, source_target_pairs={{0,8},{8,0},{16,24},{24,16},{1,9},{9,1},{17,25},{25,17},{2,10},{10... | collective-permute-start | bytes 258056 | tf_op jit(solution)/shard_map/ppermute | solution.py:19
  31.9 44.1 %collective-permute-start.2 = (bf16[48,896]{1,0:T(8,128)(2,1)S(1)}, bf16[48,896]{1,0:T(8,128)(2,1)S(1)}, u32[]{:S(2)}, u32[]{:S(2)}) collective-permute-start(bf16[48,896]{1,0:T(8,128)(2,1)S(1)} %bitcast.45), channel_id=1, source_target_pairs={{0,16},{8,24},{16,0},{24,8},{1,17},{9,25},{17,1},{25,9},{2,18},{10... | collective-permute-start | bytes 258056 | tf_op jit(solution)/shard_map/ppermute | solution.py:19
  36.0 40.1 %collective-permute-start.3 = (bf16[48,896]{1,0:T(8,128)(2,1)}, bf16[48,896]{1,0:T(8,128)(2,1)S(1)}, u32[]{:S(2)}, u32[]{:S(2)}) collective-permute-start(bf16[48,896]{1,0:T(8,128)(2,1)} %bitcast.34), channel_id=1, source_target_pairs={{0,24},{8,16},{16,8},{24,0},{1,25},{9,17},{17,9},{25,1},{2,26},{10... | collective-permute-start | bytes 258056 | tf_op jit(solution)/shard_map/ppermute | solution.py:19
  77.9 47.9 %all-to-all-start.1 = ((bf16[8,4,48,896]{3,2,1,0:T(8,128)(2,1)}), bf16[8,4,48,896]{3,2,1,0:T(8,128)(2,1)}, u32[]{:S(2)}, u32[]{:S(2)}) async-start(bf16[8,4,48,896]{3,2,1,0:T(8,128)(2,1)} %shard_map.48), calls=%async_computation.1 | async-start | bytes 5505024 | tf_op jit(solution)/shard_map/all_to_all | solution.py:186
  102.5 1.2 copy-start

commit v18 on v16

--- a/solution.py
+++ b/solution.py
@@ -97,8 +97,22 @@
     )(earlier, *arrays)
 
 
+def copy_kernel(_, array_ref, out_ref):
+    out_ref[...] = array_ref[...]
+
+
+def copy_after(earlier, array):
+    return pl.pallas_call(
+        copy_kernel,
+        in_specs=[ANYWHERE] + whole(1),
+        out_specs=whole(1)[0],
+        out_shape=jax.ShapeDtypeStruct(array.shape, array.dtype),
+        compiler_params=pltpu.CompilerParams(vmem_limit_bytes=16 << 20),
+    )(earlier, array)
+
+
 def up_kernel(first_ref, second_ref, own_ref, other_ref, out_ref):
-    units = own_ref.shape[0] // 2
+    units = own_ref.shape[0] // 3
     width = own_ref.shape[1]
     rows = [ref[...].reshape(-1, width) for ref in (first_ref, second_ref)]
     rows = jnp.concatenate(rows, axis=0)
@@ -112,7 +126,7 @@
 
 def hidden_of(first, second, own, other):
     count = 2 * first.shape[0] * first.shape[1]
-    both = own.shape[0]
+    both = own.shape[0] // 3 * 2
     return pl.pallas_call(
         up_kernel,
         grid=(1,),
@@ -180,8 +194,9 @@
     shares = shares.reshape((replicas, cores) + shares.shape[1:])
     half = experts // 2
     first = lax.all_gather(arrived[:half], "zi", axis=0, tiled=True)
-    second = lax.all_gather(arrived[half:], "zi", axis=0, tiled=True)
-    hidden = hidden_of(first, second, up, other)
+    later = copy_after(first, arrived[half:])
+    second = lax.all_gather(later, "zi", axis=0, tiled=True)
+    hidden = hidden_of(first, second, turned, other)
     gathered = lax.all_gather(hidden, "zi", axis=0)
     position = jnp.stack([place, lax.axis_index("c")]).astype(jnp.int32)
     done = outputs_of(position, gathered, shares, experts, slots)

time: 162 us -> 161 us (level)
  local copies, waits for them, and re-layouts: 6.75 us -> 4.97 us
  transfers between devices with their start and end apart: 6 -> 6, of which waited for: 2 -> 3; matrix products, arithmetic and copies ran while one was open for 4% -> 4% of each run, Pallas kernels for 3% -> 3%
where the time goes in v18:
time: 161 us; the launch traced here: 160 us
  blocking collectives  95 us (59%)
  starting transfers between devices  34.4 us (21%)
  waiting for transfers between devices  9.97 us (6%)
  Pallas kernels  8.48 us (5%)
  local copies, waits for them, and re-layouts  4.97 us (3%)
  other arithmetic  3.57 us (2%)
  matrix products  1.77 us (1%)
    all_to_all x1, blocking collectives, on_device(): lax.all_to_all(done, HOME, split_axis=0, concat_axis=0, tiled=True)  33.3 us
    all_gather x1, blocking collectives, on_device(): first = lax.all_gather(arrived[:half], 'zi', axis=0, tiled=True)  24.3 us
    all_gather x1, blocking collectives, on_device(): second = lax.all_gather(later, 'zi', axis=0, tiled=True)  20 us
    all_to_all x1, starting transfers between devices, on_device(): lax.all_to_all(packed, ROWS_OF, split_axis=0, concat_axis=0, tiled=True)  17.7 us
    all_gather x1, blocking collectives, on_device(): gathered = lax.all_gather(hidden, 'zi', axis=0)  17.5 us
    ppermute x3, starting transfers between devices, exchange(): return lax.ppermute(array, axis, [(i, i ^ step) for i in range(size)])  10.1 us
    ppermute x3, waiting for transfers between devices, exchange(): return lax.ppermute(array, axis, [(i, i ^ step) for i in range(size)])  9.96 us
    all_to_all x1, starting transfers between devices, on_device(): lax.all_to_all(shares, ('dp', 'c'), split_axis=0, concat_axis=0, tiled=True)  4.7 us
  transfers between devices with their start and end apart: 6, of which 3 were waited for; matrix products, arithmetic and copies ran while one was open for 4% of the time, Pallas kernels for 3%

profile of v18, /device:TPU:24, one launch (start us, length us, event | category | flops | bytes accessed | tf_op | source)
XLA Modules:
  0.0 159.6 jit_solution(14572455795879493889)
XLA Ops:
  0.0 0.0 copy-start.1
  0.0 0.9 copy-done.1
  0.9 0.0 copy-start.3
  0.9 0.7 copy-done.3
  1.6 0.0 copy-start.4
  1.6 0.7 copy-done.4
  2.3 1.4 shard_map.46
  3.6 0.0 copy-start.2
  3.7 17.7 %all-to-all-start = ((bf16[16,4,3584]{2,1,0:T(4,128)(2,1)}), bf16[16,4,3584]{2,1,0:T(4,128)(2,1)S(1)}, u32[]{:S(2)}, u32[]{:S(2)}) async-start(bf16[16,4,3584]{2,1,0:T(4,128)(2,1)} %get-tuple-element.8), calls=%async_computation | async-start | bytes 917504 | tf_op jit(solution)/shard_map/all_to_all | solution.py:190
  21.3 0.5 slice.14
  23.1 3.5 %slice_select_fusion = bf16[384,3584]{1,0:T(8,128)(2,1)} fusion(bf16[576,3584]{1,0:T(8,128)(2,1)} %bitcast.38, pred[]{:T(512)} %bitcast.7), kind=kLoop, calls=%fused_computation | loop fusion | flops 1376256 | bytes 5505025 | tf_op jit(solution)/shard_map/jit(_where)/select_n | solution.py:188
  26.6 1.9 %collective-permute-start = (bf16[384,3584]{1,0:T(8,128)(2,1)}, bf16[384,3584]{1,0:T(8,128)(2,1)}, u32[]{:S(2)}, u32[]{:S(2)}) collective-permute-start(bf16[384,3584]{1,0:T(8,128)(2,1)} %slice_select_fusion), channel_id=1, source_target_pairs={{0,4},{4,0},{1,5},{5,1},{2,6},{6,2},{3,7},{7,3},{8,12},{12,8},{9,1... | collective-permute-start | bytes 8257544 | tf_op jit(solution)/shard_map/ppermute | solution.py:23
  28.6 1.0 dynamic-slice_bitcast_fusion
  29.6 0.1 reshape.20
  29.7 0.7 constant_dynamic-slice_fusion
  30.4 2.9 %collective-permute-start.1 = (bf16[48,896]{1,0:T(8,128)(2,1)S(1)}, bf16[48,896]{1,0:T(8,128)(2,1)S(1)}, u32[]{:S(2)}, u32[]{:S(2)}) collective-permute-start(bf16[48,896]{1,0:T(8,128)(2,1)S(1)} %bitcast.46), channel_id=1, source_target_pairs={{0,8},{8,0},{16,24},{24,16},{1,9},{9,1},{17,25},{25,17},{2,10},{10... | collective-permute-start | bytes 258056 | tf_op jit(solution)/shard_map/ppermute | solution.py:19
  33.4 3.4 %collective-permute-start.2 = (bf16[48,896]{1,0:T(8,128)(2,1)S(1)}, bf16[48,896]{1,0:T(8,128)(2,1)S(1)}, u32[]{:S(2)}, u32[]{:S(2)}) collective-permute-start(bf16[48,896]{1,0:T(8,128)(2,1)S(1)} %bitcast.47), channel_id=1, source_target_pairs={{0,16},{8,24},{16,0},{24,8},{1,17},{9,25},{17,1},{25,9},{2,18},{10... | collective-permute-start | bytes 258056 | tf_op jit(solution)/shard_map/ppermute | solution.py:19
  36.8 3.8 %collective-permute-start.3 = (bf16[48,896]{1,0:T(8,128)(2,1)S(1)}, bf16[48,896]{1,0:T(8,128)(2,1)S(1)}, u32[]{:S(2)}, u32[]{:S(2)}) collective-permute-start(bf16[48,896]{1,0:T(8,128)(2,1)S(1)} %bitcast.48), channel_id=1, source_target_pairs={{0,24},{8,16},{16,8},{24,0},{1,25},{9,17},{17,9},{25,1},{2,26},{10... | collective-permute-start | bytes 258056 | tf_op jit(solution)/shard_map/ppermute | solution.py:19
  40.6 0.0 copy-done.2
  40.6 5.3 %collective-permute-done.1.refs_1_ = bf16[48,896]{1,0:T(8,128)(2,1)S(1)} collective-permute-done((bf16[48,896]{1,0:T(8,128)(2,1)S(1)}, bf16[48,896]{1,0:T(8,128)(2,1)S(1)}, u32[]{:S(2)}, u32[]{:S(2)}) %collective-permute-start.1) | collective-permute-done | bytes 86048 | tf_op jit(solution)/shard_map/ppermute | solution.py:19
  45.9 0.8 collective-permute-done.2.refs_2_
  46.7 3.9 %collective-permute-done.3.refs_3_ = bf16[48,896]{1,0:T(8,128)(2,1)S(1)} collective-permute-done((bf16[48,896]{1,0:T(8,128)(2,1)S(1)}, bf16[48,896]{1,0:T(8,128)(2,1)S(1)}, u32[]{:S(2)}, u32[]{:S(2)}) %collective-permute-start.3) | collective-permute-done | bytes 86048 | tf_op jit(solution)/shard_map/ppermute | solution.py:19
  50.6 0.0 all-to-all-done._
  50.6 1.8 %shard_map.49 = bf16[8,4,48,896]{3,2,1,0:T(8,128)(2,1)} custom-call(bf16[16,4,3584]{2,1,0:T(4,128)(2,1)S(1)} %all-to-all-done._, bf16[48,896]{1,0:T(8,128)(2,1)S(1)} %bitcast.43, bf16[48,896]{1,0:T(8,128)(2,1)S(1)} %collective-permute-done.1.refs_1_, bf16[48,896]{1,0:T(8,128)(2,1)S(1)} %collective-permute-done.2.refs_2_, ...), custom_call_target="tpu_custom_call" | custom-call | tf_op jit(solution)/shard_map/pallas_call | solution.py:90
  52.4 4.7 %all-to-all-start.1 = ((bf16[8,4,48,896]{3,2,1,0:T(8,128)(2,1)}), bf16[8,4,48,896]{3,2,1,0:T(8,128)(2,1)S(1)}, u32[]{:S(2)}, u32[]{:S(2)}) async-start(bf16[8,4,48,896]{3,2,1,0:T(8,128)(2,1)} %shard_map.49), calls=%async_computation.1 | async-start | bytes 5505024 | tf_op jit(solution)/shard_map/all_to_all | solution.py:193
  57.2 0.0 copy-start
  57.2 0.1 pad_add_fusion.place_ref
  57.2 0.2 fusion.3
  57.4 24.3 %all_gather.12._.first_ref = bf16[32,4,3584]{2,1,0:T(4,128)(2,1)S(1)} all-gather(bf16[8,4,3584]{2,1,0:T(4,128)(2,1)S(1)} %get-tuple-element.10), channel_id=1, replica_groups=mesh['x'=4,'zb'=4,'zi'=4,'c'=2,'dp'=4] {'zi'}, dimensions={0}, use_global_device_ids=true | all-gather | bytes 1146880 | tf_op jit(solution)/shard_map/all_gather | solution.py:196
  81.7 20.0 %all_gather.13.second_ref = bf16[32,4,3584]{2,1,0:T(4,128)(2,1)S(1)} all-gather(bf16[8,4,3584]{2,1,0:T(4,128)(2,1)S(1)} %shard_map.47), channel_id=1, replica_groups=mesh['x'=4,'zb'=4,'zi'=4,'c'=2,'dp'=4] {'zi'}, dimensions={0}, use_global_device_ids=true | all-gather | bytes 1146880 | tf_op jit(solution)/shard_map/all_gather | solution.py:198
  101.6 0.0 collective-permute-done.other_ref
  101.6 0.0 copy-done
  101.6 3.5 %shard_map.48 = bf16[256,384]{1,0:T(8,128)(2,1)S(1)} custom-call(bf16[32,4,3584]{2,1,0:T(4,128)(2,1)S(1)} %all_gather.12._.first_ref, bf16[32,4,3584]{2,1,0:T(4,128)(2,1)S(1)} %all_gather.13.second_ref, bf16[576,3584]{1,0:T(8,128)(2,1)S(1)} %bitcast.39, bf16[384,3584]{1,0:T(8,128)(2,1)} %collective-permute-done.other_ref), custom_call_target="tpu_custom_call" | custom-call | tf_op jit(solution)/shard_map/pallas_call | solution.py:130
  105.2 17.5 %all-gather = bf16[1024,384]{1,0:T(8,128)(2,1)S(1)} all-gather(bf16[256,384]{1,0:T(8,128)(2,1)S(1)} %shard_map.48), channel_id=2, replica_groups=mesh['x'=4,'zb'=4,'zi'=4,'c'=2,'dp'=4] {'zi'}, dimensions={0}, use_global_device_ids=true | all-gather | bytes 983040 | tf_op jit(solution)/shard_map/all_gather | solution.py:200
  122.6 0.0 all-to-all-done.1
  122.6 1.7 %shard_map.50 = bf16[16,4,4,896]{3,2,1,0:T(4,128)(2,1)S(1)} custom-call(s32[2]{0:T(128)S(1)} %pad_add_fusion.place_ref, bf16[4,256,384]{2,1,0:T(8,128)(2,1)S(1)} %bitcast.41, bf16[4,2,4,48,896]{4,3,2,1,0:T(8,128)(2,1)S(1)} %bitcast.40), custom_call_target="tpu_custom_call" | custom-call | tf_op jit(solution)/shard_map/pallas_call | solution.py:159
  124.4 33.3 %all_to_all.15 = bf16[64,4,896]{2,1,0:T(4,128)(2,1)S(1)} all-to-all(bf16[64,4,896]{2,1,0:T(4,128)(2,1)S(1)} %bitcast.42), channel_id=1, replica_groups=mesh['x'=4,'zb'=4,'zi'=4,'c'=2,'dp'=4] {'x','zb','zi'}, dimensions={0} | all-to-all | bytes 917504 | tf_op jit(solution)/shard_map/all_to_all | solution.py:204
  157.7 0.2 reshape.28
  157.9 1.8 %fusion = bf16[2,8,4,896]{3,1,2,0:T(8,128)(2,1)} fusion(bf16[16,4,2,2,896]{4,3,2,1,0:T(2,128)(2,1)S(1)} %reshape.28, f32[2,2,16,8]{3,2,1,0:T(8,128)} %copy-done.2), kind=kOutput, calls=%fused_computation.2 | convolution fusion | flops 22077440 | bytes 575488 | tf_op jit(solution)/shard_map/mser,ezmsd->mrzd/dot_general | solution.py:206
  (5 shorter events, 0.1 us)
Async XLA Ops:
  0.0 0.9 copy-start.1
  0.9 0.7 copy-start.3
  1.6 0.7 copy-start.4
  3.6 37.0 %copy-start.2 = (f32[2,2,16,8]{3,2,1,0:T(8,128)}, f32[2,2,16,8]{3,2,1,0:T(8,128)S(1)}, u32[]{:S(2)}) copy-start(f32[2,2,16,8]{3,2,1,0:T(8,128)S(1)} %get-tuple-element.7) | copy-start | bytes 6148
  3.7 46.9 %all-to-all-start = ((bf16[16,4,3584]{2,1,0:T(4,128)(2,1)}), bf16[16,4,3584]{2,1,0:T(4,128)(2,1)S(1)}, u32[]{:S(2)}, u32[]{:S(2)}) async-start(bf16[16,4,3584]{2,1,0:T(4,128)(2,1)} %get-tuple-element.8), calls=%async_computation | async-start | bytes 917504 | tf_op jit(solution)/shard_map/all_to_all | solution.py:190
  26.6 75.0 %collective-permute-start = (bf16[384,3584]{1,0:T(8,128)(2,1)}, bf16[384,3584]{1,0:T(8,128)(2,1)}, u32[]{:S(2)}, u32[]{:S(2)}) collective-permute-start(bf16[384,3584]{1,0:T(8,128)(2,1)} %slice_select_fusion), channel_id=1, source_target_pairs={{0,4},{4,0},{1,5},{5,1},{2,6},{6,2},{3,7},{7,3},{8,12},{12,8},{9,1... | collective-permute-start | bytes 8257544 | tf_op jit(solution)/shard_map/ppermute | solution.py:23
  30.4 15.5 %collective-permute-start.1 = (bf16[48,896]{1,0:T(8,128)(2,1)S(1)}, bf16[48,896]{1,0:T(8,128)(2,1)S(1)}, u32[]{:S(2)}, u32[]{:S(2)}) collective-permute-start(bf16[48,896]{1,0:T(8,128)(2,1)S(1)} %bitcast.46), channel_id=1, source_target_pairs={{0,8},{8,0},{16,24},{24,16},{1,9},{9,1},{17,25},{25,17},{2,10},{10... | collective-permute-start | bytes 258056 | tf_op jit(solution)/shard_map/ppermute | solution.py:19
  33.4 13.4 %collective-permute-start.2 = (bf16[48,896]{1,0:T(8,128)(2,1)S(1)}, bf16[48,896]{1,0:T(8,128)(2,1)S(1)}, u32[]{:S(2)}, u32[]{:S(2)}) collective-permute-start(bf16[48,896]{1,0:T(8,128)(2,1)S(1)} %bitcast.47), channel_id=1, source_target_pairs={{0,16},{8,24},{16,0},{24,8},{1,17},{9,25},{17,1},{25,9},{2,18},{10... | collective-permute-start | bytes 258056 | tf_op jit(solution)/shard_map/ppermute | solution.py:19
  36.8 13.8 %collective-permute-start.3 = (bf16[48,896]{1,0:T(8,128)(2,1)S(1)}, bf16[48,896]{1,0:T(8,128)(2,1)S(1)}, u32[]{:S(2)}, u32[]{:S(2)}) collective-permute-start(bf16[48,896]{1,0:T(8,128)(2,1)S(1)} %bitcast.48), channel_id=1, source_target_pairs={{0,24},{8,16},{16,8},{24,0},{1,25},{9,17},{17,9},{25,1},{2,26},{10... | collective-permute-start | bytes 258056 | tf_op jit(solution)/shard_map/ppermute | solution.py:19
  52.4 70.2 %all-to-all-start.1 = ((bf16[8,4,48,896]{3,2,1,0:T(8,128)(2,1)}), bf16[8,4,48,896]{3,2,1,0:T(8,128)(2,1)S(1)}, u32[]{:S(2)}, u32[]{:S(2)}) async-start(bf16[8,4,48,896]{3,2,1,0:T(8,128)(2,1)} %shard_map.49), calls=%async_computation.1 | async-start | bytes 5505024 | tf_op jit(solution)/shard_map/all_to_all | solution.py:193
  57.2 44.5 %copy-start = (bf16[1,3584,576]{1,2,0:T(8,128)(2,1)S(1)}, bf16[1,3584,576]{1,2,0:T(8,128)(2,1)}, u32[]{:S(2)}) copy-start(bf16[1,3584,576]{1,2,0:T(8,128)(2,1)} %param.7) | copy-start | bytes 12386308

commit v19 on v18

--- a/solution.py
+++ b/solution.py
@@ -1,3 +1,5 @@
+import functools
+
 import jax
 import jax.numpy as jnp
 from jax import lax
@@ -8,8 +10,8 @@
 FF = 1536
 BF = jnp.bfloat16
 F32 = jnp.float32
-ROWS_OF = ("x", "zb")
-HOME = ("x", "zb", "zi")
+ROWS_OF = ("zb", "x")
+HOME = ("zb", "x", "zi")
 ANYWHERE = pl.BlockSpec(memory_space=pl.ANY)
 NT = (((1,), (1,)), ((), ()))
 
@@ -23,12 +25,13 @@
     return lax.ppermute(array, "c", [(0, 1), (1, 0)])
 
 
-def pack_kernel(ids_ref, gates_ref, tokens_ref, out_ref, weights_ref):
+def pack_kernel(sides, ids_ref, gates_ref, tokens_ref, out_ref, weights_ref):
     batches, picks, rows = ids_ref.shape
     experts, slots, width = out_ref.shape
     capacity = slots // batches
     count = experts * slots
-    expert = lax.broadcasted_iota(jnp.int32, (experts, rows), 0)
+    at = lax.broadcasted_iota(jnp.int32, (experts, rows), 0)
+    expert = at % sides[0] * sides[1] + at // sides[0]
     row = lax.broadcasted_iota(jnp.int32, (rows, rows), 0)
     earlier = (row < lax.broadcasted_iota(jnp.int32, (rows, rows), 1)).astype(F32)
     owner = lax.broadcasted_iota(jnp.int32, (count, experts), 0) // slots
@@ -61,8 +64,9 @@
 
 def packed_of(expert_ids, gate_scores, tokens, experts, slots):
     batches, rows, width = tokens.shape
-    return pl.pallas_call(
-        pack_kernel,
+    sides = (lax.axis_size("x"), lax.axis_size("zb"))
+    return pl.pallas_call(
+        functools.partial(pack_kernel, sides),
         in_specs=whole(3),
         out_specs=whole(2),
         out_shape=[

time: 161 us -> 162 us (level)
    all_to_all x1, blocking collectives: 33.3 us -> 37.9 us  [on_device(): lax.all_to_all(done, HOME, split_axis=0, concat_axis=0, tiled=True)]
    all_gather x1, blocking collectives: 24.3 us -> 21.1 us  [on_device(): first = lax.all_gather(arrived[:half], 'zi', axis=0, tiled=True)]
  transfers between devices with their start and end apart: 6 -> 6, of which waited for: 3 -> 2; matrix products, arithmetic and copies ran while one was open for 4% -> 4% of each run, Pallas kernels for 3% -> 3%
where the time goes in v19:
time: 162 us; the launch traced here: 160 us
  blocking collectives  95.4 us (59%)
  starting transfers between devices  34.4 us (21%)
  waiting for transfers between devices  10.4 us (6%)
  Pallas kernels  8.5 us (5%)
  local copies, waits for them, and re-layouts  4.97 us (3%)
  other arithmetic  3.57 us (2%)
  matrix products  1.77 us (1%)
    all_to_all x1, blocking collectives, on_device(): lax.all_to_all(done, HOME, split_axis=0, concat_axis=0, tiled=True)  37.9 us
    all_gather x1, blocking collectives, on_device(): first = lax.all_gather(arrived[:half], 'zi', axis=0, tiled=True)  21.1 us
    all_gather x1, blocking collectives, on_device(): second = lax.all_gather(later, 'zi', axis=0, tiled=True)  18.9 us
    all_to_all x1, starting transfers between devices, on_device(): lax.all_to_all(packed, ROWS_OF, split_axis=0, concat_axis=0, tiled=True)  17.7 us
    all_gather x1, blocking collectives, on_device(): gathered = lax.all_gather(hidden, 'zi', axis=0)  17.4 us
    ppermute x3, waiting for transfers between devices, exchange(): return lax.ppermute(array, axis, [(i, i ^ step) for i in range(size)])  10.4 us
    ppermute x3, starting transfers between devices, exchange(): return lax.ppermute(array, axis, [(i, i ^ step) for i in range(size)])  10.1 us
    all_to_all x1, starting transfers between devices, on_device(): lax.all_to_all(shares, ('dp', 'c'), split_axis=0, concat_axis=0, tiled=True)  4.7 us
  transfers between devices with their start and end apart: 6, of which 2 were waited for; matrix products, arithmetic and copies ran while one was open for 4% of the time, Pallas kernels for 3%

profile of v19, /device:TPU:24, one launch (start us, length us, event | category | flops | bytes accessed | tf_op | source)
XLA Modules:
  0.0 160.4 jit_solution(15317453481106948216)
XLA Ops:
  0.0 0.0 copy-start.1
  0.0 0.9 copy-done.1
  0.9 0.0 copy-start.3
  0.9 0.7 copy-done.3
  1.6 0.0 copy-start.4
  1.6 0.7 copy-done.4
  2.3 1.4 shard_map.46
  3.7 0.0 copy-start.2
  3.7 17.7 %all-to-all-start = ((bf16[16,4,3584]{2,1,0:T(4,128)(2,1)}), bf16[16,4,3584]{2,1,0:T(4,128)(2,1)S(1)}, u32[]{:S(2)}, u32[]{:S(2)}) async-start(bf16[16,4,3584]{2,1,0:T(4,128)(2,1)} %get-tuple-element.8), calls=%async_computation | async-start | bytes 917504 | tf_op jit(solution)/shard_map/all_to_all | solution.py:194
  21.3 0.5 slice.14
  23.1 3.5 %slice_select_fusion = bf16[384,3584]{1,0:T(8,128)(2,1)} fusion(bf16[576,3584]{1,0:T(8,128)(2,1)} %bitcast.38, pred[]{:T(512)} %bitcast.7), kind=kLoop, calls=%fused_computation | loop fusion | flops 1376256 | bytes 5505025 | tf_op jit(solution)/shard_map/jit(_where)/select_n | solution.py:192
  26.6 1.9 %collective-permute-start = (bf16[384,3584]{1,0:T(8,128)(2,1)}, bf16[384,3584]{1,0:T(8,128)(2,1)}, u32[]{:S(2)}, u32[]{:S(2)}) collective-permute-start(bf16[384,3584]{1,0:T(8,128)(2,1)} %slice_select_fusion), channel_id=1, source_target_pairs={{0,4},{4,0},{1,5},{5,1},{2,6},{6,2},{3,7},{7,3},{8,12},{12,8},{9,1... | collective-permute-start | bytes 8257544 | tf_op jit(solution)/shard_map/ppermute | solution.py:25
  28.6 1.0 dynamic-slice_bitcast_fusion
  29.6 0.1 reshape.20
  29.7 0.7 constant_dynamic-slice_fusion
  30.4 2.9 %collective-permute-start.1 = (bf16[48,896]{1,0:T(8,128)(2,1)S(1)}, bf16[48,896]{1,0:T(8,128)(2,1)S(1)}, u32[]{:S(2)}, u32[]{:S(2)}) collective-permute-start(bf16[48,896]{1,0:T(8,128)(2,1)S(1)} %bitcast.46), channel_id=1, source_target_pairs={{0,8},{8,0},{16,24},{24,16},{1,9},{9,1},{17,25},{25,17},{2,10},{10... | collective-permute-start | bytes 258056 | tf_op jit(solution)/shard_map/ppermute | solution.py:21
  33.4 3.4 %collective-permute-start.2 = (bf16[48,896]{1,0:T(8,128)(2,1)S(1)}, bf16[48,896]{1,0:T(8,128)(2,1)S(1)}, u32[]{:S(2)}, u32[]{:S(2)}) collective-permute-start(bf16[48,896]{1,0:T(8,128)(2,1)S(1)} %bitcast.47), channel_id=1, source_target_pairs={{0,16},{8,24},{16,0},{24,8},{1,17},{9,25},{17,1},{25,9},{2,18},{10... | collective-permute-start | bytes 258056 | tf_op jit(solution)/shard_map/ppermute | solution.py:21
  36.8 3.8 %collective-permute-start.3 = (bf16[48,896]{1,0:T(8,128)(2,1)S(1)}, bf16[48,896]{1,0:T(8,128)(2,1)S(1)}, u32[]{:S(2)}, u32[]{:S(2)}) collective-permute-start(bf16[48,896]{1,0:T(8,128)(2,1)S(1)} %bitcast.48), channel_id=1, source_target_pairs={{0,24},{8,16},{16,8},{24,0},{1,25},{9,17},{17,9},{25,1},{2,26},{10... | collective-permute-start | bytes 258056 | tf_op jit(solution)/shard_map/ppermute | solution.py:21
  40.6 0.0 copy-done.2
  40.6 5.4 %collective-permute-done.1.refs_1_ = bf16[48,896]{1,0:T(8,128)(2,1)S(1)} collective-permute-done((bf16[48,896]{1,0:T(8,128)(2,1)S(1)}, bf16[48,896]{1,0:T(8,128)(2,1)S(1)}, u32[]{:S(2)}, u32[]{:S(2)}) %collective-permute-start.1) | collective-permute-done | bytes 86048 | tf_op jit(solution)/shard_map/ppermute | solution.py:21
  46.0 5.0 %collective-permute-done.2.refs_2_ = bf16[48,896]{1,0:T(8,128)(2,1)S(1)} collective-permute-done((bf16[48,896]{1,0:T(8,128)(2,1)S(1)}, bf16[48,896]{1,0:T(8,128)(2,1)S(1)}, u32[]{:S(2)}, u32[]{:S(2)}) %collective-permute-start.2) | collective-permute-done | bytes 86048 | tf_op jit(solution)/shard_map/ppermute | solution.py:21
  51.0 0.0 collective-permute-done.3.refs_3_
  51.0 0.0 all-to-all-done._
  51.0 1.8 %shard_map.49 = bf16[8,4,48,896]{3,2,1,0:T(8,128)(2,1)} custom-call(bf16[16,4,3584]{2,1,0:T(4,128)(2,1)S(1)} %all-to-all-done._, bf16[48,896]{1,0:T(8,128)(2,1)S(1)} %bitcast.43, bf16[48,896]{1,0:T(8,128)(2,1)S(1)} %collective-permute-done.1.refs_1_, bf16[48,896]{1,0:T(8,128)(2,1)S(1)} %collective-permute-done.2.refs_2_, ...), custom_call_target="tpu_custom_call" | custom-call | tf_op jit(solution)/shard_map/pallas_call | solution.py:94
  52.9 4.7 %all-to-all-start.1 = ((bf16[8,4,48,896]{3,2,1,0:T(8,128)(2,1)}), bf16[8,4,48,896]{3,2,1,0:T(8,128)(2,1)S(1)}, u32[]{:S(2)}, u32[]{:S(2)}) async-start(bf16[8,4,48,896]{3,2,1,0:T(8,128)(2,1)} %shard_map.49), calls=%async_computation.1 | async-start | bytes 5505024 | tf_op jit(solution)/shard_map/all_to_all | solution.py:197
  57.6 0.0 copy-start
  57.6 0.1 pad_add_fusion.place_ref
  57.6 0.2 fusion.3
  57.8 21.1 %all_gather.12._.first_ref = bf16[32,4,3584]{2,1,0:T(4,128)(2,1)S(1)} all-gather(bf16[8,4,3584]{2,1,0:T(4,128)(2,1)S(1)} %get-tuple-element.10), channel_id=1, replica_groups=mesh['x'=4,'zb'=4,'zi'=4,'c'=2,'dp'=4] {'zi'}, dimensions={0}, use_global_device_ids=true | all-gather | bytes 1146880 | tf_op jit(solution)/shard_map/all_gather | solution.py:200
  79.0 18.9 %all_gather.13.second_ref = bf16[32,4,3584]{2,1,0:T(4,128)(2,1)S(1)} all-gather(bf16[8,4,3584]{2,1,0:T(4,128)(2,1)S(1)} %shard_map.47), channel_id=1, replica_groups=mesh['x'=4,'zb'=4,'zi'=4,'c'=2,'dp'=4] {'zi'}, dimensions={0}, use_global_device_ids=true | all-gather | bytes 1146880 | tf_op jit(solution)/shard_map/all_gather | solution.py:202
  97.8 0.0 collective-permute-done.other_ref
  97.8 0.0 copy-done
  97.8 3.5 %shard_map.48 = bf16[256,384]{1,0:T(8,128)(2,1)S(1)} custom-call(bf16[32,4,3584]{2,1,0:T(4,128)(2,1)S(1)} %all_gather.12._.first_ref, bf16[32,4,3584]{2,1,0:T(4,128)(2,1)S(1)} %all_gather.13.second_ref, bf16[576,3584]{1,0:T(8,128)(2,1)S(1)} %bitcast.39, bf16[384,3584]{1,0:T(8,128)(2,1)} %collective-permute-done.other_ref), custom_call_target="tpu_custom_call" | custom-call | tf_op jit(solution)/shard_map/pallas_call | solution.py:134
  101.4 17.4 %all-gather = bf16[1024,384]{1,0:T(8,128)(2,1)S(1)} all-gather(bf16[256,384]{1,0:T(8,128)(2,1)S(1)} %shard_map.48), channel_id=2, replica_groups=mesh['x'=4,'zb'=4,'zi'=4,'c'=2,'dp'=4] {'zi'}, dimensions={0}, use_global_device_ids=true | all-gather | bytes 983040 | tf_op jit(solution)/shard_map/all_gather | solution.py:204
  118.8 0.0 all-to-all-done.1
  118.8 1.7 %shard_map.50 = bf16[16,4,4,896]{3,2,1,0:T(4,128)(2,1)S(1)} custom-call(s32[2]{0:T(128)S(1)} %pad_add_fusion.place_ref, bf16[4,256,384]{2,1,0:T(8,128)(2,1)S(1)} %bitcast.41, bf16[4,2,4,48,896]{4,3,2,1,0:T(8,128)(2,1)S(1)} %bitcast.40), custom_call_target="tpu_custom_call" | custom-call | tf_op jit(solution)/shard_map/pallas_call | solution.py:163
  120.5 37.9 %all_to_all.15 = bf16[64,4,896]{2,1,0:T(4,128)(2,1)S(1)} all-to-all(bf16[64,4,896]{2,1,0:T(4,128)(2,1)S(1)} %bitcast.42), channel_id=1, replica_groups=mesh['x'=4,'zb'=4,'zi'=4,'c'=2,'dp'=4] {'zb','x','zi'}, dimensions={0} | all-to-all | bytes 917504 | tf_op jit(solution)/shard_map/all_to_all | solution.py:208
  158.5 0.2 reshape.28
  158.7 1.8 %fusion = bf16[2,8,4,896]{3,1,2,0:T(8,128)(2,1)} fusion(bf16[16,4,2,2,896]{4,3,2,1,0:T(2,128)(2,1)S(1)} %reshape.28, f32[2,2,16,8]{3,2,1,0:T(8,128)} %copy-done.2), kind=kOutput, calls=%fused_computation.2 | convolution fusion | flops 22077440 | bytes 575488 | tf_op jit(solution)/shard_map/mser,ezmsd->mrzd/dot_general | solution.py:210
  (5 shorter events, 0.1 us)
Async XLA Ops:
  0.0 0.9 copy-start.1
  0.9 0.7 copy-start.3
  1.6 0.7 copy-start.4
  3.7 36.9 %copy-start.2 = (f32[2,2,16,8]{3,2,1,0:T(8,128)}, f32[2,2,16,8]{3,2,1,0:T(8,128)S(1)}, u32[]{:S(2)}) copy-start(f32[2,2,16,8]{3,2,1,0:T(8,128)S(1)} %get-tuple-element.7) | copy-start | bytes 6148
  3.7 47.3 %all-to-all-start = ((bf16[16,4,3584]{2,1,0:T(4,128)(2,1)}), bf16[16,4,3584]{2,1,0:T(4,128)(2,1)S(1)}, u32[]{:S(2)}, u32[]{:S(2)}) async-start(bf16[16,4,3584]{2,1,0:T(4,128)(2,1)} %get-tuple-element.8), calls=%async_computation | async-start | bytes 917504 | tf_op jit(solution)/shard_map/all_to_all | solution.py:194
  26.6 71.2 %collective-permute-start = (bf16[384,3584]{1,0:T(8,128)(2,1)}, bf16[384,3584]{1,0:T(8,128)(2,1)}, u32[]{:S(2)}, u32[]{:S(2)}) collective-permute-start(bf16[384,3584]{1,0:T(8,128)(2,1)} %slice_select_fusion), channel_id=1, source_target_pairs={{0,4},{4,0},{1,5},{5,1},{2,6},{6,2},{3,7},{7,3},{8,12},{12,8},{9,1... | collective-permute-start | bytes 8257544 | tf_op jit(solution)/shard_map/ppermute | solution.py:25
  30.4 15.6 %collective-permute-start.1 = (bf16[48,896]{1,0:T(8,128)(2,1)S(1)}, bf16[48,896]{1,0:T(8,128)(2,1)S(1)}, u32[]{:S(2)}, u32[]{:S(2)}) collective-permute-start(bf16[48,896]{1,0:T(8,128)(2,1)S(1)} %bitcast.46), channel_id=1, source_target_pairs={{0,8},{8,0},{16,24},{24,16},{1,9},{9,1},{17,25},{25,17},{2,10},{10... | collective-permute-start | bytes 258056 | tf_op jit(solution)/shard_map/ppermute | solution.py:21
  33.4 17.6 %collective-permute-start.2 = (bf16[48,896]{1,0:T(8,128)(2,1)S(1)}, bf16[48,896]{1,0:T(8,128)(2,1)S(1)}, u32[]{:S(2)}, u32[]{:S(2)}) collective-permute-start(bf16[48,896]{1,0:T(8,128)(2,1)S(1)} %bitcast.47), channel_id=1, source_target_pairs={{0,16},{8,24},{16,0},{24,8},{1,17},{9,25},{17,1},{25,9},{2,18},{10... | collective-permute-start | bytes 258056 | tf_op jit(solution)/shard_map/ppermute | solution.py:21
  36.8 14.2 %collective-permute-start.3 = (bf16[48,896]{1,0:T(8,128)(2,1)S(1)}, bf16[48,896]{1,0:T(8,128)(2,1)S(1)}, u32[]{:S(2)}, u32[]{:S(2)}) collective-permute-start(bf16[48,896]{1,0:T(8,128)(2,1)S(1)} %bitcast.48), channel_id=1, source_target_pairs={{0,24},{8,16},{16,8},{24,0},{1,25},{9,17},{17,9},{25,1},{2,26},{10... | collective-permute-start | bytes 258056 | tf_op jit(solution)/shard_map/ppermute | solution.py:21
  52.9 65.9 %all-to-all-start.1 = ((bf16[8,4,48,896]{3,2,1,0:T(8,128)(2,1)}), bf16[8,4,48,896]{3,2,1,0:T(8,128)(2,1)S(1)}, u32[]{:S(2)}, u32[]{:S(2)}) async-start(bf16[8,4,48,896]{3,2,1,0:T(8,128)(2,1)} %shard_map.49), calls=%async_computation.1 | async-start | bytes 5505024 | tf_op jit(solution)/shard_map/all_to_all | solution.py:197
  57.6 40.3 %copy-start = (bf16[1,3584,576]{1,2,0:T(8,128)(2,1)S(1)}, bf16[1,3584,576]{1,2,0:T(8,128)(2,1)}, u32[]{:S(2)}) copy-start(bf16[1,3584,576]{1,2,0:T(8,128)(2,1)} %param.7) | copy-start | bytes 12386308

commit v20 on v19

--- a/solution.py
+++ b/solution.py
@@ -11,7 +11,7 @@
 BF = jnp.bfloat16
 F32 = jnp.float32
 ROWS_OF = ("zb", "x")
-HOME = ("zb", "x", "zi")
+HOME = ("x", "zb", "zi")
 ANYWHERE = pl.BlockSpec(memory_space=pl.ANY)
 NT = (((1,), (1,)), ((), ()))
 
@@ -25,31 +25,37 @@
     return lax.ppermute(array, "c", [(0, 1), (1, 0)])
 
 
+def named_in(ids, expert):
+    rows = ids.shape[1]
+    row = lax.broadcasted_iota(jnp.int32, (rows, rows), 0)
+    earlier = (row < lax.broadcasted_iota(jnp.int32, (rows, rows), 1)).astype(F32)
+    hits = [ids[k : k + 1] == expert for k in range(ids.shape[0])]
+    named = jnp.zeros(expert.shape, jnp.bool_)
+    for hit in hits:
+        named = named | hit
+    named = named.astype(F32)
+    return hits, named, jnp.dot(named, earlier, preferred_element_type=F32)
+
+
 def pack_kernel(sides, ids_ref, gates_ref, tokens_ref, out_ref, weights_ref):
-    batches, picks, rows = ids_ref.shape
+    batches, _, rows = ids_ref.shape
     experts, slots, width = out_ref.shape
     capacity = slots // batches
     count = experts * slots
-    at = lax.broadcasted_iota(jnp.int32, (experts, rows), 0)
-    expert = at % sides[0] * sides[1] + at // sides[0]
-    row = lax.broadcasted_iota(jnp.int32, (rows, rows), 0)
-    earlier = (row < lax.broadcasted_iota(jnp.int32, (rows, rows), 1)).astype(F32)
+    expert = lax.broadcasted_iota(jnp.int32, (experts, rows), 0)
+    sent = expert % sides[0] * sides[1] + expert // sides[0]
     owner = lax.broadcasted_iota(jnp.int32, (count, experts), 0) // slots
     spread = (owner == lax.broadcasted_iota(jnp.int32, (count, experts), 1)).astype(F32)
     slot = lax.broadcasted_iota(jnp.int32, (count, rows), 0) % slots
     total = jnp.zeros((count, width), F32)
     for m in range(batches):
-        ids, gates = ids_ref[m], gates_ref[m]
-        named = jnp.zeros((experts, rows), jnp.bool_)
+        hits, _, before = named_in(ids_ref[m], expert)
         weight = jnp.zeros((experts, rows), F32)
-        for k in range(picks):
-            hit = ids[k : k + 1] == expert
-            named = named | hit
-            weight = jnp.where(hit, gates[k : k + 1], weight)
-        named = named.astype(F32)
-        before = jnp.dot(named, earlier, preferred_element_type=F32)
+        for k, hit in enumerate(hits):
+            weight = jnp.where(hit, gates_ref[m, k : k + 1], weight)
         for s in range(capacity):
             weights_ref[m, s] = jnp.where(before == s, weight, 0.0)
+        _, named, before = named_in(ids_ref[m], sent)
         named = jnp.dot(spread, named, preferred_element_type=F32)
         before = jnp.dot(spread, before, preferred_element_type=F32)
         here = (slot // capacity == m) & (before == (slot % capacity).astype(F32))
@@ -143,8 +149,9 @@
 
 def down_kernel(place_ref, hidden_ref, shares_ref, out_ref):
     shares, cores, line = shares_ref.shape[:3]
-    experts, _, slots, columns = out_ref.shape
-    total = jnp.zeros((line * experts * slots, columns), F32)
+    across, blocks, _, slots, columns = out_ref.shape
+    half = across * blocks // 2
+    total = jnp.zeros((2 * line * half * slots, columns), F32)
     for at in range(line):
         k = place_ref[0] ^ at
         weights = [
@@ -152,19 +159,20 @@
         ]
         weights = jnp.concatenate(weights, axis=0)
         total += jnp.dot(hidden_ref[at], weights, preferred_element_type=F32)
-    half = experts // 2
-    total = total.astype(BF).reshape(2, line, half, slots, columns)
-    for part in range(2):
+    total = total.astype(BF).reshape(2, line, blocks // 2, across, slots, columns)
+    for block in range(blocks):
         for p in range(line):
-            out_ref[part * half : (part + 1) * half, p] = total[part, p]
-
-
-def outputs_of(place, hidden, shares, experts, slots):
+            out_ref[:, block, p] = total[block // (blocks // 2), p, block % (blocks // 2)]
+
+
+def outputs_of(place, hidden, shares, slots):
+    sides = (lax.axis_size("x"), lax.axis_size("zb"))
+    line, columns = hidden.shape[0], shares.shape[-1]
     return pl.pallas_call(
         down_kernel,
         in_specs=[pl.BlockSpec(memory_space=pltpu.SMEM)] + whole(2),
         out_specs=whole(1)[0],
-        out_shape=jax.ShapeDtypeStruct((experts, hidden.shape[0], slots, shares.shape[-1]), BF),
+        out_shape=jax.ShapeDtypeStruct(sides + (line, slots, columns), BF),
         compiler_params=pltpu.CompilerParams(vmem_limit_bytes=16 << 20),
     )(place, hidden, shares)
 
@@ -203,7 +211,7 @@
     hidden = hidden_of(first, second, turned, other)
     gathered = lax.all_gather(hidden, "zi", axis=0)
     position = jnp.stack([place, lax.axis_index("c")]).astype(jnp.int32)
-    done = outputs_of(position, gathered, shares, experts, slots)
+    done = outputs_of(position, gathered, shares, slots)
     done = done.reshape(experts * line, slots, columns)
     returned = lax.all_to_all(done, HOME, split_axis=0, concat_axis=0, tiled=True)
     returned = returned.reshape(experts, line, batches, capacity, columns).astype(F32)

time: 162 us -> 161 us (level)
  no operation moved by 1% of the time
where the time goes in v20:
time: 161 us; the launch traced here: 160 us
  blocking collectives  94.5 us (59%)
  starting transfers between devices  34.4 us (21%)
  waiting for transfers between devices  10.4 us (6%)
  Pallas kernels  8.61 us (5%)
  local copies, waits for them, and re-layouts  4.97 us (3%)
  other arithmetic  3.57 us (2%)
  matrix products  1.77 us (1%)
    all_to_all x1, blocking collectives, on_device(): lax.all_to_all(done, HOME, split_axis=0, concat_axis=0, tiled=True)  37.1 us
    all_gather x1, blocking collectives, on_device(): first = lax.all_gather(arrived[:half], 'zi', axis=0, tiled=True)  21.1 us
    all_gather x1, blocking collectives, on_device(): second = lax.all_gather(later, 'zi', axis=0, tiled=True)  18.9 us
    all_to_all x1, starting transfers between devices, on_device(): lax.all_to_all(packed, ROWS_OF, split_axis=0, concat_axis=0, tiled=True)  17.6 us
    all_gather x1, blocking collectives, on_device(): gathered = lax.all_gather(hidden, 'zi', axis=0)  17.5 us
    ppermute x3, waiting for transfers between devices, exchange(): return lax.ppermute(array, axis, [(i, i ^ step) for i in range(size)])  10.4 us
    ppermute x3, starting transfers between devices, exchange(): return lax.ppermute(array, axis, [(i, i ^ step) for i in range(size)])  10.1 us
    all_to_all x1, starting transfers between devices, on_device(): lax.all_to_all(shares, ('dp', 'c'), split_axis=0, concat_axis=0, tiled=True)  4.7 us
  transfers between devices with their start and end apart: 6, of which 2 were waited for; matrix products, arithmetic and copies ran while one was open for 4% of the time, Pallas kernels for 3%

profile of v20, /device:TPU:24, one launch (start us, length us, event | category | flops | bytes accessed | tf_op | source)
XLA Modules:
  0.0 159.7 jit_solution(246282847715165521)
XLA Ops:
  0.0 0.0 copy-start.1
  0.0 0.9 copy-done.1
  0.9 0.0 copy-start.3
  0.9 0.7 copy-done.3
  1.6 0.0 copy-start.4
  1.6 0.7 copy-done.4
  2.3 1.5 shard_map.46
  3.8 0.0 copy-start.2
  3.8 17.6 %all-to-all-start = ((bf16[16,4,3584]{2,1,0:T(4,128)(2,1)}), bf16[16,4,3584]{2,1,0:T(4,128)(2,1)S(1)}, u32[]{:S(2)}, u32[]{:S(2)}) async-start(bf16[16,4,3584]{2,1,0:T(4,128)(2,1)} %get-tuple-element.8), calls=%async_computation | async-start | bytes 917504 | tf_op jit(solution)/shard_map/all_to_all | solution.py:202
  21.4 0.5 slice.14
  23.2 3.5 %slice_select_fusion = bf16[384,3584]{1,0:T(8,128)(2,1)} fusion(bf16[576,3584]{1,0:T(8,128)(2,1)} %bitcast.38, pred[]{:T(512)} %bitcast.7), kind=kLoop, calls=%fused_computation | loop fusion | flops 1376256 | bytes 5505025 | tf_op jit(solution)/shard_map/jit(_where)/select_n | solution.py:200
  26.7 1.9 %collective-permute-start = (bf16[384,3584]{1,0:T(8,128)(2,1)}, bf16[384,3584]{1,0:T(8,128)(2,1)}, u32[]{:S(2)}, u32[]{:S(2)}) collective-permute-start(bf16[384,3584]{1,0:T(8,128)(2,1)} %slice_select_fusion), channel_id=1, source_target_pairs={{0,4},{4,0},{1,5},{5,1},{2,6},{6,2},{3,7},{7,3},{8,12},{12,8},{9,1... | collective-permute-start | bytes 8257544 | tf_op jit(solution)/shard_map/ppermute | solution.py:25
  28.7 1.0 dynamic-slice_bitcast_fusion
  29.7 0.1 reshape.20
  29.8 0.7 constant_dynamic-slice_fusion
  30.5 2.9 %collective-permute-start.1 = (bf16[48,896]{1,0:T(8,128)(2,1)S(1)}, bf16[48,896]{1,0:T(8,128)(2,1)S(1)}, u32[]{:S(2)}, u32[]{:S(2)}) collective-permute-start(bf16[48,896]{1,0:T(8,128)(2,1)S(1)} %bitcast.46), channel_id=1, source_target_pairs={{0,8},{8,0},{16,24},{24,16},{1,9},{9,1},{17,25},{25,17},{2,10},{10... | collective-permute-start | bytes 258056 | tf_op jit(solution)/shard_map/ppermute | solution.py:21
  33.5 3.4 %collective-permute-start.2 = (bf16[48,896]{1,0:T(8,128)(2,1)S(1)}, bf16[48,896]{1,0:T(8,128)(2,1)S(1)}, u32[]{:S(2)}, u32[]{:S(2)}) collective-permute-start(bf16[48,896]{1,0:T(8,128)(2,1)S(1)} %bitcast.47), channel_id=1, source_target_pairs={{0,16},{8,24},{16,0},{24,8},{1,17},{9,25},{17,1},{25,9},{2,18},{10... | collective-permute-start | bytes 258056 | tf_op jit(solution)/shard_map/ppermute | solution.py:21
  36.9 3.8 %collective-permute-start.3 = (bf16[48,896]{1,0:T(8,128)(2,1)S(1)}, bf16[48,896]{1,0:T(8,128)(2,1)S(1)}, u32[]{:S(2)}, u32[]{:S(2)}) collective-permute-start(bf16[48,896]{1,0:T(8,128)(2,1)S(1)} %bitcast.48), channel_id=1, source_target_pairs={{0,24},{8,16},{16,8},{24,0},{1,25},{9,17},{17,9},{25,1},{2,26},{10... | collective-permute-start | bytes 258056 | tf_op jit(solution)/shard_map/ppermute | solution.py:21
  40.7 0.0 copy-done.2
  40.7 5.4 %collective-permute-done.1.refs_1_ = bf16[48,896]{1,0:T(8,128)(2,1)S(1)} collective-permute-done((bf16[48,896]{1,0:T(8,128)(2,1)S(1)}, bf16[48,896]{1,0:T(8,128)(2,1)S(1)}, u32[]{:S(2)}, u32[]{:S(2)}) %collective-permute-start.1) | collective-permute-done | bytes 86048 | tf_op jit(solution)/shard_map/ppermute | solution.py:21
  46.1 5.0 %collective-permute-done.2.refs_2_ = bf16[48,896]{1,0:T(8,128)(2,1)S(1)} collective-permute-done((bf16[48,896]{1,0:T(8,128)(2,1)S(1)}, bf16[48,896]{1,0:T(8,128)(2,1)S(1)}, u32[]{:S(2)}, u32[]{:S(2)}) %collective-permute-start.2) | collective-permute-done | bytes 86048 | tf_op jit(solution)/shard_map/ppermute | solution.py:21
  51.1 0.0 collective-permute-done.3.refs_3_
  51.1 0.0 all-to-all-done._
  51.1 1.8 %shard_map.49 = bf16[8,4,48,896]{3,2,1,0:T(8,128)(2,1)} custom-call(bf16[16,4,3584]{2,1,0:T(4,128)(2,1)S(1)} %all-to-all-done._, bf16[48,896]{1,0:T(8,128)(2,1)S(1)} %bitcast.43, bf16[48,896]{1,0:T(8,128)(2,1)S(1)} %collective-permute-done.1.refs_1_, bf16[48,896]{1,0:T(8,128)(2,1)S(1)} %collective-permute-done.2.refs_2_, ...), custom_call_target="tpu_custom_call" | custom-call | tf_op jit(solution)/shard_map/pallas_call | solution.py:100
  53.0 4.7 %all-to-all-start.1 = ((bf16[8,4,48,896]{3,2,1,0:T(8,128)(2,1)}), bf16[8,4,48,896]{3,2,1,0:T(8,128)(2,1)S(1)}, u32[]{:S(2)}, u32[]{:S(2)}) async-start(bf16[8,4,48,896]{3,2,1,0:T(8,128)(2,1)} %shard_map.49), calls=%async_computation.1 | async-start | bytes 5505024 | tf_op jit(solution)/shard_map/all_to_all | solution.py:205
  57.7 0.0 copy-start
  57.7 0.1 pad_add_fusion.place_ref
  57.7 0.2 fusion.3
  57.9 21.1 %all_gather.12._.first_ref = bf16[32,4,3584]{2,1,0:T(4,128)(2,1)S(1)} all-gather(bf16[8,4,3584]{2,1,0:T(4,128)(2,1)S(1)} %get-tuple-element.10), channel_id=1, replica_groups=mesh['x'=4,'zb'=4,'zi'=4,'c'=2,'dp'=4] {'zi'}, dimensions={0}, use_global_device_ids=true | all-gather | bytes 1146880 | tf_op jit(solution)/shard_map/all_gather | solution.py:208
  79.1 18.9 %all_gather.13.second_ref = bf16[32,4,3584]{2,1,0:T(4,128)(2,1)S(1)} all-gather(bf16[8,4,3584]{2,1,0:T(4,128)(2,1)S(1)} %shard_map.47), channel_id=1, replica_groups=mesh['x'=4,'zb'=4,'zi'=4,'c'=2,'dp'=4] {'zi'}, dimensions={0}, use_global_device_ids=true | all-gather | bytes 1146880 | tf_op jit(solution)/shard_map/all_gather | solution.py:210
  97.9 0.0 collective-permute-done.other_ref
  97.9 0.0 copy-done
  98.0 3.5 %shard_map.48 = bf16[256,384]{1,0:T(8,128)(2,1)S(1)} custom-call(bf16[32,4,3584]{2,1,0:T(4,128)(2,1)S(1)} %all_gather.12._.first_ref, bf16[32,4,3584]{2,1,0:T(4,128)(2,1)S(1)} %all_gather.13.second_ref, bf16[576,3584]{1,0:T(8,128)(2,1)S(1)} %bitcast.39, bf16[384,3584]{1,0:T(8,128)(2,1)} %collective-permute-done.other_ref), custom_call_target="tpu_custom_call" | custom-call | tf_op jit(solution)/shard_map/pallas_call | solution.py:140
  101.5 17.5 %all-gather = bf16[1024,384]{1,0:T(8,128)(2,1)S(1)} all-gather(bf16[256,384]{1,0:T(8,128)(2,1)S(1)} %shard_map.48), channel_id=2, replica_groups=mesh['x'=4,'zb'=4,'zi'=4,'c'=2,'dp'=4] {'zi'}, dimensions={0}, use_global_device_ids=true | all-gather | bytes 983040 | tf_op jit(solution)/shard_map/all_gather | solution.py:212
  118.9 0.0 all-to-all-done.1
  118.9 1.7 %shard_map.50 = bf16[4,4,4,4,896]{4,3,2,1,0:T(4,128)(2,1)S(1)} custom-call(s32[2]{0:T(128)S(1)} %pad_add_fusion.place_ref, bf16[4,256,384]{2,1,0:T(8,128)(2,1)S(1)} %bitcast.41, bf16[4,2,4,48,896]{4,3,2,1,0:T(8,128)(2,1)S(1)} %bitcast.40), custom_call_target="tpu_custom_call" | custom-call | tf_op jit(solution)/shard_map/pallas_call | solution.py:171
  120.7 37.1 %all_to_all.15 = bf16[64,4,896]{2,1,0:T(4,128)(2,1)S(1)} all-to-all(bf16[64,4,896]{2,1,0:T(4,128)(2,1)S(1)} %bitcast.42), channel_id=1, replica_groups=mesh['x'=4,'zb'=4,'zi'=4,'c'=2,'dp'=4] {'x','zb','zi'}, dimensions={0} | all-to-all | bytes 917504 | tf_op jit(solution)/shard_map/all_to_all | solution.py:216
  157.7 0.2 reshape.28
  157.9 1.8 %fusion = bf16[2,8,4,896]{3,1,2,0:T(8,128)(2,1)} fusion(bf16[16,4,2,2,896]{4,3,2,1,0:T(2,128)(2,1)S(1)} %reshape.28, f32[2,2,16,8]{3,2,1,0:T(8,128)} %copy-done.2), kind=kOutput, calls=%fused_computation.2 | convolution fusion | flops 22077440 | bytes 575488 | tf_op jit(solution)/shard_map/mser,ezmsd->mrzd/dot_general | solution.py:218
  (5 shorter events, 0.1 us)
Async XLA Ops:
  0.0 0.9 copy-start.1
  0.9 0.7 copy-start.3
  1.6 0.7 copy-start.4
  3.8 36.9 %copy-start.2 = (f32[2,2,16,8]{3,2,1,0:T(8,128)}, f32[2,2,16,8]{3,2,1,0:T(8,128)S(1)}, u32[]{:S(2)}) copy-start(f32[2,2,16,8]{3,2,1,0:T(8,128)S(1)} %get-tuple-element.7) | copy-start | bytes 6148
  3.8 47.3 %all-to-all-start = ((bf16[16,4,3584]{2,1,0:T(4,128)(2,1)}), bf16[16,4,3584]{2,1,0:T(4,128)(2,1)S(1)}, u32[]{:S(2)}, u32[]{:S(2)}) async-start(bf16[16,4,3584]{2,1,0:T(4,128)(2,1)} %get-tuple-element.8), calls=%async_computation | async-start | bytes 917504 | tf_op jit(solution)/shard_map/all_to_all | solution.py:202
  26.7 71.2 %collective-permute-start = (bf16[384,3584]{1,0:T(8,128)(2,1)}, bf16[384,3584]{1,0:T(8,128)(2,1)}, u32[]{:S(2)}, u32[]{:S(2)}) collective-permute-start(bf16[384,3584]{1,0:T(8,128)(2,1)} %slice_select_fusion), channel_id=1, source_target_pairs={{0,4},{4,0},{1,5},{5,1},{2,6},{6,2},{3,7},{7,3},{8,12},{12,8},{9,1... | collective-permute-start | bytes 8257544 | tf_op jit(solution)/shard_map/ppermute | solution.py:25
  30.5 15.6 %collective-permute-start.1 = (bf16[48,896]{1,0:T(8,128)(2,1)S(1)}, bf16[48,896]{1,0:T(8,128)(2,1)S(1)}, u32[]{:S(2)}, u32[]{:S(2)}) collective-permute-start(bf16[48,896]{1,0:T(8,128)(2,1)S(1)} %bitcast.46), channel_id=1, source_target_pairs={{0,8},{8,0},{16,24},{24,16},{1,9},{9,1},{17,25},{25,17},{2,10},{10... | collective-permute-start | bytes 258056 | tf_op jit(solution)/shard_map/ppermute | solution.py:21
  33.5 17.6 %collective-permute-start.2 = (bf16[48,896]{1,0:T(8,128)(2,1)S(1)}, bf16[48,896]{1,0:T(8,128)(2,1)S(1)}, u32[]{:S(2)}, u32[]{:S(2)}) collective-permute-start(bf16[48,896]{1,0:T(8,128)(2,1)S(1)} %bitcast.47), channel_id=1, source_target_pairs={{0,16},{8,24},{16,0},{24,8},{1,17},{9,25},{17,1},{25,9},{2,18},{10... | collective-permute-start | bytes 258056 | tf_op jit(solution)/shard_map/ppermute | solution.py:21
  36.9 14.2 %collective-permute-start.3 = (bf16[48,896]{1,0:T(8,128)(2,1)S(1)}, bf16[48,896]{1,0:T(8,128)(2,1)S(1)}, u32[]{:S(2)}, u32[]{:S(2)}) collective-permute-start(bf16[48,896]{1,0:T(8,128)(2,1)S(1)} %bitcast.48), channel_id=1, source_target_pairs={{0,24},{8,16},{16,8},{24,0},{1,25},{9,17},{17,9},{25,1},{2,26},{10... | collective-permute-start | bytes 258056 | tf_op jit(solution)/shard_map/ppermute | solution.py:21
  53.0 66.0 %all-to-all-start.1 = ((bf16[8,4,48,896]{3,2,1,0:T(8,128)(2,1)}), bf16[8,4,48,896]{3,2,1,0:T(8,128)(2,1)S(1)}, u32[]{:S(2)}, u32[]{:S(2)}) async-start(bf16[8,4,48,896]{3,2,1,0:T(8,128)(2,1)} %shard_map.49), calls=%async_computation.1 | async-start | bytes 5505024 | tf_op jit(solution)/shard_map/all_to_all | solution.py:205
  57.7 40.3 %copy-start = (bf16[1,3584,576]{1,2,0:T(8,128)(2,1)S(1)}, bf16[1,3584,576]{1,2,0:T(8,128)(2,1)}, u32[]{:S(2)}) copy-start(bf16[1,3584,576]{1,2,0:T(8,128)(2,1)} %param.7) | copy-start | bytes 12386308

commit v21 on v18

--- a/solution.py
+++ b/solution.py
@@ -23,30 +23,30 @@
     return lax.ppermute(array, "c", [(0, 1), (1, 0)])
 
 
-def pack_kernel(ids_ref, gates_ref, tokens_ref, out_ref, weights_ref):
-    batches, picks, rows = ids_ref.shape
+def named_in(ids, experts):
+    rows = ids.shape[1]
+    expert = lax.broadcasted_iota(jnp.int32, (experts, rows), 0)
+    row = lax.broadcasted_iota(jnp.int32, (rows, rows), 0)
+    earlier = (row < lax.broadcasted_iota(jnp.int32, (rows, rows), 1)).astype(F32)
+    hits = [ids[k : k + 1] == expert for k in range(ids.shape[0])]
+    named = jnp.zeros((experts, rows), jnp.bool_)
+    for hit in hits:
+        named = named | hit
+    named = named.astype(F32)
+    return hits, named, jnp.dot(named, earlier, preferred_element_type=F32)
+
+
+def pack_kernel(ids_ref, tokens_ref, out_ref):
+    batches, _, rows = ids_ref.shape
     experts, slots, width = out_ref.shape
     capacity = slots // batches
     count = experts * slots
-    expert = lax.broadcasted_iota(jnp.int32, (experts, rows), 0)
-    row = lax.broadcasted_iota(jnp.int32, (rows, rows), 0)
-    earlier = (row < lax.broadcasted_iota(jnp.int32, (rows, rows), 1)).astype(F32)
     owner = lax.broadcasted_iota(jnp.int32, (count, experts), 0) // slots
     spread = (owner == lax.broadcasted_iota(jnp.int32, (count, experts), 1)).astype(F32)
     slot = lax.broadcasted_iota(jnp.int32, (count, rows), 0) % slots
     total = jnp.zeros((count, width), F32)
     for m in range(batches):
-        ids, gates = ids_ref[m], gates_ref[m]
-        named = jnp.zeros((experts, rows), jnp.bool_)
-        weight = jnp.zeros((experts, rows), F32)
-        for k in range(picks):
-            hit = ids[k : k + 1] == expert
-            named = named | hit
-            weight = jnp.where(hit, gates[k : k + 1], weight)
-        named = named.astype(F32)
-        before = jnp.dot(named, earlier, preferred_element_type=F32)
-        for s in range(capacity):
-            weights_ref[m, s] = jnp.where(before == s, weight, 0.0)
+        _, named, before = named_in(ids_ref[m], experts)
         named = jnp.dot(spread, named, preferred_element_type=F32)
         before = jnp.dot(spread, before, preferred_element_type=F32)
         here = (slot // capacity == m) & (before == (slot % capacity).astype(F32))
@@ -59,22 +59,18 @@
     return [pl.BlockSpec(memory_space=pltpu.VMEM)] * count
 
 
-def packed_of(expert_ids, gate_scores, tokens, experts, slots):
-    batches, rows, width = tokens.shape
+def packed_of(expert_ids, tokens, experts, slots):
     return pl.pallas_call(
         pack_kernel,
-        in_specs=whole(3),
-        out_specs=whole(2),
-        out_shape=[
-            jax.ShapeDtypeStruct((experts, slots, width), BF),
-            jax.ShapeDtypeStruct((batches, slots // batches, experts, rows), F32),
-        ],
+        in_specs=whole(2),
+        out_specs=whole(1)[0],
+        out_shape=jax.ShapeDtypeStruct((experts, slots, tokens.shape[2]), BF),
         compiler_params=pltpu.CompilerParams(vmem_limit_bytes=16 << 20),
-    )(expert_ids.transpose(0, 2, 1), gate_scores.transpose(0, 2, 1), tokens)
-
-
-def repeat_kernel(_, *refs):
-    arrays, out_ref, done = refs[:-2], refs[-2], refs[-1]
+    )(expert_ids.transpose(0, 2, 1), tokens)
+
+
+def repeat_kernel(_, ids_ref, gates_ref, *refs):
+    arrays, out_ref, weights_ref, done = refs[:-3], refs[-3], refs[-2], refs[-1]
     copies = [
         pltpu.make_async_copy(ref, out_ref.at[copy, k], done.at[copy, k])
         for copy in range(out_ref.shape[0])
@@ -82,19 +78,31 @@
     ]
     for copy in copies:
         copy.start()
+    batches, capacity, experts, rows = weights_ref.shape
+    for m in range(batches):
+        hits, _, before = named_in(ids_ref[m], experts)
+        weight = jnp.zeros((experts, rows), F32)
+        for k, hit in enumerate(hits):
+            weight = jnp.where(hit, gates_ref[m, k : k + 1], weight)
+        for s in range(capacity):
+            weights_ref[m, s] = jnp.where(before == s, weight, 0.0)
     for copy in copies:
         copy.wait()
 
 
-def repeat_after(earlier, arrays, times):
+def repeat_after(earlier, arrays, times, expert_ids, gate_scores, experts, capacity):
+    batches, rows, _ = expert_ids.shape
     return pl.pallas_call(
         repeat_kernel,
-        in_specs=[ANYWHERE] + whole(len(arrays)),
-        out_specs=pl.BlockSpec(memory_space=pltpu.HBM),
-        out_shape=jax.ShapeDtypeStruct((times, len(arrays)) + arrays[0].shape, BF),
+        in_specs=[ANYWHERE] + whole(2 + len(arrays)),
+        out_specs=[pl.BlockSpec(memory_space=pltpu.HBM)] + whole(1),
+        out_shape=[
+            jax.ShapeDtypeStruct((times, len(arrays)) + arrays[0].shape, BF),
+            jax.ShapeDtypeStruct((batches, capacity, experts, rows), F32),
+        ],
         scratch_shapes=[pltpu.SemaphoreType.DMA((times, len(arrays)))],
         compiler_params=pltpu.CompilerParams(vmem_limit_bytes=53 << 20),
-    )(earlier, *arrays)
+    )(earlier, expert_ids.transpose(0, 2, 1), gate_scores.transpose(0, 2, 1), *arrays)
 
 
 def copy_kernel(_, array_ref, out_ref):
@@ -183,13 +191,15 @@
         return lax.dynamic_index_in_dim(down, at, 1, keepdims=False)
 
     pieces = [for_place(place)] + [exchange(for_place(place ^ k), "zi", k) for k in range(1, line)]
-    packed, weighting = packed_of(expert_ids, gate_scores, tokens, experts, slots)
-    mark = weighting[0, 0, 0, 0]
+    packed = packed_of(expert_ids, tokens, experts, slots)
+    mark = packed[0, 0, 0]
     up = jnp.where(mark == mark, turned[: 2 * units], jnp.zeros((), BF))
     other = swap(up)
     arrived = lax.all_to_all(packed, ROWS_OF, split_axis=0, concat_axis=0, tiled=True)
     replicas, cores = lax.axis_size("dp"), lax.axis_size("c")
-    shares = repeat_after(arrived, pieces, replicas * cores)
+    shares, weighting = repeat_after(
+        arrived, pieces, replicas * cores, expert_ids, gate_scores, experts, capacity
+    )
     shares = lax.all_to_all(shares, ("dp", "c"), split_axis=0, concat_axis=0, tiled=True)
     shares = shares.reshape((replicas, cores) + shares.shape[1:])
     half = experts // 2

time: 161 us -> 161 us (level)
  transfers between devices with their start and end apart: 6 -> 6, of which waited for: 3 -> 2; matrix products, arithmetic and copies ran while one was open for 4% -> 4% of each run, Pallas kernels for 3% -> 3%
where the time goes in v21:
time: 161 us; the launch traced here: 160 us
  blocking collectives  94 us (58%)
  starting transfers between devices  34.5 us (21%)
  waiting for transfers between devices  10.5 us (7%)
  Pallas kernels  8.49 us (5%)
  local copies, waits for them, and re-layouts  5.49 us (3%)
  other arithmetic  3.58 us (2%)
  matrix products  1.77 us (1%)
    all_to_all x1, blocking collectives, on_device(): lax.all_to_all(done, HOME, split_axis=0, concat_axis=0, tiled=True)  33.6 us
    all_gather x1, blocking collectives, on_device(): first = lax.all_gather(arrived[:half], 'zi', axis=0, tiled=True)  23.2 us
    all_gather x1, blocking collectives, on_device(): second = lax.all_gather(later, 'zi', axis=0, tiled=True)  19.8 us
    all_to_all x1, starting transfers between devices, on_device(): lax.all_to_all(packed, ROWS_OF, split_axis=0, concat_axis=0, tiled=True)  17.7 us
    all_gather x1, blocking collectives, on_device(): gathered = lax.all_gather(hidden, 'zi', axis=0)  17.4 us
    ppermute x3, waiting for transfers between devices, exchange(): return lax.ppermute(array, axis, [(i, i ^ step) for i in range(size)])  10.5 us
    ppermute x3, starting transfers between devices, exchange(): return lax.ppermute(array, axis, [(i, i ^ step) for i in range(size)])  10.1 us
    all_to_all x1, starting transfers between devices, on_device(): lax.all_to_all(shares, ('dp', 'c'), split_axis=0, concat_axis=0, tiled=True)  4.69 us
  transfers between devices with their start and end apart: 6, of which 2 were waited for; matrix products, arithmetic and copies ran while one was open for 4% of the time, Pallas kernels for 3%

profile of v21, /device:TPU:24, one launch (start us, length us, event | category | flops | bytes accessed | tf_op | source)
XLA Modules:
  0.0 159.8 jit_solution(17696097101181332464)
XLA Ops:
  0.0 0.0 copy-start.1
  0.0 0.9 copy-done.1
  0.9 0.0 copy-start.3
  0.9 0.7 copy-done.3
  1.6 1.4 shard_map.46
  3.0 17.7 %all-to-all-start = ((bf16[16,4,3584]{2,1,0:T(4,128)(2,1)}), bf16[16,4,3584]{2,1,0:T(4,128)(2,1)S(1)}, u32[]{:S(2)}, u32[]{:S(2)}) async-start(bf16[16,4,3584]{2,1,0:T(4,128)(2,1)} %shard_map.46), calls=%async_computation | async-start | bytes 917504 | tf_op jit(solution)/shard_map/all_to_all | solution.py:198
  20.6 1.1 slice.18
  23.1 3.5 %slice_select_fusion = bf16[384,3584]{1,0:T(8,128)(2,1)} fusion(bf16[576,3584]{1,0:T(8,128)(2,1)} %bitcast.38, pred[]{:T(512)} %bitcast.9), kind=kLoop, calls=%fused_computation | loop fusion | flops 1376256 | bytes 5505025 | tf_op jit(solution)/shard_map/jit(_where)/select_n | solution.py:196
  26.6 0.0 copy-start.4
  26.6 0.0 copy-start.5
  26.6 2.0 %collective-permute-start.3 = (bf16[384,3584]{1,0:T(8,128)(2,1)}, bf16[384,3584]{1,0:T(8,128)(2,1)}, u32[]{:S(2)}, u32[]{:S(2)}) collective-permute-start(bf16[384,3584]{1,0:T(8,128)(2,1)} %slice_select_fusion), channel_id=1, source_target_pairs={{0,4},{4,0},{1,5},{5,1},{2,6},{6,2},{3,7},{7,3},{8,12},{12,8},{9,1... | collective-permute-start | bytes 8257544 | tf_op jit(solution)/shard_map/ppermute | solution.py:23
  28.6 1.0 dynamic-slice_bitcast_fusion
  29.6 0.1 reshape.20
  29.8 0.7 constant_dynamic-slice_fusion
  30.5 2.9 %collective-permute-start = (bf16[48,896]{1,0:T(8,128)(2,1)S(1)}, bf16[48,896]{1,0:T(8,128)(2,1)S(1)}, u32[]{:S(2)}, u32[]{:S(2)}) collective-permute-start(bf16[48,896]{1,0:T(8,128)(2,1)S(1)} %bitcast.47), channel_id=1, source_target_pairs={{0,8},{8,0},{16,24},{24,16},{1,9},{9,1},{17,25},{25,17},{2,10},{10... | collective-permute-start | bytes 258056 | tf_op jit(solution)/shard_map/ppermute | solution.py:19
  33.5 3.4 %collective-permute-start.1 = (bf16[48,896]{1,0:T(8,128)(2,1)S(1)}, bf16[48,896]{1,0:T(8,128)(2,1)S(1)}, u32[]{:S(2)}, u32[]{:S(2)}) collective-permute-start(bf16[48,896]{1,0:T(8,128)(2,1)S(1)} %bitcast.48), channel_id=1, source_target_pairs={{0,16},{8,24},{16,0},{24,8},{1,17},{9,25},{17,1},{25,9},{2,18},{10... | collective-permute-start | bytes 258056 | tf_op jit(solution)/shard_map/ppermute | solution.py:19
  36.9 3.8 %collective-permute-start.2 = (bf16[48,896]{1,0:T(8,128)(2,1)S(1)}, bf16[48,896]{1,0:T(8,128)(2,1)S(1)}, u32[]{:S(2)}, u32[]{:S(2)}) collective-permute-start(bf16[48,896]{1,0:T(8,128)(2,1)S(1)} %bitcast.49), channel_id=1, source_target_pairs={{0,24},{8,16},{16,8},{24,0},{1,25},{9,17},{17,9},{25,1},{2,26},{10... | collective-permute-start | bytes 258056 | tf_op jit(solution)/shard_map/ppermute | solution.py:19
  40.7 3.2 %collective-permute-done.refs_1_ = bf16[48,896]{1,0:T(8,128)(2,1)S(1)} collective-permute-done((bf16[48,896]{1,0:T(8,128)(2,1)S(1)}, bf16[48,896]{1,0:T(8,128)(2,1)S(1)}, u32[]{:S(2)}, u32[]{:S(2)}) %collective-permute-start) | collective-permute-done | bytes 86048 | tf_op jit(solution)/shard_map/ppermute | solution.py:19
  44.0 7.3 %collective-permute-done.1.refs_2_ = bf16[48,896]{1,0:T(8,128)(2,1)S(1)} collective-permute-done((bf16[48,896]{1,0:T(8,128)(2,1)S(1)}, bf16[48,896]{1,0:T(8,128)(2,1)S(1)}, u32[]{:S(2)}, u32[]{:S(2)}) %collective-permute-start.1) | collective-permute-done | bytes 86048 | tf_op jit(solution)/shard_map/ppermute | solution.py:19
  51.2 0.0 collective-permute-done.2.refs_3_
  51.2 0.0 all-to-all-done._
  51.2 0.0 copy-done.4
  51.2 0.0 copy-done.5
  51.2 1.8 %shard_map.47 = (bf16[8,4,48,896]{3,2,1,0:T(8,128)(2,1)}, f32[2,2,16,8]{3,2,1,0:T(8,128)S(1)}) custom-call(bf16[16,4,3584]{2,1,0:T(4,128)(2,1)S(1)} %all-to-all-done._, s32[2,2,8]{2,1,0:T(2,128)S(1)} %bitcast.45, f32[2,2,8]{2,1,0:T(2,128)S(1)} %bitcast.46, bf16[48,896]{1,0:T(8,128)(2,1)S(1)} %bitcast.43, bf16[48,896]{1,0:T(8,128)(2,1)S(1)} %collective-permute-done.refs_1_, ...), custom_call_target="tpu_custom_call" | custom-call | tf_op jit(solution)/shard_map/pallas_call | solution.py:95
  53.1 0.0 copy-start.2
  53.1 0.6 copy-done.2
  53.7 4.7 %all-to-all-start.1 = ((bf16[8,4,48,896]{3,2,1,0:T(8,128)(2,1)}), bf16[8,4,48,896]{3,2,1,0:T(8,128)(2,1)S(1)}, u32[]{:S(2)}, u32[]{:S(2)}) async-start(bf16[8,4,48,896]{3,2,1,0:T(8,128)(2,1)} %get-tuple-element.8), calls=%async_computation.1 | async-start | bytes 5505024 | tf_op jit(solution)/shard_map/all_to_all | solution.py:203
  58.4 0.0 copy-start
  58.4 0.1 pad_add_fusion.place_ref
  58.4 0.2 fusion.3
  58.6 23.2 %all_gather.12._.first_ref = bf16[32,4,3584]{2,1,0:T(4,128)(2,1)S(1)} all-gather(bf16[8,4,3584]{2,1,0:T(4,128)(2,1)S(1)} %get-tuple-element.10), channel_id=1, replica_groups=mesh['x'=4,'zb'=4,'zi'=4,'c'=2,'dp'=4] {'zi'}, dimensions={0}, use_global_device_ids=true | all-gather | bytes 1146880 | tf_op jit(solution)/shard_map/all_gather | solution.py:206
  81.8 19.8 %all_gather.13.second_ref = bf16[32,4,3584]{2,1,0:T(4,128)(2,1)S(1)} all-gather(bf16[8,4,3584]{2,1,0:T(4,128)(2,1)S(1)} %shard_map.48), channel_id=1, replica_groups=mesh['x'=4,'zb'=4,'zi'=4,'c'=2,'dp'=4] {'zi'}, dimensions={0}, use_global_device_ids=true | all-gather | bytes 1146880 | tf_op jit(solution)/shard_map/all_gather | solution.py:208
  101.6 0.0 collective-permute-done.3.other_ref
  101.6 0.0 copy-done
  101.6 3.5 %shard_map.49 = bf16[256,384]{1,0:T(8,128)(2,1)S(1)} custom-call(bf16[32,4,3584]{2,1,0:T(4,128)(2,1)S(1)} %all_gather.12._.first_ref, bf16[32,4,3584]{2,1,0:T(4,128)(2,1)S(1)} %all_gather.13.second_ref, bf16[576,3584]{1,0:T(8,128)(2,1)S(1)} %bitcast.39, bf16[384,3584]{1,0:T(8,128)(2,1)} %collective-permute-done.3.other_ref), custom_call_target="tpu_custom_call" | custom-call | tf_op jit(solution)/shard_map/pallas_call | solution.py:138
  105.1 17.4 %all-gather = bf16[1024,384]{1,0:T(8,128)(2,1)S(1)} all-gather(bf16[256,384]{1,0:T(8,128)(2,1)S(1)} %shard_map.49), channel_id=2, replica_groups=mesh['x'=4,'zb'=4,'zi'=4,'c'=2,'dp'=4] {'zi'}, dimensions={0}, use_global_device_ids=true | all-gather | bytes 983040 | tf_op jit(solution)/shard_map/all_gather | solution.py:210
  122.5 0.0 all-to-all-done.1
  122.5 1.7 %shard_map.50 = bf16[16,4,4,896]{3,2,1,0:T(4,128)(2,1)S(1)} custom-call(s32[2]{0:T(128)S(1)} %pad_add_fusion.place_ref, bf16[4,256,384]{2,1,0:T(8,128)(2,1)S(1)} %bitcast.41, bf16[4,2,4,48,896]{4,3,2,1,0:T(8,128)(2,1)S(1)} %bitcast.40), custom_call_target="tpu_custom_call" | custom-call | tf_op jit(solution)/shard_map/pallas_call | solution.py:167
  124.3 33.6 %all_to_all.15 = bf16[64,4,896]{2,1,0:T(4,128)(2,1)S(1)} all-to-all(bf16[64,4,896]{2,1,0:T(4,128)(2,1)S(1)} %bitcast.42), channel_id=1, replica_groups=mesh['x'=4,'zb'=4,'zi'=4,'c'=2,'dp'=4] {'x','zb','zi'}, dimensions={0} | all-to-all | bytes 917504 | tf_op jit(solution)/shard_map/all_to_all | solution.py:214
  157.9 0.2 reshape.28
  158.0 1.8 %fusion = bf16[2,8,4,896]{3,1,2,0:T(8,128)(2,1)} fusion(bf16[16,4,2,2,896]{4,3,2,1,0:T(2,128)(2,1)S(1)} %reshape.28, f32[2,2,16,8]{3,2,1,0:T(8,128)} %copy-done.2), kind=kOutput, calls=%fused_computation.2 | convolution fusion | flops 22077440 | bytes 575488 | tf_op jit(solution)/shard_map/mser,ezmsd->mrzd/dot_general | solution.py:216
  (5 shorter events, 0.1 us)
Async XLA Ops:
  0.0 0.9 copy-start.1
  0.9 0.7 copy-start.3
  3.0 48.2 %all-to-all-start = ((bf16[16,4,3584]{2,1,0:T(4,128)(2,1)}), bf16[16,4,3584]{2,1,0:T(4,128)(2,1)S(1)}, u32[]{:S(2)}, u32[]{:S(2)}) async-start(bf16[16,4,3584]{2,1,0:T(4,128)(2,1)} %shard_map.46), calls=%async_computation | async-start | bytes 917504 | tf_op jit(solution)/shard_map/all_to_all | solution.py:198
  26.6 24.6 %copy-start.4 = (s32[2,8,2]{1,2,0:T(2,128)S(1)}, s32[2,8,2]{1,2,0:T(2,128)}, u32[]{:S(2)}) copy-start(s32[2,8,2]{1,2,0:T(2,128)} %param.5) | copy-start | bytes 388
  26.6 24.7 %copy-start.5 = (f32[2,8,2]{1,2,0:T(2,128)S(1)}, f32[2,8,2]{1,2,0:T(2,128)}, u32[]{:S(2)}) copy-start(f32[2,8,2]{1,2,0:T(2,128)} %param.6) | copy-start | bytes 388
  26.6 75.0 %collective-permute-start.3 = (bf16[384,3584]{1,0:T(8,128)(2,1)}, bf16[384,3584]{1,0:T(8,128)(2,1)}, u32[]{:S(2)}, u32[]{:S(2)}) collective-permute-start(bf16[384,3584]{1,0:T(8,128)(2,1)} %slice_select_fusion), channel_id=1, source_target_pairs={{0,4},{4,0},{1,5},{5,1},{2,6},{6,2},{3,7},{7,3},{8,12},{12,8},{9,1... | collective-permute-start | bytes 8257544 | tf_op jit(solution)/shard_map/ppermute | solution.py:23
  30.5 13.4 %collective-permute-start = (bf16[48,896]{1,0:T(8,128)(2,1)S(1)}, bf16[48,896]{1,0:T(8,128)(2,1)S(1)}, u32[]{:S(2)}, u32[]{:S(2)}) collective-permute-start(bf16[48,896]{1,0:T(8,128)(2,1)S(1)} %bitcast.47), channel_id=1, source_target_pairs={{0,8},{8,0},{16,24},{24,16},{1,9},{9,1},{17,25},{25,17},{2,10},{10... | collective-permute-start | bytes 258056 | tf_op jit(solution)/shard_map/ppermute | solution.py:19
  33.5 17.7 %collective-permute-start.1 = (bf16[48,896]{1,0:T(8,128)(2,1)S(1)}, bf16[48,896]{1,0:T(8,128)(2,1)S(1)}, u32[]{:S(2)}, u32[]{:S(2)}) collective-permute-start(bf16[48,896]{1,0:T(8,128)(2,1)S(1)} %bitcast.48), channel_id=1, source_target_pairs={{0,16},{8,24},{16,0},{24,8},{1,17},{9,25},{17,1},{25,9},{2,18},{10... | collective-permute-start | bytes 258056 | tf_op jit(solution)/shard_map/ppermute | solution.py:19
  36.9 14.3 %collective-permute-start.2 = (bf16[48,896]{1,0:T(8,128)(2,1)S(1)}, bf16[48,896]{1,0:T(8,128)(2,1)S(1)}, u32[]{:S(2)}, u32[]{:S(2)}) collective-permute-start(bf16[48,896]{1,0:T(8,128)(2,1)S(1)} %bitcast.49), channel_id=1, source_target_pairs={{0,24},{8,16},{16,8},{24,0},{1,25},{9,17},{17,9},{25,1},{2,26},{10... | collective-permute-start | bytes 258056 | tf_op jit(solution)/shard_map/ppermute | solution.py:19
  53.1 0.6 copy-start.2
  53.7 68.8 %all-to-all-start.1 = ((bf16[8,4,48,896]{3,2,1,0:T(8,128)(2,1)}), bf16[8,4,48,896]{3,2,1,0:T(8,128)(2,1)S(1)}, u32[]{:S(2)}, u32[]{:S(2)}) async-start(bf16[8,4,48,896]{3,2,1,0:T(8,128)(2,1)} %get-tuple-element.8), calls=%async_computation.1 | async-start | bytes 5505024 | tf_op jit(solution)/shard_map/all_to_all | solution.py:203
  58.4 43.2 %copy-start = (bf16[1,3584,576]{1,2,0:T(8,128)(2,1)S(1)}, bf16[1,3584,576]{1,2,0:T(8,128)(2,1)}, u32[]{:S(2)}) copy-start(bf16[1,3584,576]{1,2,0:T(8,128)(2,1)} %param.7) | copy-start | bytes 12386308

commit v22 on v21

--- a/solution.py
+++ b/solution.py
@@ -69,8 +69,8 @@
     )(expert_ids.transpose(0, 2, 1), tokens)
 
 
-def repeat_kernel(_, ids_ref, gates_ref, *refs):
-    arrays, out_ref, weights_ref, done = refs[:-3], refs[-3], refs[-2], refs[-1]
+def repeat_kernel(_, *refs):
+    arrays, out_ref, done = refs[:-2], refs[-2], refs[-1]
     copies = [
         pltpu.make_async_copy(ref, out_ref.at[copy, k], done.at[copy, k])
         for copy in range(out_ref.shape[0])
@@ -78,31 +78,19 @@
     ]
     for copy in copies:
         copy.start()
-    batches, capacity, experts, rows = weights_ref.shape
-    for m in range(batches):
-        hits, _, before = named_in(ids_ref[m], experts)
-        weight = jnp.zeros((experts, rows), F32)
-        for k, hit in enumerate(hits):
-            weight = jnp.where(hit, gates_ref[m, k : k + 1], weight)
-        for s in range(capacity):
-            weights_ref[m, s] = jnp.where(before == s, weight, 0.0)
     for copy in copies:
         copy.wait()
 
 
-def repeat_after(earlier, arrays, times, expert_ids, gate_scores, experts, capacity):
-    batches, rows, _ = expert_ids.shape
+def repeat_after(earlier, arrays, times):
     return pl.pallas_call(
         repeat_kernel,
-        in_specs=[ANYWHERE] + whole(2 + len(arrays)),
-        out_specs=[pl.BlockSpec(memory_space=pltpu.HBM)] + whole(1),
-        out_shape=[
-            jax.ShapeDtypeStruct((times, len(arrays)) + arrays[0].shape, BF),
-            jax.ShapeDtypeStruct((batches, capacity, experts, rows), F32),
-        ],
+        in_specs=[ANYWHERE] + whole(len(arrays)),
+        out_specs=pl.BlockSpec(memory_space=pltpu.HBM),
+        out_shape=jax.ShapeDtypeStruct((times, len(arrays)) + arrays[0].shape, BF),
         scratch_shapes=[pltpu.SemaphoreType.DMA((times, len(arrays)))],
         compiler_params=pltpu.CompilerParams(vmem_limit_bytes=53 << 20),
-    )(earlier, expert_ids.transpose(0, 2, 1), gate_scores.transpose(0, 2, 1), *arrays)
+    )(earlier, *arrays)
 
 
 def copy_kernel(_, array_ref, out_ref):
@@ -145,7 +133,7 @@
     )(first, second, own, other)
 
 
-def down_kernel(place_ref, hidden_ref, shares_ref, out_ref):
+def down_kernel(place_ref, hidden_ref, shares_ref, ids_ref, gates_ref, out_ref, weights_ref):
     shares, cores, line = shares_ref.shape[:3]
     experts, _, slots, columns = out_ref.shape
     total = jnp.zeros((line * experts * slots, columns), F32)
@@ -161,16 +149,28 @@
     for part in range(2):
         for p in range(line):
             out_ref[part * half : (part + 1) * half, p] = total[part, p]
-
-
-def outputs_of(place, hidden, shares, experts, slots):
+    batches, capacity, _, rows = weights_ref.shape
+    for m in range(batches):
+        hits, _, before = named_in(ids_ref[m], experts)
+        weight = jnp.zeros((experts, rows), F32)
+        for k, hit in enumerate(hits):
+            weight = jnp.where(hit, gates_ref[m, k : k + 1], weight)
+        for s in range(capacity):
+            weights_ref[m, s] = jnp.where(before == s, weight, 0.0)
+
+
+def outputs_of(place, hidden, shares, expert_ids, gate_scores, experts, slots):
+    batches, rows, _ = expert_ids.shape
     return pl.pallas_call(
         down_kernel,
-        in_specs=[pl.BlockSpec(memory_space=pltpu.SMEM)] + whole(2),
-        out_specs=whole(1)[0],
-        out_shape=jax.ShapeDtypeStruct((experts, hidden.shape[0], slots, shares.shape[-1]), BF),
+        in_specs=[pl.BlockSpec(memory_space=pltpu.SMEM)] + whole(4),
+        out_specs=whole(2),
+        out_shape=[
+            jax.ShapeDtypeStruct((experts, hidden.shape[0], slots, shares.shape[-1]), BF),
+            jax.ShapeDtypeStruct((batches, slots // batches, experts, rows), F32),
+        ],
         compiler_params=pltpu.CompilerParams(vmem_limit_bytes=16 << 20),
-    )(place, hidden, shares)
+    )(place, hidden, shares, expert_ids.transpose(0, 2, 1), gate_scores.transpose(0, 2, 1))
 
 
 def on_device(tokens, expert_ids, gate_scores, expert_weights):
@@ -197,9 +197,7 @@
     other = swap(up)
     arrived = lax.all_to_all(packed, ROWS_OF, split_axis=0, concat_axis=0, tiled=True)
     replicas, cores = lax.axis_size("dp"), lax.axis_size("c")
-    shares, weighting = repeat_after(
-        arrived, pieces, replicas * cores, expert_ids, gate_scores, experts, capacity
-    )
+    shares = repeat_after(arrived, pieces, replicas * cores)
     shares = lax.all_to_all(shares, ("dp", "c"), split_axis=0, concat_axis=0, tiled=True)
     shares = shares.reshape((replicas, cores) + shares.shape[1:])
     half = experts // 2
@@ -209,7 +207,9 @@
     hidden = hidden_of(first, second, turned, other)
     gathered = lax.all_gather(hidden, "zi", axis=0)
     position = jnp.stack([place, lax.axis_index("c")]).astype(jnp.int32)
-    done = outputs_of(position, gathered, shares, experts, slots)
+    done, weighting = outputs_of(
+        position, gathered, shares, expert_ids, gate_scores, experts, slots
+    )
     done = done.reshape(experts * line, slots, columns)
     returned = lax.all_to_all(done, HOME, split_axis=0, concat_axis=0, tiled=True)
     returned = returned.reshape(experts, line, batches, capacity, columns).astype(F32)

time: 161 us -> 161 us (level)
  no operation moved by 1% of the time
where the time goes in v22:
time: 161 us; the launch traced here: 160 us
  blocking collectives  94 us (58%)
  starting transfers between devices  34.4 us (21%)
  waiting for transfers between devices  10.5 us (7%)
  Pallas kernels  8.5 us (5%)
  local copies, waits for them, and re-layouts  5.49 us (3%)
  other arithmetic  3.58 us (2%)
  matrix products  1.77 us (1%)
    all_to_all x1, blocking collectives, on_device(): lax.all_to_all(done, HOME, split_axis=0, concat_axis=0, tiled=True)  33.4 us
    all_gather x1, blocking collectives, on_device(): first = lax.all_gather(arrived[:half], 'zi', axis=0, tiled=True)  23.2 us
    all_gather x1, blocking collectives, on_device(): second = lax.all_gather(later, 'zi', axis=0, tiled=True)  19.9 us
    all_to_all x1, starting transfers between devices, on_device(): lax.all_to_all(packed, ROWS_OF, split_axis=0, concat_axis=0, tiled=True)  17.7 us
    all_gather x1, blocking collectives, on_device(): gathered = lax.all_gather(hidden, 'zi', axis=0)  17.4 us
    ppermute x3, waiting for transfers between devices, exchange(): return lax.ppermute(array, axis, [(i, i ^ step) for i in range(size)])  10.5 us
    ppermute x3, starting transfers between devices, exchange(): return lax.ppermute(array, axis, [(i, i ^ step) for i in range(size)])  10.1 us
    all_to_all x1, starting transfers between devices, on_device(): lax.all_to_all(shares, ('dp', 'c'), split_axis=0, concat_axis=0, tiled=True)  4.7 us
  transfers between devices with their start and end apart: 6, of which 2 were waited for; matrix products, arithmetic and copies ran while one was open for 4% of the time, Pallas kernels for 3%

profile of v22, /device:TPU:24, one launch (start us, length us, event | category | flops | bytes accessed | tf_op | source)
XLA Modules:
  0.0 159.7 jit_solution(8530102308632220885)
XLA Ops:
  0.0 0.0 copy-start.1
  0.0 0.9 copy-done.1
  0.9 0.0 copy-start.3
  0.9 0.7 copy-done.3
  1.6 1.4 shard_map.46
  3.0 17.7 %all-to-all-start = ((bf16[16,4,3584]{2,1,0:T(4,128)(2,1)}), bf16[16,4,3584]{2,1,0:T(4,128)(2,1)S(1)}, u32[]{:S(2)}, u32[]{:S(2)}) async-start(bf16[16,4,3584]{2,1,0:T(4,128)(2,1)} %shard_map.46), calls=%async_computation | async-start | bytes 917504 | tf_op jit(solution)/shard_map/all_to_all | solution.py:198
  20.6 1.1 slice.18
  23.1 3.5 %slice_select_fusion = bf16[384,3584]{1,0:T(8,128)(2,1)} fusion(bf16[576,3584]{1,0:T(8,128)(2,1)} %bitcast.38, pred[]{:T(512)} %bitcast.5), kind=kLoop, calls=%fused_computation | loop fusion | flops 1376256 | bytes 5505025 | tf_op jit(solution)/shard_map/jit(_where)/select_n | solution.py:196
  26.6 1.9 %collective-permute-start = (bf16[384,3584]{1,0:T(8,128)(2,1)}, bf16[384,3584]{1,0:T(8,128)(2,1)}, u32[]{:S(2)}, u32[]{:S(2)}) collective-permute-start(bf16[384,3584]{1,0:T(8,128)(2,1)} %slice_select_fusion), channel_id=1, source_target_pairs={{0,4},{4,0},{1,5},{5,1},{2,6},{6,2},{3,7},{7,3},{8,12},{12,8},{9,1... | collective-permute-start | bytes 8257544 | tf_op jit(solution)/shard_map/ppermute | solution.py:23
  28.5 1.0 dynamic-slice_bitcast_fusion
  29.5 0.1 reshape.20
  29.6 0.7 constant_dynamic-slice_fusion
  30.4 2.9 %collective-permute-start.1 = (bf16[48,896]{1,0:T(8,128)(2,1)S(1)}, bf16[48,896]{1,0:T(8,128)(2,1)S(1)}, u32[]{:S(2)}, u32[]{:S(2)}) collective-permute-start(bf16[48,896]{1,0:T(8,128)(2,1)S(1)} %bitcast.47), channel_id=1, source_target_pairs={{0,8},{8,0},{16,24},{24,16},{1,9},{9,1},{17,25},{25,17},{2,10},{10... | collective-permute-start | bytes 258056 | tf_op jit(solution)/shard_map/ppermute | solution.py:19
  33.3 3.4 %collective-permute-start.2 = (bf16[48,896]{1,0:T(8,128)(2,1)S(1)}, bf16[48,896]{1,0:T(8,128)(2,1)S(1)}, u32[]{:S(2)}, u32[]{:S(2)}) collective-permute-start(bf16[48,896]{1,0:T(8,128)(2,1)S(1)} %bitcast.48), channel_id=1, source_target_pairs={{0,16},{8,24},{16,0},{24,8},{1,17},{9,25},{17,1},{25,9},{2,18},{10... | collective-permute-start | bytes 258056 | tf_op jit(solution)/shard_map/ppermute | solution.py:19
  36.7 3.8 %collective-permute-start.3 = (bf16[48,896]{1,0:T(8,128)(2,1)S(1)}, bf16[48,896]{1,0:T(8,128)(2,1)S(1)}, u32[]{:S(2)}, u32[]{:S(2)}) collective-permute-start(bf16[48,896]{1,0:T(8,128)(2,1)S(1)} %bitcast.49), channel_id=1, source_target_pairs={{0,24},{8,16},{16,8},{24,0},{1,25},{9,17},{17,9},{25,1},{2,26},{10... | collective-permute-start | bytes 258056 | tf_op jit(solution)/shard_map/ppermute | solution.py:19
  40.6 3.5 %collective-permute-done.1.refs_1_ = bf16[48,896]{1,0:T(8,128)(2,1)S(1)} collective-permute-done((bf16[48,896]{1,0:T(8,128)(2,1)S(1)}, bf16[48,896]{1,0:T(8,128)(2,1)S(1)}, u32[]{:S(2)}, u32[]{:S(2)}) %collective-permute-start.1) | collective-permute-done | bytes 86048 | tf_op jit(solution)/shard_map/ppermute | solution.py:19
  44.0 7.0 %collective-permute-done.2.refs_2_ = bf16[48,896]{1,0:T(8,128)(2,1)S(1)} collective-permute-done((bf16[48,896]{1,0:T(8,128)(2,1)S(1)}, bf16[48,896]{1,0:T(8,128)(2,1)S(1)}, u32[]{:S(2)}, u32[]{:S(2)}) %collective-permute-start.2) | collective-permute-done | bytes 86048 | tf_op jit(solution)/shard_map/ppermute | solution.py:19
  51.1 0.0 collective-permute-done.3.refs_3_
  51.1 0.0 all-to-all-done._
  51.1 1.8 %shard_map.49 = bf16[8,4,48,896]{3,2,1,0:T(8,128)(2,1)} custom-call(bf16[16,4,3584]{2,1,0:T(4,128)(2,1)S(1)} %all-to-all-done._, bf16[48,896]{1,0:T(8,128)(2,1)S(1)} %bitcast.43, bf16[48,896]{1,0:T(8,128)(2,1)S(1)} %collective-permute-done.1.refs_1_, bf16[48,896]{1,0:T(8,128)(2,1)S(1)} %collective-permute-done.2.refs_2_, ...), custom_call_target="tpu_custom_call" | custom-call | tf_op jit(solution)/shard_map/pallas_call | solution.py:86
  52.9 4.7 %all-to-all-start.1 = ((bf16[8,4,48,896]{3,2,1,0:T(8,128)(2,1)}), bf16[8,4,48,896]{3,2,1,0:T(8,128)(2,1)S(1)}, u32[]{:S(2)}, u32[]{:S(2)}) async-start(bf16[8,4,48,896]{3,2,1,0:T(8,128)(2,1)} %shard_map.49), calls=%async_computation.1 | async-start | bytes 5505024 | tf_op jit(solution)/shard_map/all_to_all | solution.py:201
  57.6 0.0 copy-start
  57.6 0.1 pad_add_fusion.place_ref
  57.7 0.2 fusion.3
  57.9 23.2 %all_gather.12._.first_ref = bf16[32,4,3584]{2,1,0:T(4,128)(2,1)S(1)} all-gather(bf16[8,4,3584]{2,1,0:T(4,128)(2,1)S(1)} %get-tuple-element.10), channel_id=1, replica_groups=mesh['x'=4,'zb'=4,'zi'=4,'c'=2,'dp'=4] {'zi'}, dimensions={0}, use_global_device_ids=true | all-gather | bytes 1146880 | tf_op jit(solution)/shard_map/all_gather | solution.py:204
  81.1 19.9 %all_gather.13.second_ref = bf16[32,4,3584]{2,1,0:T(4,128)(2,1)S(1)} all-gather(bf16[8,4,3584]{2,1,0:T(4,128)(2,1)S(1)} %shard_map.47), channel_id=1, replica_groups=mesh['x'=4,'zb'=4,'zi'=4,'c'=2,'dp'=4] {'zi'}, dimensions={0}, use_global_device_ids=true | all-gather | bytes 1146880 | tf_op jit(solution)/shard_map/all_gather | solution.py:206
  101.0 0.0 copy-start.4
  101.0 0.0 copy-start.5
  101.0 0.0 collective-permute-done.other_ref
  101.0 0.0 copy-done
  101.0 3.5 %shard_map.48 = bf16[256,384]{1,0:T(8,128)(2,1)S(1)} custom-call(bf16[32,4,3584]{2,1,0:T(4,128)(2,1)S(1)} %all_gather.12._.first_ref, bf16[32,4,3584]{2,1,0:T(4,128)(2,1)S(1)} %all_gather.13.second_ref, bf16[576,3584]{1,0:T(8,128)(2,1)S(1)} %bitcast.39, bf16[384,3584]{1,0:T(8,128)(2,1)} %collective-permute-done.other_ref), custom_call_target="tpu_custom_call" | custom-call | tf_op jit(solution)/shard_map/pallas_call | solution.py:126
  104.5 17.4 %all-gather = bf16[1024,384]{1,0:T(8,128)(2,1)S(1)} all-gather(bf16[256,384]{1,0:T(8,128)(2,1)S(1)} %shard_map.48), channel_id=2, replica_groups=mesh['x'=4,'zb'=4,'zi'=4,'c'=2,'dp'=4] {'zi'}, dimensions={0}, use_global_device_ids=true | all-gather | bytes 983040 | tf_op jit(solution)/shard_map/all_gather | solution.py:208
  121.9 0.0 all-to-all-done.1
  121.9 0.0 copy-done.4
  121.9 0.0 copy-done.5
  121.9 1.7 %shard_map.50 = (bf16[16,4,4,896]{3,2,1,0:T(4,128)(2,1)S(1)}, f32[2,2,16,8]{3,2,1,0:T(8,128)S(1)}) custom-call(s32[2]{0:T(128)S(1)} %pad_add_fusion.place_ref, bf16[4,256,384]{2,1,0:T(8,128)(2,1)S(1)} %bitcast.41, bf16[4,2,4,48,896]{4,3,2,1,0:T(8,128)(2,1)S(1)} %bitcast.40, s32[2,2,8]{2,1,0:T(2,128)S(1)} %bitcast.45, f32[2,2,8]{2,1,0:T(2,128)S(1)} %bitcast.46), custom_call_target="tpu_custom_call" | custom-call | tf_op jit(solution)/shard_map/pallas_call | solution.py:164
  123.7 0.0 copy-start.2
  123.7 0.6 copy-done.2
  124.3 33.4 %all_to_all.15 = bf16[64,4,896]{2,1,0:T(4,128)(2,1)S(1)} all-to-all(bf16[64,4,896]{2,1,0:T(4,128)(2,1)S(1)} %bitcast.42), channel_id=1, replica_groups=mesh['x'=4,'zb'=4,'zi'=4,'c'=2,'dp'=4] {'x','zb','zi'}, dimensions={0} | all-to-all | bytes 917504 | tf_op jit(solution)/shard_map/all_to_all | solution.py:214
  157.7 0.2 reshape.28
  157.9 1.8 %fusion = bf16[2,8,4,896]{3,1,2,0:T(8,128)(2,1)} fusion(bf16[16,4,2,2,896]{4,3,2,1,0:T(2,128)(2,1)S(1)} %reshape.28, f32[2,2,16,8]{3,2,1,0:T(8,128)} %copy-done.2), kind=kOutput, calls=%fused_computation.2 | convolution fusion | flops 22077440 | bytes 575488 | tf_op jit(solution)/shard_map/mser,ezmsd->mrzd/dot_general | solution.py:216
  (5 shorter events, 0.1 us)
Async XLA Ops:
  0.0 0.9 copy-start.1
  0.9 0.7 copy-start.3
  3.0 48.1 %all-to-all-start = ((bf16[16,4,3584]{2,1,0:T(4,128)(2,1)}), bf16[16,4,3584]{2,1,0:T(4,128)(2,1)S(1)}, u32[]{:S(2)}, u32[]{:S(2)}) async-start(bf16[16,4,3584]{2,1,0:T(4,128)(2,1)} %shard_map.46), calls=%async_computation | async-start | bytes 917504 | tf_op jit(solution)/shard_map/all_to_all | solution.py:198
  26.6 74.4 %collective-permute-start = (bf16[384,3584]{1,0:T(8,128)(2,1)}, bf16[384,3584]{1,0:T(8,128)(2,1)}, u32[]{:S(2)}, u32[]{:S(2)}) collective-permute-start(bf16[384,3584]{1,0:T(8,128)(2,1)} %slice_select_fusion), channel_id=1, source_target_pairs={{0,4},{4,0},{1,5},{5,1},{2,6},{6,2},{3,7},{7,3},{8,12},{12,8},{9,1... | collective-permute-start | bytes 8257544 | tf_op jit(solution)/shard_map/ppermute | solution.py:23
  30.4 13.7 %collective-permute-start.1 = (bf16[48,896]{1,0:T(8,128)(2,1)S(1)}, bf16[48,896]{1,0:T(8,128)(2,1)S(1)}, u32[]{:S(2)}, u32[]{:S(2)}) collective-permute-start(bf16[48,896]{1,0:T(8,128)(2,1)S(1)} %bitcast.47), channel_id=1, source_target_pairs={{0,8},{8,0},{16,24},{24,16},{1,9},{9,1},{17,25},{25,17},{2,10},{10... | collective-permute-start | bytes 258056 | tf_op jit(solution)/shard_map/ppermute | solution.py:19
  33.3 17.7 %collective-permute-start.2 = (bf16[48,896]{1,0:T(8,128)(2,1)S(1)}, bf16[48,896]{1,0:T(8,128)(2,1)S(1)}, u32[]{:S(2)}, u32[]{:S(2)}) collective-permute-start(bf16[48,896]{1,0:T(8,128)(2,1)S(1)} %bitcast.48), channel_id=1, source_target_pairs={{0,16},{8,24},{16,0},{24,8},{1,17},{9,25},{17,1},{25,9},{2,18},{10... | collective-permute-start | bytes 258056 | tf_op jit(solution)/shard_map/ppermute | solution.py:19
  36.7 14.3 %collective-permute-start.3 = (bf16[48,896]{1,0:T(8,128)(2,1)S(1)}, bf16[48,896]{1,0:T(8,128)(2,1)S(1)}, u32[]{:S(2)}, u32[]{:S(2)}) collective-permute-start(bf16[48,896]{1,0:T(8,128)(2,1)S(1)} %bitcast.49), channel_id=1, source_target_pairs={{0,24},{8,16},{16,8},{24,0},{1,25},{9,17},{17,9},{25,1},{2,26},{10... | collective-permute-start | bytes 258056 | tf_op jit(solution)/shard_map/ppermute | solution.py:19
  52.9 69.0 %all-to-all-start.1 = ((bf16[8,4,48,896]{3,2,1,0:T(8,128)(2,1)}), bf16[8,4,48,896]{3,2,1,0:T(8,128)(2,1)S(1)}, u32[]{:S(2)}, u32[]{:S(2)}) async-start(bf16[8,4,48,896]{3,2,1,0:T(8,128)(2,1)} %shard_map.49), calls=%async_computation.1 | async-start | bytes 5505024 | tf_op jit(solution)/shard_map/all_to_all | solution.py:201
  57.6 43.4 %copy-start = (bf16[1,3584,576]{1,2,0:T(8,128)(2,1)S(1)}, bf16[1,3584,576]{1,2,0:T(8,128)(2,1)}, u32[]{:S(2)}) copy-start(bf16[1,3584,576]{1,2,0:T(8,128)(2,1)} %param.7) | copy-start | bytes 12386308
  101.0 20.9 %copy-start.4 = (s32[2,8,2]{1,2,0:T(2,128)S(1)}, s32[2,8,2]{1,2,0:T(2,128)}, u32[]{:S(2)}) copy-start(s32[2,8,2]{1,2,0:T(2,128)} %param.5) | copy-start | bytes 388
  101.0 20.9 %copy-start.5 = (f32[2,8,2]{1,2,0:T(2,128)S(1)}, f32[2,8,2]{1,2,0:T(2,128)}, u32[]{:S(2)}) copy-start(f32[2,8,2]{1,2,0:T(2,128)} %param.6) | copy-start | bytes 388
  123.7 0.6 copy-start.2

commit v23 on v22

--- a/solution.py
+++ b/solution.py
@@ -192,9 +192,7 @@
 
     pieces = [for_place(place)] + [exchange(for_place(place ^ k), "zi", k) for k in range(1, line)]
     packed = packed_of(expert_ids, tokens, experts, slots)
-    mark = packed[0, 0, 0]
-    up = jnp.where(mark == mark, turned[: 2 * units], jnp.zeros((), BF))
-    other = swap(up)
+    other = swap(turned)
     arrived = lax.all_to_all(packed, ROWS_OF, split_axis=0, concat_axis=0, tiled=True)
     replicas, cores = lax.axis_size("dp"), lax.axis_size("c")
     shares = repeat_after(arrived, pieces, replicas * cores)

time: 161 us -> 163 us (1.012)
  waiting for transfers between devices: 10.5 us -> 15.4 us
  other arithmetic: 3.58 us -> 0.07 us
  blocking collectives: 94 us -> 97.3 us
    ppermute x3, waiting for transfers between devices: 10.5 us -> 14.8 us  [exchange(): return lax.ppermute(array, axis, [(i, i ^ step) for i in range(size)])]
    select_n x1 -> x0, other arithmetic: 3.51 us -> none  [on_device(): up = jnp.where(mark == mark, turned[:2 * units], jnp.zeros((), BF))]
    all_gather x1, blocking collectives: 23.2 us -> 26.5 us  [on_device(): first = lax.all_gather(arrived[:half], 'zi', axis=0, tiled=True)]
  transfers between devices with their start and end apart: 6 -> 6, of which waited for: 2 -> 2; matrix products, arithmetic and copies ran while one was open for 4% -> 1% of each run, Pallas kernels for 3% -> 4%
where the time goes in v23:
time: 163 us; the launch traced here: 162 us
  blocking collectives  97.3 us (60%)
  starting transfers between devices  34.4 us (21%)
  waiting for transfers between devices  15.4 us (9%)
  Pallas kernels  8.52 us (5%)
  local copies, waits for them, and re-layouts  4.37 us (3%)
  matrix products  1.77 us (1%)
    all_to_all x1, blocking collectives, on_device(): lax.all_to_all(done, HOME, split_axis=0, concat_axis=0, tiled=True)  33.5 us
    all_gather x1, blocking collectives, on_device(): first = lax.all_gather(arrived[:half], 'zi', axis=0, tiled=True)  26.5 us
    all_gather x1, blocking collectives, on_device(): second = lax.all_gather(later, 'zi', axis=0, tiled=True)  19.9 us
    all_to_all x1, starting transfers between devices, on_device(): lax.all_to_all(packed, ROWS_OF, split_axis=0, concat_axis=0, tiled=True)  17.7 us
    all_gather x1, blocking collectives, on_device(): gathered = lax.all_gather(hidden, 'zi', axis=0)  17.4 us
    ppermute x3, waiting for transfers between devices, exchange(): return lax.ppermute(array, axis, [(i, i ^ step) for i in range(size)])  14.8 us
    ppermute x3, starting transfers between devices, exchange(): return lax.ppermute(array, axis, [(i, i ^ step) for i in range(size)])  10.1 us
    all_to_all x1, starting transfers between devices, on_device(): lax.all_to_all(shares, ('dp', 'c'), split_axis=0, concat_axis=0, tiled=True)  4.7 us
  transfers between devices with their start and end apart: 6, of which 2 were waited for; matrix products, arithmetic and copies ran while one was open for 1% of the time, Pallas kernels for 4%

profile of v23, /device:TPU:24, one launch (start us, length us, event | category | flops | bytes accessed | tf_op | source)
XLA Modules:
  0.0 162.0 jit_solution(16773892364012602653)
XLA Ops:
  0.0 1.9 %collective-permute-start = (bf16[576,3584]{1,0:T(8,128)(2,1)}, bf16[576,3584]{1,0:T(8,128)(2,1)}, u32[]{:S(2)}, u32[]{:S(2)}) collective-permute-start(bf16[576,3584]{1,0:T(8,128)(2,1)} %bitcast.38), channel_id=1, source_target_pairs={{0,4},{4,0},{1,5},{5,1},{2,6},{6,2},{3,7},{7,3},{8,12},{12,8},{9,1... | collective-permute-start | bytes 12386312 | tf_op jit(solution)/shard_map/ppermute | solution.py:23
  1.9 0.0 copy-start.1
  1.9 0.9 copy-done.1
  2.8 0.0 copy-start.3
  2.8 0.7 copy-done.3
  3.5 1.4 shard_map.46
  4.9 17.7 %all-to-all-start = ((bf16[16,4,3584]{2,1,0:T(4,128)(2,1)}), bf16[16,4,3584]{2,1,0:T(4,128)(2,1)S(1)}, u32[]{:S(2)}, u32[]{:S(2)}) async-start(bf16[16,4,3584]{2,1,0:T(4,128)(2,1)} %shard_map.46), calls=%async_computation | async-start | bytes 917504 | tf_op jit(solution)/shard_map/all_to_all | solution.py:196
  22.6 1.0 dynamic-slice_bitcast_fusion
  23.6 0.1 reshape.19
  23.7 0.7 constant_dynamic-slice_fusion
  24.5 2.9 %collective-permute-start.1 = (bf16[48,896]{1,0:T(8,128)(2,1)S(1)}, bf16[48,896]{1,0:T(8,128)(2,1)S(1)}, u32[]{:S(2)}, u32[]{:S(2)}) collective-permute-start(bf16[48,896]{1,0:T(8,128)(2,1)S(1)} %bitcast.46), channel_id=1, source_target_pairs={{0,8},{8,0},{16,24},{24,16},{1,9},{9,1},{17,25},{25,17},{2,10},{10... | collective-permute-start | bytes 258056 | tf_op jit(solution)/shard_map/ppermute | solution.py:19
  27.4 3.4 %collective-permute-start.2 = (bf16[48,896]{1,0:T(8,128)(2,1)S(1)}, bf16[48,896]{1,0:T(8,128)(2,1)S(1)}, u32[]{:S(2)}, u32[]{:S(2)}) collective-permute-start(bf16[48,896]{1,0:T(8,128)(2,1)S(1)} %bitcast.47), channel_id=1, source_target_pairs={{0,16},{8,24},{16,0},{24,8},{1,17},{9,25},{17,1},{25,9},{2,18},{10... | collective-permute-start | bytes 258056 | tf_op jit(solution)/shard_map/ppermute | solution.py:19
  30.8 3.8 %collective-permute-start.3 = (bf16[48,896]{1,0:T(8,128)(2,1)S(1)}, bf16[48,896]{1,0:T(8,128)(2,1)S(1)}, u32[]{:S(2)}, u32[]{:S(2)}) collective-permute-start(bf16[48,896]{1,0:T(8,128)(2,1)S(1)} %bitcast.48), channel_id=1, source_target_pairs={{0,24},{8,16},{16,8},{24,0},{1,25},{9,17},{17,9},{25,1},{2,26},{10... | collective-permute-start | bytes 258056 | tf_op jit(solution)/shard_map/ppermute | solution.py:19
  34.7 14.7 %collective-permute-done.1.refs_1_ = bf16[48,896]{1,0:T(8,128)(2,1)S(1)} collective-permute-done((bf16[48,896]{1,0:T(8,128)(2,1)S(1)}, bf16[48,896]{1,0:T(8,128)(2,1)S(1)}, u32[]{:S(2)}, u32[]{:S(2)}) %collective-permute-start.1) | collective-permute-done | bytes 86048 | tf_op jit(solution)/shard_map/ppermute | solution.py:19
  49.4 0.0 collective-permute-done.2.refs_2_
  49.4 0.0 collective-permute-done.3.refs_3_
  49.4 0.7 all-to-all-done._
  50.1 1.8 %shard_map.49 = bf16[8,4,48,896]{3,2,1,0:T(8,128)(2,1)} custom-call(bf16[16,4,3584]{2,1,0:T(4,128)(2,1)S(1)} %all-to-all-done._, bf16[48,896]{1,0:T(8,128)(2,1)S(1)} %bitcast.42, bf16[48,896]{1,0:T(8,128)(2,1)S(1)} %collective-permute-done.1.refs_1_, bf16[48,896]{1,0:T(8,128)(2,1)S(1)} %collective-permute-done.2.refs_2_, ...), custom_call_target="tpu_custom_call" | custom-call | tf_op jit(solution)/shard_map/pallas_call | solution.py:86
  51.9 4.7 %all-to-all-start.1 = ((bf16[8,4,48,896]{3,2,1,0:T(8,128)(2,1)}), bf16[8,4,48,896]{3,2,1,0:T(8,128)(2,1)S(1)}, u32[]{:S(2)}, u32[]{:S(2)}) async-start(bf16[8,4,48,896]{3,2,1,0:T(8,128)(2,1)} %shard_map.49), calls=%async_computation.1 | async-start | bytes 5505024 | tf_op jit(solution)/shard_map/all_to_all | solution.py:199
  56.6 0.0 copy-start
  56.6 0.1 pad_add_fusion.place_ref
  56.7 0.2 fusion.3
  56.9 26.5 %all_gather.12._.first_ref = bf16[32,4,3584]{2,1,0:T(4,128)(2,1)S(1)} all-gather(bf16[8,4,3584]{2,1,0:T(4,128)(2,1)S(1)} %get-tuple-element.10), channel_id=1, replica_groups=mesh['x'=4,'zb'=4,'zi'=4,'c'=2,'dp'=4] {'zi'}, dimensions={0}, use_global_device_ids=true | all-gather | bytes 1146880 | tf_op jit(solution)/shard_map/all_gather | solution.py:202
  83.4 19.9 %all_gather.13.second_ref = bf16[32,4,3584]{2,1,0:T(4,128)(2,1)S(1)} all-gather(bf16[8,4,3584]{2,1,0:T(4,128)(2,1)S(1)} %shard_map.47), channel_id=1, replica_groups=mesh['x'=4,'zb'=4,'zi'=4,'c'=2,'dp'=4] {'zi'}, dimensions={0}, use_global_device_ids=true | all-gather | bytes 1146880 | tf_op jit(solution)/shard_map/all_gather | solution.py:204
  103.3 0.0 copy-start.4
  103.3 0.0 copy-start.5
  103.3 0.0 collective-permute-done.other_ref
  103.3 0.0 copy-done
  103.4 3.5 %shard_map.48 = bf16[256,384]{1,0:T(8,128)(2,1)S(1)} custom-call(bf16[32,4,3584]{2,1,0:T(4,128)(2,1)S(1)} %all_gather.12._.first_ref, bf16[32,4,3584]{2,1,0:T(4,128)(2,1)S(1)} %all_gather.13.second_ref, bf16[576,3584]{1,0:T(8,128)(2,1)S(1)} %bitcast.39, bf16[576,3584]{1,0:T(8,128)(2,1)} %collective-permute-done.other_ref), custom_call_target="tpu_custom_call" | custom-call | tf_op jit(solution)/shard_map/pallas_call | solution.py:126
  106.9 17.4 %all-gather = bf16[1024,384]{1,0:T(8,128)(2,1)S(1)} all-gather(bf16[256,384]{1,0:T(8,128)(2,1)S(1)} %shard_map.48), channel_id=2, replica_groups=mesh['x'=4,'zb'=4,'zi'=4,'c'=2,'dp'=4] {'zi'}, dimensions={0}, use_global_device_ids=true | all-gather | bytes 983040 | tf_op jit(solution)/shard_map/all_gather | solution.py:206
  124.3 0.0 all-to-all-done.1
  124.3 0.0 copy-done.4
  124.3 0.0 copy-done.5
  124.3 1.7 %shard_map.50 = (bf16[16,4,4,896]{3,2,1,0:T(4,128)(2,1)S(1)}, f32[2,2,16,8]{3,2,1,0:T(8,128)S(1)}) custom-call(s32[2]{0:T(128)S(1)} %pad_add_fusion.place_ref, bf16[4,256,384]{2,1,0:T(8,128)(2,1)S(1)} %bitcast.40, bf16[4,2,4,48,896]{4,3,2,1,0:T(8,128)(2,1)S(1)} %bitcast.37, s32[2,2,8]{2,1,0:T(2,128)S(1)} %bitcast.44, f32[2,2,8]{2,1,0:T(2,128)S(1)} %bitcast.45), custom_call_target="tpu_custom_call" | custom-call | tf_op jit(solution)/shard_map/pallas_call | solution.py:164
  126.0 0.0 copy-start.2
  126.0 0.6 copy-done.2
  126.6 33.5 %all_to_all.15 = bf16[64,4,896]{2,1,0:T(4,128)(2,1)S(1)} all-to-all(bf16[64,4,896]{2,1,0:T(4,128)(2,1)S(1)} %bitcast.41), channel_id=1, replica_groups=mesh['x'=4,'zb'=4,'zi'=4,'c'=2,'dp'=4] {'x','zb','zi'}, dimensions={0} | all-to-all | bytes 917504 | tf_op jit(solution)/shard_map/all_to_all | solution.py:212
  160.1 0.2 reshape.27
  160.3 1.8 %fusion = bf16[2,8,4,896]{3,1,2,0:T(8,128)(2,1)} fusion(bf16[16,4,2,2,896]{4,3,2,1,0:T(2,128)(2,1)S(1)} %reshape.27, f32[2,2,16,8]{3,2,1,0:T(8,128)} %copy-done.2), kind=kOutput, calls=%fused_computation.1 | convolution fusion | flops 22077440 | bytes 575488 | tf_op jit(solution)/shard_map/mser,ezmsd->mrzd/dot_general | solution.py:214
  (5 shorter events, 0.1 us)
Async XLA Ops:
  0.0 103.3 %collective-permute-start = (bf16[576,3584]{1,0:T(8,128)(2,1)}, bf16[576,3584]{1,0:T(8,128)(2,1)}, u32[]{:S(2)}, u32[]{:S(2)}) collective-permute-start(bf16[576,3584]{1,0:T(8,128)(2,1)} %bitcast.38), channel_id=1, source_target_pairs={{0,4},{4,0},{1,5},{5,1},{2,6},{6,2},{3,7},{7,3},{8,12},{12,8},{9,1... | collective-permute-start | bytes 12386312 | tf_op jit(solution)/shard_map/ppermute | solution.py:23
  1.9 0.9 copy-start.1
  2.8 0.7 copy-start.3
  4.9 45.1 %all-to-all-start = ((bf16[16,4,3584]{2,1,0:T(4,128)(2,1)}), bf16[16,4,3584]{2,1,0:T(4,128)(2,1)S(1)}, u32[]{:S(2)}, u32[]{:S(2)}) async-start(bf16[16,4,3584]{2,1,0:T(4,128)(2,1)} %shard_map.46), calls=%async_computation | async-start | bytes 917504 | tf_op jit(solution)/shard_map/all_to_all | solution.py:196
  24.5 24.9 %collective-permute-start.1 = (bf16[48,896]{1,0:T(8,128)(2,1)S(1)}, bf16[48,896]{1,0:T(8,128)(2,1)S(1)}, u32[]{:S(2)}, u32[]{:S(2)}) collective-permute-start(bf16[48,896]{1,0:T(8,128)(2,1)S(1)} %bitcast.46), channel_id=1, source_target_pairs={{0,8},{8,0},{16,24},{24,16},{1,9},{9,1},{17,25},{25,17},{2,10},{10... | collective-permute-start | bytes 258056 | tf_op jit(solution)/shard_map/ppermute | solution.py:19
  27.4 22.0 %collective-permute-start.2 = (bf16[48,896]{1,0:T(8,128)(2,1)S(1)}, bf16[48,896]{1,0:T(8,128)(2,1)S(1)}, u32[]{:S(2)}, u32[]{:S(2)}) collective-permute-start(bf16[48,896]{1,0:T(8,128)(2,1)S(1)} %bitcast.47), channel_id=1, source_target_pairs={{0,16},{8,24},{16,0},{24,8},{1,17},{9,25},{17,1},{25,9},{2,18},{10... | collective-permute-start | bytes 258056 | tf_op jit(solution)/shard_map/ppermute | solution.py:19
  30.8 18.6 %collective-permute-start.3 = (bf16[48,896]{1,0:T(8,128)(2,1)S(1)}, bf16[48,896]{1,0:T(8,128)(2,1)S(1)}, u32[]{:S(2)}, u32[]{:S(2)}) collective-permute-start(bf16[48,896]{1,0:T(8,128)(2,1)S(1)} %bitcast.48), channel_id=1, source_target_pairs={{0,24},{8,16},{16,8},{24,0},{1,25},{9,17},{17,9},{25,1},{2,26},{10... | collective-permute-start | bytes 258056 | tf_op jit(solution)/shard_map/ppermute | solution.py:19
  51.9 72.4 %all-to-all-start.1 = ((bf16[8,4,48,896]{3,2,1,0:T(8,128)(2,1)}), bf16[8,4,48,896]{3,2,1,0:T(8,128)(2,1)S(1)}, u32[]{:S(2)}, u32[]{:S(2)}) async-start(bf16[8,4,48,896]{3,2,1,0:T(8,128)(2,1)} %shard_map.49), calls=%async_computation.1 | async-start | bytes 5505024 | tf_op jit(solution)/shard_map/all_to_all | solution.py:199
  56.6 46.7 %copy-start = (bf16[1,3584,576]{1,2,0:T(8,128)(2,1)S(1)}, bf16[1,3584,576]{1,2,0:T(8,128)(2,1)}, u32[]{:S(2)}) copy-start(bf16[1,3584,576]{1,2,0:T(8,128)(2,1)} %param.7) | copy-start | bytes 12386308
  103.3 20.9 %copy-start.4 = (s32[2,8,2]{1,2,0:T(2,128)S(1)}, s32[2,8,2]{1,2,0:T(2,128)}, u32[]{:S(2)}) copy-start(s32[2,8,2]{1,2,0:T(2,128)} %param.5) | copy-start | bytes 388
  103.3 20.9 %copy-start.5 = (f32[2,8,2]{1,2,0:T(2,128)S(1)}, f32[2,8,2]{1,2,0:T(2,128)}, u32[]{:S(2)}) copy-start(f32[2,8,2]{1,2,0:T(2,128)} %param.6) | copy-start | bytes 388
  126.0 0.6 copy-start.2
